TPU v7x, 32 devices: a whole 2x2x4 slice. The times are simulated.
32 devices in a mesh: ctx: 16 (over z, y, x), tp: 2 (over core).
Axes of the slice: x: 2, y: 2, z: 4, core: 2. Of those that a mesh axis runs over, the one named last changes fastest.
Arguments:
- tokens: bfloat16 [2048, 1536], P('ctx'), may hold values from -6 to 6
- w_query: bfloat16 [1536, 1536], P(None, 'tp'), may hold values from -0.15625 to 0.15625
- w_key: bfloat16 [1536, 512], P(None, 'tp'), may hold values from -0.15625 to 0.15625
- w_value: bfloat16 [1536, 512], P(None, 'tp'), may hold values from -0.15625 to 0.15625
- w_output: bfloat16 [1536, 1536], P(None, 'tp'), may hold values from -0.625 to 0.625
- w_gate: bfloat16 [1536, 6912], P(None, 'tp'), may hold values from -0.15625 to 0.15625
- w_up: bfloat16 [1536, 6912], P(None, 'tp'), may hold values from -0.15625 to 0.15625
- w_down: bfloat16 [1536, 6912], P(None, 'tp'), may hold values from -0.078125 to 0.078125
- attn_gain: float32 [1536], replicated, may hold values from 0.1 to 1.9
- mlp_gain: float32 [1536], replicated, may hold values from 0.1 to 1.9
- query_gain: float32 [64], replicated, may hold values from 0.1 to 1.9
- key_gain: float32 [64], replicated, may hold values from 0.1 to 1.9
- segments: int32 [2048], replicated, may hold values from 0 to 20, as said below
- positions: int32 [2048], P('ctx'), may hold values from 0 to 511, as said below
- cotangent: bfloat16 [2048, 1536], P('ctx'), may hold values from -6 to 6
Outputs:
- output: bfloat16 [2048, 1536], P('ctx')
- grad_tokens: bfloat16 [2048, 1536], P('ctx')
- grad_w_query: float32 [1536, 1536], P('ctx', 'tp')
- grad_w_key: float32 [1536, 512], P('ctx', 'tp')
- grad_w_value: float32 [1536, 512], P('ctx', 'tp')
- grad_w_output: float32 [1536, 1536], P('ctx', 'tp')
- grad_w_gate: float32 [1536, 6912], P('ctx', 'tp')
- grad_w_up: float32 [1536, 6912], P('ctx', 'tp')
- grad_w_down: float32 [1536, 6912], P('ctx', 'tp')
- grad_attn_gain: float32 [1536], replicated
- grad_mlp_gain: float32 [1536], replicated
- grad_query_gain: float32 [64], replicated
- grad_key_gain: float32 [64], replicated
Inputs may be any that keep to these rules, and one draw needn't show every extreme that they name: `segments`: within each sequence (in place order) documents follow one another and fill it; each has at most 512 tokens, all but the last of a sequence 51 or more; segment numbers count a sequence's documents from 0 in place order. In every draw one sequence begins with a document of exactly 512 tokens, and another holds documents numbered up to the stated most. `positions`: each token's place within its document, counted from 0, consistent with segments.
All inputs are finite; a program needn't handle non-finite values.
Results may differ from a plain program's by a relative error of at most 0.02.
Values may be sent and summed in bfloat16 or wider, within the bound.
No kernel may reach another device: no remote copies, remote signals or barrier semaphores. Data moves between devices by JAX's collectives and lax.ppermute only.
A program may use at most 448 MiB of HBM per device.

v0:
```python
import jax
import jax.numpy as jnp
from jax import lax
from jax.sharding import PartitionSpec as P

BLK = 32
SEQS = 2


EPSILON = 1e-05
ROPE_BASE = 1000000.0
MASKED = -1e30


def split_up(x, dim, count):
    shape = x.shape
    parts = x.reshape(*shape[:dim], count, shape[dim] // count, *shape[dim + 1 :])
    return jnp.moveaxis(parts, dim, 0)


def sent_and_summed(x, axis, dim):
    count = lax.axis_size(axis)
    parts = lax.all_to_all(split_up(x, dim, count), axis, 0, 0, tiled=True)
    return jnp.sum(parts.astype(jnp.float32), axis=0)


def norm_rows(values, gain):
    factor = lax.rsqrt(jnp.mean(values * values, axis=-1, keepdims=True) + EPSILON)
    return (values * factor * gain, factor)


def norm_back(values, factor, gain, grad):
    scaled = grad * gain
    inner = jnp.mean(values * scaled, axis=-1, keepdims=True)
    return factor * scaled - values * (factor * factor * factor) * inner


def rotary_tables(positions, head_width):
    half_width = head_width // 2
    freqs = ROPE_BASE ** (-2.0 * jnp.arange(half_width, dtype=jnp.float32) / head_width)
    angles = positions.astype(jnp.float32)[:, None] * freqs[None, :]
    return (jnp.cos(angles)[:, None, :], jnp.sin(angles)[:, None, :])


def rotate(values, cosine, sine):
    half_width = values.shape[-1] // 2
    first_half = values[..., :half_width]
    second_half = values[..., half_width:]
    return jnp.concatenate(
        [first_half * cosine - second_half * sine, second_half * cosine + first_half * sine],
        axis=-1,
    )


def rotate_back(grad, cosine, sine):
    half_width = grad.shape[-1] // 2
    first_half = grad[..., :half_width]
    second_half = grad[..., half_width:]
    return jnp.concatenate(
        [first_half * cosine + second_half * sine, second_half * cosine - first_half * sine],
        axis=-1,
    )


def contract_last(left_side, right_side):
    return lax.dot_general(
        left_side, right_side, (((1,), (1,)), ((), ())), preferred_element_type=jnp.float32
    )


def block_place(half_index, device_index, offset, pair_count):
    return (
        jnp.where(half_index == 0, device_index, 2 * pair_count - 1 - device_index) * BLK + offset
    )


def weight_terms(pairs):
    pieces_out = []
    for left_side, right_side in pairs:
        pieces_out.append(
            lax.dot_general(
                left_side, right_side, (((0,), (0,)), ((), ())), preferred_element_type=jnp.float32
            )
        )
    return jnp.concatenate(pieces_out, axis=1)


def split_columns(joined, widths):
    result = []
    offset = 0
    for column_count in widths:
        result.append(joined[:, offset : offset + column_count])
        offset = offset + column_count
    return result


def shards(
    tokens,
    w_query,
    w_key,
    w_value,
    w_output,
    w_gate,
    w_up,
    w_down,
    attn_gain,
    mlp_gain,
    query_gain,
    key_gain,
    segments,
    positions,
    cotangent,
):
    pair_count = lax.axis_size("ctx")
    ctx_index = lax.axis_index("ctx")
    head_dim = query_gain.shape[0]
    rows_dev = tokens.shape[0]
    q_heads = w_query.shape[1] // head_dim
    kv_heads = w_key.shape[1] // head_dim
    group_size = q_heads // kv_heads
    pair_rows = 2 * BLK
    score_scale = head_dim ** (-0.5)
    kv_width = kv_heads * head_dim
    seg_keys = (
        segments.reshape(pair_count, SEQS, pair_rows)
        .transpose(1, 0, 2)
        .reshape(SEQS, pair_count * pair_rows)
    )
    seg_query = lax.dynamic_slice_in_dim(seg_keys, ctx_index * pair_rows, pair_rows, 1)
    offsets = jnp.arange(pair_rows, dtype=jnp.int32)
    query_place = block_place(offsets // BLK, ctx_index, offsets % BLK, pair_count)

    def visible(row_count):
        key_rows = jnp.arange(row_count, dtype=jnp.int32)
        within = key_rows % pair_rows
        key_place = block_place(within // BLK, key_rows // pair_rows, within % BLK, pair_count)
        same_doc = seg_query[:, :, None] == seg_keys[:, None, :]
        causal = key_place[None, None, :] <= query_place[None, :, None]
        return (same_doc & causal)[:, None, None]

    hidden_in = tokens.astype(jnp.float32)
    normed_one, factor_one = norm_rows(hidden_in, attn_gain)
    input_low = normed_one.astype(jnp.bfloat16)
    cosine, sine = rotary_tables(positions, head_dim)
    query_raw = jnp.dot(input_low, w_query, preferred_element_type=jnp.float32).reshape(
        rows_dev, q_heads, head_dim
    )
    query_normed, query_factor = norm_rows(query_raw, query_gain)
    queries = rotate(query_normed, cosine, sine).astype(jnp.bfloat16)
    key_raw = jnp.dot(input_low, w_key, preferred_element_type=jnp.float32).reshape(
        rows_dev, kv_heads, head_dim
    )
    key_normed, key_factor = norm_rows(key_raw, key_gain)
    keys_low = rotate(key_normed, cosine, sine).astype(jnp.bfloat16)
    values_low = jnp.dot(input_low, w_value, preferred_element_type=jnp.float32).astype(
        jnp.bfloat16
    )
    packed = jnp.concatenate([keys_low.reshape(rows_dev, kv_width), values_low], axis=1).reshape(
        SEQS, pair_rows, 2 * kv_width
    )
    query_seq = queries.reshape(SEQS, pair_rows, kv_heads, group_size, head_dim)
    stat_shape = (SEQS, kv_heads, group_size, pair_rows)
    incoming = lax.all_gather(packed, "ctx", axis=1, tiled=True)
    running_max = jnp.full(stat_shape, MASKED, jnp.float32)
    row_count = incoming.shape[1]
    key_piece = incoming[:, :, :kv_width].reshape(SEQS, row_count, kv_heads, head_dim)
    value_piece = incoming[:, :, kv_width:].reshape(SEQS, row_count, kv_heads, head_dim)
    visible_mask = visible(row_count)
    scores = (
        jnp.einsum("sqkgd,srkd->skgqr", query_seq, key_piece, preferred_element_type=jnp.float32)
        * score_scale
    )
    scores = jnp.where(visible_mask, scores, MASKED)
    new_max = jnp.maximum(running_max, jnp.max(scores, axis=-1))
    weights = jnp.where(visible_mask, jnp.exp(scores - new_max[..., None]), 0.0)
    running_sum = jnp.sum(weights, axis=-1)
    running_out = jnp.einsum(
        "skgqr,srkd->skgqd",
        weights.astype(jnp.bfloat16),
        value_piece,
        preferred_element_type=jnp.float32,
    )
    folded = (new_max, running_sum, running_out)
    run_max, run_sum, run_out = folded
    attn_f32 = run_out / run_sum[..., None]
    log_total = run_max + jnp.log(run_sum)
    attn_low = (
        attn_f32.transpose(0, 3, 1, 2, 4).reshape(rows_dev, q_heads * head_dim).astype(jnp.bfloat16)
    )
    branch_sum = lax.psum(contract_last(attn_low, w_output).astype(jnp.bfloat16), "tp").astype(
        jnp.float32
    )
    middle = hidden_in + branch_sum
    normed_two, factor_two = norm_rows(middle, mlp_gain)
    mlp_low = normed_two.astype(jnp.bfloat16)
    gate_pre = jnp.dot(mlp_low, w_gate, preferred_element_type=jnp.float32)
    up_pre = jnp.dot(mlp_low, w_up, preferred_element_type=jnp.float32)
    gate_sigmoid = jax.nn.sigmoid(gate_pre)
    silu_gate = gate_pre * gate_sigmoid
    activation = (silu_gate * up_pre).astype(jnp.bfloat16)
    down_sum = lax.psum(contract_last(activation, w_down).astype(jnp.bfloat16), "tp").astype(
        jnp.float32
    )
    output = (middle + down_sum).astype(jnp.bfloat16)
    grad_act = jnp.dot(cotangent, w_down, preferred_element_type=jnp.float32)
    silu_slope = gate_sigmoid * (1.0 + gate_pre * (1.0 - gate_sigmoid))
    grad_gate = (grad_act * up_pre * silu_slope).astype(jnp.bfloat16)
    grad_up = (grad_act * silu_gate).astype(jnp.bfloat16)
    mlp_pairs = ((mlp_low, grad_gate), (mlp_low, grad_up), (cotangent, activation))
    mlp_widths = [w_gate.shape[1], w_up.shape[1], w_down.shape[1]]
    mlp_in_part = contract_last(grad_gate, w_gate) + contract_last(grad_up, w_up)
    mlp_gain_part = jnp.sum(mlp_in_part * middle * factor_two, axis=0)
    mlp_in = lax.psum(mlp_in_part.astype(jnp.bfloat16), "tp").astype(jnp.float32)
    grad_middle = cotangent.astype(jnp.float32) + norm_back(middle, factor_two, mlp_gain, mlp_in)
    grad_branch = grad_middle.astype(jnp.bfloat16)
    grad_attn = jnp.dot(grad_branch, w_output, preferred_element_type=jnp.float32).astype(
        jnp.bfloat16
    )
    grad_seq = grad_attn.reshape(SEQS, pair_rows, kv_heads, group_size, head_dim)
    row_delta = jnp.sum(grad_seq.astype(jnp.float32).transpose(0, 2, 3, 1, 4) * attn_f32, axis=-1)
    incoming = lax.all_gather(packed, "ctx", axis=1, tiled=True)
    row_count = incoming.shape[1]
    key_piece = incoming[:, :, :kv_width].reshape(SEQS, row_count, kv_heads, head_dim)
    value_piece = incoming[:, :, kv_width:].reshape(SEQS, row_count, kv_heads, head_dim)
    visible_mask = visible(row_count)
    scores = (
        jnp.einsum("sqkgd,srkd->skgqr", query_seq, key_piece, preferred_element_type=jnp.float32)
        * score_scale
    )
    weights = jnp.where(visible_mask, jnp.exp(scores - log_total[..., None]), 0.0)
    grad_weights = jnp.einsum(
        "sqkgd,srkd->skgqr", grad_seq, value_piece, preferred_element_type=jnp.float32
    )
    grad_scores = (weights * (grad_weights - row_delta[..., None])).astype(jnp.bfloat16)
    grad_query = score_scale * jnp.einsum(
        "skgqr,srkd->skgqd", grad_scores, key_piece, preferred_element_type=jnp.float32
    )
    key_term = score_scale * jnp.einsum(
        "skgqr,sqkgd->srkd", grad_scores, query_seq, preferred_element_type=jnp.float32
    )
    value_term = jnp.einsum(
        "skgqr,sqkgd->srkd",
        weights.astype(jnp.bfloat16),
        grad_seq,
        preferred_element_type=jnp.float32,
    )
    block_grad = jnp.concatenate(
        [
            key_term.reshape(SEQS, row_count, kv_width),
            value_term.reshape(SEQS, row_count, kv_width),
        ],
        axis=-1,
    )
    grad_kv = sent_and_summed(block_grad.astype(jnp.bfloat16), "ctx", 1).reshape(
        rows_dev, 2 * kv_width
    )
    grad_q_rows = grad_query.transpose(0, 3, 1, 2, 4).reshape(rows_dev, q_heads, head_dim)
    grad_q_normed = rotate_back(grad_q_rows, cosine, sine)
    query_gain_part = jnp.sum(grad_q_normed * query_raw * query_factor, axis=(0, 1))
    grad_q_low = (
        norm_back(query_raw, query_factor, query_gain, grad_q_normed)
        .reshape(rows_dev, q_heads * head_dim)
        .astype(jnp.bfloat16)
    )
    grad_k_normed = rotate_back(
        grad_kv[:, :kv_width].reshape(rows_dev, kv_heads, head_dim), cosine, sine
    )
    key_gain_part = jnp.sum(grad_k_normed * key_raw * key_factor, axis=(0, 1))
    grad_k_low = (
        norm_back(key_raw, key_factor, key_gain, grad_k_normed)
        .reshape(rows_dev, kv_width)
        .astype(jnp.bfloat16)
    )
    grad_v_low = grad_kv[:, kv_width:].astype(jnp.bfloat16)
    attn_pairs = (
        (input_low, grad_q_low),
        (input_low, grad_k_low),
        (input_low, grad_v_low),
        (grad_branch, attn_low),
    )
    attn_widths = [w_query.shape[1], w_key.shape[1], w_value.shape[1], w_output.shape[1]]
    all_grads = split_columns(
        lax.psum_scatter(
            weight_terms(attn_pairs + mlp_pairs), "ctx", scatter_dimension=0, tiled=True
        ),
        attn_widths + mlp_widths,
    )
    attn_grads = all_grads[:4]
    mlp_grads = all_grads[4:]
    attn_in_part = (
        contract_last(grad_q_low, w_query)
        + contract_last(grad_k_low, w_key)
        + contract_last(grad_v_low, w_value)
    )
    attn_gain_part = jnp.sum(attn_in_part * hidden_in * factor_one, axis=0)
    attn_in = lax.psum(attn_in_part.astype(jnp.bfloat16), "tp").astype(jnp.float32)
    grad_tokens = (grad_middle + norm_back(hidden_in, factor_one, attn_gain, attn_in)).astype(
        jnp.bfloat16
    )
    gain_sums = lax.psum(
        (attn_gain_part, mlp_gain_part, query_gain_part, key_gain_part), ("ctx", "tp")
    )
    return (
        output,
        grad_tokens,
        attn_grads[0],
        attn_grads[1],
        attn_grads[2],
        attn_grads[3],
        mlp_grads[0],
        mlp_grads[1],
        mlp_grads[2],
        gain_sums[0],
        gain_sums[1],
        gain_sums[2],
        gain_sums[3],
    )


def solution(mesh):
    in_specs = (
        P("ctx", None),
        P(None, "tp"),
        P(None, "tp"),
        P(None, "tp"),
        P(None, "tp"),
        P(None, "tp"),
        P(None, "tp"),
        P(None, "tp"),
        P(),
        P(),
        P(),
        P(),
        P(),
        P("ctx"),
        P("ctx", None),
    )
    out_specs = (
        P("ctx", None),
        P("ctx", None),
        P("ctx", "tp"),
        P("ctx", "tp"),
        P("ctx", "tp"),
        P("ctx", "tp"),
        P("ctx", "tp"),
        P("ctx", "tp"),
        P("ctx", "tp"),
        P(),
        P(),
        P(),
        P(),
    )
    return jax.shard_map(shards, mesh=mesh, in_specs=in_specs, out_specs=out_specs, check_vma=False)
```

profile of v0, /device:TPU:0, one launch (start us, length us, event | category | flops | bytes accessed | tf_op | source)
XLA Modules:
  0.0 1406.0 jit_solution(643129345085903225)
XLA Ops:
  28.5 50.6 %all-gather.2.cloned.1.call-done = bf16[2,1024,512]{2,1,0:T(8,128)(2,1)} async-done(((bf16[2,64,512]{2,1,0:T(8,128)(2,1)}), bf16[2,1024,512]{2,1,0:T(8,128)(2,1)}) %all-gather.2.cloned.1.call-update) | async-done | bytes 2097168 | tf_op jit(solution)/shard_map/all_gather | solution.py:163
  79.1 3.0 fusion.76
  84.4 5.1 fusion.4
  92.5 4.3 fusion.6
  97.2 4.1 fusion.37
  103.8 17.0 %all-reduce.6.cloned.1.call-done = bf16[128,1536]{1,0:T(8,128)(2,1)} async-done(((bf16[128,1536]{1,0:T(8,128)(2,1)}), bf16[128,1536]{1,0:T(8,128)(2,1)}) %all-reduce.6.cloned.1.call-update) | async-done | bytes 393232 | tf_op jit(solution)/shard_map/psum | solution.py:190
  123.7 5.8 fusion.79
  129.6 5.8 fusion.80
  135.4 3.1 multiply_convert_fusion
  138.6 3.5 fusion.81
  142.0 8.6 fusion.77
  152.0 18.5 %all-reduce.8.cloned.1.call-done = bf16[128,1536]{1,0:T(8,128)(2,1)} async-done(((bf16[128,1536]{1,0:T(8,128)(2,1)}), bf16[128,1536]{1,0:T(8,128)(2,1)}) %all-reduce.8.cloned.1.call-update) | async-done | bytes 393232 | tf_op jit(solution)/shard_map/psum | solution.py:213
  179.4 5.2 fusion.21
  184.6 5.5 fusion.1
  190.0 2.9 concatenate.50
  193.0 4.2 fusion.24
  197.2 4.0 concatenate.49
  201.2 4.4 maximum_bitcast_fusion
  205.6 5.6 copy.156
  211.2 6.8 all-to-all-start
  222.8 8.4 convolution_convert_fusion
  231.2 3.2 fusion.25
  250.6 4.0 convolution_dynamic-update-slice_fusion.3
  254.5 6.8 all-to-all-done
  273.5 3.8 convolution_dynamic-update-slice_fusion.2
  277.4 8.7 convolution_dynamic-update-slice_fusion.1
  286.1 8.9 convolution_dynamic-update-slice_fusion
  296.7 8.8 bitcast_dynamic-update-slice_fusion
  306.4 14.5 %all-reduce.10.cloned.1.call-done = (bf16[128,1536]{1,0:T(8,128)(2,1)}, bf16[128,1536]{1,0:T(8,128)(2,1)}) async-done(((bf16[128,1536]{1,0:T(8,128)(2,1)}, bf16[128,1536]{1,0:T(8,128)(2,1)}), (bf16[128,1536]{1,0:T(8,128)(2,1)}, bf16[128,1536]{1,0:T(8,128)(2,1)})) %all-reduce.10.cloned.1.call-update) | async-done | bytes 786448 | tf_op jit(solution)/shard_map/psum | solution.py:201
  322.1 44.3 %all-reduce = (f32[1536]{0:T(1024)}, f32[1536]{0:T(1024)}, f32[64]{0:T(128)}, f32[64]{0:T(128)}) all-reduce(f32[1536]{0:T(1024)S(1)} %get-tuple-element.15, f32[1536]{0:T(1024)S(1)} %copy-done.43, f32[64]{0:T(128)S(1)} %reduce_sum.164, f32[64]{0:T(128)S(1)} %reduce_sum.167), channel_id=1, replica_groups=mesh['ctx'=16,'tp'=2] {'ctx','tp'}, use_global_device_ids=true, to_apply=%region_18.19 | all-reduce | flops 3200 | bytes 25600 | tf_op jit(solution)/shard_map/psum | solution.py:300
  369.4 1022.0 %reduce-scatter.2.cloned.1.call-done = f32[96,12416]{1,0:T(8,128)} async-done(((f32[1536,12416]{1,0:T(8,128)}), f32[96,12416]{1,0:T(8,128)}) %reduce-scatter.2.cloned.1.call-update) | async-done | bytes 4767760 | tf_op jit(solution)/shard_map/reduce_scatter | solution.py:283
  1391.4 4.1 fusion.73
  (239 shorter events, 85.6 us)
Async XLA Ops:
  7.2 94.7 %copy-start = (bf16[1536,768]{1,0:T(8,128)(2,1)S(1)}, bf16[1536,768]{1,0:T(8,128)(2,1)}, u32[]{:S(2)}) copy-start(bf16[1536,768]{1,0:T(8,128)(2,1)} %param.19) | copy-start | bytes 7077892
  7.2 71.9 %all-gather.2.cloned.1.call-start = ((), (), s32[]{:S(2)}) async-start(), calls=%async_computation.2 | async-start | bytes 2228224 | tf_op jit(solution)/shard_map/all_gather | solution.py:163
  15.6 105.1 %all-reduce.6.cloned.1.call-start = ((), (), s32[]{:S(2)}) async-start(), calls=%async_computation.3 | async-start | bytes 786432 | tf_op jit(solution)/shard_map/psum | solution.py:190
  18.2 71.3 %copy-start.6 = (f32[128,768]{0,1:T(8,128)}, f32[128,768]{0,1:T(8,128)S(1)}, u32[]{:S(2)}) copy-start(f32[128,768]{0,1:T(8,128)S(1)} %copy.141) | copy-start | bytes 1179652
  19.9 69.6 %copy-start.12 = (bf16[2,64,4,3,32]{4,1,3,2,0:T(8,128)(2,1)}, bf16[2,64,4,3,32]{4,1,3,2,0:T(8,128)(2,1)S(1)}, u32[]{:S(2)}) copy-start(bf16[2,64,4,3,32]{4,1,3,2,0:T(8,128)(2,1)S(1)} %copy.142) | copy-start | bytes 294916
  21.9 67.6 %copy-start.13 = (bf16[2,64,4,3,32]{4,1,3,2,0:T(8,128)(2,1)}, bf16[2,64,4,3,32]{4,1,3,2,0:T(8,128)(2,1)S(1)}, u32[]{:S(2)}) copy-start(bf16[2,64,4,3,32]{4,1,3,2,0:T(8,128)(2,1)S(1)} %copy.143) | copy-start | bytes 294916
  97.2 23.6 %copy-start.2 = (bf16[128,1536]{1,0:T(8,128)(2,1)S(1)}, bf16[128,1536]{1,0:T(8,128)(2,1)}, u32[]{:S(2)}) copy-start(bf16[128,1536]{1,0:T(8,128)(2,1)} %param.15) | copy-start | bytes 1179652
  97.2 25.4 %copy-start.38 = (f32[1536]{0:T(1024)S(1)}, f32[1536]{0:T(1024)}, u32[]{:S(2)}) copy-start(f32[1536]{0:T(1024)} %param.24) | copy-start | bytes 18436
  101.9 20.7 %copy-start.23 = (bf16[128,768]{0,1:T(8,128)(2,1)}, bf16[128,768]{0,1:T(8,128)(2,1)S(1)}, u32[]{:S(2)}) copy-start(bf16[128,768]{0,1:T(8,128)(2,1)S(1)} %convert_element_type.106) | copy-start | bytes 589828
  103.5 66.9 %all-reduce.8.cloned.1.call-start = ((), (), s32[]{:S(2)}) async-start(), calls=%async_computation.4 | async-start | bytes 786432 | tf_op jit(solution)/shard_map/psum | solution.py:213
  142.0 28.4 %copy-start.4 = (bf16[128,1536]{1,0:T(8,128)(2,1)S(1)}, bf16[128,1536]{1,0:T(8,128)(2,1)}, u32[]{:S(2)}) copy-start(bf16[128,1536]{1,0:T(8,128)(2,1)} %all-reduce.6.cloned.1.call-done) | copy-start | bytes 1179652
  205.6 15.1 %copy-start.46 = (f32[128,4]{0,1:T(4,128)S(1)}, f32[128,4]{0,1:T(4,128)}, u32[]{:S(2)}) copy-start(f32[128,4]{0,1:T(4,128)} %copy-done.45) | copy-start | bytes 6148
  205.6 15.8 %copy-start.54 = (f32[128,4]{0,1:T(4,128)S(1)}, f32[128,4]{0,1:T(4,128)}, u32[]{:S(2)}) copy-start(f32[128,4]{0,1:T(4,128)} %get-tuple-element.55) | copy-start | bytes 6148
  205.6 16.6 %copy-start.55 = (f32[64]{0:T(128)S(1)}, f32[64]{0:T(128)}, u32[]{:S(2)}) copy-start(f32[64]{0:T(128)} %param.26) | copy-start | bytes 772
  205.6 17.2 %copy-start.7 = (bf16[128,3456]{1,0:T(8,128)(2,1)S(1)}, bf16[128,3456]{1,0:T(8,128)(2,1)}, u32[]{:S(2)}) copy-start(bf16[128,3456]{1,0:T(8,128)(2,1)} %get-tuple-element.32) | copy-start | bytes 2654212
  211.2 50.1 %all-to-all-start = ((bf16[16,2,64,512]{3,2,1,0:T(8,128)(2,1)}), bf16[16,2,64,512]{3,2,1,0:T(8,128)(2,1)}, u32[]{:S(2)}, u32[]{:S(2)}) async-start(bf16[16,2,64,512]{3,2,1,0:T(8,128)(2,1)} %copy.156), calls=%async_computation | async-start | bytes 4194304 | tf_op jit(solution)/shard_map/all_to_all | solution.py:23
  218.0 102.9 %all-reduce.10.cloned.1.call-start = ((), (), s32[]{:S(2)}) async-start(), calls=%async_computation.6 | async-start | bytes 1572864 | tf_op jit(solution)/shard_map/psum | solution.py:201
  231.2 17.5 %copy-start.5 = (bf16[1536,768]{1,0:T(8,128)(2,1)S(1)}, bf16[1536,768]{1,0:T(8,128)(2,1)}, u32[]{:S(2)}) copy-start(bf16[1536,768]{1,0:T(8,128)(2,1)} %param.16) | copy-start | bytes 7077892
  250.5 19.5 %copy-start.34 = (f32[1536]{0:T(1024)S(1)}, f32[1536]{0:T(1024)}, u32[]{:S(2)}) copy-start(f32[1536]{0:T(1024)} %param.23) | copy-start | bytes 18436
  250.5 19.5 %copy-start.48 = (f32[128]{0:T(128)S(1)}, f32[128]{0:T(128)}, u32[]{:S(2)}) copy-start(f32[128]{0:T(128)} %copy-done.47) | copy-start | bytes 1540
  250.5 23.0 %copy-start.10 = (bf16[128,1536]{1,0:T(8,128)(2,1)S(1)}, bf16[128,1536]{1,0:T(8,128)(2,1)}, u32[]{:S(2)}) copy-start(bf16[128,1536]{1,0:T(8,128)(2,1)} %param.29) | copy-start | bytes 1179652
  250.5 23.0 %copy-start.14 = (bf16[128,1536]{1,0:T(8,128)(2,1)S(1)}, bf16[128,1536]{1,0:T(8,128)(2,1)}, u32[]{:S(2)}) copy-start(bf16[128,1536]{1,0:T(8,128)(2,1)} %all-reduce.8.cloned.1.call-done) | copy-start | bytes 1179652
  250.5 23.0 %copy-start.24 = (bf16[128,768]{0,1:T(8,128)(2,1)S(1)}, bf16[128,768]{0,1:T(8,128)(2,1)}, u32[]{:S(2)}) copy-start(bf16[128,768]{0,1:T(8,128)(2,1)} %copy-done.23) | copy-start | bytes 589828
  250.6 22.9 %copy-start.39 = (f32[1536]{0:T(1024)S(1)}, f32[1536]{0:T(1024)}, u32[]{:S(2)}) copy-start(f32[1536]{0:T(1024)} %param.24) | copy-start | bytes 18436
  250.6 22.9 %copy-start.53 = (f32[128]{0:T(128)S(1)}, f32[128]{0:T(128)}, u32[]{:S(2)}) copy-start(f32[128]{0:T(128)} %copy-done.52) | copy-start | bytes 1540
  296.6 1094.7 %reduce-scatter.2.cloned.1.call-start = ((), (), s32[]{:S(2)}) async-start(), calls=%async_computation.5 | async-start | bytes 81051648 | tf_op jit(solution)/shard_map/reduce_scatter | solution.py:283
  305.5 15.4 %copy-start.35 = (f32[1536]{0:T(1024)S(1)}, f32[1536]{0:T(1024)}, u32[]{:S(2)}) copy-start(f32[1536]{0:T(1024)} %param.23) | copy-start | bytes 18436
  305.5 15.4 %copy-start.49 = (f32[128]{0:T(128)S(1)}, f32[128]{0:T(128)}, u32[]{:S(2)}) copy-start(f32[128]{0:T(128)} %copy-done.47) | copy-start | bytes 1540
  305.5 16.7 %copy-start.43 = (f32[1536]{0:T(1024)S(1)}, f32[1536]{0:T(1024)}, u32[]{:S(2)}) copy-start(f32[1536]{0:T(1024)} %get-tuple-element.13) | copy-start | bytes 18436
  305.5 61.0 %copy-start.11 = (bf16[128,1536]{1,0:T(8,128)(2,1)S(1)}, bf16[128,1536]{1,0:T(8,128)(2,1)}, u32[]{:S(2)}) copy-start(bf16[128,1536]{1,0:T(8,128)(2,1)} %param.29) | copy-start | bytes 1179652
  305.5 61.0 %copy-start.40 = (f32[1536]{0:T(1024)S(1)}, f32[1536]{0:T(1024)}, u32[]{:S(2)}) copy-start(f32[1536]{0:T(1024)} %param.24) | copy-start | bytes 18436
  366.4 1032.6 %copy-start.1 = (bf16[1536,768]{1,0:T(8,128)(2,1)S(1)}, bf16[1536,768]{1,0:T(8,128)(2,1)}, u32[]{:S(2)}) copy-start(bf16[1536,768]{1,0:T(8,128)(2,1)} %param.19) | copy-start | bytes 7077892
  (40 other events, 288.1 us)
Sparse Core Ops, SparseCore 0:
  15.7 63.3 all-gather.1
  103.7 17.0 all-reduce.5
  150.8 19.6 all-reduce.7
  296.7 24.1 all-reduce.9
  327.8 1063.4 reduce-scatter.1
where the time goes:
time: 1410 us
  waiting for transfers between devices  1130 us (80%)
  matrix products  113 us (8%)
  local copies, waits for them, and re-layouts  58.5 us (4%)
  blocking collectives  44.3 us (3%)
  other arithmetic  38.5 us (3%)
  between operations  15 us (1%)
    reduce_scatter x1, waiting for transfers between devices, shards(): lax.psum_scatter(weight_terms(attn_pairs + mlp_pairs), 'ctx', scatter_dim...  1020 us
    all_gather x1, waiting for transfers between devices, shards(): incoming = lax.all_gather(packed, 'ctx', axis=1, tiled=True)  50.6 us
    psum x1, blocking collectives, shards(): lax.psum((attn_gain_part, mlp_gain_part, query_gain_part, key_gain_part),...  44.3 us
    dot_general x7, matrix products, weight_terms(): lax.dot_general(left_side, right_side, (((0,), (0,)), ((), ())), preferre...  37.6 us
  transfers between devices with their start and end apart: 6, of which 6 were waited for; matrix products, arithmetic and copies ran while one was open for 4% of the time, Pallas kernels for 0%

commit v1 on v0

v1 whole, which is shorter than its diff:
```python
import functools

import jax
import jax.numpy as jnp
from jax import lax
from jax.experimental import pallas as pl
from jax.experimental.pallas import tpu as pltpu
from jax.sharding import PartitionSpec as P

BLK = 32
SEQS = 2
EPSILON = 1e-05
ROPE_BASE = 1000000.0
MASKED = -1e30
F32 = jnp.float32
BF16 = jnp.bfloat16
VMEM_LIMIT = 56 * 1024 * 1024


def dot(left, right):
    return jnp.dot(left, right, preferred_element_type=F32)


def contract_last(left, right):
    return lax.dot_general(left, right, (((1,), (1,)), ((), ())), preferred_element_type=F32)


def permutes(count):
    nz = count // 4

    def shift(step):
        return [(i, ((i // 4 + step) % nz) * 4 + i % 4) for i in range(count)]

    flips = {j: [(i, i ^ j) for i in range(count)] for j in (1, 2, 3)}
    return nz, shift, flips


def send(value, pairs):
    return lax.ppermute(value, "ctx", pairs)


def swap_cores(value):
    return lax.ppermute(value, "tp", [(0, 1), (1, 0)])


def core_sum(part):
    low = lax.reduce_precision(part, exponent_bits=8, mantissa_bits=7)
    return low + swap_cores(low.astype(BF16)).astype(F32)


def relative_owner(ctx_index, count, j, step):
    nz = count // 4
    z = (ctx_index // 4 - step + nz) % nz
    return z * 4 + ((ctx_index % 4) ^ j)


def relative_rows(array, ctx_index, count, j):
    rows = array.shape[0] // count
    return jnp.concatenate(
        [
            lax.dynamic_slice_in_dim(array, relative_owner(ctx_index, count, j, s) * rows, rows, 0)
            for s in range(count // 4)
        ],
        axis=0,
    )


def gather_all(block, count):
    nz, shift, flips = permutes(count)
    near = [send(block, flips[j]) for j in (1, 2, 3)]
    column = jnp.concatenate([send(block, shift(s)) for s in range(1, nz)], axis=0)
    far = [send(column, flips[j]) for j in (1, 2, 3)]
    pieces = [block, column]
    for a, b in zip(near, far):
        pieces += [a, b]
    return jnp.concatenate(pieces, axis=0)


def gather_plane(block, count):
    nz, shift, flips = permutes(count)
    near = send(block, flips[2])
    column = jnp.concatenate([send(block, shift(s)) for s in range(1, nz)], axis=0)
    far = send(column, flips[2])
    return jnp.concatenate([block, near, column, far], axis=0)


def scatter_sum(parts, count):
    nz, shift, flips = permutes(count)
    total = parts[0].astype(F32)
    for j in (1, 2, 3):
        total = total + send(parts[j], flips[j]).astype(F32)
    low = total.astype(BF16).reshape(nz, -1, parts[0].shape[1])
    result = low[0].astype(F32)
    for s in range(1, nz):
        result = result + send(low[s], shift(nz - s)).astype(F32)
    return result


def sum_everywhere(value, count):
    value = value + swap_cores(value)
    bit = 1
    while bit < count:
        value = value + send(value, [(i, i ^ bit) for i in range(count)])
        bit *= 2
    return value


def cost(flops, bytes_accessed, transcendentals=0):
    return pl.CostEstimate(
        flops=int(flops), bytes_accessed=int(bytes_accessed), transcendentals=int(transcendentals)
    )


def mask_bias(seg_q, place_q, seg_k, place_k):
    return jnp.where((seg_k == seg_q) & (place_k <= place_q), 0.0, MASKED)


def attention_forward_kernel(q_ref, kv_ref, sq_ref, pq_ref, sk_ref, pk_ref, o_ref, lse_ref):
    keys = kv_ref.shape[0] * kv_ref.shape[2]
    width = kv_ref.shape[3] // 2
    heads = q_ref.shape[1]
    head = width // heads
    k = kv_ref[:, 0, :, :width].reshape(keys, width)
    v_t = kv_ref[:, 0, :, width:].reshape(keys, width).T
    bias = mask_bias(sq_ref[0], pq_ref[...], sk_ref[0], pk_ref[...])
    for h in range(heads):
        s = contract_last(k, q_ref[0, h]) + bias
        top = jnp.max(s, axis=0, keepdims=True)
        p = jnp.exp(s - top)
        total = jnp.sum(p, axis=0, keepdims=True)
        o = dot(v_t[h * head : (h + 1) * head], p.astype(BF16))
        o_ref[0, h] = o / total
        lse_ref[0, h] = top + jnp.log(total)


def attention_backward_kernel(
    q_ref, do_ref, kv_ref, lse_ref, sq_ref, pq_ref, sk_ref, pk_ref, dq_ref, dkv_ref
):
    count, _, rows, both = kv_ref.shape
    keys = count * rows
    width = both // 2
    heads = q_ref.shape[1]
    head = width // heads
    k = kv_ref[:, 0, :, :width].reshape(keys, width)
    v = kv_ref[:, 0, :, width:].reshape(keys, width)
    k_t = k.T
    bias = mask_bias(sq_ref[0], pq_ref[...], sk_ref[0], pk_ref[...])
    dk = jnp.zeros((keys, width), F32)
    dv = jnp.zeros((keys, width), F32)
    for h in range(heads):
        q = q_ref[0, h]
        do = do_ref[0, h]
        p = jnp.exp(contract_last(k, q) + (bias - lse_ref[0, h]))
        dp = contract_last(v, do)
        delta = jnp.sum(p * dp, axis=0, keepdims=True)
        ds = (p * (dp - delta)).astype(BF16)
        dv = dv + dot(p.astype(BF16), do)
        dk = dk + dot(ds, q)
        dq_ref[0, h] = dot(k_t[h * head : (h + 1) * head], ds)
    dkv_ref[:, 0, :, :width] = dk.astype(BF16).reshape(count, rows, width)
    dkv_ref[:, 0, :, width:] = dv.astype(BF16).reshape(count, rows, width)


def whole_block(array):
    return pl.BlockSpec(array.shape, lambda *_: (0,) * array.ndim)


def seq_block(array, dim=0):
    shape = tuple(1 if d == dim else n for d, n in enumerate(array.shape))
    return pl.BlockSpec(shape, lambda s: tuple(s if d == dim else 0 for d in range(array.ndim)))


def attention_forward(q_wide, kv, seg_q, place_q, seg_k, place_k):
    seqs, heads, lanes, width = q_wide.shape
    keys = kv.shape[0] * kv.shape[2]
    head = width // heads
    out_shape = (
        jax.ShapeDtypeStruct((seqs, heads, head, lanes), F32),
        jax.ShapeDtypeStruct((seqs, heads, 1, lanes), F32),
    )
    work = seqs * heads * keys * lanes
    return pl.pallas_call(
        attention_forward_kernel,
        grid=(seqs,),
        in_specs=[
            seq_block(q_wide),
            seq_block(kv, 1),
            seq_block(seg_q),
            whole_block(place_q),
            seq_block(seg_k),
            whole_block(place_k),
        ],
        out_specs=[seq_block(o) for o in out_shape],
        out_shape=out_shape,
        compiler_params=pltpu.CompilerParams(vmem_limit_bytes=VMEM_LIMIT),
        cost_estimate=cost(4 * work * width, 2 * kv.size, work),
        name="attention_forward",
    )(q_wide, kv, seg_q, place_q, seg_k, place_k)


def attention_backward(q_wide, do_wide, kv, lse, seg_q, place_q, seg_k, place_k):
    seqs, heads, lanes, width = q_wide.shape
    keys = kv.shape[0] * kv.shape[2]
    head = width // heads
    out_shape = (
        jax.ShapeDtypeStruct((seqs, heads, head, lanes), F32),
        jax.ShapeDtypeStruct(kv.shape, BF16),
    )
    work = seqs * heads * keys * lanes
    return pl.pallas_call(
        attention_backward_kernel,
        grid=(seqs,),
        in_specs=[
            seq_block(q_wide),
            seq_block(do_wide),
            seq_block(kv, 1),
            seq_block(lse),
            seq_block(seg_q),
            whole_block(place_q),
            seq_block(seg_k),
            whole_block(place_k),
        ],
        out_specs=[seq_block(out_shape[0]), seq_block(out_shape[1], 1)],
        out_shape=out_shape,
        compiler_params=pltpu.CompilerParams(vmem_limit_bytes=VMEM_LIMIT),
        cost_estimate=cost(10 * work * width, 4 * kv.size, work),
        name="attention_backward",
    )(q_wide, do_wide, kv, lse, seg_q, place_q, seg_k, place_k)


def hidden_terms(h2, g, w_gate, w_up, w_down):
    gate = dot(h2, w_gate)
    up = dot(h2, w_up)
    da = dot(g, w_down)
    sg = jax.nn.sigmoid(gate)
    silu = gate * sg
    act = (silu * up).astype(BF16)
    dgate = (da * up * (sg * (1.0 + gate * (1.0 - sg)))).astype(BF16)
    dup = (da * silu).astype(BF16)
    return act, dgate, dup


def own_mlp_kernel(h2_ref, g_ref, wg_ref, wu_ref, wd_ref, down_ref, dh_ref):
    wg, wu, wd = wg_ref[...], wu_ref[...], wd_ref[...]
    act, dgate, dup = hidden_terms(h2_ref[...], g_ref[...], wg, wu, wd)
    down = contract_last(act, wd)
    dh = contract_last(dgate, wg) + contract_last(dup, wu)

    @pl.when(pl.program_id(0) == 0)
    def _():
        down_ref[...] = down
        dh_ref[...] = dh

    @pl.when(pl.program_id(0) > 0)
    def _():
        down_ref[...] += down
        dh_ref[...] += dh


def own_mlp(h2, g, w_gate, w_up, w_down):
    rows, width = h2.shape
    hidden = w_gate.shape[1]
    tile = next(t for t in (384, 256, 128, hidden) if hidden % t == 0)
    whole = pl.BlockSpec((rows, width), lambda i: (0, 0))
    weight = pl.BlockSpec((width, tile), lambda i: (0, i))
    out = jax.ShapeDtypeStruct((rows, width), F32)
    return pl.pallas_call(
        own_mlp_kernel,
        grid=(hidden // tile,),
        in_specs=[whole, whole, weight, weight, weight],
        out_specs=[whole, whole],
        out_shape=(out, out),
        compiler_params=pltpu.CompilerParams(vmem_limit_bytes=VMEM_LIMIT),
        cost_estimate=cost(12 * rows * width * hidden, 6 * width * hidden, rows * hidden),
        name="own_mlp",
    )(h2, g, w_gate, w_up, w_down)


def bulk_mlp_kernel(
    h2_ref, g_ref, h2c_ref, gc_ref, wg_ref, wu_ref, wd_ref, *rest, row_tile
):
    own_refs, other_refs = rest[:3], rest[3:]
    own_rows = own_refs[0].shape[0]
    tokens = h2_ref.shape[0]
    wg, wu, wd = wg_ref[...], wu_ref[...], wd_ref[...]
    totals = None
    for begin in range(0, tokens, row_tile):
        rows = slice(begin, begin + row_tile)
        act, dgate, dup = hidden_terms(h2_ref[rows], g_ref[rows], wg, wu, wd)
        h2c, gc = h2c_ref[:, rows], gc_ref[:, rows]
        terms = [dot(h2c, dgate), dot(h2c, dup), dot(gc, act)]
        totals = terms if totals is None else [a + b for a, b in zip(totals, terms)]
    for own, other, total in zip(own_refs, other_refs, totals):
        own[...] = total[:own_rows]
        other[...] = total[own_rows:].astype(BF16)


def bulk_mlp(h2, g, h2c, gc, w_gate, w_up, w_down):
    tokens, width = h2.shape
    hidden = w_gate.shape[1]
    pair_rows = h2c.shape[0]
    own_rows = pair_rows // 2
    tile = 512
    whole = pl.BlockSpec((tokens, width), lambda i: (0, 0), pipeline_mode=pl.Buffered(1))
    columns = pl.BlockSpec((pair_rows, tokens), lambda i: (0, 0), pipeline_mode=pl.Buffered(1))
    weight = pl.BlockSpec((width, tile), lambda i: (0, i))
    result = pl.BlockSpec((own_rows, tile), lambda i: (0, i))
    return pl.pallas_call(
        functools.partial(bulk_mlp_kernel, row_tile=min(tokens, 1024)),
        grid=(pl.cdiv(hidden, tile),),
        in_specs=[whole, whole, columns, columns, weight, weight, weight],
        out_specs=[result] * 6,
        out_shape=[jax.ShapeDtypeStruct((own_rows, hidden), F32)] * 3
        + [jax.ShapeDtypeStruct((own_rows, hidden), BF16)] * 3,
        compiler_params=pltpu.CompilerParams(vmem_limit_bytes=VMEM_LIMIT),
        cost_estimate=cost(
            6 * tokens * (width + pair_rows) * hidden,
            6 * width * hidden + 4 * tokens * width,
            tokens * hidden,
        ),
        name="bulk_mlp",
    )(h2, g, h2c, gc, w_gate, w_up, w_down)


def norm_rows(values, gain):
    factor = lax.rsqrt(jnp.mean(values * values, axis=-1, keepdims=True) + EPSILON)
    return (values * factor * gain, factor)


def norm_back(values, factor, gain, grad):
    scaled = grad * gain
    inner = jnp.mean(values * scaled, axis=-1, keepdims=True)
    return factor * scaled - values * (factor * factor * factor) * inner


def rotary_tables(positions, head_width):
    half_width = head_width // 2
    freqs = ROPE_BASE ** (-2.0 * jnp.arange(half_width, dtype=F32) / head_width)
    angles = positions.astype(F32)[:, None] * freqs[None, :]
    return (jnp.cos(angles)[:, None, :], jnp.sin(angles)[:, None, :])


def rotate(values, cosine, sine):
    half = values.shape[-1] // 2
    a, b = values[..., :half], values[..., half:]
    return jnp.concatenate([a * cosine - b * sine, b * cosine + a * sine], axis=-1)


def rotate_back(grad, cosine, sine):
    return rotate(grad, cosine, -sine)


def block_place(half_index, device_index, offset, pair_count):
    return (
        jnp.where(half_index == 0, device_index, 2 * pair_count - 1 - device_index) * BLK + offset
    )


def widen(values, seqs, kv_heads, group):
    rows, width = values.shape
    tokens = rows // seqs
    head = width // (kv_heads * group)
    parts = values.reshape(seqs, tokens, kv_heads, group, head).transpose(0, 2, 3, 1, 4)
    parts = parts.reshape(seqs, kv_heads, group * tokens, 1, head)
    eye = jnp.eye(kv_heads, dtype=values.dtype).reshape(1, kv_heads, 1, kv_heads, 1)
    return (parts * eye).reshape(seqs, kv_heads, group * tokens, kv_heads * head)


def narrow(values, group):
    seqs, kv_heads, head, lanes = values.shape
    tokens = lanes // group
    parts = values.reshape(seqs, kv_heads, head, group, tokens).transpose(0, 4, 1, 3, 2)
    return parts.reshape(seqs * tokens, kv_heads * group * head)


def shards(
    tokens,
    w_query,
    w_key,
    w_value,
    w_output,
    w_gate,
    w_up,
    w_down,
    attn_gain,
    mlp_gain,
    query_gain,
    key_gain,
    segments,
    positions,
    cotangent,
):
    count = lax.axis_size("ctx")
    me = lax.axis_index("ctx")
    core = lax.axis_index("tp")
    nz = count // 4
    _, _, flips = permutes(count)
    head = query_gain.shape[0]
    rows, model = tokens.shape
    q_heads = w_query.shape[1] // head
    kv_heads = w_key.shape[1] // head
    group = q_heads // kv_heads
    pair = rows // SEQS
    kv_width = kv_heads * head
    scale = head ** (-0.5)
    half_rows = rows // 2

    g_half = lax.dynamic_slice_in_dim(cotangent, core * half_rows, half_rows, 0)
    g_plane = gather_plane(g_half, count)
    g_bulk = jnp.concatenate([g_plane, swap_cores(g_plane)], axis=0)

    hidden_in = tokens.astype(F32)
    normed_one, factor_one = norm_rows(hidden_in, attn_gain)
    h1 = normed_one.astype(BF16)
    cosine, sine = rotary_tables(positions, head)
    key_raw = dot(h1, w_key).reshape(rows, kv_heads, head)
    key_normed, key_factor = norm_rows(key_raw, key_gain)
    keys_low = rotate(key_normed, cosine, sine).astype(BF16).reshape(rows, kv_width)
    values_low = dot(h1, w_value).astype(BF16)
    packed = jnp.concatenate([keys_low, values_low], axis=1)
    kv = gather_all(packed, count).reshape(count, SEQS, pair, 2 * kv_width)

    query_raw = dot(h1, w_query).reshape(rows, q_heads, head)
    query_normed, query_factor = norm_rows(query_raw, query_gain)
    queries = (rotate(query_normed, cosine, sine).astype(BF16) * BF16(scale)).reshape(rows, -1)
    q_wide = widen(queries, SEQS, kv_heads, group)

    offsets = jnp.arange(pair, dtype=jnp.int32)
    seg_rows = segments.reshape(count, SEQS * pair)
    owners = [relative_owner(me, count, j, s) for j in range(4) for s in range(nz)]
    seg_k = jnp.concatenate([lax.dynamic_slice_in_dim(seg_rows, o, 1, 0) for o in owners], axis=0)
    seg_k = seg_k.reshape(count, SEQS, pair).transpose(1, 0, 2).reshape(SEQS, count * pair, 1)
    place_k = jnp.concatenate([block_place(offsets // BLK, o, offsets % BLK, count) for o in owners])
    place_k = place_k.reshape(count * pair, 1)
    seg_q = lax.dynamic_slice_in_dim(seg_rows, me, 1, 0).reshape(SEQS, 1, pair)
    seg_q = jnp.tile(seg_q, (1, 1, group))
    place_q = jnp.tile(block_place(offsets // BLK, me, offsets % BLK, count), group)[None, :]

    o_t, lse = attention_forward(q_wide, kv, seg_q, place_q, seg_k, place_k)
    attn_low = narrow(o_t, group).astype(BF16)

    branch = core_sum(contract_last(attn_low, w_output))
    middle = hidden_in + branch
    normed_two, factor_two = norm_rows(middle, mlp_gain)
    h2 = normed_two.astype(BF16)
    h2_half = lax.dynamic_slice_in_dim(h2, core * half_rows, half_rows, 0)
    h2_plane = gather_plane(h2_half, count)
    h2_bulk = jnp.concatenate([h2_plane, swap_cores(h2_plane)], axis=0)

    down_part, dh2_part = own_mlp(h2, cotangent, w_gate, w_up, w_down)
    dh2 = core_sum(dh2_part)
    output = (middle + core_sum(down_part)).astype(BF16)
    mlp_gain_part = jnp.sum(dh2_part * middle * factor_two, axis=0)
    grad_middle = cotangent.astype(F32) + norm_back(middle, factor_two, mlp_gain, dh2)
    dy = grad_middle.astype(BF16)
    do = dot(dy, w_output).astype(BF16)
    do_wide = widen(do, SEQS, kv_heads, group)

    dq_t, dkv_part = attention_backward(
        q_wide, do_wide, kv, lse, seg_q, place_q, seg_k, place_k
    )
    dkv_part = dkv_part.reshape(4, nz * rows, 2 * kv_width)
    dkv = scatter_sum([dkv_part[j] for j in range(4)], count)

    dy_t = dy.T
    dy_rel = [relative_rows(dy_t, me, count, j) for j in range(4)]
    grad_wo = scatter_sum([dot(part, attn_low).astype(BF16) for part in dy_rel], count)

    own_cols = model // count
    other = me ^ 1

    def pair_columns(array):
        mine = lax.dynamic_slice_in_dim(array, me * own_cols, own_cols, 1)
        theirs = lax.dynamic_slice_in_dim(array, other * own_cols, own_cols, 1)
        return jnp.concatenate([mine, theirs], axis=1).T

    bulk = bulk_mlp(
        h2_bulk, g_bulk, pair_columns(h2_bulk), pair_columns(g_bulk), w_gate, w_up, w_down
    )
    mlp_grads = [a + send(b, flips[1]).astype(F32) for a, b in zip(bulk[:3], bulk[3:])]

    grad_q_rows = (narrow(dq_t, group) * scale).reshape(rows, q_heads, head)
    grad_q_normed = rotate_back(grad_q_rows, cosine, sine)
    query_gain_part = jnp.sum(grad_q_normed * query_raw * query_factor, axis=(0, 1))
    dq = (
        norm_back(query_raw, query_factor, query_gain, grad_q_normed)
        .reshape(rows, q_heads * head)
        .astype(BF16)
    )
    h1_t = h1.T
    h1_rel = [relative_rows(h1_t, me, count, j) for j in range(4)]
    grad_wq = scatter_sum([dot(part, dq).astype(BF16) for part in h1_rel], count)

    grad_k_normed = rotate_back(dkv[:, :kv_width].reshape(rows, kv_heads, head), cosine, sine)
    key_gain_part = jnp.sum(grad_k_normed * key_raw * key_factor, axis=(0, 1))
    dk = (
        norm_back(key_raw, key_factor, key_gain, grad_k_normed)
        .reshape(rows, kv_width)
        .astype(BF16)
    )
    dv = dkv[:, kv_width:].astype(BF16)
    dkv_low = jnp.concatenate([dk, dv], axis=1)
    grad_wkv = scatter_sum([dot(part, dkv_low).astype(BF16) for part in h1_rel], count)

    dh1_part = contract_last(dq, w_query) + contract_last(dk, w_key) + contract_last(dv, w_value)
    attn_gain_part = jnp.sum(dh1_part * hidden_in * factor_one, axis=0)
    dh1 = core_sum(dh1_part)
    grad_tokens = (grad_middle + norm_back(hidden_in, factor_one, attn_gain, dh1)).astype(BF16)

    gains = sum_everywhere(
        jnp.concatenate([attn_gain_part, mlp_gain_part, query_gain_part, key_gain_part]), count
    )
    return (
        output,
        grad_tokens,
        grad_wq,
        grad_wkv[:, :kv_width],
        grad_wkv[:, kv_width:],
        grad_wo,
        mlp_grads[0],
        mlp_grads[1],
        mlp_grads[2],
        gains[:model],
        gains[model : 2 * model],
        gains[2 * model : 2 * model + head],
        gains[2 * model + head :],
    )


def solution(mesh):
    rows = P("ctx", None)
    columns = P(None, "tp")
    both = P("ctx", "tp")
    in_specs = (rows,) + (columns,) * 7 + (P(),) * 5 + (P("ctx"), rows)
    out_specs = (rows, rows) + (both,) * 7 + (P(),) * 4
    return jax.shard_map(shards, mesh=mesh, in_specs=in_specs, out_specs=out_specs, check_vma=False)
```

time: 1410 us -> 489 us (0.35)
  waiting for transfers between devices: 1130 us -> 96.9 us
  matrix products: 113 us -> 24.3 us
  Pallas kernels: 0 us -> 88.1 us
  starting transfers between devices: 7.22 us -> 79.4 us
  local copies, waits for them, and re-layouts: 58.5 us -> 129 us
  blocking collectives: 44.3 us -> 0 us
  other arithmetic: 38.5 us -> 62 us
    reduce_scatter x1 -> x0, waiting for transfers between devices: 1020 us -> none  [shards(): lax.psum_scatter(weight_terms(attn_pairs + mlp_pairs), 'ctx', scatter_dim...]
    ppermute x0 -> x57, waiting for transfers between devices: none -> 96.9 us  [the longest x50 95.7 us: send(): return lax.ppermute(value, 'ctx', pairs)]
    dot_general x27 -> x20, matrix products: 113 us -> 24.3 us  [the longest x16 19.3 us: dot(): return jnp.dot(left, right, preferred_element_type=F32)]
    pallas_call x0 -> x4, Pallas kernels: none -> 88.1 us  [the longest x1 48.7 us: bulk_mlp(): pl.pallas_call(functools.partial(bulk_mlp_kernel, row_tile=min(tokens, 10...]
    ppermute x0 -> x57, starting transfers between devices: none -> 79.4 us  [the longest x50 78.4 us: send(): return lax.ppermute(value, 'ctx', pairs)]
    all_gather x1 -> x0, waiting for transfers between devices: 50.6 us -> none  [shards(): incoming = lax.all_gather(packed, 'ctx', axis=1, tiled=True)]
    psum x3 -> x0, waiting for transfers between devices: 50 us -> none  [the longest x1 18.5 us: shards(): lax.psum(mlp_in_part.astype(jnp.bfloat16), 'tp').astype(jnp.float32)]
    psum x1 -> x0, blocking collectives: 44.3 us -> none  [shards(): lax.psum((attn_gain_part, mlp_gain_part, query_gain_part, key_gain_part),...]
  transfers between devices with their start and end apart: 6 -> 57, of which waited for: 6 -> 16; matrix products, arithmetic and copies ran while one was open for 4% -> 40% of each run, Pallas kernels for 0% -> 18%
where the time goes in v1:
time: 489 us; the launch traced here: 482 us
  local copies, waits for them, and re-layouts  129 us (26%)
  waiting for transfers between devices  96.9 us (20%)
  Pallas kernels  88.1 us (18%)
  starting transfers between devices  79.4 us (16%)
  other arithmetic  62 us (13%)
  matrix products  24.3 us (5%)
    ppermute x50, waiting for transfers between devices, send(): return lax.ppermute(value, 'ctx', pairs)  95.7 us
    ppermute x50, starting transfers between devices, send(): return lax.ppermute(value, 'ctx', pairs)  78.4 us
    pallas_call x1, Pallas kernels, bulk_mlp(): pl.pallas_call(functools.partial(bulk_mlp_kernel, row_tile=min(tokens, 10...  48.7 us
    pallas_call x1, Pallas kernels, own_mlp(): pl.pallas_call(own_mlp_kernel, grid=(hidden // tile,), in_specs=[whole, w...  21.5 us
    dot_general x16, matrix products, dot(): return jnp.dot(left, right, preferred_element_type=F32)  19.3 us
    unnamed x179, local copies, waits for them, and re-layouts  19 us
    concatenate x2, local copies, waits for them, and re-layouts, gather_plane(): return jnp.concatenate([block, near, column, far], axis=0)  10.1 us
    pallas_call x1, Pallas kernels, attention_backward(): pl.pallas_call(attention_backward_kernel, grid=(seqs,), in_specs=[seq_blo...  10.1 us
  transfers between devices with their start and end apart: 57, of which 16 were waited for; matrix products, arithmetic and copies ran while one was open for 40% of the time, Pallas kernels for 18%

profile of v1, /device:TPU:0, one launch (start us, length us, event | category | flops | bytes accessed | tf_op | source)
XLA Modules:
  0.0 481.9 jit_solution(17774791464879334229)
XLA Ops:
  10.7 3.0 collective-permute-start
  22.5 2.9 fusion.74
  54.0 3.3 collective-permute-start.46
  93.7 2.8 collective-permute-done.5
  98.1 6.9 %collective-permute-done.6 = bf16[384,512]{1,0:T(8,128)(2,1)} collective-permute-done((bf16[384,512]{1,0:T(8,128)(2,1)}, bf16[384,512]{1,0:T(8,128)(2,1)}, u32[]{:S(2)}, u32[]{:S(2)}) %collective-permute-start.6) | collective-permute-done | bytes 393248 | tf_op jit(solution)/shard_map/ppermute | solution.py:39
  110.1 7.8 %attention_forward.1 = (f32[2,4,64,192]{3,2,1,0:T(8,128)}, f32[2,4,1,192]{3,2,1,0:T(1,128)}) custom-call(bf16[2,4,192,256]{3,2,1,0:T(8,128)(2,1)} %broadcast_multiply_fusion.1.q_ref, bf16[16,2,64,512]{3,2,1,0:T(8,128)(2,1)} %bitcast.163, s32[2,1,192]{2,1,0:T(1,128)} %tile.20.sq_ref, s32[1,192]{1,0:T(1,128)} %broadcast_in_dim_tile.3.pq_ref, ...), custom_call_target="tpu_custom_call" | custom-call | flops 1610612736 | bytes 2097152 | tf_op jit(solution)/shard_map/attention_forward/pallas_call | solution.py:182
  137.7 5.0 %concatenate.123 = bf16[512,1536]{0,1:T(8,128)(2,1)} concatenate(bf16[64,1536]{0,1:T(8,128)(2,1)} %constant_dynamic-slice_fusion.4, bf16[64,1536]{0,1:T(8,128)(2,1)} %collective-permute-done.43, bf16[64,1536]{0,1:T(8,128)(2,1)} %collective-permute-done.44, bf16[64,1536]{0,1:T(8,128)(2,1)} %copy-done.11, bf16[64,1536]{0,1:T(8,128)(2,1)} %collective-permute-done.46, ...), dimensions={0} | concatenate | bytes 3145728 | tf_op jit(solution)/shard_map/concatenate | solution.py:84
  152.8 3.1 collective-permute-start.40
  155.8 21.5 %own_mlp.1 = (f32[128,1536]{1,0:T(8,128)}, f32[128,1536]{1,0:T(8,128)}) custom-call(bf16[128,1536]{1,0:T(8,128)(2,1)} %copy.209.h2_ref, bf16[128,1536]{1,0:T(8,128)(2,1)} %g_ref.1, bf16[1536,3456]{1,0:T(8,128)(2,1)} %wg_ref.3, bf16[1536,3456]{1,0:T(8,128)(2,1)} %wu_ref.3, bf16[1536,3456]{1,0:T(8,128)(2,1)} %wd_ref.3), custom_call_target="tpu_custom_call" | custom-call | flops 8153726976 | bytes 31850496 | tf_op jit(solution)/shard_map/own_mlp/pallas_call | solution.py:267
  201.0 10.1 %attention_backward.1 = (f32[2,4,64,192]{3,2,1,0:T(8,128)}, bf16[16,2,64,512]{3,2,1,0:T(8,128)(2,1)}) custom-call(bf16[2,4,192,256]{3,2,1,0:T(8,128)(2,1)} %broadcast_multiply_fusion.1.q_ref, bf16[2,4,192,256]{3,2,1,0:T(8,128)(2,1)} %broadcast_multiply_fusion.do_ref, bf16[16,2,64,512]{3,2,1,0:T(8,128)(2,1)} %bitcast.164, ...), custom_call_target="tpu_custom_call" | custom-call | flops 4026531840 | bytes 4194304 | tf_op jit(solution)/shard_map/attention_backward/pallas_call | solution.py:210
  236.6 3.5 collective-permute-done.14
  245.6 5.1 %concatenate.120 = bf16[512,1536]{0,1:T(8,128)(2,1)} concatenate(bf16[64,1536]{0,1:T(8,128)(2,1)} %constant_dynamic-slice_fusion.5, bf16[64,1536]{0,1:T(8,128)(2,1)} %collective-permute-done.37, bf16[64,1536]{0,1:T(8,128)(2,1)} %collective-permute-done.38, bf16[64,1536]{0,1:T(8,128)(2,1)} %collective-permute-done.39, bf16[64,1536]{0,1:T(8,128)(2,1)} %collective-permute-done.40, ...), dimensions={0} | concatenate | bytes 3145728 | tf_op jit(solution)/shard_map/concatenate | solution.py:84
  256.1 8.0 %collective-permute-done.21 = bf16[384,768]{1,0:T(8,128)(2,1)} collective-permute-done((bf16[384,768]{1,0:T(8,128)(2,1)}, bf16[384,768]{1,0:T(8,128)(2,1)}, u32[]{:S(2)}, u32[]{:S(2)}) %collective-permute-start.21) | collective-permute-done | bytes 589856 | tf_op jit(solution)/shard_map/ppermute | solution.py:39
  265.7 11.1 %collective-permute-done.20 = bf16[384,768]{1,0:T(8,128)(2,1)} collective-permute-done((bf16[384,768]{1,0:T(8,128)(2,1)}, bf16[384,768]{1,0:T(8,128)(2,1)}, u32[]{:S(2)}, u32[]{:S(2)}) %collective-permute-start.20) | collective-permute-done | bytes 589856 | tf_op jit(solution)/shard_map/ppermute | solution.py:39
  276.8 3.2 collective-permute-start.17
  282.5 6.8 %collective-permute-done.33 = bf16[384,768]{1,0:T(8,128)(2,1)S(1)} collective-permute-done((bf16[384,768]{1,0:T(8,128)(2,1)}, bf16[384,768]{1,0:T(8,128)(2,1)S(1)}, u32[]{:S(2)}, u32[]{:S(2)}) %collective-permute-start.33) | collective-permute-done | bytes 589856 | tf_op jit(solution)/shard_map/ppermute | solution.py:39
  291.5 9.1 %collective-permute-done.32 = bf16[384,768]{1,0:T(8,128)(2,1)S(1)} collective-permute-done((bf16[384,768]{1,0:T(8,128)(2,1)}, bf16[384,768]{1,0:T(8,128)(2,1)S(1)}, u32[]{:S(2)}, u32[]{:S(2)}) %collective-permute-start.32) | collective-permute-done | bytes 589856 | tf_op jit(solution)/shard_map/ppermute | solution.py:39
  300.6 3.1 collective-permute-start.15
  305.8 3.0 collective-permute-start.22
  323.1 3.1 collective-permute-start.35
  329.9 3.5 collective-permute-done.35
  343.9 6.8 %collective-permute-done.26 = bf16[384,512]{1,0:T(8,128)(2,1)} collective-permute-done((bf16[384,512]{1,0:T(8,128)(2,1)}, bf16[384,512]{1,0:T(8,128)(2,1)}, u32[]{:S(2)}, u32[]{:S(2)}) %collective-permute-start.26) | collective-permute-done | bytes 393248 | tf_op jit(solution)/shard_map/ppermute | solution.py:39
  356.3 3.9 collective-permute-start.30
  360.2 3.3 collective-permute-start.29
  363.5 5.6 %concatenate.124 = bf16[1024,1536]{0,1:T(8,128)(2,1)S(1)} concatenate(bf16[64,1536]{0,1:T(8,128)(2,1)} %constant_dynamic-slice_fusion.4, bf16[64,1536]{0,1:T(8,128)(2,1)} %collective-permute-done.43, bf16[64,1536]{0,1:T(8,128)(2,1)} %collective-permute-done.44, bf16[64,1536]{0,1:T(8,128)(2,1)S(1)} %copy-done.12, bf16[64,1536]{0,1:T(8,128)(2,1)} %collective-permute-done.46, ...), dimensions={0} | concatenate | bytes 6291456 | tf_op jit(solution)/shard_map/concatenate | solution.py:410
  375.8 3.0 copy.242.g_ref
  379.3 5.3 %concatenate.121 = bf16[1024,1536]{0,1:T(8,128)(2,1)S(1)} concatenate(bf16[64,1536]{0,1:T(8,128)(2,1)} %constant_dynamic-slice_fusion.5, bf16[64,1536]{0,1:T(8,128)(2,1)} %collective-permute-done.37, bf16[64,1536]{0,1:T(8,128)(2,1)} %collective-permute-done.38, bf16[64,1536]{0,1:T(8,128)(2,1)} %collective-permute-done.39, bf16[64,1536]{0,1:T(8,128)(2,1)} %collective-permute-done.40, ...), dimensions={0} | concatenate | bytes 6291456 | tf_op jit(solution)/shard_map/concatenate | solution.py:448
  384.7 3.0 copy.241.h2_ref
  388.5 48.7 %bulk_mlp.1 = (f32[96,3456]{1,0:T(8,128)}, f32[96,3456]{1,0:T(8,128)}, f32[96,3456]{1,0:T(8,128)}, bf16[96,3456]{1,0:T(8,128)(2,1)}, bf16[96,3456]{1,0:T(8,128)(2,1)}, /*index=5*/bf16[96,3456]{1,0:T(8,128)(2,1)}) custom-call(bf16[1024,1536]{1,0:T(8,128)(2,1)} %copy.241.h2_ref, bf16[1024,1536]{1,0:T(8,128)(2,1)} %copy.242.g_ref, ...), custom_call_target="tpu_custom_call" | custom-call | flops 36691771392 | bytes 38141952 | tf_op jit(solution)/shard_map/bulk_mlp/pallas_call | solution.py:308
  443.1 12.1 %collective-permute-done.49 = bf16[96,3456]{1,0:T(8,128)(2,1)S(1)} collective-permute-done((bf16[96,3456]{1,0:T(8,128)(2,1)}, bf16[96,3456]{1,0:T(8,128)(2,1)S(1)}, u32[]{:S(2)}, u32[]{:S(2)}) %collective-permute-start.49) | collective-permute-done | bytes 663584 | tf_op jit(solution)/shard_map/ppermute | solution.py:39
  457.8 11.7 %collective-permute-done.50 = bf16[96,3456]{1,0:T(8,128)(2,1)S(1)} collective-permute-done((bf16[96,3456]{1,0:T(8,128)(2,1)}, bf16[96,3456]{1,0:T(8,128)(2,1)S(1)}, u32[]{:S(2)}, u32[]{:S(2)}) %collective-permute-start.50) | collective-permute-done | bytes 663584 | tf_op jit(solution)/shard_map/ppermute | solution.py:39
  470.7 9.7 %collective-permute-done.51 = bf16[96,3456]{1,0:T(8,128)(2,1)S(1)} collective-permute-done((bf16[96,3456]{1,0:T(8,128)(2,1)}, bf16[96,3456]{1,0:T(8,128)(2,1)S(1)}, u32[]{:S(2)}, u32[]{:S(2)}) %collective-permute-start.51) | collective-permute-done | bytes 663584 | tf_op jit(solution)/shard_map/ppermute | solution.py:39
  (443 shorter events, 240.9 us)
Async XLA Ops:
  10.7 41.4 %collective-permute-start = (bf16[128,512]{1,0:T(8,128)(2,1)}, bf16[128,512]{1,0:T(8,128)(2,1)}, u32[]{:S(2)}, u32[]{:S(2)}) collective-permute-start(bf16[128,512]{1,0:T(8,128)(2,1)} %get-tuple-element.187), channel_id=1, source_target_pairs={{0,8},{2,10},{4,12},{6,14},{8,16},{10,18},{12,20},{14,22},{16,24},... | collective-permute-start | bytes 393224 | tf_op jit(solution)/shard_map/ppermute | solution.py:39
  13.7 40.3 %collective-permute-start.1 = (bf16[128,512]{1,0:T(8,128)(2,1)}, bf16[128,512]{1,0:T(8,128)(2,1)}, u32[]{:S(2)}, u32[]{:S(2)}) collective-permute-start(bf16[128,512]{1,0:T(8,128)(2,1)} %get-tuple-element.187), channel_id=1, source_target_pairs={{0,16},{2,18},{4,20},{6,22},{8,24},{10,26},{12,28},{14,30},{16,0},... | collective-permute-start | bytes 393224 | tf_op jit(solution)/shard_map/ppermute | solution.py:39
  16.3 42.7 %collective-permute-start.2 = (bf16[128,512]{1,0:T(8,128)(2,1)}, bf16[128,512]{1,0:T(8,128)(2,1)}, u32[]{:S(2)}, u32[]{:S(2)}) collective-permute-start(bf16[128,512]{1,0:T(8,128)(2,1)} %get-tuple-element.187), channel_id=1, source_target_pairs={{0,24},{2,26},{4,28},{6,30},{8,0},{10,2},{12,4},{14,6},{16,8},{18,... | collective-permute-start | bytes 393224 | tf_op jit(solution)/shard_map/ppermute | solution.py:39
  17.6 61.7 %collective-permute-start.3 = (bf16[128,512]{1,0:T(8,128)(2,1)}, bf16[128,512]{1,0:T(8,128)(2,1)}, u32[]{:S(2)}, u32[]{:S(2)}) collective-permute-start(bf16[128,512]{1,0:T(8,128)(2,1)} %get-tuple-element.187), channel_id=1, source_target_pairs={{0,2},{2,0},{4,6},{6,4},{8,10},{10,8},{12,14},{14,12},{16,18},{18,... | collective-permute-start | bytes 393224 | tf_op jit(solution)/shard_map/ppermute | solution.py:39
  21.3 61.1 %collective-permute-start.44 = (bf16[64,1536]{0,1:T(8,128)(2,1)}, bf16[64,1536]{0,1:T(8,128)(2,1)}, u32[]{:S(2)}, u32[]{:S(2)}) collective-permute-start(bf16[64,1536]{0,1:T(8,128)(2,1)} %constant_dynamic-slice_fusion.4), channel_id=1, source_target_pairs={{0,8},{2,10},{4,12},{6,14},{8,16},{10,18},{12,20},{14,22},{16,24},... | collective-permute-start | bytes 589832 | tf_op jit(solution)/shard_map/ppermute | solution.py:39
  52.0 31.8 %collective-permute-start.45 = (bf16[64,1536]{0,1:T(8,128)(2,1)}, bf16[64,1536]{0,1:T(8,128)(2,1)S(1)}, u32[]{:S(2)}, u32[]{:S(2)}) collective-permute-start(bf16[64,1536]{0,1:T(8,128)(2,1)} %constant_dynamic-slice_fusion.4), channel_id=1, source_target_pairs={{0,16},{2,18},{4,20},{6,22},{8,24},{10,26},{12,28},{14,30},{16,0},... | collective-permute-start | bytes 589832 | tf_op jit(solution)/shard_map/ppermute | solution.py:39
  54.0 31.4 %collective-permute-start.46 = (bf16[64,1536]{0,1:T(8,128)(2,1)}, bf16[64,1536]{0,1:T(8,128)(2,1)}, u32[]{:S(2)}, u32[]{:S(2)}) collective-permute-start(bf16[64,1536]{0,1:T(8,128)(2,1)} %constant_dynamic-slice_fusion.4), channel_id=1, source_target_pairs={{0,24},{2,26},{4,28},{6,30},{8,0},{10,2},{12,4},{14,6},{16,8},{18,... | collective-permute-start | bytes 589832 | tf_op jit(solution)/shard_map/ppermute | solution.py:39
  60.5 29.9 %collective-permute-start.4 = (bf16[384,512]{1,0:T(8,128)(2,1)}, bf16[384,512]{1,0:T(8,128)(2,1)}, u32[]{:S(2)}, u32[]{:S(2)}) collective-permute-start(bf16[384,512]{1,0:T(8,128)(2,1)} %get-tuple-element.181), channel_id=1, source_target_pairs={{0,2},{2,0},{4,6},{6,4},{8,10},{10,8},{12,14},{14,12},{16,18},{18,... | collective-permute-start | bytes 1179656 | tf_op jit(solution)/shard_map/ppermute | solution.py:39
  82.4 24.4 %collective-permute-start.7 = (bf16[128,512]{1,0:T(8,128)(2,1)}, bf16[128,512]{1,0:T(8,128)(2,1)}, u32[]{:S(2)}, u32[]{:S(2)}) collective-permute-start(bf16[128,512]{1,0:T(8,128)(2,1)} %get-tuple-element.187), channel_id=1, source_target_pairs={{0,6},{2,4},{4,2},{6,0},{8,14},{10,12},{12,10},{14,8},{16,22},{18,... | collective-permute-start | bytes 393224 | tf_op jit(solution)/shard_map/ppermute | solution.py:39
  85.3 23.0 %collective-permute-start.8 = (bf16[384,512]{1,0:T(8,128)(2,1)}, bf16[384,512]{1,0:T(8,128)(2,1)}, u32[]{:S(2)}, u32[]{:S(2)}) collective-permute-start(bf16[384,512]{1,0:T(8,128)(2,1)} %get-tuple-element.181), channel_id=1, source_target_pairs={{0,6},{2,4},{4,2},{6,0},{8,14},{10,12},{12,10},{14,8},{16,22},{18,... | collective-permute-start | bytes 1179656 | tf_op jit(solution)/shard_map/ppermute | solution.py:39
  90.4 45.9 %collective-permute-start.47 = (bf16[192,1536]{1,0:T(8,128)(2,1)}, bf16[192,1536]{1,0:T(8,128)(2,1)}, u32[]{:S(2)}, u32[]{:S(2)}) collective-permute-start(bf16[192,1536]{1,0:T(8,128)(2,1)} %copy.238), channel_id=1, source_target_pairs={{0,4},{2,6},{4,0},{6,2},{8,12},{10,14},{12,8},{14,10},{16,20},{18,... | collective-permute-start | bytes 1769480 | tf_op jit(solution)/shard_map/ppermute | solution.py:39
  150.1 82.2 %collective-permute-start.37 = (bf16[64,1536]{0,1:T(8,128)(2,1)}, bf16[64,1536]{0,1:T(8,128)(2,1)}, u32[]{:S(2)}, u32[]{:S(2)}) collective-permute-start(bf16[64,1536]{0,1:T(8,128)(2,1)} %constant_dynamic-slice_fusion.5), channel_id=1, source_target_pairs={{0,4},{2,6},{4,0},{6,2},{8,12},{10,14},{12,8},{14,10},{16,20},{18,... | collective-permute-start | bytes 589832 | tf_op jit(solution)/shard_map/ppermute | solution.py:39
  150.8 35.0 %collective-permute-start.38 = (bf16[64,1536]{0,1:T(8,128)(2,1)}, bf16[64,1536]{0,1:T(8,128)(2,1)}, u32[]{:S(2)}, u32[]{:S(2)}) collective-permute-start(bf16[64,1536]{0,1:T(8,128)(2,1)} %constant_dynamic-slice_fusion.5), channel_id=1, source_target_pairs={{0,8},{2,10},{4,12},{6,14},{8,16},{10,18},{12,20},{14,22},{16,24},... | collective-permute-start | bytes 589832 | tf_op jit(solution)/shard_map/ppermute | solution.py:39
  151.3 34.9 %collective-permute-start.39 = (bf16[64,1536]{0,1:T(8,128)(2,1)}, bf16[64,1536]{0,1:T(8,128)(2,1)}, u32[]{:S(2)}, u32[]{:S(2)}) collective-permute-start(bf16[64,1536]{0,1:T(8,128)(2,1)} %constant_dynamic-slice_fusion.5), channel_id=1, source_target_pairs={{0,16},{2,18},{4,20},{6,22},{8,24},{10,26},{12,28},{14,30},{16,0},... | collective-permute-start | bytes 589832 | tf_op jit(solution)/shard_map/ppermute | solution.py:39
  152.8 33.5 %collective-permute-start.40 = (bf16[64,1536]{0,1:T(8,128)(2,1)}, bf16[64,1536]{0,1:T(8,128)(2,1)}, u32[]{:S(2)}, u32[]{:S(2)}) collective-permute-start(bf16[64,1536]{0,1:T(8,128)(2,1)} %constant_dynamic-slice_fusion.5), channel_id=1, source_target_pairs={{0,24},{2,26},{4,28},{6,30},{8,0},{10,2},{12,4},{14,6},{16,8},{18,... | collective-permute-start | bytes 589832 | tf_op jit(solution)/shard_map/ppermute | solution.py:39
  191.0 44.6 %collective-permute-start.41 = (bf16[192,1536]{1,0:T(8,128)(2,1)}, bf16[192,1536]{1,0:T(8,128)(2,1)}, u32[]{:S(2)}, u32[]{:S(2)}) collective-permute-start(bf16[192,1536]{1,0:T(8,128)(2,1)} %copy.234), channel_id=1, source_target_pairs={{0,4},{2,6},{4,0},{6,2},{8,12},{10,14},{12,8},{14,10},{16,20},{18,... | collective-permute-start | bytes 1769480 | tf_op jit(solution)/shard_map/ppermute | solution.py:39
  226.4 25.1 %collective-permute-start.13 = (bf16[512,512]{1,0:T(8,128)(2,1)}, bf16[512,512]{1,0:T(8,128)(2,1)}, u32[]{:S(2)}, u32[]{:S(2)}) collective-permute-start(bf16[512,512]{1,0:T(8,128)(2,1)} %bitcast.24), channel_id=1, source_target_pairs={{0,4},{2,6},{4,0},{6,2},{8,12},{10,14},{12,8},{14,10},{16,20},{18,... | collective-permute-start | bytes 1572872 | tf_op jit(solution)/shard_map/ppermute | solution.py:39
  227.4 26.2 %collective-permute-start.12 = (bf16[512,512]{1,0:T(8,128)(2,1)}, bf16[512,512]{1,0:T(8,128)(2,1)}, u32[]{:S(2)}, u32[]{:S(2)}) collective-permute-start(bf16[512,512]{1,0:T(8,128)(2,1)} %bitcast.23), channel_id=1, source_target_pairs={{0,2},{2,0},{4,6},{6,4},{8,10},{10,8},{12,14},{14,12},{16,18},{18,... | collective-permute-start | bytes 1572872 | tf_op jit(solution)/shard_map/ppermute | solution.py:39
  232.4 31.7 %collective-permute-start.21 = (bf16[384,768]{1,0:T(8,128)(2,1)}, bf16[384,768]{1,0:T(8,128)(2,1)}, u32[]{:S(2)}, u32[]{:S(2)}) collective-permute-start(bf16[384,768]{1,0:T(8,128)(2,1)} %convolution_convert_fusion.4), channel_id=1, source_target_pairs={{0,6},{2,4},{4,2},{6,0},{8,14},{10,12},{12,10},{14,8},{16,22},{18,... | collective-permute-start | bytes 1769480 | tf_op jit(solution)/shard_map/ppermute | solution.py:39
  235.6 41.1 %collective-permute-start.20 = (bf16[384,768]{1,0:T(8,128)(2,1)}, bf16[384,768]{1,0:T(8,128)(2,1)}, u32[]{:S(2)}, u32[]{:S(2)}) collective-permute-start(bf16[384,768]{1,0:T(8,128)(2,1)} %convolution_convert_fusion.5), channel_id=1, source_target_pairs={{0,4},{2,6},{4,0},{6,2},{8,12},{10,14},{12,8},{14,10},{16,20},{18,... | collective-permute-start | bytes 1769480 | tf_op jit(solution)/shard_map/ppermute | solution.py:39
  240.1 36.7 %collective-permute-start.19 = (bf16[384,768]{1,0:T(8,128)(2,1)S(1)}, bf16[384,768]{1,0:T(8,128)(2,1)}, u32[]{:S(2)}, u32[]{:S(2)}) collective-permute-start(bf16[384,768]{1,0:T(8,128)(2,1)S(1)} %convolution_convert_fusion.6), channel_id=1, source_target_pairs={{0,2},{2,0},{4,6},{6,4},{8,10},{10,8},{12,14},{14,12},{16,18},{18,... | collective-permute-start | bytes 1769480 | tf_op jit(solution)/shard_map/ppermute | solution.py:39
  251.5 37.8 %collective-permute-start.33 = (bf16[384,768]{1,0:T(8,128)(2,1)}, bf16[384,768]{1,0:T(8,128)(2,1)S(1)}, u32[]{:S(2)}, u32[]{:S(2)}) collective-permute-start(bf16[384,768]{1,0:T(8,128)(2,1)} %convolution_convert_fusion), channel_id=1, source_target_pairs={{0,6},{2,4},{4,2},{6,0},{8,14},{10,12},{12,10},{14,8},{16,22},{18,... | collective-permute-start | bytes 1769480 | tf_op jit(solution)/shard_map/ppermute | solution.py:39
  253.5 47.1 %collective-permute-start.32 = (bf16[384,768]{1,0:T(8,128)(2,1)}, bf16[384,768]{1,0:T(8,128)(2,1)S(1)}, u32[]{:S(2)}, u32[]{:S(2)}) collective-permute-start(bf16[384,768]{1,0:T(8,128)(2,1)} %convolution_convert_fusion.1), channel_id=1, source_target_pairs={{0,4},{2,6},{4,0},{6,2},{8,12},{10,14},{12,8},{14,10},{16,20},{18,... | collective-permute-start | bytes 1769480 | tf_op jit(solution)/shard_map/ppermute | solution.py:39
  264.1 39.5 %collective-permute-start.31 = (bf16[384,768]{1,0:T(8,128)(2,1)S(1)}, bf16[384,768]{1,0:T(8,128)(2,1)S(1)}, u32[]{:S(2)}, u32[]{:S(2)}) collective-permute-start(bf16[384,768]{1,0:T(8,128)(2,1)S(1)} %copy-done.35), channel_id=1, source_target_pairs={{0,2},{2,0},{4,6},{6,4},{8,10},{10,8},{12,14},{14,12},{16,18},{18,... | collective-permute-start | bytes 1769480 | tf_op jit(solution)/shard_map/ppermute | solution.py:39
  276.8 86.7 %collective-permute-start.48 = (bf16[512,1536]{0,1:T(8,128)(2,1)}, bf16[512,1536]{0,1:T(8,128)(2,1)}, u32[]{:S(2)}, u32[]{:S(2)}) collective-permute-start(bf16[512,1536]{0,1:T(8,128)(2,1)} %concatenate.123), channel_id=1, source_target_pairs={{0,1},{1,0},{2,3},{3,2},{4,5},{5,4},{6,7},{7,6},{8,9},{9,8},{10,11... | collective-permute-start | bytes 4718600 | tf_op jit(solution)/shard_map/ppermute | solution.py:43
  276.8 28.2 %collective-permute-start.17 = (bf16[128,512]{1,0:T(8,128)(2,1)S(1)}, bf16[128,512]{1,0:T(8,128)(2,1)S(1)}, u32[]{:S(2)}, u32[]{:S(2)}) collective-permute-start(bf16[128,512]{1,0:T(8,128)(2,1)S(1)} %get-tuple-element.128), channel_id=1, source_target_pairs={{0,8},{2,10},{4,12},{6,14},{8,16},{10,18},{12,20},{14,22},{16,24},... | collective-permute-start | bytes 393224 | tf_op jit(solution)/shard_map/ppermute | solution.py:39
  329.4 49.9 %collective-permute-start.42 = (bf16[512,1536]{0,1:T(8,128)(2,1)}, bf16[512,1536]{0,1:T(8,128)(2,1)}, u32[]{:S(2)}, u32[]{:S(2)}) collective-permute-start(bf16[512,1536]{0,1:T(8,128)(2,1)} %concatenate.120), channel_id=1, source_target_pairs={{0,1},{1,0},{2,3},{3,2},{4,5},{5,4},{6,7},{7,6},{8,9},{9,8},{10,11... | collective-permute-start | bytes 4718600 | tf_op jit(solution)/shard_map/ppermute | solution.py:43
  356.3 83.0 %collective-permute-start.30 = (bf16[96,512]{1,0:T(8,128)(2,1)}, bf16[96,512]{1,0:T(8,128)(2,1)}, u32[]{:S(2)}, u32[]{:S(2)}) collective-permute-start(bf16[96,512]{1,0:T(8,128)(2,1)} %get-tuple-element.153), channel_id=1, source_target_pairs={{0,8},{2,10},{4,12},{6,14},{8,16},{10,18},{12,20},{14,22},{16,24},... | collective-permute-start | bytes 294920 | tf_op jit(solution)/shard_map/ppermute | solution.py:39
  360.2 79.0 %collective-permute-start.29 = (bf16[96,512]{1,0:T(8,128)(2,1)}, bf16[96,512]{1,0:T(8,128)(2,1)}, u32[]{:S(2)}, u32[]{:S(2)}) collective-permute-start(bf16[96,512]{1,0:T(8,128)(2,1)} %get-tuple-element.154), channel_id=1, source_target_pairs={{0,16},{2,18},{4,20},{6,22},{8,24},{10,26},{12,28},{14,30},{16,0},... | collective-permute-start | bytes 294920 | tf_op jit(solution)/shard_map/ppermute | solution.py:39
  363.5 75.8 %collective-permute-start.28 = (bf16[96,512]{1,0:T(8,128)(2,1)}, bf16[96,512]{1,0:T(8,128)(2,1)}, u32[]{:S(2)}, u32[]{:S(2)}) collective-permute-start(bf16[96,512]{1,0:T(8,128)(2,1)} %get-tuple-element.152), channel_id=1, source_target_pairs={{0,24},{2,26},{4,28},{6,30},{8,0},{10,2},{12,4},{14,6},{16,8},{18,... | collective-permute-start | bytes 294920 | tf_op jit(solution)/shard_map/ppermute | solution.py:39
  441.1 28.4 %collective-permute-start.50 = (bf16[96,3456]{1,0:T(8,128)(2,1)}, bf16[96,3456]{1,0:T(8,128)(2,1)S(1)}, u32[]{:S(2)}, u32[]{:S(2)}) collective-permute-start(bf16[96,3456]{1,0:T(8,128)(2,1)} %get-tuple-element.34), channel_id=1, source_target_pairs={{0,2},{2,0},{4,6},{6,4},{8,10},{10,8},{12,14},{14,12},{16,18},{18,... | collective-permute-start | bytes 1990664 | tf_op jit(solution)/shard_map/ppermute | solution.py:39
  441.7 38.7 %collective-permute-start.51 = (bf16[96,3456]{1,0:T(8,128)(2,1)}, bf16[96,3456]{1,0:T(8,128)(2,1)S(1)}, u32[]{:S(2)}, u32[]{:S(2)}) collective-permute-start(bf16[96,3456]{1,0:T(8,128)(2,1)} %get-tuple-element.36), channel_id=1, source_target_pairs={{0,2},{2,0},{4,6},{6,4},{8,10},{10,8},{12,14},{14,12},{16,18},{18,... | collective-permute-start | bytes 1990664 | tf_op jit(solution)/shard_map/ppermute | solution.py:39
  (109 other events, 1308.5 us)

commit v2 on v1

v2 whole, which is shorter than its diff:
```python
import functools

import jax
import jax.numpy as jnp
from jax import lax
from jax.experimental import pallas as pl
from jax.experimental.pallas import tpu as pltpu
from jax.sharding import PartitionSpec as P

BLK = 32
SEQS = 2
QUAD = 4
EPSILON = 1e-05
ROPE_BASE = 1000000.0
MASKED = -1e30
F32 = jnp.float32
BF16 = jnp.bfloat16
VMEM_LIMIT = 56 * 1024 * 1024


def dot(left, right):
    return jnp.dot(left, right, preferred_element_type=F32)


def contract_last(left, right):
    return lax.dot_general(left, right, (((1,), (1,)), ((), ())), preferred_element_type=F32)


def contract_first(left, right):
    return lax.dot_general(left, right, (((0,), (0,)), ((), ())), preferred_element_type=F32)


def shift_pairs(count, step):
    nz = count // QUAD
    return [(i, ((i // QUAD + step) % nz) * QUAD + i % QUAD) for i in range(count)]


def flip_pairs(count, bits):
    return [(i, i ^ bits) for i in range(count)]


def send(value, pairs):
    return lax.ppermute(value, "ctx", pairs)


def swap_cores(value):
    return lax.ppermute(value, "tp", [(0, 1), (1, 0)])


def gather_group(block, count):
    nz = count // QUAD
    pieces = []
    for step in range(nz):
        pairs = []
        for i, to in shift_pairs(count, step):
            pairs += [(2 * i, 2 * to), (2 * i + 1, 2 * (to ^ 2) + 1)]
        pieces.append(lax.ppermute(block, ("ctx", "tp"), pairs))
    return pieces + [swap_cores(p) for p in pieces]


def sum_everywhere(value, count):
    value = value + swap_cores(value)
    bit = 1
    while bit < count:
        value = value + send(value, flip_pairs(count, bit))
        bit *= 2
    return value


def cost(flops, bytes_accessed, transcendentals=0):
    return pl.CostEstimate(
        flops=int(flops), bytes_accessed=int(bytes_accessed), transcendentals=int(transcendentals)
    )


SCALARS = pl.BlockSpec(memory_space=pltpu.SMEM)


def kernel_call(body, name, args, out_shape, flops=0, scalars=False, scratch=()):
    vmem = pl.BlockSpec(memory_space=pltpu.VMEM)
    bytes_accessed = sum(a.size * a.dtype.itemsize for a in (*args, *out_shape))
    return pl.pallas_call(
        body,
        in_specs=[SCALARS if scalars and i == 0 else vmem for i in range(len(args))],
        out_specs=[vmem] * len(out_shape),
        out_shape=list(out_shape),
        scratch_shapes=list(scratch),
        compiler_params=pltpu.CompilerParams(vmem_limit_bytes=VMEM_LIMIT),
        cost_estimate=cost(flops, bytes_accessed),
        name=name,
    )(*args)


def shape(dims, dtype):
    return jax.ShapeDtypeStruct(dims, dtype)


def row_factor(x):
    return lax.rsqrt(jnp.mean(x * x, axis=-1, keepdims=True) + EPSILON)


def head_means(x, blocks):
    high = x.astype(BF16)
    low = (x - high.astype(F32)).astype(BF16)
    return dot(high, blocks) + dot(low, blocks)


def lanes_of(x):
    return lax.broadcasted_iota(jnp.int32, x.shape, 1)


def partner(x):
    return jnp.where(lanes_of(x) % 64 < 32, pltpu.roll(x, 96, 1), pltpu.roll(x, 32, 1))


def mask_kernel(ids_ref, seg_row_ref, seg_col_ref, bias_ref):
    me = ids_ref[0]
    count = seg_row_ref.shape[0]
    nz = count // QUAD
    tokens = seg_col_ref.shape[2]
    z, m = me // QUAD, me % QUAD

    def place(chip, offset):
        return jnp.where(offset < BLK, chip * BLK, (2 * count - 2 - chip) * BLK) + offset

    row_offset = lax.broadcasted_iota(jnp.int32, (1, tokens), 1)
    col_offset = lax.broadcasted_iota(jnp.int32, (tokens, 1), 0)
    place_q = jnp.concatenate([place(z * QUAD + (m ^ j), row_offset) for j in range(QUAD)], axis=1)
    for seq in range(SEQS):
        seg_q = jnp.concatenate(
            [
                seg_row_ref[pl.ds(z * QUAD + (m ^ j), 1), seq * tokens : (seq + 1) * tokens]
                for j in range(QUAD)
            ],
            axis=1,
        )
        for step in range(nz):
            for j in range(QUAD):
                chip = ((z + nz - step) % nz) * QUAD + (m ^ j)
                seen = (seg_col_ref[chip, seq] == seg_q) & (place(chip, col_offset) <= place_q)
                begin = (step * QUAD + j) * tokens
                bias_ref[seq, begin : begin + tokens, :] = jnp.where(seen, 0.0, MASKED)


def qkv_kernel(ids_ref, own_ref, *refs):
    mine, theirs = refs[:3], refs[3:6]
    gain_ref, w_ref, gains_ref, scale_ref, cos_ref, sin_ref, blocks_ref = refs[6:13]
    h1_ref, raw_ref, q_ref, kv_ref = refs[13:]
    core = ids_ref[1]
    gain = gain_ref[...]

    def put(seq, j, piece):
        x = piece.astype(F32)
        h1_ref[seq, j] = (x * row_factor(x) * gain).astype(BF16)

    put(0, 0, own_ref[0])
    put(1, 0, own_ref[1])
    for j in range(1, QUAD):
        put(core, j, mine[j - 1][...])
        put(1 - core, j, theirs[j - 1][...])
    rows = raw_ref.shape[0]
    raw = dot(h1_ref[...].reshape(rows, -1), w_ref[...])
    raw_ref[...] = raw
    cos, sin, blocks = cos_ref[...], sin_ref[...], blocks_ref[...]
    out = []
    for c in range(3):
        lanes = slice(128 * c, 128 * (c + 1))
        x = raw[:, lanes]
        n = x * lax.rsqrt(head_means(x * x, blocks) + EPSILON) * gains_ref[:, lanes]
        out.append((n * cos + partner(n) * sin) * scale_ref[:, lanes])
    kv_ref[...] = jnp.where(lanes_of(out[0]) < 64, out[0], raw[:, :128]).astype(BF16)
    q_ref[...] = jnp.concatenate(out[1:], axis=1).astype(BF16)


def head_lanes(x, g, upper):
    part = x[:, 128 * (g // 2) : 128 * (g // 2) + 128]
    if (g % 2 == 1) != upper:
        part = pltpu.roll(part, 64, 1)
    keep = (lanes_of(part) >= 64) if upper else (lanes_of(part) < 64)
    return jnp.where(keep, part, 0.0).astype(BF16)


def attention_forward_kernel(q_ref, bias_ref, *refs):
    kv_refs, o_ref, lse_ref = refs[:-2], refs[-2], refs[-1]
    group = lse_ref.shape[1]
    kv = jnp.concatenate([r[...] for r in kv_refs], axis=0)
    v_t = kv.T[64:]
    q = q_ref[...].astype(F32)
    bias = bias_ref[0]
    out = []
    for g in range(group):
        s = contract_last(kv, head_lanes(q, g, False)) + bias
        top = jnp.max(s, axis=0, keepdims=True)
        p = jnp.exp(s - top)
        total = jnp.sum(p, axis=0, keepdims=True)
        out.append(dot(v_t, p.astype(BF16)) / total)
        lse_ref[0, g] = top + jnp.log(total)
    o = jnp.concatenate(out, axis=0).T.astype(BF16)
    o_ref[:, 0] = o.reshape(QUAD, -1, o.shape[1])


def attention_backward_kernel(q_ref, bias_ref, lse_ref, *refs):
    do_refs, kv_refs, dq_ref, dkv_refs = refs[:QUAD], None, None, None
    rest = refs[QUAD:]
    pieces = (len(rest) - 1) // 2
    kv_refs, dq_ref, dkv_refs = rest[:pieces], rest[pieces], rest[pieces + 1 :]
    group = lse_ref.shape[1]
    kv = jnp.concatenate([r[...] for r in kv_refs], axis=0)
    k_t = kv.T[:64]
    q = q_ref[...].astype(F32)
    do = jnp.concatenate([r[0].astype(F32) for r in do_refs], axis=0)
    do = jnp.concatenate([do, jnp.zeros((do.shape[0], 64), F32)], axis=1)
    rows = q.shape[0]
    bias = bias_ref[0]
    total = jnp.zeros(kv.shape, F32)
    dq = []
    for g in range(group):
        both = jnp.concatenate([head_lanes(q, g, False), head_lanes(do, g, True)], axis=0)
        products = contract_last(kv, both)
        p = jnp.exp(products[:, :rows] + (bias - lse_ref[0, g]))
        dp = products[:, rows:]
        delta = jnp.sum(p * dp, axis=0, keepdims=True)
        ds = (p * (dp - delta)).astype(BF16)
        total = total + dot(jnp.concatenate([ds, p.astype(BF16)], axis=1), both)
        dq.append(dot(k_t, ds))
    dq.append(jnp.zeros(dq[0].shape, F32))
    dq_ref[...] = jnp.concatenate(dq, axis=0).T
    for i, ref in enumerate(dkv_refs):
        ref[...] = total[i * rows : (i + 1) * rows].astype(BF16)


def attention_specs(rows, keys, pieces):
    q = pl.BlockSpec((rows, 256), lambda s: (s, 0))
    bias = pl.BlockSpec((1, keys, rows), lambda s: (s, 0, 0))
    kv = [pl.BlockSpec((rows, 128), lambda s: (s, 0))] * pieces
    return q, bias, kv


def attention_forward(q, bias, kv, group):
    seqs, keys, rows = bias.shape
    q_spec, bias_spec, kv_specs = attention_specs(rows, keys, len(kv))
    work = seqs * group * keys * rows
    return pl.pallas_call(
        attention_forward_kernel,
        grid=(seqs,),
        in_specs=[q_spec, bias_spec, *kv_specs],
        out_specs=[
            pl.BlockSpec((QUAD, 1, rows // QUAD, group * 64), lambda s: (0, s, 0, 0)),
            pl.BlockSpec((1, group, 1, rows), lambda s: (s, 0, 0, 0)),
        ],
        out_shape=[
            shape((QUAD, seqs, rows // QUAD, group * 64), BF16),
            shape((seqs, group, 1, rows), F32),
        ],
        compiler_params=pltpu.CompilerParams(vmem_limit_bytes=VMEM_LIMIT),
        cost_estimate=cost(6 * work * 128, 4 * bias.size, work),
        name="attention_forward",
    )(q, bias, *kv)


def attention_backward(q, bias, lse, do, kv):
    seqs, keys, rows = bias.shape
    group = lse.shape[1]
    q_spec, bias_spec, kv_specs = attention_specs(rows, keys, len(kv))
    work = seqs * group * keys * rows
    return pl.pallas_call(
        attention_backward_kernel,
        grid=(seqs,),
        in_specs=[
            q_spec,
            bias_spec,
            pl.BlockSpec((1, group, 1, rows), lambda s: (s, 0, 0, 0)),
            *[pl.BlockSpec((1, rows // QUAD, group * 64), lambda s: (s, 0, 0))] * QUAD,
            *kv_specs,
        ],
        out_specs=[q_spec, *kv_specs],
        out_shape=[shape(q.shape, F32)] + [shape(k.shape, BF16) for k in kv],
        compiler_params=pltpu.CompilerParams(vmem_limit_bytes=VMEM_LIMIT),
        cost_estimate=cost(10 * work * 128, 4 * bias.size, work),
        name="attention_backward",
    )(q, bias, lse, *do, *kv)


def branch_kernel(ids_ref, *refs):
    pieces, w_ref, out_ref, stack_ref = refs[:QUAD], refs[QUAD], refs[QUAD + 1], refs[QUAD + 2]
    m = ids_ref[0] % QUAD
    for j in range(QUAD):
        stack_ref[j] = pieces[j][...]
    attn = jnp.concatenate([stack_ref[m ^ k] for k in range(QUAD)], axis=1)
    out_ref[...] = contract_last(attn, w_ref[...]).astype(BF16)


def middle_kernel(x_ref, a_ref, b_ref, gain_ref, mid_ref, h2_ref):
    mid = x_ref[...].astype(F32) + (a_ref[...].astype(F32) + b_ref[...].astype(F32))
    mid_ref[...] = mid
    h2_ref[...] = (mid * row_factor(mid) * gain_ref[...]).astype(BF16)


def hidden_terms(h2, g, w_gate, w_up, w_down):
    gate = dot(h2, w_gate)
    up = dot(h2, w_up)
    da = dot(g, w_down)
    sg = jax.nn.sigmoid(gate)
    silu = gate * sg
    act = (silu * up).astype(BF16)
    dgate = (da * up * (sg * (1.0 + gate * (1.0 - sg)))).astype(BF16)
    dup = (da * silu).astype(BF16)
    return act, dgate, dup


def own_mlp_kernel(h2_ref, g_ref, wg_ref, wu_ref, wd_ref, down_ref, dh_ref, down_sum, dh_sum):
    step = pl.program_id(0)

    @pl.when(step == 0)
    def _():
        down_sum[...] = jnp.zeros_like(down_sum)
        dh_sum[...] = jnp.zeros_like(dh_sum)

    wg, wu, wd = wg_ref[...], wu_ref[...], wd_ref[...]
    act, dgate, dup = hidden_terms(h2_ref[...], g_ref[...], wg, wu, wd)
    down_sum[...] += contract_last(act, wd)
    dh_sum[...] += contract_last(dgate, wg) + contract_last(dup, wu)

    @pl.when(step == pl.num_programs(0) - 1)
    def _():
        down_ref[...] = down_sum[...].astype(BF16)
        dh_ref[...] = dh_sum[...].astype(BF16)


def own_mlp(h2, g, w_gate, w_up, w_down):
    rows, width = h2.shape
    hidden = w_gate.shape[1]
    tile = next(t for t in (384, 256, 128, hidden) if hidden % t == 0)
    whole = pl.BlockSpec((rows, width), lambda i: (0, 0))
    weight = pl.BlockSpec((width, tile), lambda i: (0, i))
    return pl.pallas_call(
        own_mlp_kernel,
        grid=(hidden // tile,),
        in_specs=[whole, whole, weight, weight, weight],
        out_specs=[whole, whole],
        out_shape=[shape((rows, width), BF16)] * 2,
        scratch_shapes=[pltpu.VMEM((rows, width), F32)] * 2,
        compiler_params=pltpu.CompilerParams(vmem_limit_bytes=VMEM_LIMIT),
        cost_estimate=cost(12 * rows * width * hidden, 6 * width * hidden, rows * hidden),
        name="own_mlp",
    )(h2, g, w_gate, w_up, w_down)


def back_kernel(ids_ref, mid_ref, a_ref, b_ref, g_ref, gain_ref, w_ref, dx_ref, dy_ref, part_ref, *do_refs):
    m = ids_ref[0] % QUAD
    stack_ref, do_refs = do_refs[-1], do_refs[:-1]
    mid = mid_ref[...]
    factor = row_factor(mid)
    dh2 = a_ref[...].astype(F32) + b_ref[...].astype(F32)
    part_ref[...] = jnp.sum(dh2 * mid * factor, axis=0, keepdims=True)
    scaled = dh2 * gain_ref[...]
    inner = jnp.mean(mid * scaled, axis=-1, keepdims=True)
    dx = g_ref[...].astype(F32) + (factor * scaled - mid * (factor * factor * factor) * inner)
    dx_ref[...] = dx
    dy = dx.astype(BF16)
    dy_ref[...] = dy
    do = dot(dy, w_ref[...]).astype(BF16)
    columns = do.shape[1] // QUAD
    for k in range(QUAD):
        stack_ref[m ^ k] = do[:, k * columns : (k + 1) * columns]
    for j in range(QUAD):
        do_refs[j][...] = stack_ref[j]


def norm_rotate_back(grad, raw, gain, cos, sin, blocks):
    normed = grad * cos - partner(grad) * sin
    factor = lax.rsqrt(head_means(raw * raw, blocks) + EPSILON)
    scaled = normed * gain
    inner = head_means(raw * scaled, blocks)
    part = jnp.sum(normed * raw * factor, axis=0, keepdims=True)
    return factor * scaled - raw * (factor * factor * factor) * inner, part


def store_by_owner(ids_ref, total_ref, out_refs):
    nz = len(out_refs)
    z = ids_ref[0] // QUAD
    rows = out_refs[0].shape[0]
    for step, ref in enumerate(out_refs):
        begin = pl.multiple_of(((z + nz - step) % nz) * rows, 8)
        ref[...] = total_ref[pl.ds(begin, rows), :].astype(BF16)


def query_kernel(ids_ref, dq_ref, raw_ref, h1_ref, attn_ref, *refs):
    dy_refs, refs = refs[:QUAD], refs[QUAD:]
    gains_ref, cos_ref, sin_ref, blocks_ref = refs[:4]
    out_ref, part_ref, *w_refs = refs[4:-2]
    total_ref, dy_all = refs[-2:]
    cos, sin, blocks = cos_ref[...], sin_ref[...], blocks_ref[...]
    scale = 64 ** (-0.5)
    for c in range(2):
        lanes = slice(128 * c, 128 * (c + 1))
        raw_lanes = slice(128 * (c + 1), 128 * (c + 2))
        grad, part = norm_rotate_back(
            dq_ref[:, lanes] * scale,
            raw_ref[:, raw_lanes],
            gains_ref[:, raw_lanes],
            cos,
            sin,
            blocks,
        )
        out_ref[:, lanes] = grad.astype(BF16)
        part_ref[:, lanes] = part
    rows = out_ref.shape[0]
    attn = []
    for seq in range(SEQS):
        for j in range(QUAD):
            dy_all[seq, j] = dy_refs[j][seq]
            attn.append(attn_ref[j, seq])
    columns = attn[0].shape[1]
    dy = dy_all[...].reshape(rows, -1)
    grad_wq = contract_first(h1_ref[...].reshape(rows, -1), out_ref[...])
    grad_wo = contract_first(dy, jnp.concatenate(attn, axis=0))
    total_ref[...] = jnp.concatenate([grad_wq[:, :columns], grad_wo], axis=1)
    store_by_owner(ids_ref, total_ref, w_refs)


def key_kernel(ids_ref, raw_ref, h1_ref, dq_ref, gains_ref, cos_ref, sin_ref, blocks_ref, *refs):
    nz = (len(refs) - 2 - QUAD) // 2
    dkv_refs, refs = refs[:nz], refs[nz:]
    part_ref, piece_refs, w_refs, total_ref = refs[0], refs[1 : 1 + QUAD], refs[1 + QUAD : -1], refs[-1]
    dkv = dkv_refs[0][...].astype(F32)
    for ref in dkv_refs[1:]:
        dkv = dkv + ref[...].astype(F32)
    grad, part = norm_rotate_back(
        dkv, raw_ref[:, :128], gains_ref[:, :128], cos_ref[...], sin_ref[...], blocks_ref[...]
    )
    part_ref[...] = part
    low = jnp.where(lanes_of(dkv) < 64, grad, dkv).astype(BF16)
    rows = low.shape[0]
    tokens = rows // (SEQS * QUAD)
    for j in range(QUAD):
        for seq in range(SEQS):
            begin = (seq * QUAD + j) * tokens
            to = slice(seq * tokens, (seq + 1) * tokens)
            piece_refs[j][to, :128] = low[begin : begin + tokens]
            piece_refs[j][to, 128:] = dq_ref[begin : begin + tokens]
    total_ref[...] = contract_first(h1_ref[...].reshape(rows, -1), low)
    store_by_owner(ids_ref, total_ref, w_refs)


def spread_kernel(ids_ref, *refs):
    nz = (len(refs) - QUAD - 1) // 2
    first, second, (own_ref, *out_refs), total_ref = (
        refs[:nz],
        refs[nz : 2 * nz],
        refs[2 * nz : -1],
        refs[-1],
    )
    sums = []
    for group in (first, second):
        total = group[0][...].astype(F32)
        for ref in group[1:]:
            total = total + ref[...].astype(F32)
        sums.append(total)
    total_ref[...] = jnp.concatenate(sums, axis=1)
    m = ids_ref[0] % QUAD
    rows = own_ref.shape[0]
    for j in range(QUAD):
        part = total_ref[pl.ds(pl.multiple_of((m ^ j) * rows, 8), rows), :]
        if j == 0:
            own_ref[...] = part
        else:
            out_refs[j - 1][...] = part.astype(BF16)


def assemble_kernel(ids_ref, own_ref, a_ref, b_ref, c_ref, wq_ref, wk_ref, wv_ref, wo_ref, stack_ref):
    m = ids_ref[0] % QUAD
    stack_ref[0] = own_ref[...]
    for j, ref in enumerate((a_ref, b_ref, c_ref)):
        stack_ref[j + 1] = ref[...].astype(F32)
    parts = [stack_ref[m ^ k] for k in range(QUAD)]
    columns = wq_ref.shape[1] // QUAD
    wq_ref[...] = jnp.concatenate([p[:, :columns] for p in parts], axis=1)
    wo_ref[...] = jnp.concatenate([p[:, columns : 2 * columns] for p in parts], axis=1)
    wk_ref[...] = jnp.concatenate([p[:, 2 * columns : 2 * columns + 64] for p in parts], axis=1)
    wv_ref[...] = jnp.concatenate([p[:, 2 * columns + 64 : 2 * columns + 128] for p in parts], axis=1)


def input_grad_kernel(ids_ref, *refs):
    pieces, (x_ref, wq_ref, wk_ref, wv_ref, out_ref, part_ref, stack_ref) = refs[:QUAD], refs[QUAD:]
    m = ids_ref[0] % QUAD
    for j in range(QUAD):
        stack_ref[j] = pieces[j][...]
    parts = [stack_ref[m ^ k] for k in range(QUAD)]
    columns = wq_ref.shape[1] // QUAD
    dk = jnp.concatenate([p[:, :64] for p in parts], axis=1)
    dv = jnp.concatenate([p[:, 64:128] for p in parts], axis=1)
    dq = jnp.concatenate([p[:, 128 : 128 + columns] for p in parts], axis=1)
    total = (
        contract_last(dq, wq_ref[...])
        + contract_last(dk, wk_ref[...])
        + contract_last(dv, wv_ref[...])
    )
    out_ref[...] = total.astype(BF16)
    x = x_ref[...].astype(F32)
    part_ref[...] = jnp.sum(total * x * row_factor(x), axis=0, keepdims=True)


def tokens_kernel(x_ref, dx_ref, a_ref, b_ref, gain_ref, out_ref):
    x = x_ref[...].astype(F32)
    factor = row_factor(x)
    scaled = (a_ref[...].astype(F32) + b_ref[...].astype(F32)) * gain_ref[...]
    inner = jnp.mean(x * scaled, axis=-1, keepdims=True)
    back = factor * scaled - x * (factor * factor * factor) * inner
    out_ref[...] = (dx_ref[...] + back).astype(BF16)


def output_kernel(mid_ref, a_ref, b_ref, out_ref):
    out_ref[...] = (mid_ref[...] + (a_ref[...].astype(F32) + b_ref[...].astype(F32))).astype(BF16)


def bulk_mlp_kernel(ids_ref, *refs, pieces, row_tile):
    h2_pieces, g_pieces = refs[:pieces], refs[pieces : 2 * pieces]
    wg_ref, wu_ref, wd_ref = refs[2 * pieces : 2 * pieces + 3]
    own_refs, other_refs = refs[2 * pieces + 3 : 2 * pieces + 6], refs[2 * pieces + 6 : 2 * pieces + 9]
    h2_ref, g_ref, h2c_ref, gc_ref, sems = refs[2 * pieces + 9 :]
    rows = h2_pieces[0].shape[0]
    tokens, width = h2_ref.shape
    own_rows = own_refs[0].shape[0]
    pair_rows = 2 * own_rows

    @pl.when(pl.program_id(0) == 0)
    def _():
        copies = []
        for side, (source, target) in enumerate(((h2_pieces, h2_ref), (g_pieces, g_ref))):
            for i in range(pieces):
                copies.append(
                    pltpu.make_async_copy(
                        source[i], target.at[pl.ds(i * rows, rows)], sems.at[side * pieces + i]
                    )
                )
        for copy in copies:
            copy.start()
        me = ids_ref[0]
        row = lax.broadcasted_iota(jnp.int32, (pair_rows, width), 0)
        col = lax.broadcasted_iota(jnp.int32, (pair_rows, width), 1)
        target = jnp.where(row < own_rows, me * own_rows + row, ((me ^ 1) - 1) * own_rows + row)
        chosen = jnp.where(col == target, 1.0, 0.0).astype(BF16)
        for copy in copies:
            copy.wait()
        h2c_ref[...] = contract_last(chosen, h2_ref[...]).astype(BF16)
        gc_ref[...] = contract_last(chosen, g_ref[...]).astype(BF16)

    wg, wu, wd = wg_ref[...], wu_ref[...], wd_ref[...]
    totals = None
    for begin in range(0, tokens, row_tile):
        part = slice(begin, begin + row_tile)
        act, dgate, dup = hidden_terms(h2_ref[part], g_ref[part], wg, wu, wd)
        h2c, gc = h2c_ref[:, part], gc_ref[:, part]
        terms = [dot(h2c, dgate), dot(h2c, dup), dot(gc, act)]
        totals = terms if totals is None else [a + b for a, b in zip(totals, terms)]
    for own, other, total in zip(own_refs, other_refs, totals):
        own[...] = total[:own_rows]
        other[...] = total[own_rows:].astype(BF16)


def bulk_mlp(ids, h2, g, weights, own_rows, begin, end, tile):
    rows, width = h2[0].shape
    pieces = len(h2)
    tokens = pieces * rows
    hidden = weights[0].shape[1]
    out_hidden = min(end * tile, hidden) - begin * tile
    anywhere = pl.BlockSpec(memory_space=pl.ANY)
    weight = pl.BlockSpec((width, tile), lambda i: (0, i + begin))
    result = pl.BlockSpec((own_rows, tile), lambda i: (0, i))
    return pl.pallas_call(
        functools.partial(bulk_mlp_kernel, pieces=pieces, row_tile=min(tokens, 1024)),
        grid=(end - begin,),
        in_specs=[SCALARS] + [anywhere] * (2 * pieces) + [weight] * 3,
        out_specs=[result] * 6,
        out_shape=[shape((own_rows, out_hidden), F32)] * 3 + [shape((own_rows, out_hidden), BF16)] * 3,
        scratch_shapes=[pltpu.VMEM((tokens, width), BF16)] * 2
        + [pltpu.VMEM((2 * own_rows, tokens), BF16)] * 2
        + [pltpu.SemaphoreType.DMA((2 * pieces,))],
        compiler_params=pltpu.CompilerParams(vmem_limit_bytes=VMEM_LIMIT),
        cost_estimate=cost(
            6 * tokens * (width + 2 * own_rows) * out_hidden,
            6 * width * out_hidden + 4 * tokens * width,
            tokens * out_hidden,
        ),
        name="bulk_mlp",
    )(ids, *h2, *g, *weights)


def shards(
    tokens,
    w_query,
    w_key,
    w_value,
    w_output,
    w_gate,
    w_up,
    w_down,
    attn_gain,
    mlp_gain,
    query_gain,
    key_gain,
    segments,
    positions,
    cotangent,
):
    count = lax.axis_size("ctx")
    me = lax.axis_index("ctx")
    core = lax.axis_index("tp")
    nz = count // QUAD
    m = me % QUAD
    head = query_gain.shape[0]
    rows, model = tokens.shape
    q_heads = w_query.shape[1] // head
    kv_heads = w_key.shape[1] // head
    group = q_heads // kv_heads
    pair = rows // SEQS
    quad_rows = QUAD * rows
    columns = group * head
    own_rows = model // count
    flips = [flip_pairs(count, j) for j in range(QUAD)]
    ids = jnp.stack([me, core]).astype(jnp.int32)
    attn_gain_row = attn_gain[None, :]
    mlp_gain_row = mlp_gain[None, :]

    def quad_exchange(pieces):
        return [pieces[0]] + [send(pieces[j], flips[j]) for j in range(1, QUAD)]

    own_tokens = tokens.reshape(SEQS, pair, model)
    half = lax.dynamic_index_in_dim(own_tokens, core, 0, keepdims=False)
    mine = [send(half, flips[j]) for j in range(1, QUAD)]
    theirs = [swap_cores(p) for p in mine]
    quad_positions = [positions] + [send(positions, flips[j]) for j in range(1, QUAD)]
    g_group = gather_group(cotangent, count)

    place = jnp.stack(quad_positions).reshape(QUAD, SEQS, pair).transpose(1, 0, 2).reshape(-1, 1)
    freqs = ROPE_BASE ** (-2.0 * jnp.arange(head // 2, dtype=F32) / head)
    angles = place.astype(F32) * jnp.tile(freqs, 4)[None, :]
    sign = jnp.tile(jnp.repeat(jnp.array([-1.0, 1.0], F32), head // 2), 2)[None, :]
    cos, sin = jnp.cos(angles), jnp.sin(angles) * sign
    lane_head = jnp.arange(2 * head) // head
    blocks = jnp.where(lane_head[:, None] == lane_head[None, :], 1.0 / head, 0.0).astype(BF16)
    ones = jnp.ones((head,), F32)
    head_gains = jnp.concatenate([key_gain, ones] + [query_gain] * group + [ones])[None, :]
    lane_scale = jnp.repeat(jnp.array([1.0] * 2 + [head ** (-0.5)] * (group + 1), F32), head)[None, :]
    w_head = jnp.concatenate(
        [
            lax.dynamic_slice_in_dim(w_key, m * head, head, 1),
            lax.dynamic_slice_in_dim(w_value, m * head, head, 1),
            lax.dynamic_slice_in_dim(w_query, m * columns, columns, 1),
            jnp.zeros((model, head), BF16),
        ],
        axis=1,
    )
    seg_rows = segments.reshape(count, SEQS * pair)
    (bias,) = kernel_call(
        mask_kernel,
        "visible",
        (ids, seg_rows, seg_rows.reshape(count, SEQS, pair, 1)),
        [shape((SEQS, count * pair, QUAD * pair), F32)],
        scalars=True,
    )

    h1, raw, q, kv_own = kernel_call(
        qkv_kernel,
        "query_key_value",
        (
            ids,
            own_tokens,
            *mine,
            *theirs,
            attn_gain_row,
            w_head,
            head_gains,
            lane_scale,
            cos,
            sin,
            blocks,
        ),
        [
            shape((SEQS, QUAD, pair, model), BF16),
            shape((quad_rows, 6 * head), F32),
            shape((quad_rows, 4 * head), BF16),
            shape((quad_rows, 2 * head), BF16),
        ],
        flops=2 * quad_rows * model * 6 * head,
        scalars=True,
    )
    kv = [kv_own] + [send(kv_own, shift_pairs(count, s)) for s in range(1, nz)]
    attn, lse = attention_forward(q, bias, kv, group)
    attn_pieces = quad_exchange([attn[j].reshape(rows, columns) for j in range(QUAD)])
    (branch,) = kernel_call(
        branch_kernel,
        "branch",
        (ids, *attn_pieces, w_output),
        [shape((rows, model), BF16)],
        flops=2 * rows * model * w_output.shape[1],
        scalars=True,
        scratch=[pltpu.VMEM((QUAD, rows, columns), BF16)],
    )
    middle, h2 = kernel_call(
        middle_kernel,
        "middle",
        (tokens, branch, swap_cores(branch), mlp_gain_row),
        [shape((rows, model), F32), shape((rows, model), BF16)],
    )
    h2_group = gather_group(h2, count)

    down, dh2 = own_mlp(h2, cotangent, w_gate, w_up, w_down)
    grad_middle, dy, mlp_gain_part, *do = kernel_call(
        back_kernel,
        "back",
        (ids, middle, dh2, swap_cores(dh2), cotangent, mlp_gain_row, w_output),
        [
            shape((rows, model), F32),
            shape((rows, model), BF16),
            shape((1, model), F32),
            *[shape((rows, columns), BF16)] * QUAD,
        ],
        flops=2 * rows * model * w_output.shape[1],
        scalars=True,
        scratch=[pltpu.VMEM((QUAD, rows, columns), BF16)],
    )
    (output,) = kernel_call(
        output_kernel, "output", (middle, down, swap_cores(down)), [shape((rows, model), BF16)]
    )
    do_pieces = [d.reshape(SEQS, pair, columns) for d in quad_exchange(do)]
    dq, *dkv = attention_backward(q, bias, lse, do_pieces, kv)
    dkv = [dkv[0]] + [send(dkv[s], shift_pairs(count, nz - s)) for s in range(1, nz)]

    dy_pieces = [p.reshape(SEQS, pair, model) for p in quad_exchange([dy] * QUAD)]
    z_rows = model // nz
    dq_low, query_part, *w_first = kernel_call(
        query_kernel,
        "query_grad",
        (ids, dq, raw, h1, attn, *dy_pieces, head_gains, cos, sin, blocks),
        [
            shape((quad_rows, 4 * head), BF16),
            shape((1, 4 * head), F32),
            *[shape((z_rows, 2 * columns), BF16)] * nz,
        ],
        flops=2 * quad_rows * model * 7 * head,
        scalars=True,
        scratch=[
            pltpu.VMEM((model, 2 * columns), F32),
            pltpu.VMEM((SEQS, QUAD, pair, model), BF16),
        ],
    )
    w_first = [w_first[0]] + [send(w_first[s], shift_pairs(count, nz - s)) for s in range(1, nz)]

    key_part, *rest = kernel_call(
        key_kernel,
        "key_grad",
        (ids, raw, h1, dq_low, head_gains, cos, sin, blocks, *dkv),
        [
            shape((1, 2 * head), F32),
            *[shape((rows, 6 * head), BF16)] * QUAD,
            *[shape((z_rows, 2 * head), BF16)] * nz,
        ],
        flops=2 * quad_rows * model * 2 * head,
        scalars=True,
        scratch=[pltpu.VMEM((model, 2 * head), F32)],
    )
    grad_pieces, w_second = quad_exchange(rest[:QUAD]), rest[QUAD:]
    w_second = [w_second[0]] + [send(w_second[s], shift_pairs(count, nz - s)) for s in range(1, nz)]
    dh1, attn_gain_part = kernel_call(
        input_grad_kernel,
        "input_grad",
        (ids, *grad_pieces, tokens, w_query, w_key, w_value),
        [shape((rows, model), BF16), shape((1, model), F32)],
        flops=2 * rows * model * (q_heads + 2 * kv_heads) * head,
        scalars=True,
        scratch=[pltpu.VMEM((QUAD, rows, 6 * head), BF16)],
    )
    (grad_tokens,) = kernel_call(
        tokens_kernel,
        "tokens_grad",
        (tokens, grad_middle, dh1, swap_cores(dh1), attn_gain_row),
        [shape((rows, model), BF16)],
    )
    spread = kernel_call(
        spread_kernel,
        "spread",
        (ids, *w_first, *w_second),
        [shape((own_rows, 8 * head), F32)] + [shape((own_rows, 8 * head), BF16)] * (QUAD - 1),
        scalars=True,
        scratch=[pltpu.VMEM((z_rows, 8 * head), F32)],
    )
    grad_wq, grad_wk, grad_wv, grad_wo = kernel_call(
        assemble_kernel,
        "assemble",
        (ids, *quad_exchange(spread)),
        [
            shape((own_rows, q_heads * head), F32),
            shape((own_rows, kv_heads * head), F32),
            shape((own_rows, kv_heads * head), F32),
            shape((own_rows, q_heads * head), F32),
        ],
        scalars=True,
        scratch=[pltpu.VMEM((QUAD, own_rows, 8 * head), F32)],
    )

    tile = 512
    tiles = pl.cdiv(w_gate.shape[1], tile)
    bulk = bulk_mlp(ids, h2_group, g_group, (w_gate, w_up, w_down), own_rows, 0, tiles, tile)
    mlp_grads = [a + send(b, flips[1]).astype(F32) for a, b in zip(bulk[:3], bulk[3:])]

    gains = sum_everywhere(
        jnp.concatenate([attn_gain_part, 0.5 * mlp_gain_part, query_part, key_part], axis=1)[0], count
    )
    query_sum = gains[2 * model : 2 * model + columns].reshape(group, head)
    return (
        output,
        grad_tokens,
        grad_wq,
        grad_wk,
        grad_wv,
        grad_wo,
        mlp_grads[0],
        mlp_grads[1],
        mlp_grads[2],
        gains[:model],
        gains[model : 2 * model],
        jnp.sum(query_sum, axis=0),
        gains[2 * model + 4 * head : 2 * model + 5 * head],
    )


def solution(mesh):
    rows = P("ctx", None)
    columns = P(None, "tp")
    both = P("ctx", "tp")
    in_specs = (rows,) + (columns,) * 7 + (P(),) * 5 + (P("ctx"), rows)
    out_specs = (rows, rows) + (both,) * 7 + (P(),) * 4
    return jax.shard_map(shards, mesh=mesh, in_specs=in_specs, out_specs=out_specs, check_vma=False)
```

time: 489 us -> 313 us (0.64); the launches traced: 482 us -> 312 us
  local copies, waits for them, and re-layouts: 129 us -> 18.6 us
  other arithmetic: 62 us -> 9.5 us
  Pallas kernels: 88.1 us -> 130 us
  waiting for transfers between devices: 96.9 us -> 70.5 us
  matrix products: 24.3 us -> 0 us
    concatenate x17 -> x2, local copies, waits for them, and re-layouts: 44.5 us -> 0.15 us  [the longest x1 0.08 us: shards(): jnp.concatenate([key_gain, ones] + [query_gain] * group + [ones])[None, :]]
    pallas_call x3 -> x15, Pallas kernels: 66.6 us -> 109 us  [the longest x1 52.5 us: bulk_mlp(): pl.pallas_call(functools.partial(bulk_mlp_kernel, pieces=pieces, row_tile...]
    ppermute x50 -> x40, waiting for transfers between devices: 95.7 us -> 65.9 us  [send(): return lax.ppermute(value, 'ctx', pairs)]
    dot_general x20 -> x0, matrix products: 24.3 us -> none  [the longest x16 19.3 us: dot(): return jnp.dot(left, right, preferred_element_type=F32)]
    ppermute x50 -> x40, starting transfers between devices: 78.4 us -> 55.3 us  [send(): return lax.ppermute(value, 'ctx', pairs)]
    mul x27 -> x2, local copies, waits for them, and re-layouts: 21.5 us -> 0.17 us  [the longest x1 0.09 us: shards(): angles = place.astype(F32) * jnp.tile(freqs, 4)[None, :]]
    convert_element_type x11 -> x2, other arithmetic: 15.7 us -> 0.69 us  [the longest x1 0.69 us: shards(): jnp.where(lane_head[:, None] == lane_head[None, :], 1.0 / head, 0.0)]
    ppermute x7 -> x16, starting transfers between devices: 1.04 us -> 14.4 us  [swap_cores(): return lax.ppermute(value, 'tp', [(0, 1), (1, 0)])]
  transfers between devices with their start and end apart: 57 -> 64, of which waited for: 16 -> 20; matrix products, arithmetic and copies ran while one was open for 40% -> 6% of each run, Pallas kernels for 18% -> 38%
where the time goes in v2:
time: 313 us; the launch traced here: 312 us
  Pallas kernels  130 us (42%)
  starting transfers between devices  82.7 us (26%)
  waiting for transfers between devices  70.5 us (23%)
  local copies, waits for them, and re-layouts  18.6 us (6%)
  other arithmetic  9.5 us (3%)
    ppermute x40, waiting for transfers between devices, send(): return lax.ppermute(value, 'ctx', pairs)  65.9 us
    ppermute x40, starting transfers between devices, send(): return lax.ppermute(value, 'ctx', pairs)  55.3 us
    pallas_call x1, Pallas kernels, bulk_mlp(): pl.pallas_call(functools.partial(bulk_mlp_kernel, pieces=pieces, row_tile...  52.5 us
    pallas_call x12, Pallas kernels, kernel_call(): pl.pallas_call(body, in_specs=[SCALARS if scalars and i == 0 else vmem fo...  40.9 us
    pallas_call x1, Pallas kernels, own_mlp(): pl.pallas_call(own_mlp_kernel, grid=(hidden // tile,), in_specs=[whole, w...  20.8 us
    ppermute x16, starting transfers between devices, swap_cores(): return lax.ppermute(value, 'tp', [(0, 1), (1, 0)])  14.4 us
    ppermute x8, starting transfers between devices, gather_group(): pieces.append(lax.ppermute(block, ('ctx', 'tp'), pairs))  13 us
    pallas_call x1, Pallas kernels, attention_backward(): pl.pallas_call(attention_backward_kernel, grid=(seqs,), in_specs=[q_spec,...  8.98 us
  transfers between devices with their start and end apart: 64, of which 20 were waited for; matrix products, arithmetic and copies ran while one was open for 6% of the time, Pallas kernels for 38%

profile of v2, /device:TPU:0, one launch (start us, length us, event | category | flops | bytes accessed | tf_op | source)
XLA Modules:
  0.0 312.4 jit_solution(2419004596037115480)
XLA Ops:
  1.7 3.0 collective-permute-start
  6.3 2.9 collective-permute-start.8
  17.9 2.9 collective-permute-done.6
  24.3 4.9 %query_key_value.1 = (bf16[2,4,64,1536]{3,2,1,0:T(8,128)(2,1)}, f32[512,384]{1,0:T(8,128)}, bf16[512,256]{1,0:T(8,128)(2,1)}, bf16[512,128]{1,0:T(8,128)(2,1)}) custom-call(s32[2]{0:T(128)} %pad_add_fusion.ids_ref, bf16[2,64,1536]{2,1,0:T(8,128)(2,1)} %bitcast.21, bf16[64,1536]{1,0:T(8,128)(2,1)} %copy-done.18, bf16[64,1536]{1,0:T(8,128)(2,1)} %copy-done.19, ...), custom_call_target="tpu_custom_call" | custom-call | flops 603979776 | bytes 6071304 | tf_op jit(solution)/shard_map/query_key_value/pallas_call | solution.py:82
  30.7 2.6 collective-permute-start.10
  36.5 2.9 visible.1.bias_ref
  39.5 3.3 %collective-permute-done.10.refs_2_.refs_6_ = bf16[512,128]{1,0:T(8,128)(2,1)S(1)} collective-permute-done((bf16[512,128]{1,0:T(8,128)(2,1)}, bf16[512,128]{1,0:T(8,128)(2,1)S(1)}, u32[]{:S(2)}, u32[]{:S(2)}) %collective-permute-start.10) | collective-permute-done | bytes 131104 | tf_op jit(solution)/shard_map/ppermute | solution.py:43
  43.5 6.4 %attention_forward.1 = (bf16[4,2,64,192]{3,2,1,0:T(8,128)(2,1)}, f32[2,3,1,256]{3,2,1,0:T(1,128)}) custom-call(bf16[512,256]{1,0:T(8,128)(2,1)} %get-tuple-element.66.q_ref, f32[2,1024,256]{2,1,0:T(8,128)} %visible.1.bias_ref, bf16[512,128]{1,0:T(8,128)(2,1)} %get-tuple-element.67.refs_0_.refs_4_, bf16[512,128]{1,0:T(8,128)(2,1)} %copy-done.69, ...), custom_call_target="tpu_custom_call" | custom-call | flops 1207959552 | bytes 2097152 | tf_op jit(solution)/shard_map/attention_forward/pallas_call | solution.py:243
  55.6 3.3 %collective-permute-start.49 = (bf16[128,1536]{1,0:T(8,128)(2,1)S(1)}, bf16[128,1536]{1,0:T(8,128)(2,1)S(1)}, u32[]{:S(2)}, u32[]{:S(2)}) collective-permute-start(bf16[128,1536]{1,0:T(8,128)(2,1)S(1)} %copy-done.2), channel_id=1, source_target_pairs={{0,8},{1,13},{2,10},{3,15},{4,12},{5,9},{6,14},{7,11},{8,16},{9,21... | collective-permute-start | bytes 1179656 | tf_op jit(solution)/shard_map/ppermute | solution.py:57
  59.6 3.5 %branch.1.a_ref = bf16[128,1536]{1,0:T(8,128)(2,1)} custom-call(s32[2]{0:T(128)} %pad_add_fusion.ids_ref, bf16[128,192]{1,0:T(8,128)(2,1)} %bitcast.26, bf16[128,192]{1,0:T(8,128)(2,1)} %copy-done.36, bf16[128,192]{1,0:T(8,128)(2,1)} %copy-done.37, bf16[128,192]{1,0:T(8,128)(2,1)} %copy-done.38, bf16[1536,768]{1,0:T(8,128)(2,1)} %w_ref.1), custom_call_target="tpu_custom_call" | custom-call | flops 301989888 | bytes 2949128 | tf_op jit(solution)/shard_map/branch/pallas_call | solution.py:82
  74.2 20.8 %own_mlp.1 = (bf16[128,1536]{1,0:T(8,128)(2,1)}, bf16[128,1536]{1,0:T(8,128)(2,1)}) custom-call(bf16[128,1536]{1,0:T(8,128)(2,1)} %get-tuple-element.70.h2_ref, bf16[128,1536]{1,0:T(8,128)(2,1)} %g_ref.3, bf16[1536,3456]{1,0:T(8,128)(2,1)} %refs_16_.1, bf16[1536,3456]{1,0:T(8,128)(2,1)} %refs_17_.1, bf16[1536,3456]{1,0:T(8,128)(2,1)} %refs_18_.1), custom_call_target="tpu_custom_call" | custom-call | flops 8153726976 | bytes 31850496 | tf_op jit(solution)/shard_map/own_mlp/pallas_call | solution.py:336
  98.1 2.7 collective-permute-start.42
  101.5 3.9 %back.1 = (f32[128,1536]{1,0:T(8,128)}, bf16[128,1536]{1,0:T(8,128)(2,1)}, f32[1,1536]{1,0:T(1,128)}, bf16[128,192]{1,0:T(8,128)(2,1)}, bf16[128,192]{1,0:T(8,12...) custom-call(s32[2]{0:T(128)} %pad_add_fusion.ids_ref, f32[128,1536]{1,0:T(8,128)} %get-tuple-element.69.mid_ref, ...), custom_call_target="tpu_custom_call" | custom-call | flops 301989888 | bytes 5713928 | tf_op jit(solution)/shard_map/back/pallas_call | solution.py:82
  106.1 2.8 collective-permute-done.41.refs_1_
  114.6 2.8 collective-permute-start.23
  117.5 9.0 %attention_backward.1 = (f32[512,256]{1,0:T(8,128)}, bf16[512,128]{1,0:T(8,128)(2,1)}, bf16[512,128]{1,0:T(8,128)(2,1)}, bf16[512,128]{1,0:T(8,128)(2,1)}, bf16[512,128]{1,0:T(8,128)(2,1)}) custom-call(bf16[512,256]{1,0:T(8,128)(2,1)} %get-tuple-element.66.q_ref, f32[2,1024,256]{2,1,0:T(8,128)} %visible.1.bias_ref, ...), custom_call_target="tpu_custom_call" | custom-call | flops 2013265920 | bytes 2097152 | tf_op jit(solution)/shard_map/attention_backward/pallas_call | solution.py:266
  127.1 7.9 %collective-permute-start.24 = (bf16[512,128]{1,0:T(8,128)(2,1)}, bf16[512,128]{1,0:T(8,128)(2,1)S(1)}, u32[]{:S(2)}, u32[]{:S(2)}) collective-permute-start(bf16[512,128]{1,0:T(8,128)(2,1)} %get-tuple-element.85), channel_id=1, source_target_pairs={{0,24},{2,26},{4,28},{6,30},{8,0},{10,2},{12,4},{14,6},{16,8},{18,... | collective-permute-start | bytes 393224 | tf_op jit(solution)/shard_map/ppermute | solution.py:43
  135.0 2.8 collective-permute-done.24.refs_1_
  137.9 4.6 %collective-permute-done.25.refs_2_ = bf16[512,128]{1,0:T(8,128)(2,1)S(1)} collective-permute-done((bf16[512,128]{1,0:T(8,128)(2,1)}, bf16[512,128]{1,0:T(8,128)(2,1)S(1)}, u32[]{:S(2)}, u32[]{:S(2)}) %collective-permute-start.25) | collective-permute-done | bytes 131104 | tf_op jit(solution)/shard_map/ppermute | solution.py:43
  142.5 8.2 %collective-permute-start.55 = (bf16[128,1536]{1,0:T(8,128)(2,1)S(1)}, bf16[128,1536]{1,0:T(8,128)(2,1)S(1)}, u32[]{:S(2)}, u32[]{:S(2)}) collective-permute-start(bf16[128,1536]{1,0:T(8,128)(2,1)S(1)} %collective-permute-done.51.refs_11_), channel_id=1, source_target_pairs={{0,1},{1,0},{2,3},{3,2},{4,5},{5,4},{6,7},{7,6},{8,9},{9,8},{10,11... | collective-permute-start | bytes 1179656 | tf_op jit(solution)/shard_map/ppermute | solution.py:47
  152.2 5.3 %query_grad.1 = (bf16[512,256]{1,0:T(8,128)(2,1)}, f32[1,256]{1,0:T(1,128)}, bf16[384,384]{1,0:T(8,128)(2,1)}, bf16[384,384]{1,0:T(8,128)(2,1)}, bf16[384,384]{1,0:T(8,128)(2,1)}, /*index=5*/bf16[384,384]{1,0:T(8,128)(2,1)}) custom-call(s32[2]{0:T(128)} %pad_add_fusion.ids_ref, f32[512,256]{1,0:T(8,128)} %get-tuple-element.81.dq_ref, ...), custom_call_target="tpu_custom_call" | custom-call | flops 704643072 | bytes 6654472 | tf_op jit(solution)/shard_map/query_grad/pallas_call | solution.py:82
  157.5 3.8 %key_grad.1 = (f32[1,128]{1,0:T(1,128)}, bf16[128,384]{1,0:T(8,128)(2,1)}, bf16[128,384]{1,0:T(8,128)(2,1)}, bf16[128,384]{1,0:T(8,128)(2,1)}, bf16[128,384]{1,0...) custom-call(s32[2]{0:T(128)} %pad_add_fusion.ids_ref, ...), custom_call_target="tpu_custom_call" | custom-call | flops 201326592 | bytes 4491272 | tf_op jit(solution)/shard_map/key_grad/pallas_call | solution.py:82
  166.1 52.5 %bulk_mlp.1 = (f32[96,3456]{1,0:T(8,128)}, f32[96,3456]{1,0:T(8,128)}, f32[96,3456]{1,0:T(8,128)}, bf16[96,3456]{1,0:T(8,128)(2,1)}, bf16[96,3456]{1,0:T(8,128)(2,1)}, /*index=5*/bf16[96,3456]{1,0:T(8,128)(2,1)}) custom-call(s32[2]{0:T(128)} %pad_add_fusion.ids_ref, bf16[128,1536]{1,0:T(8,128)(2,1)} %copy-done.57, bf16[128,1536]{1,0:T(8,128)(2,1)} %copy-done.58, ...), custom_call_target="tpu_custom_call" | custom-call | flops 36691771392 | bytes 38141952 | tf_op jit(solution)/shard_map/bulk_mlp/pallas_call | solution.py:571
  220.5 4.7 %input_grad.1 = (bf16[128,1536]{1,0:T(8,128)(2,1)}, f32[1,1536]{1,0:T(1,128)}) custom-call(s32[2]{0:T(128)} %pad_add_fusion.ids_ref, bf16[128,384]{1,0:T(8,128)(2,1)} %get-tuple-element.88.refs_0_, bf16[128,384]{1,0:T(8,128)(2,1)} %copy-done.33, bf16[128,384]{1,0:T(8,128)(2,1)} %copy-done.34, bf16[128,384]{1,0:T(8,128)(2,1)} %copy-done.35, ...), custom_call_target="tpu_custom_call" | custom-call | flops 503316480 | bytes 5117960 | tf_op jit(solution)/shard_map/input_grad/pallas_call | solution.py:82
  229.1 7.0 %collective-permute-done.60 = f32[3456]{0:T(1024)S(1)} collective-permute-done((f32[3456]{0:T(1024)S(1)}, f32[3456]{0:T(1024)S(1)}, u32[]{:S(2)}, u32[]{:S(2)}) %collective-permute-start.60) | collective-permute-done | bytes 13856 | tf_op jit(solution)/shard_map/ppermute | solution.py:43
  236.4 2.8 collective-permute-start.31
  242.9 14.0 %collective-permute-done.62 = f32[3456]{0:T(1024)S(1)} collective-permute-done((f32[3456]{0:T(1024)S(1)}, f32[3456]{0:T(1024)S(1)}, u32[]{:S(2)}, u32[]{:S(2)}) %collective-permute-start.62) | collective-permute-done | bytes 13856 | tf_op jit(solution)/shard_map/ppermute | solution.py:43
  259.4 4.0 %collective-permute-done.36.refs_7_ = bf16[384,128]{1,0:T(8,128)(2,1)S(1)} collective-permute-done((bf16[384,128]{1,0:T(8,128)(2,1)S(1)}, bf16[384,128]{1,0:T(8,128)(2,1)S(1)}, u32[]{:S(2)}, u32[]{:S(2)}) %collective-permute-start.36) | collective-permute-done | bytes 98336 | tf_op jit(solution)/shard_map/ppermute | solution.py:43
  263.4 4.2 %collective-permute-start.63 = (f32[3456]{0:T(1024)S(1)}, f32[3456]{0:T(1024)S(1)}, u32[]{:S(2)}, u32[]{:S(2)}) collective-permute-start(f32[3456]{0:T(1024)S(1)} %add.58), channel_id=1, source_target_pairs={{0,16},{2,18},{4,20},{6,22},{8,24},{10,26},{12,28},{14,30},{16,0},... | collective-permute-start | bytes 41480 | tf_op jit(solution)/shard_map/ppermute | solution.py:43
  287.1 2.6 tokens_grad.1
  290.9 7.4 %collective-permute-done.57 = bf16[96,3456]{1,0:T(8,128)(2,1)S(1)} collective-permute-done((bf16[96,3456]{1,0:T(8,128)(2,1)S(1)}, bf16[96,3456]{1,0:T(8,128)(2,1)S(1)}, u32[]{:S(2)}, u32[]{:S(2)}) %collective-permute-start.57) | collective-permute-done | bytes 663584 | tf_op jit(solution)/shard_map/ppermute | solution.py:43
  299.5 11.6 %collective-permute-done.58 = bf16[96,3456]{1,0:T(8,128)(2,1)S(1)} collective-permute-done((bf16[96,3456]{1,0:T(8,128)(2,1)S(1)}, bf16[96,3456]{1,0:T(8,128)(2,1)S(1)}, u32[]{:S(2)}, u32[]{:S(2)}) %collective-permute-start.58) | collective-permute-done | bytes 663584 | tf_op jit(solution)/shard_map/ppermute | solution.py:43
  (318 shorter events, 89.7 us)
Async XLA Ops:
  1.7 19.3 %collective-permute-start = (bf16[64,1536]{1,0:T(8,128)(2,1)S(1)}, bf16[64,1536]{1,0:T(8,128)(2,1)S(1)}, u32[]{:S(2)}, u32[]{:S(2)}) collective-permute-start(bf16[64,1536]{1,0:T(8,128)(2,1)S(1)} %dynamic-slice_bitcast_fusion), channel_id=1, source_target_pairs={{0,2},{2,0},{4,6},{6,4},{8,10},{10,8},{12,14},{14,12},{16,18},{18,... | collective-permute-start | bytes 589832 | tf_op jit(solution)/shard_map/ppermute | solution.py:43
  4.7 16.3 %collective-permute-start.1 = (bf16[64,1536]{1,0:T(8,128)(2,1)S(1)}, bf16[64,1536]{1,0:T(8,128)(2,1)S(1)}, u32[]{:S(2)}, u32[]{:S(2)}) collective-permute-start(bf16[64,1536]{1,0:T(8,128)(2,1)S(1)} %dynamic-slice_bitcast_fusion), channel_id=1, source_target_pairs={{0,4},{2,6},{4,0},{6,2},{8,12},{10,14},{12,8},{14,10},{16,20},{18,... | collective-permute-start | bytes 589832 | tf_op jit(solution)/shard_map/ppermute | solution.py:43
  6.3 15.3 %collective-permute-start.2 = (bf16[64,1536]{1,0:T(8,128)(2,1)S(1)}, bf16[64,1536]{1,0:T(8,128)(2,1)S(1)}, u32[]{:S(2)}, u32[]{:S(2)}) collective-permute-start(bf16[64,1536]{1,0:T(8,128)(2,1)S(1)} %dynamic-slice_bitcast_fusion), channel_id=1, source_target_pairs={{0,6},{2,4},{4,2},{6,0},{8,14},{10,12},{12,10},{14,8},{16,22},{18,... | collective-permute-start | bytes 589832 | tf_op jit(solution)/shard_map/ppermute | solution.py:43
  55.0 14.0 %collective-permute-start.48 = (bf16[128,1536]{1,0:T(8,128)(2,1)S(1)}, bf16[128,1536]{1,0:T(8,128)(2,1)S(1)}, u32[]{:S(2)}, u32[]{:S(2)}) collective-permute-start(bf16[128,1536]{1,0:T(8,128)(2,1)S(1)} %copy-done.2), channel_id=1, source_target_pairs={{0,0},{1,5},{2,2},{3,7},{4,4},{5,1},{6,6},{7,3},{8,8},{9,13},{10,1... | collective-permute-start | bytes 1179656 | tf_op jit(solution)/shard_map/ppermute | solution.py:57
  55.6 14.1 %collective-permute-start.49 = (bf16[128,1536]{1,0:T(8,128)(2,1)S(1)}, bf16[128,1536]{1,0:T(8,128)(2,1)S(1)}, u32[]{:S(2)}, u32[]{:S(2)}) collective-permute-start(bf16[128,1536]{1,0:T(8,128)(2,1)S(1)} %copy-done.2), channel_id=1, source_target_pairs={{0,8},{1,13},{2,10},{3,15},{4,12},{5,9},{6,14},{7,11},{8,16},{9,21... | collective-permute-start | bytes 1179656 | tf_op jit(solution)/shard_map/ppermute | solution.py:57
  64.5 30.6 %collective-permute-start.50 = (bf16[128,1536]{1,0:T(8,128)(2,1)S(1)}, bf16[128,1536]{1,0:T(8,128)(2,1)S(1)}, u32[]{:S(2)}, u32[]{:S(2)}) collective-permute-start(bf16[128,1536]{1,0:T(8,128)(2,1)S(1)} %copy-done.2), channel_id=1, source_target_pairs={{0,16},{1,21},{2,18},{3,23},{4,20},{5,17},{6,22},{7,19},{8,24},{9,... | collective-permute-start | bytes 1179656 | tf_op jit(solution)/shard_map/ppermute | solution.py:57
  65.7 29.8 %collective-permute-start.51 = (bf16[128,1536]{1,0:T(8,128)(2,1)S(1)}, bf16[128,1536]{1,0:T(8,128)(2,1)S(1)}, u32[]{:S(2)}, u32[]{:S(2)}) collective-permute-start(bf16[128,1536]{1,0:T(8,128)(2,1)S(1)} %copy-done.2), channel_id=1, source_target_pairs={{0,24},{1,29},{2,26},{3,31},{4,28},{5,25},{6,30},{7,27},{8,0},{9,5... | collective-permute-start | bytes 1179656 | tf_op jit(solution)/shard_map/ppermute | solution.py:57
  68.9 27.3 %collective-permute-start.52 = (bf16[128,1536]{1,0:T(8,128)(2,1)S(1)}, bf16[128,1536]{1,0:T(8,128)(2,1)S(1)}, u32[]{:S(2)}, u32[]{:S(2)}) collective-permute-start(bf16[128,1536]{1,0:T(8,128)(2,1)S(1)} %collective-permute-done.48.refs_8_), channel_id=1, source_target_pairs={{0,1},{1,0},{2,3},{3,2},{4,5},{5,4},{6,7},{7,6},{8,9},{9,8},{10,11... | collective-permute-start | bytes 1179656 | tf_op jit(solution)/shard_map/ppermute | solution.py:47
  69.8 28.3 %collective-permute-start.53 = (bf16[128,1536]{1,0:T(8,128)(2,1)S(1)}, bf16[128,1536]{1,0:T(8,128)(2,1)S(1)}, u32[]{:S(2)}, u32[]{:S(2)}) collective-permute-start(bf16[128,1536]{1,0:T(8,128)(2,1)S(1)} %collective-permute-done.49.refs_9_), channel_id=1, source_target_pairs={{0,1},{1,0},{2,3},{3,2},{4,5},{5,4},{6,7},{7,6},{8,9},{9,8},{10,11... | collective-permute-start | bytes 1179656 | tf_op jit(solution)/shard_map/ppermute | solution.py:47
  96.3 12.6 %collective-permute-start.41 = (bf16[128,1536]{1,0:T(8,128)(2,1)S(1)}, bf16[128,1536]{1,0:T(8,128)(2,1)S(1)}, u32[]{:S(2)}, u32[]{:S(2)}) collective-permute-start(bf16[128,1536]{1,0:T(8,128)(2,1)S(1)} %copy-done.6), channel_id=1, source_target_pairs={{0,8},{1,13},{2,10},{3,15},{4,12},{5,9},{6,14},{7,11},{8,16},{9,21... | collective-permute-start | bytes 1179656 | tf_op jit(solution)/shard_map/ppermute | solution.py:57
  98.1 29.0 %collective-permute-start.42 = (bf16[128,1536]{1,0:T(8,128)(2,1)S(1)}, bf16[128,1536]{1,0:T(8,128)(2,1)S(1)}, u32[]{:S(2)}, u32[]{:S(2)}) collective-permute-start(bf16[128,1536]{1,0:T(8,128)(2,1)S(1)} %copy-done.6), channel_id=1, source_target_pairs={{0,16},{1,21},{2,18},{3,23},{4,20},{5,17},{6,22},{7,19},{8,24},{9,... | collective-permute-start | bytes 1179656 | tf_op jit(solution)/shard_map/ppermute | solution.py:57
  100.7 34.3 %collective-permute-start.43 = (bf16[128,1536]{1,0:T(8,128)(2,1)S(1)}, bf16[128,1536]{1,0:T(8,128)(2,1)S(1)}, u32[]{:S(2)}, u32[]{:S(2)}) collective-permute-start(bf16[128,1536]{1,0:T(8,128)(2,1)S(1)} %copy-done.6), channel_id=1, source_target_pairs={{0,24},{1,29},{2,26},{3,31},{4,28},{5,25},{6,30},{7,27},{8,0},{9,5... | collective-permute-start | bytes 1179656 | tf_op jit(solution)/shard_map/ppermute | solution.py:57
  109.9 40.9 %collective-permute-start.21 = (bf16[128,1536]{1,0:T(8,128)(2,1)}, bf16[128,1536]{1,0:T(8,128)(2,1)S(1)}, u32[]{:S(2)}, u32[]{:S(2)}) collective-permute-start(bf16[128,1536]{1,0:T(8,128)(2,1)} %get-tuple-element.82), channel_id=1, source_target_pairs={{0,2},{2,0},{4,6},{6,4},{8,10},{10,8},{12,14},{14,12},{16,18},{18,... | collective-permute-start | bytes 1179656 | tf_op jit(solution)/shard_map/ppermute | solution.py:43
  113.3 38.0 %collective-permute-start.22 = (bf16[128,1536]{1,0:T(8,128)(2,1)}, bf16[128,1536]{1,0:T(8,128)(2,1)S(1)}, u32[]{:S(2)}, u32[]{:S(2)}) collective-permute-start(bf16[128,1536]{1,0:T(8,128)(2,1)} %get-tuple-element.82), channel_id=1, source_target_pairs={{0,4},{2,6},{4,0},{6,2},{8,12},{10,14},{12,8},{14,10},{16,20},{18,... | collective-permute-start | bytes 1179656 | tf_op jit(solution)/shard_map/ppermute | solution.py:43
  114.6 36.8 %collective-permute-start.23 = (bf16[128,1536]{1,0:T(8,128)(2,1)}, bf16[128,1536]{1,0:T(8,128)(2,1)S(1)}, u32[]{:S(2)}, u32[]{:S(2)}) collective-permute-start(bf16[128,1536]{1,0:T(8,128)(2,1)} %get-tuple-element.82), channel_id=1, source_target_pairs={{0,6},{2,4},{4,2},{6,0},{8,14},{10,12},{12,10},{14,8},{16,22},{18,... | collective-permute-start | bytes 1179656 | tf_op jit(solution)/shard_map/ppermute | solution.py:43
  137.9 12.8 %collective-permute-start.26 = (bf16[512,128]{1,0:T(8,128)(2,1)}, bf16[512,128]{1,0:T(8,128)(2,1)S(1)}, u32[]{:S(2)}, u32[]{:S(2)}) collective-permute-start(bf16[512,128]{1,0:T(8,128)(2,1)} %get-tuple-element.87), channel_id=1, source_target_pairs={{0,8},{2,10},{4,12},{6,14},{8,16},{10,18},{12,20},{14,22},{16,24},... | collective-permute-start | bytes 393224 | tf_op jit(solution)/shard_map/ppermute | solution.py:43
  142.5 18.9 %collective-permute-start.55 = (bf16[128,1536]{1,0:T(8,128)(2,1)S(1)}, bf16[128,1536]{1,0:T(8,128)(2,1)S(1)}, u32[]{:S(2)}, u32[]{:S(2)}) collective-permute-start(bf16[128,1536]{1,0:T(8,128)(2,1)S(1)} %collective-permute-done.51.refs_11_), channel_id=1, source_target_pairs={{0,1},{1,0},{2,3},{3,2},{4,5},{5,4},{6,7},{7,6},{8,9},{9,8},{10,11... | collective-permute-start | bytes 1179656 | tf_op jit(solution)/shard_map/ppermute | solution.py:47
  151.4 13.9 %collective-permute-start.47 = (bf16[128,1536]{1,0:T(8,128)(2,1)S(1)}, bf16[128,1536]{1,0:T(8,128)(2,1)S(1)}, u32[]{:S(2)}, u32[]{:S(2)}) collective-permute-start(bf16[128,1536]{1,0:T(8,128)(2,1)S(1)} %collective-permute-done.43.refs_3_), channel_id=1, source_target_pairs={{0,1},{1,0},{2,3},{3,2},{4,5},{5,4},{6,7},{7,6},{8,9},{9,8},{10,11... | collective-permute-start | bytes 1179656 | tf_op jit(solution)/shard_map/ppermute | solution.py:47
  161.4 75.0 %collective-permute-start.16 = (bf16[128,1536]{1,0:T(8,128)(2,1)S(1)}, bf16[128,1536]{1,0:T(8,128)(2,1)S(1)}, u32[]{:S(2)}, u32[]{:S(2)}) collective-permute-start(bf16[128,1536]{1,0:T(8,128)(2,1)S(1)} %copy-done.12), channel_id=1, source_target_pairs={{0,1},{1,0},{2,3},{3,2},{4,5},{5,4},{6,7},{7,6},{8,9},{9,8},{10,11... | collective-permute-start | bytes 1179656 | tf_op jit(solution)/shard_map/ppermute | solution.py:47
  161.8 56.8 %collective-permute-start.27 = (bf16[128,384]{1,0:T(8,128)(2,1)}, bf16[128,384]{1,0:T(8,128)(2,1)S(1)}, u32[]{:S(2)}, u32[]{:S(2)}) collective-permute-start(bf16[128,384]{1,0:T(8,128)(2,1)} %get-tuple-element.89), channel_id=1, source_target_pairs={{0,2},{2,0},{4,6},{6,4},{8,10},{10,8},{12,14},{14,12},{16,18},{18,... | collective-permute-start | bytes 294920 | tf_op jit(solution)/shard_map/ppermute | solution.py:43
  162.4 57.3 %collective-permute-start.28 = (bf16[128,384]{1,0:T(8,128)(2,1)}, bf16[128,384]{1,0:T(8,128)(2,1)S(1)}, u32[]{:S(2)}, u32[]{:S(2)}) collective-permute-start(bf16[128,384]{1,0:T(8,128)(2,1)} %get-tuple-element.90), channel_id=1, source_target_pairs={{0,4},{2,6},{4,0},{6,2},{8,12},{10,14},{12,8},{14,10},{16,20},{18,... | collective-permute-start | bytes 294920 | tf_op jit(solution)/shard_map/ppermute | solution.py:43
  163.1 56.7 %collective-permute-start.29 = (bf16[128,384]{1,0:T(8,128)(2,1)}, bf16[128,384]{1,0:T(8,128)(2,1)S(1)}, u32[]{:S(2)}, u32[]{:S(2)}) collective-permute-start(bf16[128,384]{1,0:T(8,128)(2,1)} %get-tuple-element.91), channel_id=1, source_target_pairs={{0,6},{2,4},{4,2},{6,0},{8,14},{10,12},{12,10},{14,8},{16,22},{18,... | collective-permute-start | bytes 294920 | tf_op jit(solution)/shard_map/ppermute | solution.py:43
  165.4 73.9 %collective-permute-start.34 = (bf16[384,128]{1,0:T(8,128)(2,1)}, bf16[384,128]{1,0:T(8,128)(2,1)S(1)}, u32[]{:S(2)}, u32[]{:S(2)}) collective-permute-start(bf16[384,128]{1,0:T(8,128)(2,1)} %get-tuple-element.98), channel_id=1, source_target_pairs={{0,24},{2,26},{4,28},{6,30},{8,0},{10,2},{12,4},{14,6},{16,8},{18,... | collective-permute-start | bytes 294920 | tf_op jit(solution)/shard_map/ppermute | solution.py:43
  218.7 22.5 %collective-permute-start.35 = (bf16[384,128]{1,0:T(8,128)(2,1)S(1)}, bf16[384,128]{1,0:T(8,128)(2,1)S(1)}, u32[]{:S(2)}, u32[]{:S(2)}) collective-permute-start(bf16[384,128]{1,0:T(8,128)(2,1)S(1)} %copy-done.73), channel_id=1, source_target_pairs={{0,16},{2,18},{4,20},{6,22},{8,24},{10,26},{12,28},{14,30},{16,0},... | collective-permute-start | bytes 294920 | tf_op jit(solution)/shard_map/ppermute | solution.py:43
  219.7 70.0 %collective-permute-start.56 = (bf16[96,3456]{1,0:T(8,128)(2,1)}, bf16[96,3456]{1,0:T(8,128)(2,1)S(1)}, u32[]{:S(2)}, u32[]{:S(2)}) collective-permute-start(bf16[96,3456]{1,0:T(8,128)(2,1)} %get-tuple-element.110), channel_id=1, source_target_pairs={{0,2},{2,0},{4,6},{6,4},{8,10},{10,8},{12,14},{14,12},{16,18},{18,... | collective-permute-start | bytes 1990664 | tf_op jit(solution)/shard_map/ppermute | solution.py:43
  236.4 35.2 %collective-permute-start.31 = (bf16[384,384]{1,0:T(8,128)(2,1)S(1)}, bf16[384,384]{1,0:T(8,128)(2,1)S(1)}, u32[]{:S(2)}, u32[]{:S(2)}) collective-permute-start(bf16[384,384]{1,0:T(8,128)(2,1)S(1)} %copy-done.68), channel_id=1, source_target_pairs={{0,24},{2,26},{4,28},{6,30},{8,0},{10,2},{12,4},{14,6},{16,8},{18,... | collective-permute-start | bytes 884744 | tf_op jit(solution)/shard_map/ppermute | solution.py:43
  239.2 32.4 %collective-permute-start.32 = (bf16[384,384]{1,0:T(8,128)(2,1)S(1)}, bf16[384,384]{1,0:T(8,128)(2,1)S(1)}, u32[]{:S(2)}, u32[]{:S(2)}) collective-permute-start(bf16[384,384]{1,0:T(8,128)(2,1)S(1)} %copy-done.67), channel_id=1, source_target_pairs={{0,16},{2,18},{4,20},{6,22},{8,24},{10,26},{12,28},{14,30},{16,0},... | collective-permute-start | bytes 884744 | tf_op jit(solution)/shard_map/ppermute | solution.py:43
  239.8 31.9 %collective-permute-start.33 = (bf16[384,384]{1,0:T(8,128)(2,1)S(1)}, bf16[384,384]{1,0:T(8,128)(2,1)S(1)}, u32[]{:S(2)}, u32[]{:S(2)}) collective-permute-start(bf16[384,384]{1,0:T(8,128)(2,1)S(1)} %copy-done.66), channel_id=1, source_target_pairs={{0,8},{2,10},{4,12},{6,14},{8,16},{10,18},{12,20},{14,22},{16,24},... | collective-permute-start | bytes 884744 | tf_op jit(solution)/shard_map/ppermute | solution.py:43
  241.1 15.8 %collective-permute-start.62 = (f32[3456]{0:T(1024)S(1)}, f32[3456]{0:T(1024)S(1)}, u32[]{:S(2)}, u32[]{:S(2)}) collective-permute-start(f32[3456]{0:T(1024)S(1)} %add.57), channel_id=1, source_target_pairs={{0,8},{2,10},{4,12},{6,14},{8,0},{10,2},{12,4},{14,6},{16,24},{18,... | collective-permute-start | bytes 41480 | tf_op jit(solution)/shard_map/ppermute | solution.py:43
  269.4 17.0 %collective-permute-start.30 = (bf16[128,1536]{1,0:T(8,128)(2,1)}, bf16[128,1536]{1,0:T(8,128)(2,1)S(1)}, u32[]{:S(2)}, u32[]{:S(2)}) collective-permute-start(bf16[128,1536]{1,0:T(8,128)(2,1)} %get-tuple-element.92.a_ref), channel_id=1, source_target_pairs={{0,1},{1,0},{2,3},{3,2},{4,5},{5,4},{6,7},{7,6},{8,9},{9,8},{10,11... | collective-permute-start | bytes 1179656 | tf_op jit(solution)/shard_map/ppermute | solution.py:47
  280.5 17.8 %collective-permute-start.57 = (bf16[96,3456]{1,0:T(8,128)(2,1)S(1)}, bf16[96,3456]{1,0:T(8,128)(2,1)S(1)}, u32[]{:S(2)}, u32[]{:S(2)}) collective-permute-start(bf16[96,3456]{1,0:T(8,128)(2,1)S(1)} %copy-done.49), channel_id=1, source_target_pairs={{0,2},{2,0},{4,6},{6,4},{8,10},{10,8},{12,14},{14,12},{16,18},{18,... | collective-permute-start | bytes 1990664 | tf_op jit(solution)/shard_map/ppermute | solution.py:43
  282.6 28.6 %collective-permute-start.58 = (bf16[96,3456]{1,0:T(8,128)(2,1)S(1)}, bf16[96,3456]{1,0:T(8,128)(2,1)S(1)}, u32[]{:S(2)}, u32[]{:S(2)}) collective-permute-start(bf16[96,3456]{1,0:T(8,128)(2,1)S(1)} %copy-done.48), channel_id=1, source_target_pairs={{0,2},{2,0},{4,6},{6,4},{8,10},{10,8},{12,14},{14,12},{16,18},{18,... | collective-permute-start | bytes 1990664 | tf_op jit(solution)/shard_map/ppermute | solution.py:43
  (111 other events, 1148.4 us)

commit v3 on v2

v3 whole, which is shorter than its diff:
```python
import functools

import jax
import jax.numpy as jnp
import numpy as np
from jax import lax
from jax.experimental import pallas as pl
from jax.experimental.pallas import tpu as pltpu
from jax.sharding import PartitionSpec as P

BLK = 32
SEQS = 2
QUAD = 4
EPSILON = 1e-05
ROPE_BASE = 1000000.0
MASKED = -1e30
F32 = jnp.float32
BF16 = jnp.bfloat16
VMEM_LIMIT = 56 * 1024 * 1024


def dot(left, right):
    return jnp.dot(left, right, preferred_element_type=F32)


def contract_last(left, right):
    return lax.dot_general(left, right, (((1,), (1,)), ((), ())), preferred_element_type=F32)


def contract_first(left, right):
    return lax.dot_general(left, right, (((0,), (0,)), ((), ())), preferred_element_type=F32)


def shift_pairs(count, step):
    nz = count // QUAD
    return [(i, ((i // QUAD + step) % nz) * QUAD + i % QUAD) for i in range(count)]


def flip_pairs(count, bits):
    return [(i, i ^ bits) for i in range(count)]


def send(value, pairs):
    return lax.ppermute(value, "ctx", pairs)


def swap_cores(value):
    return lax.ppermute(value, "tp", [(0, 1), (1, 0)])


def core_pairs(count):
    return [pair for i in range(count) for pair in ((2 * i, 2 * i), (2 * i + 1, 2 * (i ^ 2) + 1))]


def gather_column(half, count):
    return [half] + [send(half, shift_pairs(count, s)) for s in range(1, count // QUAD)]


def sum_but_x(value, count):
    value = value + swap_cores(value)
    bit = 2
    while bit < count:
        value = value + send(value, flip_pairs(count, bit))
        bit *= 2
    return value


COST_SCALE = 0.01


def cost(flops, bytes_accessed, transcendentals=0, scale=COST_SCALE):
    return pl.CostEstimate(
        flops=int(flops * scale),
        bytes_accessed=int(bytes_accessed * scale),
        transcendentals=int(transcendentals * scale),
    )


SCALARS = pl.BlockSpec(memory_space=pltpu.SMEM)


ANYWHERE = pl.BlockSpec(memory_space=pl.ANY)


def ordered(body, extra):
    return lambda *refs: body(*refs[extra:])


def kernel_call(
    body, name, args, out_shape, flops=0, scalars=False, scratch=(), after=(), scale=COST_SCALE
):
    vmem = pl.BlockSpec(memory_space=pltpu.VMEM)
    bytes_accessed = sum(a.size * a.dtype.itemsize for a in (*args, *out_shape))
    return pl.pallas_call(
        ordered(body, len(after)),
        in_specs=[ANYWHERE] * len(after)
        + [SCALARS if scalars and i == 0 else vmem for i in range(len(args))],
        out_specs=[vmem] * len(out_shape),
        out_shape=list(out_shape),
        scratch_shapes=list(scratch),
        compiler_params=pltpu.CompilerParams(vmem_limit_bytes=VMEM_LIMIT),
        cost_estimate=cost(flops, bytes_accessed, scale=scale),
        name=name,
    )(*after, *args)


def shape(dims, dtype):
    return jax.ShapeDtypeStruct(dims, dtype)


def pack_kernel(*refs):
    pieces, out_ref = refs[:-1], refs[-1]
    rows = pieces[0].shape[0]
    for i, piece in enumerate(pieces):
        out_ref[i * rows : (i + 1) * rows] = piece[...]


def pack(pieces, after=()):
    rows, width = pieces[0].shape
    out = shape((len(pieces) * rows, width), pieces[0].dtype)
    return kernel_call(pack_kernel, "pack", pieces, [out], after=after)[0]


def touch(value, after):
    return pl.pallas_call(
        lambda *refs: None,
        in_specs=[ANYWHERE] * (1 + len(after)),
        out_specs=ANYWHERE,
        out_shape=shape(value.shape, value.dtype),
        input_output_aliases={0: 0},
        name="touch",
    )(value, *after)


def row_factor(x):
    return lax.rsqrt(jnp.mean(x * x, axis=-1, keepdims=True) + EPSILON)


def head_means(x, blocks):
    high = x.astype(BF16)
    low = (x - high.astype(F32)).astype(BF16)
    return dot(high, blocks) + dot(low, blocks)


def head_blocks():
    row = lax.broadcasted_iota(jnp.int32, (128, 128), 0)
    col = lax.broadcasted_iota(jnp.int32, (128, 128), 1)
    return jnp.where(row // 64 == col // 64, 1.0 / 64, 0.0).astype(BF16)


def row_of(ref):
    return ref[...].reshape(1, -1)


def head_gain_rows(key_ref, query_ref):
    key, query = row_of(key_ref), row_of(query_ref)
    return jnp.concatenate([key, key], axis=1), jnp.concatenate([query, query], axis=1)


def lanes_of(x):
    return lax.broadcasted_iota(jnp.int32, x.shape, 1)


def partner(x):
    return jnp.where(lanes_of(x) % 64 < 32, pltpu.roll(x, 96, 1), pltpu.roll(x, 32, 1))


def mask_kernel(ids_ref, freq_ref, seg_ref, bias_ref, angle_ref):
    me = ids_ref[0]
    count = seg_ref.shape[0]
    nz = count // QUAD
    tokens = seg_ref.shape[1] // SEQS
    z, m = me // QUAD, me % QUAD

    def place(chip, offset):
        return jnp.where(offset < BLK, chip * BLK, (2 * count - 2 - chip) * BLK) + offset

    chips = [((z + nz - step) % nz) * QUAD + (m ^ j) for step in range(nz) for j in range(QUAD)]
    seg_rows = [seg_ref[pl.ds(chip, 1), :].astype(F32) for chip in chips]
    fill = jnp.zeros((128 - count, SEQS * tokens), F32)
    seg_cols = jnp.concatenate([*seg_rows, fill], axis=0).T
    row_offset = lax.broadcasted_iota(jnp.int32, (1, tokens), 1)
    col_offset = lax.broadcasted_iota(jnp.int32, (tokens, 1), 0)
    place_q = jnp.concatenate([place(chip, row_offset) for chip in chips[:QUAD]], axis=1)
    far = 2 * count * BLK
    for seq in range(SEQS):
        of_seq = slice(seq * tokens, (seq + 1) * tokens)
        seg_q = jnp.concatenate([row[:, of_seq] for row in seg_rows[:QUAD]], axis=1)
        first = jnp.full((tokens, QUAD * tokens), far, jnp.int32)
        for i, chip in enumerate(chips):
            place_k = place(chip, col_offset)
            same = seg_cols[of_seq, i : i + 1] == seg_q
            bias_ref[seq, i * tokens : (i + 1) * tokens, :] = jnp.where(
                same & (place_k <= place_q), 0.0, MASKED
            )
            first = jnp.minimum(first, jnp.where(same, place_k, far))
        position = (place_q - jnp.min(first, axis=0, keepdims=True)).astype(F32)
        rows = position.shape[1]
        angle_ref[seq * rows : (seq + 1) * rows, :] = (
            jnp.broadcast_to(position, (128, rows)).T * freq_ref[...]
        )


def qkv_kernel(ids_ref, own_ref, *refs):
    mine, theirs = refs[:3], refs[3:6]
    gain_ref, w_ref, key_gain_ref, query_gain_ref, cos_ref, sin_ref, g_ref = refs[6:13]
    h1_ref, raw_ref, q_ref, kv_ref, copy_ref = refs[13:]
    core = ids_ref[1]
    gain = row_of(gain_ref)
    copy_ref[...] = g_ref[...]

    def put(seq, j, piece):
        x = piece.astype(F32)
        h1_ref[seq, j] = (x * row_factor(x) * gain).astype(BF16)

    put(0, 0, own_ref[0])
    put(1, 0, own_ref[1])
    for j in range(1, QUAD):
        put(core, j, mine[j - 1][...])
        put(1 - core, j, theirs[j - 1][...])
    rows = raw_ref.shape[0]
    raw = dot(h1_ref[...].reshape(rows, -1), w_ref[...])
    raw_ref[...] = raw
    cos, sin, blocks = cos_ref[...], sin_ref[...], head_blocks()
    key_gain, query_gain = head_gain_rows(key_gain_ref, query_gain_ref)
    out = []
    for c in range(3):
        x = raw[:, 128 * c : 128 * (c + 1)]
        gain = key_gain if c == 0 else query_gain * 64 ** (-0.5)
        n = x * lax.rsqrt(head_means(x * x, blocks) + EPSILON) * gain
        out.append(n * cos + partner(n) * sin)
    kv_ref[...] = jnp.where(lanes_of(out[0]) < 64, out[0], raw[:, :128]).astype(BF16)
    q_ref[...] = jnp.concatenate(out[1:], axis=1).astype(BF16)


def head_lanes(x, g, upper):
    part = x[:, 128 * (g // 2) : 128 * (g // 2) + 128]
    if (g % 2 == 1) != upper:
        part = pltpu.roll(part, 64, 1)
    keep = (lanes_of(part) >= 64) if upper else (lanes_of(part) < 64)
    return jnp.where(keep, part, 0.0).astype(BF16)


def attention_forward_kernel(q_ref, bias_ref, *refs):
    kv_refs, o_refs, lse_ref = refs[: -QUAD - 1], refs[-QUAD - 1 : -1], refs[-1]
    group = lse_ref.shape[1]
    kv = jnp.concatenate([r[...] for r in kv_refs], axis=0)
    v_t = kv.T[64:]
    q = q_ref[...].astype(F32)
    bias = bias_ref[0]
    out = []
    for g in range(group):
        s = contract_last(kv, head_lanes(q, g, False)) + bias
        top = jnp.max(s, axis=0, keepdims=True)
        p = jnp.exp(s - top)
        total = jnp.sum(p, axis=0, keepdims=True)
        out.append(dot(v_t, p.astype(BF16)) / total)
        lse_ref[0, g] = top + jnp.log(total)
    o = jnp.concatenate(out, axis=0).T.astype(BF16)
    rows = o.shape[0] // QUAD
    for j in range(QUAD):
        o_refs[j][0] = o[j * rows : (j + 1) * rows]


def attention_backward_kernel(q_ref, bias_ref, lse_ref, *refs):
    do_refs, kv_refs, dq_ref, dkv_refs = refs[:QUAD], None, None, None
    rest = refs[QUAD:]
    pieces = (len(rest) - 1) // 2
    kv_refs, dq_ref, dkv_refs = rest[:pieces], rest[pieces], rest[pieces + 1 :]
    group = lse_ref.shape[1]
    kv = jnp.concatenate([r[...] for r in kv_refs], axis=0)
    k_t = kv.T[:64]
    q = q_ref[...].astype(F32)
    do = jnp.concatenate([r[0].astype(F32) for r in do_refs], axis=0)
    do = jnp.concatenate([do, jnp.zeros((do.shape[0], 64), F32)], axis=1)
    rows = q.shape[0]
    bias = bias_ref[0]
    total = jnp.zeros(kv.shape, F32)
    dq = []
    for g in range(group):
        both = jnp.concatenate([head_lanes(q, g, False), head_lanes(do, g, True)], axis=0)
        products = contract_last(kv, both)
        p = jnp.exp(products[:, :rows] + (bias - lse_ref[0, g]))
        dp = products[:, rows:]
        delta = jnp.sum(p * dp, axis=0, keepdims=True)
        ds = (p * (dp - delta)).astype(BF16)
        total = total + dot(jnp.concatenate([ds, p.astype(BF16)], axis=1), both)
        dq.append(dot(k_t, ds))
    dq.append(jnp.zeros(dq[0].shape, F32))
    dq_ref[...] = jnp.concatenate(dq, axis=0).T
    for i, ref in enumerate(dkv_refs):
        ref[...] = total[i * rows : (i + 1) * rows].astype(BF16)


def attention_specs(rows, keys, pieces):
    q = pl.BlockSpec((rows, 256), lambda s: (s, 0))
    bias = pl.BlockSpec((1, keys, rows), lambda s: (s, 0, 0))
    kv = [pl.BlockSpec((rows, 128), lambda s: (s, 0))] * pieces
    return q, bias, kv


def attention_forward(q, bias, kv, group, after):
    seqs, keys, rows = bias.shape
    q_spec, bias_spec, kv_specs = attention_specs(rows, keys, len(kv))
    work = seqs * group * keys * rows
    return pl.pallas_call(
        ordered(attention_forward_kernel, len(after)),
        grid=(seqs,),
        in_specs=[*[ANYWHERE] * len(after), q_spec, bias_spec, *kv_specs],
        out_specs=[
            *[pl.BlockSpec((1, rows // QUAD, group * 64), lambda s: (s, 0, 0))] * QUAD,
            pl.BlockSpec((1, group, 1, rows), lambda s: (s, 0, 0, 0)),
        ],
        out_shape=[
            *[shape((seqs, rows // QUAD, group * 64), BF16)] * QUAD,
            shape((seqs, group, 1, rows), F32),
        ],
        compiler_params=pltpu.CompilerParams(vmem_limit_bytes=VMEM_LIMIT),
        cost_estimate=cost(6 * work * 128, 4 * bias.size, work),
        name="attention_forward",
    )(*after, q, bias, *kv)


def attention_backward(q, bias, lse, do, kv, after=()):
    seqs, keys, rows = bias.shape
    group = lse.shape[1]
    q_spec, bias_spec, kv_specs = attention_specs(rows, keys, len(kv))
    work = seqs * group * keys * rows
    return pl.pallas_call(
        ordered(attention_backward_kernel, len(after)),
        grid=(seqs,),
        in_specs=[
            *[ANYWHERE] * len(after),
            q_spec,
            bias_spec,
            pl.BlockSpec((1, group, 1, rows), lambda s: (s, 0, 0, 0)),
            *[pl.BlockSpec((1, rows // QUAD, group * 64), lambda s: (s, 0, 0))] * QUAD,
            *kv_specs,
        ],
        out_specs=[q_spec, *kv_specs],
        out_shape=[shape(q.shape, F32)] + [shape(k.shape, BF16) for k in kv],
        compiler_params=pltpu.CompilerParams(vmem_limit_bytes=VMEM_LIMIT),
        cost_estimate=cost(10 * work * 128, 4 * bias.size, work),
        name="attention_backward",
    )(*after, q, bias, lse, *do, *kv)


def put_halves(refs, value):
    rows = refs[0].shape[0]
    for i, ref in enumerate(refs):
        ref[...] = value[i * rows : (i + 1) * rows].astype(ref.dtype)


def sum_halves(refs):
    own = jnp.concatenate([refs[0][...], refs[1][...]], axis=0).astype(F32)
    return own + jnp.concatenate([refs[2][...], refs[3][...]], axis=0).astype(F32)


def branch_kernel(ids_ref, *refs):
    pieces, w_ref, out_refs, stack_ref = refs[:QUAD], refs[QUAD], refs[QUAD + 1 : -1], refs[-1]
    m = ids_ref[0] % QUAD
    for j in range(QUAD):
        stack_ref[j] = pieces[j][...]
    attn = jnp.concatenate([stack_ref[m ^ k] for k in range(QUAD)], axis=1)
    put_halves(out_refs, contract_last(attn, w_ref[...]))


def middle_kernel(ids_ref, x_ref, *refs):
    branch_refs, (gain_ref, mid_ref, h2_ref, half_ref) = refs[:4], refs[4:]
    mid = x_ref[...].astype(F32) + sum_halves(branch_refs)
    mid_ref[...] = mid
    h2 = (mid * row_factor(mid) * row_of(gain_ref)).astype(BF16)
    h2_ref[...] = h2
    rows = half_ref.shape[0]
    half_ref[...] = jnp.where(ids_ref[1] == 0, h2[:rows], h2[rows:])


def hidden_terms(gate, up, da):
    sg = jax.nn.sigmoid(gate)
    silu = gate * sg
    act = (silu * up).astype(BF16)
    dgate = (da * up * (sg + silu * (1.0 - sg))).astype(BF16)
    dup = (da * silu).astype(BF16)
    return act, dgate, dup


def hidden_tile(hidden):
    return next(t for t in (1152, 384, 128, hidden) if hidden % t == 0)


def hidden_call(body, name, args, out_shape, scratch=(), matmuls=1, after=()):
    hidden = max(a.shape[-1] for a in args)
    tile = hidden_tile(hidden)

    def spec(a):
        if a.shape[-1] == hidden:
            return pl.BlockSpec((a.shape[0], tile), lambda i: (0, i))
        return pl.BlockSpec(a.shape, lambda i: (0, 0))

    rows, width = args[0].shape[0], 1536
    return pl.pallas_call(
        ordered(body, len(after)),
        grid=(hidden // tile,),
        in_specs=[ANYWHERE] * len(after) + [spec(a) for a in args],
        out_specs=[spec(o) for o in out_shape],
        out_shape=list(out_shape),
        scratch_shapes=list(scratch),
        compiler_params=pltpu.CompilerParams(vmem_limit_bytes=VMEM_LIMIT),
        cost_estimate=cost(
            4 * matmuls * rows * width * hidden,
            sum(a.size * a.dtype.itemsize for a in (*args, *out_shape)),
        ),
        name=name,
    )(*after, *args)


def accumulate(total_ref, out_refs, term):
    step = pl.program_id(0)

    @pl.when(step == 0)
    def _():
        total_ref[...] = term

    @pl.when(step > 0)
    def _():
        total_ref[...] += term

    @pl.when(step == pl.num_programs(0) - 1)
    def _():
        put_halves(out_refs, total_ref[...].T)


def hidden_grad_kernel(g_ref, wd_ref, da_ref):
    da_ref[...] = dot(g_ref[...], wd_ref[...])


def own_mlp_kernel(
    h2_ref, da_ref, wg_ref, wu_ref, dh_top_ref, dh_ref, act_ref, dgate_ref, dup_ref, total_ref
):
    wg, wu, h2 = wg_ref[...], wu_ref[...], h2_ref[...]
    act, dgate, dup = hidden_terms(dot(h2, wg), dot(h2, wu), da_ref[...])
    act_ref[...] = act
    dgate_ref[...] = dgate
    dup_ref[...] = dup
    accumulate(
        total_ref, (dh_top_ref, dh_ref), contract_last(wg, dgate) + contract_last(wu, dup)
    )


def down_kernel(act_ref, wd_ref, down_ref, total_ref):
    accumulate(total_ref, (down_ref,), contract_last(wd_ref[...], act_ref[...]))


def back_kernel(
    ids_ref, mid_ref, a_ref, b_ref, c_ref, d_ref, g_ref, gain_ref, w_ref, dx_ref, dy_ref, *refs
):
    half_ref, part_ref, do_refs = refs[0], refs[1], refs[2:]
    m = ids_ref[0] % QUAD
    stack_ref, do_refs = do_refs[-1], do_refs[:-1]
    mid = mid_ref[...]
    factor = row_factor(mid)
    dh2 = sum_halves((a_ref, b_ref, c_ref, d_ref))
    part_ref[...] = jnp.sum(dh2 * mid * factor, axis=0, keepdims=True)
    scaled = dh2 * row_of(gain_ref)
    inner = jnp.mean(mid * scaled, axis=-1, keepdims=True)
    dx = g_ref[...].astype(F32) + (factor * scaled - mid * (factor * factor * factor) * inner)
    dx_ref[...] = dx
    dy = dx.astype(BF16)
    dy_ref[...] = dy
    half = half_ref.shape[0]
    half_ref[...] = jnp.where(ids_ref[1] == 0, dy[:half], dy[half:])
    do = dot(dy, w_ref[...]).astype(BF16)
    columns = do.shape[1] // QUAD
    for k in range(QUAD):
        stack_ref[m ^ k] = do[:, k * columns : (k + 1) * columns]
    for j in range(QUAD):
        do_refs[j][...] = stack_ref[j]


def norm_rotate_back(grad, raw, gain, cos, sin, blocks):
    normed = grad * cos - partner(grad) * sin
    factor = lax.rsqrt(head_means(raw * raw, blocks) + EPSILON)
    scaled = normed * gain
    inner = head_means(raw * scaled, blocks)
    part = jnp.sum(normed * raw * factor, axis=0, keepdims=True)
    return factor * scaled - raw * (factor * factor * factor) * inner, part


def head_grad_kernel(ids_ref, dq_ref, raw_ref, h1_ref, *refs):
    attn_refs, dy_ref, mine, theirs, refs = refs[:4], refs[4], refs[5:8], refs[8:11], refs[11:]
    core = ids_ref[1]
    key_gain_ref, query_gain_ref, cos_ref, sin_ref, refs = *refs[:4], refs[4:]
    nz = (len(refs) - QUAD - 3) // 2
    dkv_refs, refs = refs[:nz], refs[nz:]
    part_ref, piece_refs, w_refs = refs[0], refs[1 : 1 + QUAD], refs[1 + QUAD : -2]
    total_ref, dy_all = refs[-2:]
    cos, sin, blocks = cos_ref[...], sin_ref[...], head_blocks()
    key_gain, query_gain = head_gain_rows(key_gain_ref, query_gain_ref)
    dkv = dkv_refs[0][...].astype(F32)
    for ref in dkv_refs[1:]:
        dkv = dkv + ref[...].astype(F32)
    scale = 64 ** (-0.5)
    low = []
    for c in range(3):
        lanes = slice(128 * c, 128 * (c + 1))
        given = dkv if c == 0 else dq_ref[:, 128 * (c - 1) : 128 * c] * scale
        gain = key_gain if c == 0 else query_gain
        grad, part = norm_rotate_back(given, raw_ref[:, lanes], gain, cos, sin, blocks)
        if c == 0:
            grad = jnp.where(lanes_of(grad) < 64, grad, dkv)
        part_ref[:, lanes] = part
        low.append(grad.astype(BF16))
    low = jnp.concatenate(low, axis=1)
    rows = low.shape[0]
    tokens = rows // (SEQS * QUAD)
    attn = []
    for seq in range(SEQS):
        for j in range(QUAD):
            begin = (seq * QUAD + j) * tokens
            piece_refs[j][seq * tokens : (seq + 1) * tokens] = low[begin : begin + tokens]
            if j == 0:
                dy_all[seq, j] = dy_ref[seq]
            attn.append(attn_refs[j][seq])
    for j in range(1, QUAD):
        dy_all[core, j] = mine[j - 1][...]
        dy_all[1 - core, j] = theirs[j - 1][...]
    columns = attn[0].shape[1]
    grad_wqkv = contract_first(h1_ref[...].reshape(rows, -1), low)
    grad_wo = contract_first(dy_all[...].reshape(rows, -1), jnp.concatenate(attn, axis=0))
    total_ref[...] = jnp.concatenate([grad_wqkv[:, : 128 + columns], grad_wo], axis=1)
    z = ids_ref[0] // QUAD
    owned = w_refs[0].shape[0]
    for step, ref in enumerate(w_refs):
        begin = pl.multiple_of(((z + nz - step) % nz) * owned, 8)
        ref[...] = total_ref[pl.ds(begin, owned), :].astype(BF16)


def spread_kernel(ids_ref, *refs):
    nz = len(refs) - QUAD - 1
    terms, (own_ref, *out_refs), total_ref = refs[:nz], refs[nz:-1], refs[-1]
    total = terms[0][...].astype(F32)
    for ref in terms[1:]:
        total = total + ref[...].astype(F32)
    total_ref[...] = total
    m = ids_ref[0] % QUAD
    rows = own_ref.shape[0]
    for j in range(QUAD):
        part = total_ref[pl.ds(pl.multiple_of((m ^ j) * rows, 8), rows), :]
        if j == 0:
            own_ref[...] = part
        else:
            out_refs[j - 1][...] = part.astype(BF16)


def assemble_kernel(ids_ref, own_ref, a_ref, b_ref, c_ref, wq_ref, wk_ref, wv_ref, wo_ref, stack_ref):
    m = ids_ref[0] % QUAD
    stack_ref[0] = own_ref[...]
    for j, ref in enumerate((a_ref, b_ref, c_ref)):
        stack_ref[j + 1] = ref[...].astype(F32)
    parts = [stack_ref[m ^ k] for k in range(QUAD)]
    columns = wq_ref.shape[1] // QUAD
    wk_ref[...] = jnp.concatenate([p[:, :64] for p in parts], axis=1)
    wv_ref[...] = jnp.concatenate([p[:, 64:128] for p in parts], axis=1)
    wq_ref[...] = jnp.concatenate([p[:, 128 : 128 + columns] for p in parts], axis=1)
    wo_ref[...] = jnp.concatenate([p[:, 128 + columns :] for p in parts], axis=1)


def input_grad_kernel(ids_ref, *refs):
    pieces, (x_ref, wq_ref, wk_ref, wv_ref, out_ref, part_ref, stack_ref) = refs[:QUAD], refs[QUAD:]
    m = ids_ref[0] % QUAD
    for j in range(QUAD):
        stack_ref[j] = pieces[j][...]
    parts = [stack_ref[m ^ k] for k in range(QUAD)]
    columns = wq_ref.shape[1] // QUAD
    dk = jnp.concatenate([p[:, :64] for p in parts], axis=1)
    dv = jnp.concatenate([p[:, 64:128] for p in parts], axis=1)
    dq = jnp.concatenate([p[:, 128 : 128 + columns] for p in parts], axis=1)
    total = (
        contract_last(dq, wq_ref[...])
        + contract_last(dk, wk_ref[...])
        + contract_last(dv, wv_ref[...])
    )
    out_ref[...] = total.astype(BF16)
    x = x_ref[...].astype(F32)
    part_ref[...] = jnp.sum(total * x * row_factor(x), axis=0, keepdims=True)


def tokens_kernel(x_ref, dx_ref, a_ref, b_ref, gain_ref, out_ref):
    x = x_ref[...].astype(F32)
    factor = row_factor(x)
    scaled = (a_ref[...].astype(F32) + b_ref[...].astype(F32)) * row_of(gain_ref)
    inner = jnp.mean(x * scaled, axis=-1, keepdims=True)
    back = factor * scaled - x * (factor * factor * factor) * inner
    out_ref[...] = (dx_ref[...] + back).astype(BF16)


def output_kernel(mid_ref, a_ref, b_ref, out_ref):
    out_ref[...] = (mid_ref[...] + (a_ref[...].astype(F32) + b_ref[...].astype(F32))).astype(BF16)


def bulk_mlp_kernel(ids_ref, *refs, pieces, row_tile, first):
    sides, refs = (refs[: pieces[0]], refs[pieces[0] : sum(pieces)]), refs[sum(pieces) :]
    act_ref, dgate_ref, dup_ref, wg_ref, wu_ref, wd_ref, refs = *refs[:6], refs[6:]
    if first:
        own_refs, other_ref, h2c_ref, gc_ref, h2_ref, g_ref, sems = refs[:3], *refs[3:]
    else:
        h2c_ref, gc_ref, own_refs, other_ref, h2_ref, g_ref, sems = *refs[:2], refs[2:5], *refs[5:]
    rows = act_ref.shape[0]
    tokens, width = h2_ref.shape
    own_rows = own_refs[0].shape[0]
    pair_rows = 2 * own_rows

    @pl.when(pl.program_id(0) == 0)
    def _():
        half = rows // 2
        places = pieces[1] // 2
        copies = []

        def copy_rows(source, skip, size, target, begin, sem):
            return pltpu.make_async_copy(
                source.at[pl.ds(skip, size)], target.at[pl.ds(begin, size)], sems.at[sem]
            )

        begin = 0
        for i, source in enumerate(sides[0]):
            skip = half if i in (0, 2) else 0
            copies.append(copy_rows(source, skip, source.shape[0] - skip, h2_ref, begin, i))
            begin += source.shape[0] - skip
        for copy in copies:
            copy.start()
        for core in range(2):

            @pl.when(ids_ref[1] == core)
            def _():
                own_y, other_y = sides[1][:places], sides[1][places : 2 * places]
                if core == 1:
                    own_y, other_y = other_y, own_y
                blocks = [*own_y[1:], *other_y]
                for i, source in enumerate(blocks):
                    for part in range(2):
                        to = (i + part * len(blocks)) * half
                        sem = len(sides[0]) + 2 * i + part
                        copy_rows(source, (core ^ part) * half, half, g_ref, to, sem).start()
                last = len(sides[0]) + 4 * places - 2
                copy_rows(sides[1][-1], 0, rows, g_ref, tokens - rows, last).start()

        for i in range(2 * (2 * places - 1)):
            copies.append(copy_rows(sides[1][0], 0, half, g_ref, 0, len(sides[0]) + i))
        last = len(sides[0]) + 4 * places - 2
        copies.append(copy_rows(sides[1][-1], 0, rows, g_ref, tokens - rows, last))
        if first:
            me = ids_ref[0]
            row = lax.broadcasted_iota(jnp.int32, (width, pair_rows), 0)
            col = lax.broadcasted_iota(jnp.int32, (width, pair_rows), 1)
            target = jnp.where(col < own_rows, me * own_rows + col, ((me ^ 1) - 1) * own_rows + col)
            chosen = jnp.where(row == target, 1.0, 0.0).astype(BF16)
        for copy in copies:
            copy.wait()
        if first:
            h2c_ref[...] = dot(h2_ref[...], chosen).T.astype(BF16)
            gc_ref[...] = dot(g_ref[...], chosen).T.astype(BF16)

    wg, wu, wd = wg_ref[...], wu_ref[...], wd_ref[...]
    last = slice(tokens - rows, tokens)
    totals = [
        dot(left[:, last], term[...])
        for left, term in ((h2c_ref, dgate_ref), (h2c_ref, dup_ref), (gc_ref, act_ref))
    ]
    for begin in range(0, tokens - rows, row_tile):
        part = slice(begin, min(begin + row_tile, tokens - rows))
        h2 = h2_ref[part]
        act, dgate, dup = hidden_terms(dot(h2, wg), dot(h2, wu), dot(g_ref[part], wd))
        h2c, gc = h2c_ref[:, part], gc_ref[:, part]
        terms = [dot(h2c, dgate), dot(h2c, dup), dot(gc, act)]
        totals = [a + b for a, b in zip(totals, terms)]
    for i, (own, total) in enumerate(zip(own_refs, totals)):
        own[...] = total[:own_rows]
        other_ref[i] = total[own_rows:].astype(BF16)


def bulk_mlp(ids, h2, g, own_terms, weights, chosen, own_rows, begin, end, tile, after):
    width = h2[0].shape[1]
    rows, hidden = own_terms[0].shape
    tokens = sum(piece.shape[0] for piece in h2) - rows
    out_hidden = min(end * tile, hidden) - begin * tile
    weight = pl.BlockSpec((width, tile), lambda i: (0, i + begin))
    term = pl.BlockSpec((rows, tile), lambda i: (0, i + begin))
    result = pl.BlockSpec((own_rows, tile), lambda i: (0, i))
    columns = pl.BlockSpec((2 * own_rows, tokens), lambda i: (0, 0))
    first = not chosen
    pieces = (len(h2), len(g))
    body = functools.partial(
        bulk_mlp_kernel, pieces=pieces, row_tile=min(tokens, 1024), first=first
    )
    return pl.pallas_call(
        ordered(body, len(after)),
        grid=(end - begin,),
        in_specs=[ANYWHERE] * len(after)
        + [SCALARS]
        + [ANYWHERE] * sum(pieces)
        + [term] * 3
        + [weight] * 3
        + [columns] * len(chosen),
        out_specs=[result] * 3
        + [pl.BlockSpec((3, own_rows, tile), lambda i: (0, 0, i))]
        + [columns] * (2 if first else 0),
        out_shape=[shape((own_rows, out_hidden), F32)] * 3
        + [shape((3, own_rows, out_hidden), BF16)]
        + [shape((2 * own_rows, tokens), BF16)] * (2 if first else 0),
        scratch_shapes=[pltpu.VMEM((tokens, width), BF16)] * 2 + [pltpu.SemaphoreType.DMA((len(h2) + 2 * len(g) - 3,))],
        compiler_params=pltpu.CompilerParams(vmem_limit_bytes=VMEM_LIMIT),
        cost_estimate=cost(
            6 * tokens * (width + 2 * own_rows) * out_hidden,
            6 * width * out_hidden + 4 * tokens * width,
            tokens * out_hidden,
            scale=0.12,
        ),
        name="bulk_mlp",
    )(*after, ids, *h2, *g, *own_terms, *weights, *chosen)


def shards(
    tokens,
    w_query,
    w_key,
    w_value,
    w_output,
    w_gate,
    w_up,
    w_down,
    attn_gain,
    mlp_gain,
    query_gain,
    key_gain,
    segments,
    positions,
    cotangent,
):
    count = lax.axis_size("ctx")
    me = lax.axis_index("ctx")
    core = lax.axis_index("tp")
    nz = count // QUAD
    m = me % QUAD
    head = query_gain.shape[0]
    rows, model = tokens.shape
    q_heads = w_query.shape[1] // head
    kv_heads = w_key.shape[1] // head
    group = q_heads // kv_heads
    pair = rows // SEQS
    quad_rows = QUAD * rows
    columns = group * head
    own_rows = model // count
    flips = [flip_pairs(count, j) for j in range(QUAD)]
    ids = jnp.stack([me, core]).astype(jnp.int32)

    def quad_exchange(pieces):
        return [pieces[0]] + [send(pieces[j], flips[j]) for j in range(1, QUAD)]

    own_tokens = tokens.reshape(SEQS, pair, model)
    half = lax.dynamic_index_in_dim(own_tokens, core, 0, keepdims=False)
    mine = [send(half, flips[j]) for j in range(1, QUAD)]
    theirs = [swap_cores(p) for p in mine]

    freqs = ROPE_BASE ** (-2.0 * np.arange(head // 2) / head)
    freqs = jnp.asarray(np.tile(freqs, 4)[None, :], F32)
    bias, angles = kernel_call(
        mask_kernel,
        "visible",
        (ids, freqs, segments.reshape(count, SEQS * pair)),
        [shape((SEQS, count * pair, QUAD * pair), F32), shape((quad_rows, 2 * head), F32)],
        scalars=True,
    )
    sign = jnp.asarray(np.tile(np.repeat([-1.0, 1.0], head // 2), 2)[None, :], F32)
    cos, sin = jnp.cos(angles), jnp.sin(angles) * sign
    w_head = jnp.concatenate(
        [
            lax.dynamic_slice_in_dim(w_key, m * head, head, 1),
            lax.dynamic_slice_in_dim(w_value, m * head, head, 1),
            lax.dynamic_slice_in_dim(w_query, m * columns, columns, 1),
            jnp.zeros((model, head), BF16),
        ],
        axis=1,
    )
    h1, raw, q, kv_own, g_copy = kernel_call(
        qkv_kernel,
        "query_key_value",
        (
            ids,
            own_tokens,
            *mine,
            *theirs,
            attn_gain,
            w_head,
            key_gain,
            query_gain,
            cos,
            sin,
            cotangent,
        ),
        [
            shape((SEQS, QUAD, pair, model), BF16),
            shape((quad_rows, 6 * head), F32),
            shape((quad_rows, 4 * head), BF16),
            shape((quad_rows, 2 * head), BF16),
            shape((rows, model), BF16),
        ],
        flops=2 * quad_rows * model * 6 * head,
        scalars=True,
    )
    kv = [kv_own] + [send(kv_own, shift_pairs(count, s)) for s in range(1, nz)]
    hidden = w_down.shape[1]
    (da,) = hidden_call(
        hidden_grad_kernel,
        "hidden_grad",
        (cotangent, w_down),
        [shape((rows, hidden), F32)],
        after=(kv_own,),
    )
    g_blocks = [lax.ppermute(g_copy, ("ctx", "tp"), core_pairs(count))]

    def next_cotangents(after):
        g_blocks.append(send(touch(g_blocks[-1], after), shift_pairs(count, 1)))

    *attn, lse = attention_forward(q, bias, kv, group, (da,))
    next_cotangents((lse,))
    attn_pieces = quad_exchange([a.reshape(rows, columns) for a in attn])
    branch = kernel_call(
        branch_kernel,
        "branch",
        (ids, *attn_pieces, w_output),
        [shape((rows // 2, model), BF16)] * 2,
        flops=2 * rows * model * w_output.shape[1],
        scalars=True,
        scratch=[pltpu.VMEM((QUAD, rows, columns), BF16)],
    )
    for _ in range(2, nz - 1):
        next_cotangents((branch[0],))
    middle, h2, h2_half = kernel_call(
        middle_kernel,
        "middle",
        (ids, tokens, *branch, *[swap_cores(b) for b in branch], mlp_gain),
        [shape((rows, model), F32), shape((rows, model), BF16), shape((rows // 2, model), BF16)],
        scalars=True,
    )
    h2_pieces = gather_column(h2_half, count)

    g_first = swap_cores(g_blocks[0])
    *dh2, act, dgate, dup = hidden_call(
        own_mlp_kernel,
        "own_mlp",
        (h2, da, w_gate, w_up),
        [shape((rows // 2, model), BF16)] * 2 + [shape((rows, hidden), BF16)] * 3,
        scratch=[pltpu.VMEM((model, rows), F32)],
        matmuls=4,
        after=(g_first,),
    )
    h2_packed = pack(h2_pieces, (act,))
    next_cotangents((act,))
    g_swapped = [g_first] + [swap_cores(g) for g in g_blocks[1:-1]]
    grad_middle, dy, dy_half, mlp_gain_part, *do = kernel_call(
        back_kernel,
        "back",
        (ids, middle, *dh2, *[swap_cores(d) for d in dh2], cotangent, mlp_gain, w_output),
        [
            shape((rows, model), F32),
            shape((rows, model), BF16),
            shape((rows // 2, model), BF16),
            shape((1, model), F32),
            *[shape((rows, columns), BF16)] * QUAD,
        ],
        flops=2 * rows * model * w_output.shape[1],
        scalars=True,
        scratch=[pltpu.VMEM((QUAD, rows, columns), BF16)],
        after=(h2_packed, *g_blocks[2:-1], *g_swapped[1:-1]),
    )
    do_pieces = [d.reshape(SEQS, pair, columns) for d in quad_exchange(do)]
    dy_half = touch(dy_half, do_pieces[1:])
    dy_mine = [send(dy_half, flips[j]) for j in range(1, QUAD)]
    dy_theirs = [swap_cores(p) for p in dy_mine]
    dy_pieces = (dy.reshape(SEQS, pair, model), *dy_mine, *dy_theirs)
    dq, *dkv = attention_backward(
        q, bias, lse, do_pieces, kv, (g_blocks[-1], *g_swapped[-1:])
    )
    h2_column = touch(h2_packed, (dq, *dy_mine))
    h2_other = send(h2_column, flips[2])
    (down,) = hidden_call(
        down_kernel,
        "down",
        (act, w_down),
        [shape((rows, model), BF16)],
        scratch=[pltpu.VMEM((model, rows), F32)],
        after=(dq,),
    )
    dkv = [dkv[0]] + [send(dkv[s], shift_pairs(count, nz - s)) for s in range(1, nz)]

    (output,) = kernel_call(
        output_kernel, "output", (middle, down, swap_cores(down)), [shape((rows, model), BF16)]
    )

    h2_column = touch(h2_column, (down, h2_other, *dkv[1:]))
    h2_other = touch(h2_other, (h2_column,))
    g_blocks[-1] = touch(g_blocks[-1], (h2_column,))
    h2_rows = (h2_column, h2_other, swap_cores(h2_column), swap_cores(h2_other), h2)
    g_rows = (*g_blocks, *g_swapped, swap_cores(g_blocks[-1]), cotangent)

    tile = 512
    tiles = pl.cdiv(hidden, tile)
    cut = (2 * tiles + 2) // 3

    def bulk_part(chosen, begin, end, after):
        result = bulk_mlp(
            ids,
            h2_rows,
            g_rows,
            (act, dgate, dup),
            (w_gate, w_up, w_down),
            chosen,
            own_rows,
            begin,
            end,
            tile,
            after,
        )
        return result[:3], result[3], result[4:]

    z_rows = model // nz
    head_part, *rest = kernel_call(
        head_grad_kernel,
        "head_grad",
        (ids, dq, raw, h1, *attn, *dy_pieces, key_gain, query_gain, cos, sin, *dkv),
        [
            shape((1, 6 * head), F32),
            *[shape((rows, 6 * head), BF16)] * QUAD,
            *[shape((z_rows, 8 * head), BF16)] * nz,
        ],
        flops=2 * quad_rows * model * 9 * head,
        scalars=True,
        scratch=[
            pltpu.VMEM((model, 8 * head), F32),
            pltpu.VMEM((SEQS, QUAD, pair, model), BF16),
        ],
        after=(down,),
    )
    grad_pieces, w_parts = quad_exchange(rest[:QUAD]), rest[QUAD:]
    w_parts = [w_parts[0]] + [send(w_parts[s], shift_pairs(count, nz - s)) for s in range(1, nz)]
    bulk_first = bulk_part((), 0, cut, (head_part,))
    dh1, attn_gain_part = kernel_call(
        input_grad_kernel,
        "input_grad",
        (ids, *grad_pieces, tokens, w_query, w_key, w_value),
        [shape((rows, model), BF16), shape((1, model), F32)],
        flops=2 * rows * model * (q_heads + 2 * kv_heads) * head,
        scalars=True,
        scratch=[pltpu.VMEM((QUAD, rows, 6 * head), BF16)],
        after=(bulk_first[0][0], *w_parts),
    )
    (grad_tokens,) = kernel_call(
        tokens_kernel,
        "tokens_grad",
        (tokens, grad_middle, dh1, swap_cores(dh1), attn_gain),
        [shape((rows, model), BF16)],
    )
    spread = kernel_call(
        spread_kernel,
        "spread",
        (ids, *w_parts),
        [shape((own_rows, 8 * head), F32)] + [shape((own_rows, 8 * head), BF16)] * (QUAD - 1),
        scalars=True,
        scratch=[pltpu.VMEM((z_rows, 8 * head), F32)],
        after=(bulk_first[0][0],),
    )
    gains = sum_but_x(
        jnp.concatenate([attn_gain_part, 0.5 * mlp_gain_part, head_part], axis=1)[0], count
    )
    theirs_first = send(bulk_first[1], flips[1])
    bulk_second = bulk_part(
        bulk_first[2], cut, tiles, (spread[0], grad_tokens, output, gains)
    )
    gains = gains + send(gains, flips[1])
    spread = quad_exchange(spread)
    theirs_second = send(touch(bulk_second[1], (gains, *spread[1:])), flips[1])
    mlp_grads = [
        jnp.concatenate(
            [
                bulk_first[0][i] + theirs_first[i].astype(F32),
                bulk_second[0][i] + theirs_second[i].astype(F32),
            ],
            axis=1,
        )
        for i in range(3)
    ]
    grad_wq, grad_wk, grad_wv, grad_wo = kernel_call(
        assemble_kernel,
        "assemble",
        (ids, *spread),
        [
            shape((own_rows, q_heads * head), F32),
            shape((own_rows, kv_heads * head), F32),
            shape((own_rows, kv_heads * head), F32),
            shape((own_rows, q_heads * head), F32),
        ],
        scalars=True,
        scratch=[pltpu.VMEM((QUAD, own_rows, 8 * head), F32)],
    )

    head_sums = gains[2 * model :].reshape(-1, head)
    return (
        output,
        grad_tokens,
        grad_wq,
        grad_wk,
        grad_wv,
        grad_wo,
        mlp_grads[0],
        mlp_grads[1],
        mlp_grads[2],
        gains[:model],
        gains[model : 2 * model],
        jnp.sum(head_sums[2 : 2 + group], axis=0),
        head_sums[0],
    )


def solution(mesh):
    rows = P("ctx", None)
    columns = P(None, "tp")
    both = P("ctx", "tp")
    in_specs = (rows,) + (columns,) * 7 + (P(),) * 5 + (P("ctx"), rows)
    out_specs = (rows, rows) + (both,) * 7 + (P(),) * 4
    return jax.shard_map(shards, mesh=mesh, in_specs=in_specs, out_specs=out_specs, check_vma=False)
```

time: 313 us -> 276 us (0.88)
  starting transfers between devices: 82.7 us -> 52 us
  waiting for transfers between devices: 70.5 us -> 50 us
  Pallas kernels: 130 us -> 142 us
    ppermute x40, waiting for transfers between devices: 65.9 us -> 45.6 us  [send(): return lax.ppermute(value, 'ctx', pairs)]
    pallas_call x16 -> x28, Pallas kernels: 130 us -> 142 us  [the longest x2 56 us: bulk_mlp(): pl.pallas_call(ordered(body, len(after)), grid=(end - begin,), in_specs=[...]
    ppermute x8 -> x1, starting transfers between devices: 13 us -> 1.64 us  [shards(): g_blocks = [lax.ppermute(g_copy, ('ctx', 'tp'), core_pairs(count))]]
    ppermute x16 -> x19, starting transfers between devices: 14.4 us -> 3.39 us  [swap_cores(): return lax.ppermute(value, 'tp', [(0, 1), (1, 0)])]
    unnamed x158 -> x157, local copies, waits for them, and re-layouts: 7.02 us -> 15.5 us
    ppermute x40, starting transfers between devices: 55.3 us -> 47 us  [send(): return lax.ppermute(value, 'ctx', pairs)]
    another operation x9 -> x0, local copies, waits for them, and re-layouts: 3.58 us -> none  [the longest x1 1.85 us: shards(): seg_rows.reshape(count, SEQS, pair, 1)]
    concatenate x1 -> x4, other arithmetic: 0.74 us -> 4.18 us  [the longest x3 3.44 us: shards(): jnp.concatenate([bulk_first[0][i] + theirs_first[i].astype(F32), bulk_sec...]
  transfers between devices with their start and end apart: 64 -> 60, of which waited for: 20 -> 23; matrix products, arithmetic and copies ran while one was open for 6% -> 4% of each run, Pallas kernels for 38% -> 50%
where the time goes in v3:
time: 276 us; the launch traced here: 275 us
  Pallas kernels  142 us (51%)
  starting transfers between devices  52 us (19%)
  waiting for transfers between devices  50 us (18%)
  local copies, waits for them, and re-layouts  19.7 us (7%)
  other arithmetic  10.5 us (4%)
    pallas_call x2, Pallas kernels, bulk_mlp(): pl.pallas_call(ordered(body, len(after)), grid=(end - begin,), in_specs=[...  56 us
    ppermute x40, starting transfers between devices, send(): return lax.ppermute(value, 'ctx', pairs)  47 us
    ppermute x40, waiting for transfers between devices, send(): return lax.ppermute(value, 'ctx', pairs)  45.6 us
    pallas_call x12, Pallas kernels, kernel_call(): pl.pallas_call(ordered(body, len(after)), in_specs=[ANYWHERE] * len(after...  40.4 us
    pallas_call x3, Pallas kernels, hidden_call(): pl.pallas_call(ordered(body, len(after)), grid=(hidden // tile,), in_spec...  29.9 us
    unnamed x157, local copies, waits for them, and re-layouts  15.5 us
    pallas_call x1, Pallas kernels, attention_backward(): pl.pallas_call(ordered(attention_backward_kernel, len(after)), grid=(seqs...  8.97 us
    pallas_call x1, Pallas kernels, attention_forward(): pl.pallas_call(ordered(attention_forward_kernel, len(after)), grid=(seqs,...  6.33 us
  transfers between devices with their start and end apart: 60, of which 23 were waited for; matrix products, arithmetic and copies ran while one was open for 4% of the time, Pallas kernels for 50%

profile of v3, /device:TPU:0, one launch (start us, length us, event | category | flops | bytes accessed | tf_op | source)
XLA Modules:
  0.0 275.3 jit_solution(2841161876781852997)
XLA Ops:
  1.7 4.0 %collective-permute-start.2 = (bf16[64,1536]{1,0:T(8,128)(2,1)S(1)}, bf16[64,1536]{1,0:T(8,128)(2,1)S(1)}, u32[]{:S(2)}, u32[]{:S(2)}) collective-permute-start(bf16[64,1536]{1,0:T(8,128)(2,1)S(1)} %dynamic-slice_bitcast_fusion), channel_id=1, source_target_pairs={{0,6},{2,4},{4,2},{6,0},{8,14},{10,12},{12,10},{14,8},{16,22},{18,... | collective-permute-start | bytes 589832 | tf_op jit(solution)/shard_map/ppermute | solution.py:44
  10.5 2.7 visible.1
  15.3 2.6 sine_multiply_fusion
  18.7 5.1 %query_key_value.1 = (bf16[2,4,64,1536]{3,2,1,0:T(8,128)(2,1)}, f32[512,384]{1,0:T(8,128)}, bf16[512,256]{1,0:T(8,128)(2,1)}, bf16[512,128]{1,0:T(8,128)(2,1)}, bf16[128,1536]{1,0:T(8,128)(2,1)}) custom-call(s32[2]{0:T(128)} %pad_add_fusion.refs_0_.refs_3_.refs_1_.refs_5_.refs_4_, bf16[2,64,1536]{2,1,0:T(8,128)(2,1)} %bitcast.46, ...), custom_call_target="tpu_custom_call" | custom-call | flops 6039797 | bytes 68224 | tf_op jit(solution)/shard_map/query_key_value/pallas_call | solution.py:94
  25.4 3.8 %collective-permute-start.8 = (bf16[512,128]{1,0:T(8,128)(2,1)}, bf16[512,128]{1,0:T(8,128)(2,1)S(1)}, u32[]{:S(2)}, u32[]{:S(2)}) collective-permute-start(bf16[512,128]{1,0:T(8,128)(2,1)} %get-tuple-element.78.refs_0_.refs_3_.refs_9_), channel_id=1, source_target_pairs={{0,24},{2,26},{4,28},{6,30},{8,0},{10,2},{12,4},{14,6},{16,8},{18,... | collective-permute-start | bytes 393224 | tf_op jit(solution)/shard_map/ppermute | solution.py:44
  30.2 6.9 %hidden_grad.1.refs_0_.refs_2_ = f32[128,3456]{1,0:T(8,128)} custom-call(bf16[512,128]{1,0:T(8,128)(2,1)} %get-tuple-element.78.refs_0_.refs_3_.refs_9_, bf16[128,1536]{1,0:T(8,128)(2,1)} %refs_18_.1, bf16[1536,3456]{1,0:T(8,128)(2,1)} %refs_24_.1), custom_call_target="tpu_custom_call" | custom-call | flops 27179088 | bytes 127795 | tf_op jit(solution)/shard_map/hidden_grad/pallas_call | solution.py:401
  37.1 4.9 %collective-permute-done.7.refs_5_.refs_11_ = bf16[512,128]{1,0:T(8,128)(2,1)S(1)} collective-permute-done((bf16[512,128]{1,0:T(8,128)(2,1)}, bf16[512,128]{1,0:T(8,128)(2,1)S(1)}, u32[]{:S(2)}, u32[]{:S(2)}) %collective-permute-start.7) | collective-permute-done | bytes 131104 | tf_op jit(solution)/shard_map/ppermute | solution.py:44
  42.7 6.3 %attention_forward.1 = (bf16[2,64,192]{2,1,0:T(8,128)(2,1)}, bf16[2,64,192]{2,1,0:T(8,128)(2,1)}, bf16[2,64,192]{2,1,0:T(8,128)(2,1)}, bf16[2,64,192]{2,1,0:T(8,128)(2,1)}, f32[2,3,1,256]{3,2,1,0:T(1,128)}) custom-call(f32[128,3456]{1,0:T(8,128)} %hidden_grad.1.refs_0_.refs_2_, bf16[512,256]{1,0:T(8,128)(2,1)} %get-tuple-element.79.refs_1_.refs_2_, ...), custom_call_target="tpu_custom_call" | custom-call | flops 12079595 | bytes 20971 | tf_op jit(solution)/shard_map/attention_forward/pallas_call | solution.py:306
  58.2 3.5 %branch.1 = (bf16[64,1536]{1,0:T(8,128)(2,1)}, bf16[64,1536]{1,0:T(8,128)(2,1)}) custom-call(s32[2]{0:T(128)} %pad_add_fusion.refs_0_.refs_3_.refs_1_.refs_5_.refs_4_, bf16[128,192]{1,0:T(8,128)(2,1)} %bitcast.48, bf16[128,192]{1,0:T(8,128)(2,1)} %copy-done.70, bf16[128,192]{1,0:T(8,128)(2,1)} %copy-done.69, bf16[128,192]{1,0:T(8,128)(2,1)} %copy-done.68, ...), custom_call_target="tpu_custom_call" | custom-call | flops 3019898 | bytes 29491 | tf_op jit(solution)/shard_map/branch/pallas_call | solution.py:94
  66.7 2.7 middle.1
  72.9 15.6 %own_mlp.1 = (bf16[64,1536]{1,0:T(8,128)(2,1)}, bf16[64,1536]{1,0:T(8,128)(2,1)}, bf16[128,3456]{1,0:T(8,128)(2,1)}, bf16[128,3456]{1,0:T(8,128)(2,1)}, bf16[128,3456]{1,0:T(8,128)(2,1)}) custom-call(bf16[128,1536]{1,0:T(8,128)(2,1)} %copy-done.10, bf16[128,1536]{1,0:T(8,128)(2,1)} %get-tuple-element.90.refs_1_.refs_6_.refs_9_, ...), custom_call_target="tpu_custom_call" | custom-call | flops 108716360 | bytes 264437 | tf_op jit(solution)/shard_map/own_mlp/pallas_call | solution.py:401
  89.8 3.1 %collective-permute-done.21.refs_3_ = bf16[64,1536]{1,0:T(8,128)(2,1)S(1)} collective-permute-done((bf16[64,1536]{1,0:T(8,128)(2,1)}, bf16[64,1536]{1,0:T(8,128)(2,1)S(1)}, u32[]{:S(2)}, u32[]{:S(2)}) %collective-permute-start.21) | collective-permute-done | bytes 196640 | tf_op jit(solution)/shard_map/ppermute | solution.py:44
  96.8 4.0 %back.1 = (f32[128,1536]{1,0:T(8,128)}, bf16[128,1536]{1,0:T(8,128)(2,1)}, bf16[64,1536]{1,0:T(8,128)(2,1)}, f32[1,1536]{1,0:T(1,128)}, bf16[128,192]{1,0:T(8,12...) custom-call(bf16[256,1536]{1,0:T(8,128)(2,1)} %pack.1.refs_0_, ...), custom_call_target="tpu_custom_call" | custom-call | flops 3019898 | bytes 59105 | tf_op jit(solution)/shard_map/back/pallas_call | solution.py:94
  106.4 2.3 collective-permute-done.28
  113.8 9.0 %attention_backward.1 = (f32[512,256]{1,0:T(8,128)}, bf16[512,128]{1,0:T(8,128)(2,1)}, bf16[512,128]{1,0:T(8,128)(2,1)}, bf16[512,128]{1,0:T(8,128)(2,1)}, bf16[512,128]{1,0:T(8,128)(2,1)}) custom-call(bf16[128,1536]{1,0:T(8,128)(2,1)} %copy-done.4, bf16[128,1536]{1,0:T(8,128)(2,1)} %copy-done.7, bf16[512,256]{1,0:T(8,128)(2,1)} %get-tuple-element.79.refs_1_.refs_2_, ...), custom_call_target="tpu_custom_call" | custom-call | flops 20132660 | bytes 20971 | tf_op jit(solution)/shard_map/attention_backward/pallas_call | solution.py:329
  124.2 3.2 %collective-permute-start.36 = (bf16[512,128]{1,0:T(8,128)(2,1)S(1)}, bf16[512,128]{1,0:T(8,128)(2,1)S(1)}, u32[]{:S(2)}, u32[]{:S(2)}) collective-permute-start(bf16[512,128]{1,0:T(8,128)(2,1)S(1)} %copy-done.76), channel_id=1, source_target_pairs={{0,24},{2,26},{4,28},{6,30},{8,0},{10,2},{12,4},{14,6},{16,8},{18,... | collective-permute-start | bytes 393224 | tf_op jit(solution)/shard_map/ppermute | solution.py:44
  128.0 7.4 %down.1.refs_1_.refs_0_ = bf16[128,1536]{1,0:T(8,128)(2,1)} custom-call(f32[512,256]{1,0:T(8,128)} %get-tuple-element.99.refs_0_.refs_2_.refs_1_, bf16[128,3456]{1,0:T(8,128)(2,1)} %get-tuple-element.91.refs_1_.refs_0_.refs_16_.refs_19_, bf16[1536,3456]{1,0:T(8,128)(2,1)} %refs_24_.1), custom_call_target="tpu_custom_call" | custom-call | flops 27179088 | bytes 118947 | tf_op jit(solution)/shard_map/down/pallas_call | solution.py:401
  136.9 4.3 %collective-permute-done.39.refs_2_.refs_0_ = bf16[256,1536]{1,0:T(8,128)(2,1)S(1)} collective-permute-done((bf16[256,1536]{1,0:T(8,128)(2,1)}, bf16[256,1536]{1,0:T(8,128)(2,1)S(1)}, u32[]{:S(2)}, u32[]{:S(2)}) %collective-permute-start.39) | collective-permute-done | bytes 786464 | tf_op jit(solution)/shard_map/ppermute | solution.py:44
  148.3 6.1 %head_grad.1 = (f32[1,384]{1,0:T(1,128)}, bf16[128,384]{1,0:T(8,128)(2,1)}, bf16[128,384]{1,0:T(8,128)(2,1)}, bf16[128,384]{1,0:T(8,128)(2,1)}, bf16[128,384]{1,...) custom-call(bf16[128,1536]{1,0:T(8,128)(2,1)} %down.1.refs_1_.refs_0, ...), custom_call_target="tpu_custom_call" | custom-call | flops 9059696 | bytes 76697 | tf_op jit(solution)/shard_map/head_grad/pallas_call | solution.py:94
  155.0 3.0 %collective-permute-start.43 = (bf16[384,512]{1,0:T(8,128)(2,1)}, bf16[384,512]{1,0:T(8,128)(2,1)S(1)}, u32[]{:S(2)}, u32[]{:S(2)}) collective-permute-start(bf16[384,512]{1,0:T(8,128)(2,1)} %get-tuple-element.114), channel_id=1, source_target_pairs={{0,24},{2,26},{4,28},{6,30},{8,0},{10,2},{12,4},{14,6},{16,8},{18,... | collective-permute-start | bytes 1179656 | tf_op jit(solution)/shard_map/ppermute | solution.py:44
  159.6 3.4 %collective-permute-start.45 = (bf16[384,512]{1,0:T(8,128)(2,1)}, bf16[384,512]{1,0:T(8,128)(2,1)S(1)}, u32[]{:S(2)}, u32[]{:S(2)}) collective-permute-start(bf16[384,512]{1,0:T(8,128)(2,1)} %get-tuple-element.116), channel_id=1, source_target_pairs={{0,8},{2,10},{4,12},{6,14},{8,16},{10,18},{12,20},{14,22},{16,24},... | collective-permute-start | bytes 1179656 | tf_op jit(solution)/shard_map/ppermute | solution.py:44
  165.1 37.6 %bulk_mlp.2 = (f32[96,2560]{1,0:T(8,128)}, f32[96,2560]{1,0:T(8,128)}, f32[96,2560]{1,0:T(8,128)}, bf16[3,96,2560]{2,1,0:T(8,128)(2,1)}, bf16[192,1024]{1,0:T(8,128)(2,1)}, /*index=5*/bf16[192,1024]{1,0:T(8,128)(2,1)}) custom-call(f32[1,384]{1,0:T(1,128)} %get-tuple-element.109.refs_0_, s32[2]{0:T(128)} %pad_add_fusion.refs_0_.refs_3_.refs_1_.refs_5_.refs_4_, ...), custom_call_target="tpu_custom_call" | custom-call | flops 3261490688 | bytes 3586129 | tf_op jit(solution)/shard_map/bulk_mlp/pallas_call | solution.py:695
  205.3 4.6 %input_grad.1 = (bf16[128,1536]{1,0:T(8,128)(2,1)}, f32[1,1536]{1,0:T(1,128)}) custom-call(f32[96,2560]{1,0:T(8,128)} %get-tuple-element.112.refs_0_, bf16[384,512]{1,0:T(8,128)(2,1)} %get-tuple-element.113.refs_1_.refs_2_, bf16[384,512]{1,0:T(8,128)(2,1)} %copy-done.16, bf16[384,512]{1,0:T(8,128)(2,1)} %copy-done.17, bf16[384,512]{1,0:T(8,128)(2,1)} %copy-done.18, ...), custom_call_target="tpu_custom_call" | custom-call | flops 5033164 | bytes 51179 | tf_op jit(solution)/shard_map/input_grad/pallas_call | solution.py:94
  213.1 3.1 %collective-permute-done.55 = f32[3456]{0:T(1024)S(1)} collective-permute-done((f32[3456]{0:T(1024)S(1)}, f32[3456]{0:T(1024)S(1)}, u32[]{:S(2)}, u32[]{:S(2)}) %collective-permute-start.55) | collective-permute-done | bytes 13856 | tf_op jit(solution)/shard_map/ppermute | solution.py:44
  216.3 3.6 %collective-permute-done.56 = f32[3456]{0:T(1024)S(1)} collective-permute-done((f32[3456]{0:T(1024)S(1)}, f32[3456]{0:T(1024)S(1)}, u32[]{:S(2)}, u32[]{:S(2)}) %collective-permute-start.56) | collective-permute-done | bytes 13856 | tf_op jit(solution)/shard_map/ppermute | solution.py:44
  220.2 4.4 %collective-permute-done.57 = f32[3456]{0:T(1024)S(1)} collective-permute-done((f32[3456]{0:T(1024)S(1)}, f32[3456]{0:T(1024)S(1)}, u32[]{:S(2)}, u32[]{:S(2)}) %collective-permute-start.57) | collective-permute-done | bytes 13856 | tf_op jit(solution)/shard_map/ppermute | solution.py:44
  228.2 2.5 spread.1
  232.7 4.5 %collective-permute-done.58 = f32[3456]{0:T(1024)S(1)} collective-permute-done((f32[3456]{0:T(1024)S(1)}, f32[3456]{0:T(1024)S(1)}, u32[]{:S(2)}, u32[]{:S(2)}) %collective-permute-start.58) | collective-permute-done | bytes 13856 | tf_op jit(solution)/shard_map/ppermute | solution.py:44
  239.9 2.6 tokens_grad.1.refs_1_
  242.5 18.4 %bulk_mlp.3 = (f32[96,896]{1,0:T(8,128)}, f32[96,896]{1,0:T(8,128)}, f32[96,896]{1,0:T(8,128)}, bf16[3,96,896]{2,1,0:T(8,128)(2,1)}) custom-call(f32[96,512]{1,0:T(8,128)} %get-tuple-element.122.refs_1_.refs_0_, bf16[128,1536]{1,0:T(8,128)(2,1)} %tokens_grad.1.refs_1_, bf16[128,1536]{1,0:T(8,128)(2,1)} %output.1.refs_2_, f32[3456]{0:T(1024)} %copy-done.61, ...), custom_call_target="tpu_custom_call" | custom-call | flops 1141521792 | bytes 1745879 | tf_op jit(solution)/shard_map/bulk_mlp/pallas_call | solution.py:695
  264.7 2.3 assemble.1
  267.0 4.3 %collective-permute-done.59 = bf16[3,96,896]{2,1,0:T(8,128)(2,1)S(1)} collective-permute-done((bf16[3,96,896]{2,1,0:T(8,128)(2,1)}, bf16[3,96,896]{2,1,0:T(8,128)(2,1)S(1)}, u32[]{:S(2)}, u32[]{:S(2)}) %collective-permute-start.59) | collective-permute-done | bytes 516128 | tf_op jit(solution)/shard_map/ppermute | solution.py:44
  (298 shorter events, 82.3 us)
Async XLA Ops:
  1.7 11.5 %collective-permute-start.2 = (bf16[64,1536]{1,0:T(8,128)(2,1)S(1)}, bf16[64,1536]{1,0:T(8,128)(2,1)S(1)}, u32[]{:S(2)}, u32[]{:S(2)}) collective-permute-start(bf16[64,1536]{1,0:T(8,128)(2,1)S(1)} %dynamic-slice_bitcast_fusion), channel_id=1, source_target_pairs={{0,6},{2,4},{4,2},{6,0},{8,14},{10,12},{12,10},{14,8},{16,22},{18,... | collective-permute-start | bytes 589832 | tf_op jit(solution)/shard_map/ppermute | solution.py:44
  23.8 25.3 %collective-permute-start.14 = (bf16[128,1536]{1,0:T(8,128)(2,1)}, bf16[128,1536]{1,0:T(8,128)(2,1)S(1)}, u32[]{:S(2)}, u32[]{:S(2)}) collective-permute-start(bf16[128,1536]{1,0:T(8,128)(2,1)} %get-tuple-element.88), channel_id=1, source_target_pairs={{0,0},{1,5},{2,2},{3,7},{4,4},{5,1},{6,6},{7,3},{8,8},{9,13},{10,1... | collective-permute-start | bytes 1179656 | tf_op jit(solution)/shard_map/ppermute | solution.py:819
  25.4 11.7 %collective-permute-start.8 = (bf16[512,128]{1,0:T(8,128)(2,1)}, bf16[512,128]{1,0:T(8,128)(2,1)S(1)}, u32[]{:S(2)}, u32[]{:S(2)}) collective-permute-start(bf16[512,128]{1,0:T(8,128)(2,1)} %get-tuple-element.78.refs_0_.refs_3_.refs_9_), channel_id=1, source_target_pairs={{0,24},{2,26},{4,28},{6,30},{8,0},{10,2},{12,4},{14,6},{16,8},{18,... | collective-permute-start | bytes 393224 | tf_op jit(solution)/shard_map/ppermute | solution.py:44
  29.2 12.8 %collective-permute-start.7 = (bf16[512,128]{1,0:T(8,128)(2,1)}, bf16[512,128]{1,0:T(8,128)(2,1)S(1)}, u32[]{:S(2)}, u32[]{:S(2)}) collective-permute-start(bf16[512,128]{1,0:T(8,128)(2,1)} %get-tuple-element.78.refs_0_.refs_3_.refs_9_), channel_id=1, source_target_pairs={{0,16},{2,18},{4,20},{6,22},{8,24},{10,26},{12,28},{14,30},{16,0},... | collective-permute-start | bytes 393224 | tf_op jit(solution)/shard_map/ppermute | solution.py:44
  29.2 12.8 %collective-permute-start.6 = (bf16[512,128]{1,0:T(8,128)(2,1)}, bf16[512,128]{1,0:T(8,128)(2,1)S(1)}, u32[]{:S(2)}, u32[]{:S(2)}) collective-permute-start(bf16[512,128]{1,0:T(8,128)(2,1)} %get-tuple-element.78.refs_0_.refs_3_.refs_9_), channel_id=1, source_target_pairs={{0,8},{2,10},{4,12},{6,14},{8,16},{10,18},{12,20},{14,22},{16,24},... | collective-permute-start | bytes 393224 | tf_op jit(solution)/shard_map/ppermute | solution.py:44
  49.8 13.1 %collective-permute-start.15 = (bf16[128,1536]{1,0:T(8,128)(2,1)}, bf16[128,1536]{1,0:T(8,128)(2,1)S(1)}, u32[]{:S(2)}, u32[]{:S(2)}) collective-permute-start(bf16[128,1536]{1,0:T(8,128)(2,1)} %touch.9), channel_id=1, source_target_pairs={{0,8},{2,10},{4,12},{6,14},{8,16},{10,18},{12,20},{14,22},{16,24},... | collective-permute-start | bytes 1179656 | tf_op jit(solution)/shard_map/ppermute | solution.py:44
  50.4 21.2 %collective-permute-start.17 = (bf16[128,1536]{1,0:T(8,128)(2,1)S(1)}, bf16[128,1536]{1,0:T(8,128)(2,1)S(1)}, u32[]{:S(2)}, u32[]{:S(2)}) collective-permute-start(bf16[128,1536]{1,0:T(8,128)(2,1)S(1)} %collective-permute-done.14.refs_7_.refs_10_), channel_id=1, source_target_pairs={{0,1},{1,0},{2,3},{3,2},{4,5},{5,4},{6,7},{7,6},{8,9},{9,8},{10,11... | collective-permute-start | bytes 1179656 | tf_op jit(solution)/shard_map/ppermute | solution.py:48
  63.8 24.8 %collective-permute-start.16 = (bf16[128,1536]{1,0:T(8,128)(2,1)}, bf16[128,1536]{1,0:T(8,128)(2,1)S(1)}, u32[]{:S(2)}, u32[]{:S(2)}) collective-permute-start(bf16[128,1536]{1,0:T(8,128)(2,1)} %touch.10), channel_id=1, source_target_pairs={{0,8},{2,10},{4,12},{6,14},{8,16},{10,18},{12,20},{14,22},{16,24},... | collective-permute-start | bytes 1179656 | tf_op jit(solution)/shard_map/ppermute | solution.py:44
  69.4 19.1 %collective-permute-start.22 = (bf16[64,1536]{1,0:T(8,128)(2,1)}, bf16[64,1536]{1,0:T(8,128)(2,1)S(1)}, u32[]{:S(2)}, u32[]{:S(2)}) collective-permute-start(bf16[64,1536]{1,0:T(8,128)(2,1)} %get-tuple-element.92.refs_1_), channel_id=1, source_target_pairs={{0,24},{2,26},{4,28},{6,30},{8,0},{10,2},{12,4},{14,6},{16,8},{18,... | collective-permute-start | bytes 589832 | tf_op jit(solution)/shard_map/ppermute | solution.py:44
  71.6 24.3 %collective-permute-start.23 = (bf16[128,1536]{1,0:T(8,128)(2,1)S(1)}, bf16[128,1536]{1,0:T(8,128)(2,1)S(1)}, u32[]{:S(2)}, u32[]{:S(2)}) collective-permute-start(bf16[128,1536]{1,0:T(8,128)(2,1)S(1)} %collective-permute-done.15.refs_8_.refs_11_), channel_id=1, source_target_pairs={{0,1},{1,0},{2,3},{3,2},{4,5},{5,4},{6,7},{7,6},{8,9},{9,8},{10,11... | collective-permute-start | bytes 1179656 | tf_op jit(solution)/shard_map/ppermute | solution.py:48
  71.6 21.3 %collective-permute-start.21 = (bf16[64,1536]{1,0:T(8,128)(2,1)}, bf16[64,1536]{1,0:T(8,128)(2,1)S(1)}, u32[]{:S(2)}, u32[]{:S(2)}) collective-permute-start(bf16[64,1536]{1,0:T(8,128)(2,1)} %get-tuple-element.92.refs_1_), channel_id=1, source_target_pairs={{0,16},{2,18},{4,20},{6,22},{8,24},{10,26},{12,28},{14,30},{16,0},... | collective-permute-start | bytes 589832 | tf_op jit(solution)/shard_map/ppermute | solution.py:44
  71.6 21.3 %collective-permute-start.20 = (bf16[64,1536]{1,0:T(8,128)(2,1)}, bf16[64,1536]{1,0:T(8,128)(2,1)S(1)}, u32[]{:S(2)}, u32[]{:S(2)}) collective-permute-start(bf16[64,1536]{1,0:T(8,128)(2,1)} %get-tuple-element.92.refs_1_), channel_id=1, source_target_pairs={{0,8},{2,10},{4,12},{6,14},{8,16},{10,18},{12,20},{14,22},{16,24},... | collective-permute-start | bytes 589832 | tf_op jit(solution)/shard_map/ppermute | solution.py:44
  92.9 19.9 %collective-permute-start.19 = (bf16[128,1536]{1,0:T(8,128)(2,1)S(1)}, bf16[128,1536]{1,0:T(8,128)(2,1)S(1)}, u32[]{:S(2)}, u32[]{:S(2)}) collective-permute-start(bf16[128,1536]{1,0:T(8,128)(2,1)S(1)} %collective-permute-done.16.refs_1_.refs_9_.refs_12_), channel_id=1, source_target_pairs={{0,1},{1,0},{2,3},{3,2},{4,5},{5,4},{6,7},{7,6},{8,9},{9,8},{10,11... | collective-permute-start | bytes 1179656 | tf_op jit(solution)/shard_map/ppermute | solution.py:48
  93.0 19.9 %collective-permute-start.18 = (bf16[128,1536]{1,0:T(8,128)(2,1)}, bf16[128,1536]{1,0:T(8,128)(2,1)S(1)}, u32[]{:S(2)}, u32[]{:S(2)}) collective-permute-start(bf16[128,1536]{1,0:T(8,128)(2,1)} %touch.11), channel_id=1, source_target_pairs={{0,8},{2,10},{4,12},{6,14},{8,16},{10,18},{12,20},{14,22},{16,24},... | collective-permute-start | bytes 1179656 | tf_op jit(solution)/shard_map/ppermute | solution.py:44
  109.4 13.4 %collective-permute-start.32 = (bf16[64,1536]{1,0:T(8,128)(2,1)}, bf16[64,1536]{1,0:T(8,128)(2,1)S(1)}, u32[]{:S(2)}, u32[]{:S(2)}) collective-permute-start(bf16[64,1536]{1,0:T(8,128)(2,1)} %touch.12), channel_id=1, source_target_pairs={{0,6},{2,4},{4,2},{6,0},{8,14},{10,12},{12,10},{14,8},{16,22},{18,... | collective-permute-start | bytes 589832 | tf_op jit(solution)/shard_map/ppermute | solution.py:44
  110.3 12.5 %collective-permute-start.31 = (bf16[64,1536]{1,0:T(8,128)(2,1)}, bf16[64,1536]{1,0:T(8,128)(2,1)S(1)}, u32[]{:S(2)}, u32[]{:S(2)}) collective-permute-start(bf16[64,1536]{1,0:T(8,128)(2,1)} %touch.12), channel_id=1, source_target_pairs={{0,4},{2,6},{4,0},{6,2},{8,12},{10,14},{12,8},{14,10},{16,20},{18,... | collective-permute-start | bytes 589832 | tf_op jit(solution)/shard_map/ppermute | solution.py:44
  123.6 17.6 %collective-permute-start.39 = (bf16[256,1536]{1,0:T(8,128)(2,1)}, bf16[256,1536]{1,0:T(8,128)(2,1)S(1)}, u32[]{:S(2)}, u32[]{:S(2)}) collective-permute-start(bf16[256,1536]{1,0:T(8,128)(2,1)} %touch.13.refs_0_), channel_id=1, source_target_pairs={{0,4},{2,6},{4,0},{6,2},{8,12},{10,14},{12,8},{14,10},{16,20},{18,... | collective-permute-start | bytes 2359304 | tf_op jit(solution)/shard_map/ppermute | solution.py:44
  142.1 20.9 %collective-permute-start.41 = (bf16[256,1536]{1,0:T(8,128)(2,1)}, bf16[256,1536]{1,0:T(8,128)(2,1)S(1)}, u32[]{:S(2)}, u32[]{:S(2)}) collective-permute-start(bf16[256,1536]{1,0:T(8,128)(2,1)} %touch.15.refs_3_.refs_6_), channel_id=1, source_target_pairs={{0,1},{1,0},{2,3},{3,2},{4,5},{5,4},{6,7},{7,6},{8,9},{9,8},{10,11... | collective-permute-start | bytes 2359304 | tf_op jit(solution)/shard_map/ppermute | solution.py:48
  143.2 20.4 %collective-permute-start.40 = (bf16[256,1536]{1,0:T(8,128)(2,1)S(1)}, bf16[256,1536]{1,0:T(8,128)(2,1)S(1)}, u32[]{:S(2)}, u32[]{:S(2)}) collective-permute-start(bf16[256,1536]{1,0:T(8,128)(2,1)S(1)} %copy-done), channel_id=1, source_target_pairs={{0,1},{1,0},{2,3},{3,2},{4,5},{5,4},{6,7},{7,6},{8,9},{9,8},{10,11... | collective-permute-start | bytes 2359304 | tf_op jit(solution)/shard_map/ppermute | solution.py:48
  143.7 15.8 %collective-permute-start.42 = (bf16[128,1536]{1,0:T(8,128)(2,1)}, bf16[128,1536]{1,0:T(8,128)(2,1)S(1)}, u32[]{:S(2)}, u32[]{:S(2)}) collective-permute-start(bf16[128,1536]{1,0:T(8,128)(2,1)} %touch.16.refs_10_.refs_13_), channel_id=1, source_target_pairs={{0,1},{1,0},{2,3},{3,2},{4,5},{5,4},{6,7},{7,6},{8,9},{9,8},{10,11... | collective-permute-start | bytes 1179656 | tf_op jit(solution)/shard_map/ppermute | solution.py:48
  155.0 49.3 %collective-permute-start.43 = (bf16[384,512]{1,0:T(8,128)(2,1)}, bf16[384,512]{1,0:T(8,128)(2,1)S(1)}, u32[]{:S(2)}, u32[]{:S(2)}) collective-permute-start(bf16[384,512]{1,0:T(8,128)(2,1)} %get-tuple-element.114), channel_id=1, source_target_pairs={{0,24},{2,26},{4,28},{6,30},{8,0},{10,2},{12,4},{14,6},{16,8},{18,... | collective-permute-start | bytes 1179656 | tf_op jit(solution)/shard_map/ppermute | solution.py:44
  159.5 44.8 %collective-permute-start.44 = (bf16[384,512]{1,0:T(8,128)(2,1)}, bf16[384,512]{1,0:T(8,128)(2,1)S(1)}, u32[]{:S(2)}, u32[]{:S(2)}) collective-permute-start(bf16[384,512]{1,0:T(8,128)(2,1)} %get-tuple-element.115), channel_id=1, source_target_pairs={{0,16},{2,18},{4,20},{6,22},{8,24},{10,26},{12,28},{14,30},{16,0},... | collective-permute-start | bytes 1179656 | tf_op jit(solution)/shard_map/ppermute | solution.py:44
  159.6 44.8 %collective-permute-start.45 = (bf16[384,512]{1,0:T(8,128)(2,1)}, bf16[384,512]{1,0:T(8,128)(2,1)S(1)}, u32[]{:S(2)}, u32[]{:S(2)}) collective-permute-start(bf16[384,512]{1,0:T(8,128)(2,1)} %get-tuple-element.116), channel_id=1, source_target_pairs={{0,8},{2,10},{4,12},{6,14},{8,16},{10,18},{12,20},{14,22},{16,24},... | collective-permute-start | bytes 1179656 | tf_op jit(solution)/shard_map/ppermute | solution.py:44
  163.0 39.8 %collective-permute-start.47 = (bf16[128,384]{1,0:T(8,128)(2,1)}, bf16[128,384]{1,0:T(8,128)(2,1)S(1)}, u32[]{:S(2)}, u32[]{:S(2)}) collective-permute-start(bf16[128,384]{1,0:T(8,128)(2,1)} %get-tuple-element.119), channel_id=1, source_target_pairs={{0,4},{2,6},{4,0},{6,2},{8,12},{10,14},{12,8},{14,10},{16,20},{18,... | collective-permute-start | bytes 294920 | tf_op jit(solution)/shard_map/ppermute | solution.py:44
  163.7 40.6 %collective-permute-start.48 = (bf16[128,384]{1,0:T(8,128)(2,1)}, bf16[128,384]{1,0:T(8,128)(2,1)S(1)}, u32[]{:S(2)}, u32[]{:S(2)}) collective-permute-start(bf16[128,384]{1,0:T(8,128)(2,1)} %get-tuple-element.120), channel_id=1, source_target_pairs={{0,6},{2,4},{4,2},{6,0},{8,14},{10,12},{12,10},{14,8},{16,22},{18,... | collective-permute-start | bytes 294920 | tf_op jit(solution)/shard_map/ppermute | solution.py:44
  202.8 68.6 %collective-permute-start.53 = (bf16[3,96,2560]{2,1,0:T(8,128)(2,1)}, bf16[3,96,2560]{2,1,0:T(8,128)(2,1)S(1)}, u32[]{:S(2)}, u32[]{:S(2)}) collective-permute-start(bf16[3,96,2560]{2,1,0:T(8,128)(2,1)} %get-tuple-element.130), channel_id=1, source_target_pairs={{0,2},{2,0},{4,6},{6,4},{8,10},{10,8},{12,14},{14,12},{16,18},{18,... | collective-permute-start | bytes 4423688 | tf_op jit(solution)/shard_map/ppermute | solution.py:44
  204.3 21.0 %collective-permute-start.29 = (bf16[128,1536]{1,0:T(8,128)(2,1)S(1)}, bf16[128,1536]{1,0:T(8,128)(2,1)S(1)}, u32[]{:S(2)}, u32[]{:S(2)}) collective-permute-start(bf16[128,1536]{1,0:T(8,128)(2,1)S(1)} %copy-done.5), channel_id=1, source_target_pairs={{0,1},{1,0},{2,3},{3,2},{4,5},{5,4},{6,7},{7,6},{8,9},{9,8},{10,11... | collective-permute-start | bytes 1179656 | tf_op jit(solution)/shard_map/ppermute | solution.py:48
  210.0 29.2 %collective-permute-start.49 = (bf16[128,1536]{1,0:T(8,128)(2,1)}, bf16[128,1536]{1,0:T(8,128)(2,1)S(1)}, u32[]{:S(2)}, u32[]{:S(2)}) collective-permute-start(bf16[128,1536]{1,0:T(8,128)(2,1)} %get-tuple-element.121.refs_2_), channel_id=1, source_target_pairs={{0,1},{1,0},{2,3},{3,2},{4,5},{5,4},{6,7},{7,6},{8,9},{9,8},{10,11... | collective-permute-start | bytes 1179656 | tf_op jit(solution)/shard_map/ppermute | solution.py:48
  224.6 12.7 %collective-permute-start.58 = (f32[3456]{0:T(1024)S(1)}, f32[3456]{0:T(1024)S(1)}, u32[]{:S(2)}, u32[]{:S(2)}) collective-permute-start(f32[3456]{0:T(1024)S(1)} %add.56.refs_3_), channel_id=1, source_target_pairs={{0,2},{2,0},{4,6},{6,4},{8,10},{10,8},{12,14},{14,12},{16,18},{18,... | collective-permute-start | bytes 41480 | tf_op jit(solution)/shard_map/ppermute | solution.py:44
  230.7 30.2 %collective-permute-start.50 = (bf16[96,512]{1,0:T(8,128)(2,1)}, bf16[96,512]{1,0:T(8,128)(2,1)S(1)}, u32[]{:S(2)}, u32[]{:S(2)}) collective-permute-start(bf16[96,512]{1,0:T(8,128)(2,1)} %get-tuple-element.123), channel_id=1, source_target_pairs={{0,2},{2,0},{4,6},{6,4},{8,10},{10,8},{12,14},{14,12},{16,18},{18,... | collective-permute-start | bytes 294920 | tf_op jit(solution)/shard_map/ppermute | solution.py:44
  232.0 28.9 %collective-permute-start.51 = (bf16[96,512]{1,0:T(8,128)(2,1)}, bf16[96,512]{1,0:T(8,128)(2,1)S(1)}, u32[]{:S(2)}, u32[]{:S(2)}) collective-permute-start(bf16[96,512]{1,0:T(8,128)(2,1)} %get-tuple-element.124), channel_id=1, source_target_pairs={{0,4},{2,6},{4,0},{6,2},{8,12},{10,14},{12,8},{14,10},{16,20},{18,... | collective-permute-start | bytes 294920 | tf_op jit(solution)/shard_map/ppermute | solution.py:44
  237.3 23.7 %collective-permute-start.52 = (bf16[96,512]{1,0:T(8,128)(2,1)}, bf16[96,512]{1,0:T(8,128)(2,1)S(1)}, u32[]{:S(2)}, u32[]{:S(2)}) collective-permute-start(bf16[96,512]{1,0:T(8,128)(2,1)} %get-tuple-element.125), channel_id=1, source_target_pairs={{0,6},{2,4},{4,2},{6,0},{8,14},{10,12},{12,10},{14,8},{16,22},{18,... | collective-permute-start | bytes 294920 | tf_op jit(solution)/shard_map/ppermute | solution.py:44
  (105 other events, 496.0 us)

commit v4 on v3

--- a/solution.py
+++ b/solution.py
@@ -54,15 +54,6 @@
 
 def gather_column(half, count):
     return [half] + [send(half, shift_pairs(count, s)) for s in range(1, count // QUAD)]
-
-
-def sum_but_x(value, count):
-    value = value + swap_cores(value)
-    bit = 2
-    while bit < count:
-        value = value + send(value, flip_pairs(count, bit))
-        bit *= 2
-    return value
 
 
 COST_SCALE = 0.01
@@ -713,10 +704,54 @@
             6 * tokens * (width + 2 * own_rows) * out_hidden,
             6 * width * out_hidden + 4 * tokens * width,
             tokens * out_hidden,
-            scale=0.12,
+            scale=1,
         ),
         name="bulk_mlp",
     )(*after, ids, *h2, *g, *own_terms, *weights, *chosen)
+
+
+def finish_kernel(*refs):
+    first, second, theirs, outs = refs[:3], refs[3:6], refs[6:8], refs[8:]
+    cut = first[0].shape[1]
+    for i in range(3):
+        outs[i][:, :cut] = first[i][...] + theirs[0][i].astype(F32)
+        outs[i][:, cut:] = second[i][...] + theirs[1][i].astype(F32)
+
+
+def bulk_finish(first, second, theirs_first, theirs_second):
+    rows, first_hidden = first[0].shape
+    second_hidden = second[0].shape[1]
+    hidden = first_hidden + second_hidden
+    block = rows // 3 if rows % 48 == 0 else rows
+
+    def spec(columns):
+        return pl.BlockSpec((block, columns), lambda i: (i, 0))
+
+    def theirs_spec(columns):
+        return pl.BlockSpec((3, block, columns), lambda i: (0, i, 0))
+
+    return pl.pallas_call(
+        finish_kernel,
+        grid=(rows // block,),
+        in_specs=[spec(first_hidden)] * 3
+        + [spec(second_hidden)] * 3
+        + [theirs_spec(first_hidden), theirs_spec(second_hidden)],
+        out_specs=[spec(hidden)] * 3,
+        out_shape=[shape((rows, hidden), F32)] * 3,
+        compiler_params=pltpu.CompilerParams(vmem_limit_bytes=VMEM_LIMIT),
+        cost_estimate=cost(rows * hidden, 30 * rows * hidden),
+        name="bulk_finish",
+    )(*first, *second, theirs_first, theirs_second)
+
+
+def gains_kernel(a_ref, b_ref, attn_ref, mlp_ref, query_ref, key_ref):
+    total = a_ref[...] + b_ref[...]
+    width = attn_ref.shape[0]
+    attn_ref[...] = total[:width]
+    mlp_ref[...] = total[width : 2 * width]
+    heads = total[2 * width :]
+    key_ref[...] = heads[:64]
+    query_ref[...] = heads[128:192] + heads[192:256] + heads[256:320]
 
 
 def shards(
@@ -819,7 +854,8 @@
     g_blocks = [lax.ppermute(g_copy, ("ctx", "tp"), core_pairs(count))]
 
     def next_cotangents(after):
-        g_blocks.append(send(touch(g_blocks[-1], after), shift_pairs(count, 1)))
+        g_blocks[-1] = touch(g_blocks[-1], after)
+        g_blocks.append(send(g_blocks[-1], shift_pairs(count, 1)))
 
     *attn, lse = attention_forward(q, bias, kv, group, (da,))
     next_cotangents((lse,))
@@ -893,35 +929,6 @@
     )
     dkv = [dkv[0]] + [send(dkv[s], shift_pairs(count, nz - s)) for s in range(1, nz)]
 
-    (output,) = kernel_call(
-        output_kernel, "output", (middle, down, swap_cores(down)), [shape((rows, model), BF16)]
-    )
-
-    h2_column = touch(h2_column, (down, h2_other, *dkv[1:]))
-    h2_other = touch(h2_other, (h2_column,))
-    g_blocks[-1] = touch(g_blocks[-1], (h2_column,))
-    h2_rows = (h2_column, h2_other, swap_cores(h2_column), swap_cores(h2_other), h2)
-    g_rows = (*g_blocks, *g_swapped, swap_cores(g_blocks[-1]), cotangent)
-
-    tile = 512
-    tiles = pl.cdiv(hidden, tile)
-    cut = (2 * tiles + 2) // 3
-
-    def bulk_part(chosen, begin, end, after):
-        result = bulk_mlp(
-            ids,
-            h2_rows,
-            g_rows,
-            (act, dgate, dup),
-            (w_gate, w_up, w_down),
-            chosen,
-            own_rows,
-            begin,
-            end,
-            tile,
-            after,
-        )
-        return result[:3], result[3], result[4:]
 
     z_rows = model // nz
     head_part, *rest = kernel_call(
@@ -943,7 +950,41 @@
     )
     grad_pieces, w_parts = quad_exchange(rest[:QUAD]), rest[QUAD:]
     w_parts = [w_parts[0]] + [send(w_parts[s], shift_pairs(count, nz - s)) for s in range(1, nz)]
+    h2_column = touch(h2_column, (h2_other, head_part))
+    h2_other = touch(h2_other, (h2_column,))
+    g_blocks[-1] = touch(g_blocks[-1], (h2_column,))
+    h2_rows = (h2_column, h2_other, swap_cores(h2_column), swap_cores(h2_other), h2)
+    g_rows = (*g_blocks, *g_swapped, swap_cores(g_blocks[-1]), cotangent)
+
+    tile = 512
+    tiles = pl.cdiv(hidden, tile)
+    cut = (2 * tiles + 2) // 3
+
+    def bulk_part(chosen, begin, end, after):
+        result = bulk_mlp(
+            ids,
+            h2_rows,
+            g_rows,
+            (act, dgate, dup),
+            (w_gate, w_up, w_down),
+            chosen,
+            own_rows,
+            begin,
+            end,
+            tile,
+            after,
+        )
+        return result[:3], result[3], result[4:]
+
     bulk_first = bulk_part((), 0, cut, (head_part,))
+    theirs_first = send(touch(bulk_first[1], grad_pieces[1:]), flips[1])
+    bulk_second = bulk_part(bulk_first[2], cut, tiles, ())
+    theirs_second = send(bulk_second[1], flips[1])
+    after_bulk = (bulk_second[0][0],)
+    down = touch(down, after_bulk)
+    (output,) = kernel_call(
+        output_kernel, "output", (middle, down, swap_cores(down)), [shape((rows, model), BF16)]
+    )
     dh1, attn_gain_part = kernel_call(
         input_grad_kernel,
         "input_grad",
@@ -952,7 +993,7 @@
         flops=2 * rows * model * (q_heads + 2 * kv_heads) * head,
         scalars=True,
         scratch=[pltpu.VMEM((QUAD, rows, 6 * head), BF16)],
-        after=(bulk_first[0][0], *w_parts),
+        after=after_bulk,
     )
     (grad_tokens,) = kernel_call(
         tokens_kernel,
@@ -967,28 +1008,23 @@
         [shape((own_rows, 8 * head), F32)] + [shape((own_rows, 8 * head), BF16)] * (QUAD - 1),
         scalars=True,
         scratch=[pltpu.VMEM((z_rows, 8 * head), F32)],
-        after=(bulk_first[0][0],),
-    )
-    gains = sum_but_x(
-        jnp.concatenate([attn_gain_part, 0.5 * mlp_gain_part, head_part], axis=1)[0], count
-    )
-    theirs_first = send(bulk_first[1], flips[1])
-    bulk_second = bulk_part(
-        bulk_first[2], cut, tiles, (spread[0], grad_tokens, output, gains)
-    )
-    gains = gains + send(gains, flips[1])
+        after=after_bulk,
+    )
+    gains = jnp.concatenate([attn_gain_part, 0.5 * mlp_gain_part, head_part], axis=1)[0]
+    gains = gains + swap_cores(gains)
+    gains = gains + send(gains, flips[2])
+    fillers = [spread[0], output]
+    for i in range(2, count.bit_length() - 1):
+        gains = touch(gains, (fillers[min(i, 3) - 2],))
+        gains = gains + send(gains, flip_pairs(count, 1 << i))
+    gains = touch(gains, (grad_tokens,))
+    grad_attn_gain, grad_mlp_gain, grad_query_gain, grad_key_gain = kernel_call(
+        gains_kernel,
+        "gains",
+        (gains, send(gains, flips[1])),
+        [shape((model,), F32)] * 2 + [shape((head,), F32)] * 2,
+    )
     spread = quad_exchange(spread)
-    theirs_second = send(touch(bulk_second[1], (gains, *spread[1:])), flips[1])
-    mlp_grads = [
-        jnp.concatenate(
-            [
-                bulk_first[0][i] + theirs_first[i].astype(F32),
-                bulk_second[0][i] + theirs_second[i].astype(F32),
-            ],
-            axis=1,
-        )
-        for i in range(3)
-    ]
     grad_wq, grad_wk, grad_wv, grad_wo = kernel_call(
         assemble_kernel,
         "assemble",
@@ -1003,7 +1039,7 @@
         scratch=[pltpu.VMEM((QUAD, own_rows, 8 * head), F32)],
     )
 
-    head_sums = gains[2 * model :].reshape(-1, head)
+    mlp_grads = bulk_finish(bulk_first[0], bulk_second[0], theirs_first, theirs_second)
     return (
         output,
         grad_tokens,
@@ -1014,10 +1050,10 @@
         mlp_grads[0],
         mlp_grads[1],
         mlp_grads[2],
-        gains[:model],
-        gains[model : 2 * model],
-        jnp.sum(head_sums[2 : 2 + group], axis=0),
-        head_sums[0],
+        grad_attn_gain,
+        grad_mlp_gain,
+        grad_query_gain,
+        grad_key_gain,
     )
 
 

time: 276 us -> 260 us (0.942)
  waiting for transfers between devices: 50 us -> 28.7 us
  Pallas kernels: 142 us -> 148 us
    ppermute x40, waiting for transfers between devices: 45.6 us -> 27.7 us  [send(): return lax.ppermute(value, 'ctx', pairs)]
    pallas_call x0 -> x1, Pallas kernels: none -> 5.32 us  [bulk_finish(): pl.pallas_call(finish_kernel, grid=(rows // block,), in_specs=[spec(first...]
    concatenate x3 -> x0, other arithmetic: 3.44 us -> none  [shards(): jnp.concatenate([bulk_first[0][i] + theirs_first[i].astype(F32), bulk_sec...]
    ppermute x19, waiting for transfers between devices: 4.41 us -> 1.03 us  [swap_cores(): return lax.ppermute(value, 'tp', [(0, 1), (1, 0)])]
    pallas_call x12 -> x13, Pallas kernels: 40.4 us -> 41.5 us  [kernel_call(): pl.pallas_call(ordered(body, len(after)), in_specs=[ANYWHERE] * len(after...]
    unnamed x157 -> x140, local copies, waits for them, and re-layouts: 15.5 us -> 16.3 us
  transfers between devices with their start and end apart: 60 -> 60, of which waited for: 23 -> 17; matrix products, arithmetic and copies ran while one was open for 4% -> 4% of each run, Pallas kernels for 50% -> 53%
where the time goes in v4:
time: 260 us
  Pallas kernels  148 us (57%)
  starting transfers between devices  54.3 us (21%)
  waiting for transfers between devices  28.7 us (11%)
  local copies, waits for them, and re-layouts  19.3 us (7%)
  other arithmetic  8.03 us (3%)
    pallas_call x2, Pallas kernels, bulk_mlp(): pl.pallas_call(ordered(body, len(after)), grid=(end - begin,), in_specs=[...  56.1 us
    ppermute x40, starting transfers between devices, send(): return lax.ppermute(value, 'ctx', pairs)  49.3 us
    pallas_call x13, Pallas kernels, kernel_call(): pl.pallas_call(ordered(body, len(after)), in_specs=[ANYWHERE] * len(after...  41.5 us
    pallas_call x3, Pallas kernels, hidden_call(): pl.pallas_call(ordered(body, len(after)), grid=(hidden // tile,), in_spec...  29.8 us
    ppermute x40, waiting for transfers between devices, send(): return lax.ppermute(value, 'ctx', pairs)  27.7 us
    unnamed x140, local copies, waits for them, and re-layouts  16.3 us
    pallas_call x1, Pallas kernels, attention_backward(): pl.pallas_call(ordered(attention_backward_kernel, len(after)), grid=(seqs...  8.98 us
    pallas_call x1, Pallas kernels, attention_forward(): pl.pallas_call(ordered(attention_forward_kernel, len(after)), grid=(seqs,...  6.34 us
  transfers between devices with their start and end apart: 60, of which 17 were waited for; matrix products, arithmetic and copies ran while one was open for 4% of the time, Pallas kernels for 53%

profile of v4, /device:TPU:0, one launch (start us, length us, event | category | flops | bytes accessed | tf_op | source)
XLA Modules:
  0.0 259.6 jit_solution(5005058256502840086)
XLA Ops:
  1.7 4.0 %collective-permute-start.2 = (bf16[64,1536]{1,0:T(8,128)(2,1)S(1)}, bf16[64,1536]{1,0:T(8,128)(2,1)S(1)}, u32[]{:S(2)}, u32[]{:S(2)}) collective-permute-start(bf16[64,1536]{1,0:T(8,128)(2,1)S(1)} %dynamic-slice_bitcast_fusion), channel_id=1, source_target_pairs={{0,6},{2,4},{4,2},{6,0},{8,14},{10,12},{12,10},{14,8},{16,22},{18,... | collective-permute-start | bytes 589832 | tf_op jit(solution)/shard_map/ppermute | solution.py:44
  10.5 2.7 %visible.1 = (f32[2,1024,256]{2,1,0:T(8,128)}, f32[512,128]{1,0:T(8,128)}) custom-call(s32[2]{0:T(128)} %pad_add_fusion.refs_0_.refs_3_.refs_1_, f32[1,128]{1,0:T(1,128)} %constant.43.clone.refs_1_, s32[16,128]{1,0:T(8,128)} %bitcast.29), custom_call_target="tpu_custom_call" | custom-call | bytes 23680 | tf_op jit(solution)/shard_map/visible/pallas_call | solution.py:85
  15.3 2.6 sine_multiply_fusion
  18.7 5.1 %query_key_value.1 = (bf16[2,4,64,1536]{3,2,1,0:T(8,128)(2,1)}, f32[512,384]{1,0:T(8,128)}, bf16[512,256]{1,0:T(8,128)(2,1)}, bf16[512,128]{1,0:T(8,128)(2,1)}, bf16[128,1536]{1,0:T(8,128)(2,1)}) custom-call(s32[2]{0:T(128)} %pad_add_fusion.refs_0_.refs_3_.refs_1_, bf16[2,64,1536]{2,1,0:T(8,128)(2,1)} %bitcast.16, bf16[64,1536]{1,0:T(8,128)(2,1)} %copy-done.33, ...), custom_call_target="tpu_custom_call" | custom-call | flops 6039797 | bytes 68224 | tf_op jit(solution)/shard_map/query_key_value/pallas_call | solution.py:85
  25.4 3.8 %collective-permute-start.8 = (bf16[512,128]{1,0:T(8,128)(2,1)}, bf16[512,128]{1,0:T(8,128)(2,1)S(1)}, u32[]{:S(2)}, u32[]{:S(2)}) collective-permute-start(bf16[512,128]{1,0:T(8,128)(2,1)} %get-tuple-element.85.refs_0_.refs_3_.refs_9_), channel_id=1, source_target_pairs={{0,24},{2,26},{4,28},{6,30},{8,0},{10,2},{12,4},{14,6},{16,8},{18,... | collective-permute-start | bytes 393224 | tf_op jit(solution)/shard_map/ppermute | solution.py:44
  30.2 6.8 %hidden_grad.1.refs_0_.refs_2_ = f32[128,3456]{1,0:T(8,128)} custom-call(bf16[512,128]{1,0:T(8,128)(2,1)} %get-tuple-element.85.refs_0_.refs_3_.refs_9_, bf16[128,1536]{1,0:T(8,128)(2,1)} %refs_14_.3, bf16[1536,3456]{1,0:T(8,128)(2,1)} %refs_20_.3), custom_call_target="tpu_custom_call" | custom-call | flops 27179088 | bytes 127795 | tf_op jit(solution)/shard_map/hidden_grad/pallas_call | solution.py:392
  37.1 4.9 %collective-permute-done.7.refs_5_.refs_11_ = bf16[512,128]{1,0:T(8,128)(2,1)S(1)} collective-permute-done((bf16[512,128]{1,0:T(8,128)(2,1)}, bf16[512,128]{1,0:T(8,128)(2,1)S(1)}, u32[]{:S(2)}, u32[]{:S(2)}) %collective-permute-start.7) | collective-permute-done | bytes 131104 | tf_op jit(solution)/shard_map/ppermute | solution.py:44
  42.7 6.3 %attention_forward.1 = (bf16[2,64,192]{2,1,0:T(8,128)(2,1)}, bf16[2,64,192]{2,1,0:T(8,128)(2,1)}, bf16[2,64,192]{2,1,0:T(8,128)(2,1)}, bf16[2,64,192]{2,1,0:T(8,128)(2,1)}, f32[2,3,1,256]{3,2,1,0:T(1,128)}) custom-call(f32[128,3456]{1,0:T(8,128)} %hidden_grad.1.refs_0_.refs_2_, bf16[512,256]{1,0:T(8,128)(2,1)} %get-tuple-element.86.refs_1_.refs_2_, ...), custom_call_target="tpu_custom_call" | custom-call | flops 12079595 | bytes 20971 | tf_op jit(solution)/shard_map/attention_forward/pallas_call | solution.py:297
  54.0 2.0 collective-permute-done.11.refs_4_
  58.4 3.5 %branch.1 = (bf16[64,1536]{1,0:T(8,128)(2,1)}, bf16[64,1536]{1,0:T(8,128)(2,1)}) custom-call(s32[2]{0:T(128)} %pad_add_fusion.refs_0_.refs_3_.refs_1_, bf16[128,192]{1,0:T(8,128)(2,1)} %bitcast.18, bf16[128,192]{1,0:T(8,128)(2,1)} %copy-done.56, bf16[128,192]{1,0:T(8,128)(2,1)} %copy-done.55, bf16[128,192]{1,0:T(8,128)(2,1)} %copy-done.54, ...), custom_call_target="tpu_custom_call" | custom-call | flops 3019898 | bytes 29491 | tf_op jit(solution)/shard_map/branch/pallas_call | solution.py:85
  66.9 2.6 middle.1
  69.4 2.0 collective-permute-start.22
  72.9 15.5 %own_mlp.1 = (bf16[64,1536]{1,0:T(8,128)(2,1)}, bf16[64,1536]{1,0:T(8,128)(2,1)}, bf16[128,3456]{1,0:T(8,128)(2,1)}, bf16[128,3456]{1,0:T(8,128)(2,1)}, bf16[128,3456]{1,0:T(8,128)(2,1)}) custom-call(bf16[128,1536]{1,0:T(8,128)(2,1)} %copy-done.10, bf16[128,1536]{1,0:T(8,128)(2,1)} %get-tuple-element.97.refs_1_.refs_6_.refs_5_, ...), custom_call_target="tpu_custom_call" | custom-call | flops 108716360 | bytes 264437 | tf_op jit(solution)/shard_map/own_mlp/pallas_call | solution.py:392
  89.3 3.8 %collective-permute-done.21.refs_3_ = bf16[64,1536]{1,0:T(8,128)(2,1)S(1)} collective-permute-done((bf16[64,1536]{1,0:T(8,128)(2,1)}, bf16[64,1536]{1,0:T(8,128)(2,1)S(1)}, u32[]{:S(2)}, u32[]{:S(2)}) %collective-permute-start.21) | collective-permute-done | bytes 196640 | tf_op jit(solution)/shard_map/ppermute | solution.py:44
  93.8 2.2 pack.1.refs_0_
  96.9 4.0 %back.1 = (f32[128,1536]{1,0:T(8,128)}, bf16[128,1536]{1,0:T(8,128)(2,1)}, bf16[64,1536]{1,0:T(8,128)(2,1)}, f32[1,1536]{1,0:T(1,128)}, bf16[128,192]{1,0:T(8,12...) custom-call(bf16[256,1536]{1,0:T(8,128)(2,1)} %pack.1.refs_0_, ...), custom_call_target="tpu_custom_call" | custom-call | flops 3019898 | bytes 59105 | tf_op jit(solution)/shard_map/back/pallas_call | solution.py:85
  106.6 2.1 collective-permute-done.28
  113.8 9.0 %attention_backward.1 = (f32[512,256]{1,0:T(8,128)}, bf16[512,128]{1,0:T(8,128)(2,1)}, bf16[512,128]{1,0:T(8,128)(2,1)}, bf16[512,128]{1,0:T(8,128)(2,1)}, bf16[512,128]{1,0:T(8,128)(2,1)}) custom-call(bf16[128,1536]{1,0:T(8,128)(2,1)} %copy-done.2, bf16[128,1536]{1,0:T(8,128)(2,1)} %copy-done.7, bf16[512,256]{1,0:T(8,128)(2,1)} %get-tuple-element.86.refs_1_.refs_2_, ...), custom_call_target="tpu_custom_call" | custom-call | flops 20132660 | bytes 20971 | tf_op jit(solution)/shard_map/attention_backward/pallas_call | solution.py:320
  124.9 3.2 %collective-permute-start.36 = (bf16[512,128]{1,0:T(8,128)(2,1)S(1)}, bf16[512,128]{1,0:T(8,128)(2,1)S(1)}, u32[]{:S(2)}, u32[]{:S(2)}) collective-permute-start(bf16[512,128]{1,0:T(8,128)(2,1)S(1)} %copy-done.63), channel_id=1, source_target_pairs={{0,24},{2,26},{4,28},{6,30},{8,0},{10,2},{12,4},{14,6},{16,8},{18,... | collective-permute-start | bytes 393224 | tf_op jit(solution)/shard_map/ppermute | solution.py:44
  130.1 7.5 %down.1.refs_0_ = bf16[128,1536]{1,0:T(8,128)(2,1)} custom-call(f32[512,256]{1,0:T(8,128)} %get-tuple-element.106.refs_0_.refs_1_.refs_2_, bf16[128,3456]{1,0:T(8,128)(2,1)} %get-tuple-element.98.refs_1_.refs_0_.refs_16_.refs_15_, bf16[1536,3456]{1,0:T(8,128)(2,1)} %refs_20_.3), custom_call_target="tpu_custom_call" | custom-call | flops 27179088 | bytes 118947 | tf_op jit(solution)/shard_map/down/pallas_call | solution.py:392
  137.6 2.7 %collective-permute-done.37.refs_22_ = bf16[512,128]{1,0:T(8,128)(2,1)S(1)} collective-permute-done((bf16[512,128]{1,0:T(8,128)(2,1)S(1)}, bf16[512,128]{1,0:T(8,128)(2,1)S(1)}, u32[]{:S(2)}, u32[]{:S(2)}) %collective-permute-start.37) | collective-permute-done | bytes 131104 | tf_op jit(solution)/shard_map/ppermute | solution.py:44
  141.0 6.1 %head_grad.1 = (f32[1,384]{1,0:T(1,128)}, bf16[128,384]{1,0:T(8,128)(2,1)}, bf16[128,384]{1,0:T(8,128)(2,1)}, bf16[128,384]{1,0:T(8,128)(2,1)}, bf16[128,384]{1,...) custom-call(bf16[128,1536]{1,0:T(8,128)(2,1)} %down.1.refs_0_, ...), custom_call_target="tpu_custom_call" | custom-call | flops 9059696 | bytes 76697 | tf_op jit(solution)/shard_map/head_grad/pallas_call | solution.py:85
  156.3 37.7 %bulk_mlp.2 = (f32[96,2560]{1,0:T(8,128)}, f32[96,2560]{1,0:T(8,128)}, f32[96,2560]{1,0:T(8,128)}, bf16[3,96,2560]{2,1,0:T(8,128)(2,1)}, bf16[192,1024]{1,0:T(8,128)(2,1)}, /*index=5*/bf16[192,1024]{1,0:T(8,128)(2,1)}) custom-call(f32[1,384]{1,0:T(1,128)} %get-tuple-element.115.refs_2_.refs_0_, s32[2]{0:T(128)} %pad_add_fusion.refs_0_.refs_3_.refs_1_, ...), custom_call_target="tpu_custom_call" | custom-call | flops 27179089920 | bytes 29884416 | tf_op jit(solution)/shard_map/bulk_mlp/pallas_call | solution.py:686
  194.0 2.3 collective-permute-start.49
  198.3 18.3 %bulk_mlp.3 = (f32[96,896]{1,0:T(8,128)}, f32[96,896]{1,0:T(8,128)}, f32[96,896]{1,0:T(8,128)}, bf16[3,96,896]{2,1,0:T(8,128)(2,1)}) custom-call(s32[2]{0:T(128)} %pad_add_fusion.refs_0_.refs_3_.refs_1_, bf16[256,1536]{1,0:T(8,128)(2,1)} %touch.18.refs_1_.refs_2_, bf16[256,1536]{1,0:T(8,128)(2,1)} %touch.19.refs_3_.refs_2_, bf16[256,1536]{1,0:T(8,128)(2,1)} %copy-done.16, ...), custom_call_target="tpu_custom_call" | custom-call | flops 9512681472 | bytes 14548992 | tf_op jit(solution)/shard_map/bulk_mlp/pallas_call | solution.py:686
  217.4 4.6 %input_grad.1 = (bf16[128,1536]{1,0:T(8,128)(2,1)}, f32[1,1536]{1,0:T(1,128)}) custom-call(f32[96,896]{1,0:T(8,128)} %get-tuple-element.120.refs_1_.refs_0_.refs_3_, s32[2]{0:T(128)} %pad_add_fusion.refs_0_.refs_3_.refs_1_, bf16[128,384]{1,0:T(8,128)(2,1)} %get-tuple-element.122.refs_2_, bf16[128,384]{1,0:T(8,128)(2,1)} %copy-done.25, ...), custom_call_target="tpu_custom_call" | custom-call | flops 5033164 | bytes 51179 | tf_op jit(solution)/shard_map/input_grad/pallas_call | solution.py:85
  225.4 2.5 spread.1
  228.6 3.9 %collective-permute-done.57 = f32[3456]{0:T(1024)S(1)} collective-permute-done((f32[3456]{0:T(1024)}, f32[3456]{0:T(1024)S(1)}, u32[]{:S(2)}, u32[]{:S(2)}) %collective-permute-start.57) | collective-permute-done | bytes 13856 | tf_op jit(solution)/shard_map/ppermute | solution.py:44
  234.6 2.2 output.1.refs_1_
  243.3 2.6 %tokens_grad.1.refs_1_ = bf16[128,1536]{1,0:T(8,128)(2,1)} custom-call(bf16[128,1536]{1,0:T(8,128)(2,1)} %refs_0_.1, f32[128,1536]{1,0:T(8,128)} %get-tuple-element.121.refs_1_, bf16[128,1536]{1,0:T(8,128)(2,1)} %get-tuple-element.126.refs_2_, bf16[128,1536]{1,0:T(8,128)(2,1)} %copy-done.22, f32[1536]{0:T(1024)} %refs_4_.3), custom_call_target="tpu_custom_call" | custom-call | bytes 23654 | tf_op jit(solution)/shard_map/tokens_grad/pallas_call | solution.py:85
  248.9 2.1 assemble.1
  254.2 5.3 %bulk_finish.1 = (f32[96,3456]{1,0:T(8,128)}, f32[96,3456]{1,0:T(8,128)}, f32[96,3456]{1,0:T(8,128)}) custom-call(f32[96,2560]{1,0:T(8,128)} %get-tuple-element.139.refs_0_, f32[96,2560]{1,0:T(8,128)} %get-tuple-element.140.refs_1_, f32[96,2560]{1,0:T(8,128)} %get-tuple-element.141.refs_2_, f32[96,896]{1,0:T(8,128)} %get-tuple-element.120.refs_1_.refs_0_.refs_3_, ...), custom_call_target="tpu_custom_call" | custom-call | flops 3317 | bytes 99532 | tf_op jit(solution)/shard_map/bulk_finish/pallas_call | solution.py:733
  (276 shorter events, 74.4 us)
Async XLA Ops:
  1.7 11.5 %collective-permute-start.2 = (bf16[64,1536]{1,0:T(8,128)(2,1)S(1)}, bf16[64,1536]{1,0:T(8,128)(2,1)S(1)}, u32[]{:S(2)}, u32[]{:S(2)}) collective-permute-start(bf16[64,1536]{1,0:T(8,128)(2,1)S(1)} %dynamic-slice_bitcast_fusion), channel_id=1, source_target_pairs={{0,6},{2,4},{4,2},{6,0},{8,14},{10,12},{12,10},{14,8},{16,22},{18,... | collective-permute-start | bytes 589832 | tf_op jit(solution)/shard_map/ppermute | solution.py:44
  23.8 25.2 %collective-permute-start.14 = (bf16[128,1536]{1,0:T(8,128)(2,1)}, bf16[128,1536]{1,0:T(8,128)(2,1)S(1)}, u32[]{:S(2)}, u32[]{:S(2)}) collective-permute-start(bf16[128,1536]{1,0:T(8,128)(2,1)} %get-tuple-element.95), channel_id=1, source_target_pairs={{0,0},{1,5},{2,2},{3,7},{4,4},{5,1},{6,6},{7,3},{8,8},{9,13},{10,1... | collective-permute-start | bytes 1179656 | tf_op jit(solution)/shard_map/ppermute | solution.py:854
  25.4 11.6 %collective-permute-start.8 = (bf16[512,128]{1,0:T(8,128)(2,1)}, bf16[512,128]{1,0:T(8,128)(2,1)S(1)}, u32[]{:S(2)}, u32[]{:S(2)}) collective-permute-start(bf16[512,128]{1,0:T(8,128)(2,1)} %get-tuple-element.85.refs_0_.refs_3_.refs_9_), channel_id=1, source_target_pairs={{0,24},{2,26},{4,28},{6,30},{8,0},{10,2},{12,4},{14,6},{16,8},{18,... | collective-permute-start | bytes 393224 | tf_op jit(solution)/shard_map/ppermute | solution.py:44
  29.2 12.8 %collective-permute-start.7 = (bf16[512,128]{1,0:T(8,128)(2,1)}, bf16[512,128]{1,0:T(8,128)(2,1)S(1)}, u32[]{:S(2)}, u32[]{:S(2)}) collective-permute-start(bf16[512,128]{1,0:T(8,128)(2,1)} %get-tuple-element.85.refs_0_.refs_3_.refs_9_), channel_id=1, source_target_pairs={{0,16},{2,18},{4,20},{6,22},{8,24},{10,26},{12,28},{14,30},{16,0},... | collective-permute-start | bytes 393224 | tf_op jit(solution)/shard_map/ppermute | solution.py:44
  29.2 12.8 %collective-permute-start.6 = (bf16[512,128]{1,0:T(8,128)(2,1)}, bf16[512,128]{1,0:T(8,128)(2,1)S(1)}, u32[]{:S(2)}, u32[]{:S(2)}) collective-permute-start(bf16[512,128]{1,0:T(8,128)(2,1)} %get-tuple-element.85.refs_0_.refs_3_.refs_9_), channel_id=1, source_target_pairs={{0,8},{2,10},{4,12},{6,14},{8,16},{10,18},{12,20},{14,22},{16,24},... | collective-permute-start | bytes 393224 | tf_op jit(solution)/shard_map/ppermute | solution.py:44
  49.8 13.1 %collective-permute-start.15 = (bf16[128,1536]{1,0:T(8,128)(2,1)}, bf16[128,1536]{1,0:T(8,128)(2,1)S(1)}, u32[]{:S(2)}, u32[]{:S(2)}) collective-permute-start(bf16[128,1536]{1,0:T(8,128)(2,1)} %touch.13.refs_7_.refs_6_), channel_id=1, source_target_pairs={{0,8},{2,10},{4,12},{6,14},{8,16},{10,18},{12,20},{14,22},{16,24},... | collective-permute-start | bytes 1179656 | tf_op jit(solution)/shard_map/ppermute | solution.py:44
  50.3 21.1 %collective-permute-start.17 = (bf16[128,1536]{1,0:T(8,128)(2,1)}, bf16[128,1536]{1,0:T(8,128)(2,1)S(1)}, u32[]{:S(2)}, u32[]{:S(2)}) collective-permute-start(bf16[128,1536]{1,0:T(8,128)(2,1)} %touch.13.refs_7_.refs_6_), channel_id=1, source_target_pairs={{0,1},{1,0},{2,3},{3,2},{4,5},{5,4},{6,7},{7,6},{8,9},{9,8},{10,11... | collective-permute-start | bytes 1179656 | tf_op jit(solution)/shard_map/ppermute | solution.py:48
  63.7 24.8 %collective-permute-start.16 = (bf16[128,1536]{1,0:T(8,128)(2,1)}, bf16[128,1536]{1,0:T(8,128)(2,1)S(1)}, u32[]{:S(2)}, u32[]{:S(2)}) collective-permute-start(bf16[128,1536]{1,0:T(8,128)(2,1)} %touch.14.refs_8_.refs_7_), channel_id=1, source_target_pairs={{0,8},{2,10},{4,12},{6,14},{8,16},{10,18},{12,20},{14,22},{16,24},... | collective-permute-start | bytes 1179656 | tf_op jit(solution)/shard_map/ppermute | solution.py:44
  69.4 19.0 %collective-permute-start.22 = (bf16[64,1536]{1,0:T(8,128)(2,1)}, bf16[64,1536]{1,0:T(8,128)(2,1)S(1)}, u32[]{:S(2)}, u32[]{:S(2)}) collective-permute-start(bf16[64,1536]{1,0:T(8,128)(2,1)} %get-tuple-element.99.refs_1_), channel_id=1, source_target_pairs={{0,24},{2,26},{4,28},{6,30},{8,0},{10,2},{12,4},{14,6},{16,8},{18,... | collective-permute-start | bytes 589832 | tf_op jit(solution)/shard_map/ppermute | solution.py:44
  71.4 24.6 %collective-permute-start.23 = (bf16[128,1536]{1,0:T(8,128)(2,1)}, bf16[128,1536]{1,0:T(8,128)(2,1)S(1)}, u32[]{:S(2)}, u32[]{:S(2)}) collective-permute-start(bf16[128,1536]{1,0:T(8,128)(2,1)} %touch.14.refs_8_.refs_7_), channel_id=1, source_target_pairs={{0,1},{1,0},{2,3},{3,2},{4,5},{5,4},{6,7},{7,6},{8,9},{9,8},{10,11... | collective-permute-start | bytes 1179656 | tf_op jit(solution)/shard_map/ppermute | solution.py:48
  71.4 21.6 %collective-permute-start.21 = (bf16[64,1536]{1,0:T(8,128)(2,1)}, bf16[64,1536]{1,0:T(8,128)(2,1)S(1)}, u32[]{:S(2)}, u32[]{:S(2)}) collective-permute-start(bf16[64,1536]{1,0:T(8,128)(2,1)} %get-tuple-element.99.refs_1_), channel_id=1, source_target_pairs={{0,16},{2,18},{4,20},{6,22},{8,24},{10,26},{12,28},{14,30},{16,0},... | collective-permute-start | bytes 589832 | tf_op jit(solution)/shard_map/ppermute | solution.py:44
  71.4 21.6 %collective-permute-start.20 = (bf16[64,1536]{1,0:T(8,128)(2,1)}, bf16[64,1536]{1,0:T(8,128)(2,1)S(1)}, u32[]{:S(2)}, u32[]{:S(2)}) collective-permute-start(bf16[64,1536]{1,0:T(8,128)(2,1)} %get-tuple-element.99.refs_1_), channel_id=1, source_target_pairs={{0,8},{2,10},{4,12},{6,14},{8,16},{10,18},{12,20},{14,22},{16,24},... | collective-permute-start | bytes 589832 | tf_op jit(solution)/shard_map/ppermute | solution.py:44
  93.0 19.8 %collective-permute-start.19 = (bf16[128,1536]{1,0:T(8,128)(2,1)}, bf16[128,1536]{1,0:T(8,128)(2,1)S(1)}, u32[]{:S(2)}, u32[]{:S(2)}) collective-permute-start(bf16[128,1536]{1,0:T(8,128)(2,1)} %touch.15.refs_1_.refs_9_.refs_8_), channel_id=1, source_target_pairs={{0,1},{1,0},{2,3},{3,2},{4,5},{5,4},{6,7},{7,6},{8,9},{9,8},{10,11... | collective-permute-start | bytes 1179656 | tf_op jit(solution)/shard_map/ppermute | solution.py:48
  93.1 19.8 %collective-permute-start.18 = (bf16[128,1536]{1,0:T(8,128)(2,1)}, bf16[128,1536]{1,0:T(8,128)(2,1)S(1)}, u32[]{:S(2)}, u32[]{:S(2)}) collective-permute-start(bf16[128,1536]{1,0:T(8,128)(2,1)} %touch.15.refs_1_.refs_9_.refs_8_), channel_id=1, source_target_pairs={{0,8},{2,10},{4,12},{6,14},{8,16},{10,18},{12,20},{14,22},{16,24},... | collective-permute-start | bytes 1179656 | tf_op jit(solution)/shard_map/ppermute | solution.py:44
  109.3 13.4 %collective-permute-start.31 = (bf16[64,1536]{1,0:T(8,128)(2,1)}, bf16[64,1536]{1,0:T(8,128)(2,1)S(1)}, u32[]{:S(2)}, u32[]{:S(2)}) collective-permute-start(bf16[64,1536]{1,0:T(8,128)(2,1)} %touch.16), channel_id=1, source_target_pairs={{0,6},{2,4},{4,2},{6,0},{8,14},{10,12},{12,10},{14,8},{16,22},{18,... | collective-permute-start | bytes 589832 | tf_op jit(solution)/shard_map/ppermute | solution.py:44
  110.5 12.3 %collective-permute-start.30 = (bf16[64,1536]{1,0:T(8,128)(2,1)}, bf16[64,1536]{1,0:T(8,128)(2,1)S(1)}, u32[]{:S(2)}, u32[]{:S(2)}) collective-permute-start(bf16[64,1536]{1,0:T(8,128)(2,1)} %touch.16), channel_id=1, source_target_pairs={{0,4},{2,6},{4,0},{6,2},{8,12},{10,14},{12,8},{14,10},{16,20},{18,... | collective-permute-start | bytes 589832 | tf_op jit(solution)/shard_map/ppermute | solution.py:44
  111.5 11.3 %collective-permute-start.29 = (bf16[64,1536]{1,0:T(8,128)(2,1)}, bf16[64,1536]{1,0:T(8,128)(2,1)S(1)}, u32[]{:S(2)}, u32[]{:S(2)}) collective-permute-start(bf16[64,1536]{1,0:T(8,128)(2,1)} %touch.16), channel_id=1, source_target_pairs={{0,2},{2,0},{4,6},{6,4},{8,10},{10,8},{12,14},{14,12},{16,18},{18,... | collective-permute-start | bytes 589832 | tf_op jit(solution)/shard_map/ppermute | solution.py:44
  123.6 23.5 %collective-permute-start.32 = (bf16[256,1536]{1,0:T(8,128)(2,1)}, bf16[256,1536]{1,0:T(8,128)(2,1)S(1)}, u32[]{:S(2)}, u32[]{:S(2)}) collective-permute-start(bf16[256,1536]{1,0:T(8,128)(2,1)} %touch.17.refs_0_), channel_id=1, source_target_pairs={{0,4},{2,6},{4,0},{6,2},{8,12},{10,14},{12,8},{14,10},{16,20},{18,... | collective-permute-start | bytes 2359304 | tf_op jit(solution)/shard_map/ppermute | solution.py:44
  124.9 12.6 %collective-permute-start.33 = (bf16[64,1536]{1,0:T(8,128)(2,1)}, bf16[64,1536]{1,0:T(8,128)(2,1)S(1)}, u32[]{:S(2)}, u32[]{:S(2)}) collective-permute-start(bf16[64,1536]{1,0:T(8,128)(2,1)} %copy-done.14), channel_id=1, source_target_pairs={{0,1},{1,0},{2,3},{3,2},{4,5},{5,4},{6,7},{7,6},{8,9},{9,8},{10,11... | collective-permute-start | bytes 589832 | tf_op jit(solution)/shard_map/ppermute | solution.py:48
  124.9 12.6 %collective-permute-start.36 = (bf16[512,128]{1,0:T(8,128)(2,1)S(1)}, bf16[512,128]{1,0:T(8,128)(2,1)S(1)}, u32[]{:S(2)}, u32[]{:S(2)}) collective-permute-start(bf16[512,128]{1,0:T(8,128)(2,1)S(1)} %copy-done.63), channel_id=1, source_target_pairs={{0,24},{2,26},{4,28},{6,30},{8,0},{10,2},{12,4},{14,6},{16,8},{18,... | collective-permute-start | bytes 393224 | tf_op jit(solution)/shard_map/ppermute | solution.py:44
  128.1 12.2 %collective-permute-start.37 = (bf16[512,128]{1,0:T(8,128)(2,1)S(1)}, bf16[512,128]{1,0:T(8,128)(2,1)S(1)}, u32[]{:S(2)}, u32[]{:S(2)}) collective-permute-start(bf16[512,128]{1,0:T(8,128)(2,1)S(1)} %copy-done.62), channel_id=1, source_target_pairs={{0,16},{2,18},{4,20},{6,22},{8,24},{10,26},{12,28},{14,30},{16,0},... | collective-permute-start | bytes 393224 | tf_op jit(solution)/shard_map/ppermute | solution.py:44
  128.2 12.1 %collective-permute-start.38 = (bf16[512,128]{1,0:T(8,128)(2,1)S(1)}, bf16[512,128]{1,0:T(8,128)(2,1)S(1)}, u32[]{:S(2)}, u32[]{:S(2)}) collective-permute-start(bf16[512,128]{1,0:T(8,128)(2,1)S(1)} %copy-done.61), channel_id=1, source_target_pairs={{0,8},{2,10},{4,12},{6,14},{8,16},{10,18},{12,20},{14,22},{16,24},... | collective-permute-start | bytes 393224 | tf_op jit(solution)/shard_map/ppermute | solution.py:44
  149.7 44.4 %collective-permute-start.43 = (bf16[128,384]{1,0:T(8,128)(2,1)S(1)}, bf16[128,384]{1,0:T(8,128)(2,1)S(1)}, u32[]{:S(2)}, u32[]{:S(2)}) collective-permute-start(bf16[128,384]{1,0:T(8,128)(2,1)S(1)} %copy-done.66), channel_id=1, source_target_pairs={{0,2},{2,0},{4,6},{6,4},{8,10},{10,8},{12,14},{14,12},{16,18},{18,... | collective-permute-start | bytes 294920 | tf_op jit(solution)/shard_map/ppermute | solution.py:44
  150.6 45.7 %collective-permute-start.44 = (bf16[128,384]{1,0:T(8,128)(2,1)S(1)}, bf16[128,384]{1,0:T(8,128)(2,1)S(1)}, u32[]{:S(2)}, u32[]{:S(2)}) collective-permute-start(bf16[128,384]{1,0:T(8,128)(2,1)S(1)} %copy-done.65), channel_id=1, source_target_pairs={{0,4},{2,6},{4,0},{6,2},{8,12},{10,14},{12,8},{14,10},{16,20},{18,... | collective-permute-start | bytes 294920 | tf_op jit(solution)/shard_map/ppermute | solution.py:44
  151.9 44.4 %collective-permute-start.45 = (bf16[128,384]{1,0:T(8,128)(2,1)S(1)}, bf16[128,384]{1,0:T(8,128)(2,1)S(1)}, u32[]{:S(2)}, u32[]{:S(2)}) collective-permute-start(bf16[128,384]{1,0:T(8,128)(2,1)S(1)} %copy-done.64), channel_id=1, source_target_pairs={{0,6},{2,4},{4,2},{6,0},{8,14},{10,12},{12,10},{14,8},{16,22},{18,... | collective-permute-start | bytes 294920 | tf_op jit(solution)/shard_map/ppermute | solution.py:44
  153.3 69.4 %collective-permute-start.47 = (bf16[384,512]{1,0:T(8,128)(2,1)}, bf16[384,512]{1,0:T(8,128)(2,1)}, u32[]{:S(2)}, u32[]{:S(2)}) collective-permute-start(bf16[384,512]{1,0:T(8,128)(2,1)} %get-tuple-element.128), channel_id=1, source_target_pairs={{0,24},{2,26},{4,28},{6,30},{8,0},{10,2},{12,4},{14,6},{16,8},{18,... | collective-permute-start | bytes 1179656 | tf_op jit(solution)/shard_map/ppermute | solution.py:44
  154.6 68.3 %collective-permute-start.48 = (bf16[384,512]{1,0:T(8,128)(2,1)}, bf16[384,512]{1,0:T(8,128)(2,1)}, u32[]{:S(2)}, u32[]{:S(2)}) collective-permute-start(bf16[384,512]{1,0:T(8,128)(2,1)} %get-tuple-element.129), channel_id=1, source_target_pairs={{0,16},{2,18},{4,20},{6,22},{8,24},{10,26},{12,28},{14,30},{16,0},... | collective-permute-start | bytes 1179656 | tf_op jit(solution)/shard_map/ppermute | solution.py:44
  194.0 30.1 %collective-permute-start.49 = (bf16[384,512]{1,0:T(8,128)(2,1)}, bf16[384,512]{1,0:T(8,128)(2,1)S(1)}, u32[]{:S(2)}, u32[]{:S(2)}) collective-permute-start(bf16[384,512]{1,0:T(8,128)(2,1)} %get-tuple-element.130), channel_id=1, source_target_pairs={{0,8},{2,10},{4,12},{6,14},{8,16},{10,18},{12,20},{14,22},{16,24},... | collective-permute-start | bytes 1179656 | tf_op jit(solution)/shard_map/ppermute | solution.py:44
  197.0 56.0 %collective-permute-start.53 = (bf16[3,96,2560]{2,1,0:T(8,128)(2,1)}, bf16[3,96,2560]{2,1,0:T(8,128)(2,1)S(1)}, u32[]{:S(2)}, u32[]{:S(2)}) collective-permute-start(bf16[3,96,2560]{2,1,0:T(8,128)(2,1)} %touch.22), channel_id=1, source_target_pairs={{0,2},{2,0},{4,6},{6,4},{8,10},{10,8},{12,14},{14,12},{16,18},{18,... | collective-permute-start | bytes 4423688 | tf_op jit(solution)/shard_map/ppermute | solution.py:44
  216.7 36.3 %collective-permute-start.54 = (bf16[3,96,896]{2,1,0:T(8,128)(2,1)}, bf16[3,96,896]{2,1,0:T(8,128)(2,1)S(1)}, u32[]{:S(2)}, u32[]{:S(2)}) collective-permute-start(bf16[3,96,896]{2,1,0:T(8,128)(2,1)} %get-tuple-element.145), channel_id=1, source_target_pairs={{0,2},{2,0},{4,6},{6,4},{8,10},{10,8},{12,14},{14,12},{16,18},{18,... | collective-permute-start | bytes 1548296 | tf_op jit(solution)/shard_map/ppermute | solution.py:44
  222.9 11.0 %collective-permute-start.42 = (bf16[128,1536]{1,0:T(8,128)(2,1)}, bf16[128,1536]{1,0:T(8,128)(2,1)S(1)}, u32[]{:S(2)}, u32[]{:S(2)}) collective-permute-start(bf16[128,1536]{1,0:T(8,128)(2,1)} %touch.21.refs_1_), channel_id=1, source_target_pairs={{0,1},{1,0},{2,3},{3,2},{4,5},{5,4},{6,7},{7,6},{8,9},{9,8},{10,11... | collective-permute-start | bytes 1179656 | tf_op jit(solution)/shard_map/ppermute | solution.py:48
  224.0 15.0 %collective-permute-start.46 = (bf16[128,1536]{1,0:T(8,128)(2,1)}, bf16[128,1536]{1,0:T(8,128)(2,1)S(1)}, u32[]{:S(2)}, u32[]{:S(2)}) collective-permute-start(bf16[128,1536]{1,0:T(8,128)(2,1)} %get-tuple-element.126.refs_2_), channel_id=1, source_target_pairs={{0,1},{1,0},{2,3},{3,2},{4,5},{5,4},{6,7},{7,6},{8,9},{9,8},{10,11... | collective-permute-start | bytes 1179656 | tf_op jit(solution)/shard_map/ppermute | solution.py:48
  (98 other events, 350.6 us)

commit v5 on v4

--- a/solution.py
+++ b/solution.py
@@ -16,7 +16,9 @@
 MASKED = -1e30
 F32 = jnp.float32
 BF16 = jnp.bfloat16
-VMEM_LIMIT = 56 * 1024 * 1024
+MIB = 1024 * 1024
+VMEM_LIMIT = 56 * MIB
+ROOMY = ("pack", "back", "spread", "head_grad", "middle",)
 
 
 def dot(left, right):
@@ -81,6 +83,7 @@
     body, name, args, out_shape, flops=0, scalars=False, scratch=(), after=(), scale=COST_SCALE
 ):
     vmem = pl.BlockSpec(memory_space=pltpu.VMEM)
+    roomy = name in ROOMY
     bytes_accessed = sum(a.size * a.dtype.itemsize for a in (*args, *out_shape))
     return pl.pallas_call(
         ordered(body, len(after)),
@@ -89,7 +92,9 @@
         out_specs=[vmem] * len(out_shape),
         out_shape=list(out_shape),
         scratch_shapes=list(scratch),
-        compiler_params=pltpu.CompilerParams(vmem_limit_bytes=VMEM_LIMIT),
+        compiler_params=pltpu.CompilerParams(
+            vmem_limit_bytes=VMEM_LIMIT if roomy else min(3 * bytes_accessed + 8 * MIB, VMEM_LIMIT)
+        ),
         cost_estimate=cost(flops, bytes_accessed, scale=scale),
         name=name,
     )(*after, *args)
@@ -869,8 +874,6 @@
         scalars=True,
         scratch=[pltpu.VMEM((QUAD, rows, columns), BF16)],
     )
-    for _ in range(2, nz - 1):
-        next_cotangents((branch[0],))
     middle, h2, h2_half = kernel_call(
         middle_kernel,
         "middle",
@@ -891,8 +894,10 @@
         after=(g_first,),
     )
     h2_packed = pack(h2_pieces, (act,))
-    next_cotangents((act,))
-    g_swapped = [g_first] + [swap_cores(g) for g in g_blocks[1:-1]]
+    g_blocks[1] = touch(g_blocks[1], (h2,))
+    g_second = swap_cores(g_blocks[1])
+    for _ in range(2, nz - 1):
+        next_cotangents((act,))
     grad_middle, dy, dy_half, mlp_gain_part, *do = kernel_call(
         back_kernel,
         "back",
@@ -907,7 +912,7 @@
         flops=2 * rows * model * w_output.shape[1],
         scalars=True,
         scratch=[pltpu.VMEM((QUAD, rows, columns), BF16)],
-        after=(h2_packed, *g_blocks[2:-1], *g_swapped[1:-1]),
+        after=(h2_packed, g_second),
     )
     do_pieces = [d.reshape(SEQS, pair, columns) for d in quad_exchange(do)]
     dy_half = touch(dy_half, do_pieces[1:])
@@ -915,8 +920,10 @@
     dy_theirs = [swap_cores(p) for p in dy_mine]
     dy_pieces = (dy.reshape(SEQS, pair, model), *dy_mine, *dy_theirs)
     dq, *dkv = attention_backward(
-        q, bias, lse, do_pieces, kv, (g_blocks[-1], *g_swapped[-1:])
-    )
+        q, bias, lse, do_pieces, kv, (g_blocks[-1],)
+    )
+    next_cotangents((dq,))
+    g_swapped = [g_first, g_second] + [swap_cores(g) for g in g_blocks[2:-1]]
     h2_column = touch(h2_packed, (dq, *dy_mine))
     h2_other = send(h2_column, flips[2])
     (down,) = hidden_call(

time: 260 us -> 249 us (0.958)
  Pallas kernels: 148 us -> 137 us
  other arithmetic: 8.03 us -> 4.16 us
  local copies, waits for them, and re-layouts: 19.3 us -> 22.9 us
    pallas_call x13, Pallas kernels: 41.5 us -> 29.1 us  [kernel_call(): pl.pallas_call(ordered(body, len(after)), in_specs=[ANYWHERE] * len(after...]
    unnamed x140 -> x170, local copies, waits for them, and re-layouts: 16.3 us -> 19.9 us
  transfers between devices with their start and end apart: 60 -> 60, of which waited for: 17 -> 20; matrix products, arithmetic and copies ran while one was open for 4% -> 2% of each run, Pallas kernels for 53% -> 52%
where the time goes in v5:
time: 249 us; the launch traced here: 248 us
  Pallas kernels  137 us (55%)
  starting transfers between devices  54.1 us (22%)
  waiting for transfers between devices  29.1 us (12%)
  local copies, waits for them, and re-layouts  22.9 us (9%)
  other arithmetic  4.16 us (2%)
    pallas_call x2, Pallas kernels, bulk_mlp(): pl.pallas_call(ordered(body, len(after)), grid=(end - begin,), in_specs=[...  56.8 us
    ppermute x40, starting transfers between devices, send(): return lax.ppermute(value, 'ctx', pairs)  50.7 us
    pallas_call x3, Pallas kernels, hidden_call(): pl.pallas_call(ordered(body, len(after)), grid=(hidden // tile,), in_spec...  29.8 us
    pallas_call x13, Pallas kernels, kernel_call(): pl.pallas_call(ordered(body, len(after)), in_specs=[ANYWHERE] * len(after...  29.1 us
    ppermute x40, waiting for transfers between devices, send(): return lax.ppermute(value, 'ctx', pairs)  27.2 us
    unnamed x170, local copies, waits for them, and re-layouts  19.9 us
    pallas_call x1, Pallas kernels, attention_backward(): pl.pallas_call(ordered(attention_backward_kernel, len(after)), grid=(seqs...  8.99 us
    pallas_call x1, Pallas kernels, attention_forward(): pl.pallas_call(ordered(attention_forward_kernel, len(after)), grid=(seqs,...  6.52 us
  transfers between devices with their start and end apart: 60, of which 20 were waited for; matrix products, arithmetic and copies ran while one was open for 2% of the time, Pallas kernels for 52%

profile of v5, /device:TPU:0, one launch (start us, length us, event | category | flops | bytes accessed | tf_op | source)
XLA Modules:
  0.0 248.5 jit_solution(96439309192167221)
XLA Ops:
  1.7 4.0 %collective-permute-start.2 = (bf16[64,1536]{1,0:T(8,128)(2,1)S(1)}, bf16[64,1536]{1,0:T(8,128)(2,1)S(1)}, u32[]{:S(2)}, u32[]{:S(2)}) collective-permute-start(bf16[64,1536]{1,0:T(8,128)(2,1)S(1)} %dynamic-slice_bitcast_fusion), channel_id=1, source_target_pairs={{0,6},{2,4},{4,2},{6,0},{8,14},{10,12},{12,10},{14,8},{16,22},{18,... | collective-permute-start | bytes 589832 | tf_op jit(solution)/shard_map/ppermute | solution.py:46
  6.4 1.6 constant_dynamic-slice_fusion
  11.7 3.1 %collective-permute-done.1.refs_3_ = bf16[64,1536]{1,0:T(8,128)(2,1)S(1)} collective-permute-done((bf16[64,1536]{1,0:T(8,128)(2,1)S(1)}, bf16[64,1536]{1,0:T(8,128)(2,1)S(1)}, u32[]{:S(2)}, u32[]{:S(2)}) %collective-permute-start.1) | collective-permute-done | bytes 196640 | tf_op jit(solution)/shard_map/ppermute | solution.py:46
  16.6 2.8 %query_key_value.1 = (bf16[2,4,64,1536]{3,2,1,0:T(8,128)(2,1)S(1)}, f32[512,384]{1,0:T(8,128)S(1)}, bf16[512,256]{1,0:T(8,128)(2,1)S(1)}, bf16[512,128]{1,0:T(8,128)(2,1)S(1)}, bf16[128,1536]{1,0:T(8,128)(2,1)S(1)}) custom-call(s32[2]{0:T(128)S(1)} %pad_add_fusion.refs_0_.refs_2_.refs_1_, bf16[2,64,1536]{2,1,0:T(8,128)(2,1)S(1)} %bitcast.16, ...), custom_call_target="tpu_custom_call" | custom-call | flops 6039797 | bytes 68224 | tf_op jit(solution)/shard_map/query_key_value/pallas_call | solution.py:88
  22.8 3.8 %collective-permute-start.8 = (bf16[512,128]{1,0:T(8,128)(2,1)S(1)}, bf16[512,128]{1,0:T(8,128)(2,1)S(1)}, u32[]{:S(2)}, u32[]{:S(2)}) collective-permute-start(bf16[512,128]{1,0:T(8,128)(2,1)S(1)} %get-tuple-element.85.refs_0_.refs_3_.refs_8_), channel_id=1, source_target_pairs={{0,24},{2,26},{4,28},{6,30},{8,0},{10,2},{12,4},{14,6},{16,8},{18,... | collective-permute-start | bytes 393224 | tf_op jit(solution)/shard_map/ppermute | solution.py:46
  27.7 6.9 %hidden_grad.1.refs_0_.refs_2_ = f32[128,3456]{1,0:T(8,128)} custom-call(bf16[512,128]{1,0:T(8,128)(2,1)} %copy-done.16, bf16[128,1536]{1,0:T(8,128)(2,1)} %refs_14_.3, bf16[1536,3456]{1,0:T(8,128)(2,1)} %refs_20_.3), custom_call_target="tpu_custom_call" | custom-call | flops 27179088 | bytes 127795 | tf_op jit(solution)/shard_map/hidden_grad/pallas_call | solution.py:397
  34.5 4.2 %collective-permute-done.7.refs_5_.refs_10_ = bf16[512,128]{1,0:T(8,128)(2,1)S(1)} collective-permute-done((bf16[512,128]{1,0:T(8,128)(2,1)S(1)}, bf16[512,128]{1,0:T(8,128)(2,1)S(1)}, u32[]{:S(2)}, u32[]{:S(2)}) %collective-permute-start.7) | collective-permute-done | bytes 131104 | tf_op jit(solution)/shard_map/ppermute | solution.py:46
  39.5 6.5 %attention_forward.1 = (bf16[2,64,192]{2,1,0:T(8,128)(2,1)}, bf16[2,64,192]{2,1,0:T(8,128)(2,1)}, bf16[2,64,192]{2,1,0:T(8,128)(2,1)}, bf16[2,64,192]{2,1,0:T(8,128)(2,1)}, f32[2,3,1,256]{3,2,1,0:T(1,128)}) custom-call(f32[128,3456]{1,0:T(8,128)} %hidden_grad.1.refs_0_.refs_2_, bf16[512,256]{1,0:T(8,128)(2,1)} %copy-done.17, f32[2,1024,256]{2,1,0:T(8,128)} %copy-done.1, ...), custom_call_target="tpu_custom_call" | custom-call | flops 12079595 | bytes 20971 | tf_op jit(solution)/shard_map/attention_forward/pallas_call | solution.py:302
  47.3 1.8 collective-permute-start.11
  50.8 2.1 collective-permute-done.11.refs_4_
  60.1 2.6 %middle.1 = (f32[128,1536]{1,0:T(8,128)}, bf16[128,1536]{1,0:T(8,128)(2,1)}, bf16[64,1536]{1,0:T(8,128)(2,1)}) custom-call(s32[2]{0:T(128)} %copy-done.32, bf16[128,1536]{1,0:T(8,128)(2,1)} %refs_0_.1, bf16[64,1536]{1,0:T(8,128)(2,1)} %copy-done.28, bf16[64,1536]{1,0:T(8,128)(2,1)} %copy-done.29, bf16[64,1536]{1,0:T(8,128)(2,1)} %copy-done.72, ...), custom_call_target="tpu_custom_call" | custom-call | bytes 25620 | tf_op jit(solution)/shard_map/middle/pallas_call | solution.py:88
  63.5 3.3 %collective-permute-start.20 = (bf16[64,1536]{1,0:T(8,128)(2,1)}, bf16[64,1536]{1,0:T(8,128)(2,1)S(1)}, u32[]{:S(2)}, u32[]{:S(2)}) collective-permute-start(bf16[64,1536]{1,0:T(8,128)(2,1)} %get-tuple-element.99.refs_1_), channel_id=1, source_target_pairs={{0,24},{2,26},{4,28},{6,30},{8,0},{10,2},{12,4},{14,6},{16,8},{18,... | collective-permute-start | bytes 589832 | tf_op jit(solution)/shard_map/ppermute | solution.py:46
  68.2 15.5 %own_mlp.1 = (bf16[64,1536]{1,0:T(8,128)(2,1)}, bf16[64,1536]{1,0:T(8,128)(2,1)}, bf16[128,3456]{1,0:T(8,128)(2,1)}, bf16[128,3456]{1,0:T(8,128)(2,1)}, bf16[128,3456]{1,0:T(8,128)(2,1)}) custom-call(bf16[128,1536]{1,0:T(8,128)(2,1)} %copy-done.49, bf16[128,1536]{1,0:T(8,128)(2,1)} %get-tuple-element.97.refs_1_.refs_6_.refs_5_, ...), custom_call_target="tpu_custom_call" | custom-call | flops 108716360 | bytes 264437 | tf_op jit(solution)/shard_map/own_mlp/pallas_call | solution.py:397
  84.2 2.8 %collective-permute-start.17 = (bf16[128,1536]{1,0:T(8,128)(2,1)}, bf16[128,1536]{1,0:T(8,128)(2,1)S(1)}, u32[]{:S(2)}, u32[]{:S(2)}) collective-permute-start(bf16[128,1536]{1,0:T(8,128)(2,1)} %touch.16.refs_8_.refs_7_), channel_id=1, source_target_pairs={{0,8},{2,10},{4,12},{6,14},{8,16},{10,18},{12,20},{14,22},{16,24},... | collective-permute-start | bytes 1179656 | tf_op jit(solution)/shard_map/ppermute | solution.py:46
  88.4 2.2 pack.1.refs_0_
  91.4 4.0 %back.1 = (f32[128,1536]{1,0:T(8,128)}, bf16[128,1536]{1,0:T(8,128)(2,1)}, bf16[64,1536]{1,0:T(8,128)(2,1)}, f32[1,1536]{1,0:T(1,128)}, bf16[128,192]{1,0:T(8,12...) custom-call(bf16[256,1536]{1,0:T(8,128)(2,1)} %pack.1.refs_0_, ...), custom_call_target="tpu_custom_call" | custom-call | flops 3019898 | bytes 59105 | tf_op jit(solution)/shard_map/back/pallas_call | solution.py:88
  95.9 1.9 collective-permute-start.25
  100.4 2.8 %collective-permute-done.26 = bf16[128,192]{1,0:T(8,128)(2,1)S(1)} collective-permute-done((bf16[128,192]{1,0:T(8,128)(2,1)}, bf16[128,192]{1,0:T(8,128)(2,1)S(1)}, u32[]{:S(2)}, u32[]{:S(2)}) %collective-permute-start.26) | collective-permute-done | bytes 49184 | tf_op jit(solution)/shard_map/ppermute | solution.py:46
  105.7 1.6 collective-permute-start.27
  108.1 9.0 %attention_backward.1 = (f32[512,256]{1,0:T(8,128)}, bf16[512,128]{1,0:T(8,128)(2,1)}, bf16[512,128]{1,0:T(8,128)(2,1)}, bf16[512,128]{1,0:T(8,128)(2,1)}, bf16[512,128]{1,0:T(8,128)(2,1)}) custom-call(bf16[128,1536]{1,0:T(8,128)(2,1)} %copy-done.43, bf16[512,256]{1,0:T(8,128)(2,1)} %copy-done.17, f32[2,1024,256]{2,1,0:T(8,128)} %copy-done.1, ...), custom_call_target="tpu_custom_call" | custom-call | flops 20132660 | bytes 20971 | tf_op jit(solution)/shard_map/attention_backward/pallas_call | solution.py:325
  122.4 7.5 %down.1.refs_0_ = bf16[128,1536]{1,0:T(8,128)(2,1)} custom-call(f32[512,256]{1,0:T(8,128)} %get-tuple-element.106.refs_0_.refs_1_.refs_2_, bf16[128,3456]{1,0:T(8,128)(2,1)} %get-tuple-element.98.refs_1_.refs_0_.refs_16_.refs_15_, bf16[1536,3456]{1,0:T(8,128)(2,1)} %refs_20_.3), custom_call_target="tpu_custom_call" | custom-call | flops 27179088 | bytes 118947 | tf_op jit(solution)/shard_map/down/pallas_call | solution.py:397
  133.6 6.1 %head_grad.1 = (f32[1,384]{1,0:T(1,128)}, bf16[128,384]{1,0:T(8,128)(2,1)}, bf16[128,384]{1,0:T(8,128)(2,1)}, bf16[128,384]{1,0:T(8,128)(2,1)}, bf16[128,384]{1,...) custom-call(bf16[128,1536]{1,0:T(8,128)(2,1)} %down.1.refs_0_, ...), custom_call_target="tpu_custom_call" | custom-call | flops 9059696 | bytes 76697 | tf_op jit(solution)/shard_map/head_grad/pallas_call | solution.py:88
  149.5 37.7 %bulk_mlp.2 = (f32[96,2560]{1,0:T(8,128)}, f32[96,2560]{1,0:T(8,128)}, f32[96,2560]{1,0:T(8,128)}, bf16[3,96,2560]{2,1,0:T(8,128)(2,1)}, bf16[192,1024]{1,0:T(8,128)(2,1)}, /*index=5*/bf16[192,1024]{1,0:T(8,128)(2,1)}) custom-call(f32[1,384]{1,0:T(1,128)} %get-tuple-element.115.refs_2_.refs_0_, s32[2]{0:T(128)} %copy-done.32, ...), custom_call_target="tpu_custom_call" | custom-call | flops 27179089920 | bytes 29884416 | tf_op jit(solution)/shard_map/bulk_mlp/pallas_call | solution.py:691
  187.2 2.3 collective-permute-start.49
  191.5 19.1 %bulk_mlp.3 = (f32[96,896]{1,0:T(8,128)}, f32[96,896]{1,0:T(8,128)}, f32[96,896]{1,0:T(8,128)}, bf16[3,96,896]{2,1,0:T(8,128)(2,1)}) custom-call(s32[2]{0:T(128)} %copy-done.32, bf16[256,1536]{1,0:T(8,128)(2,1)} %touch.19.refs_1_.refs_2_, bf16[256,1536]{1,0:T(8,128)(2,1)} %touch.20.refs_3_.refs_2_, ...), custom_call_target="tpu_custom_call" | custom-call | flops 9512681472 | bytes 14548992 | tf_op jit(solution)/shard_map/bulk_mlp/pallas_call | solution.py:691
  212.6 2.0 input_grad.1
  217.2 2.5 %spread.1 = (f32[96,512]{1,0:T(8,128)}, bf16[96,512]{1,0:T(8,128)(2,1)}, bf16[96,512]{1,0:T(8,128)(2,1)}, bf16[96,512]{1,0:T(8,128)(2,1)}) custom-call(f32[96,896]{1,0:T(8,128)} %get-tuple-element.120.refs_1_.refs_0_.refs_3_, s32[2]{0:T(128)} %copy-done.32, bf16[384,512]{1,0:T(8,128)(2,1)} %get-tuple-element.127.refs_2_, bf16[384,512]{1,0:T(8,128)(2,1)} %copy-done.59, ...), custom_call_target="tpu_custom_call" | custom-call | bytes 20643 | tf_op jit(solution)/shard_map/spread/pallas_call | solution.py:88
  221.0 3.4 %collective-permute-done.57 = f32[3456]{0:T(1024)S(1)} collective-permute-done((f32[3456]{0:T(1024)}, f32[3456]{0:T(1024)S(1)}, u32[]{:S(2)}, u32[]{:S(2)}) %collective-permute-start.57) | collective-permute-done | bytes 13856 | tf_op jit(solution)/shard_map/ppermute | solution.py:46
  229.6 2.0 collective-permute-done.58
  231.6 1.7 collective-permute-start.52
  235.1 2.7 %collective-permute-done.50.refs_2_ = bf16[96,512]{1,0:T(8,128)(2,1)S(1)} collective-permute-done((bf16[96,512]{1,0:T(8,128)(2,1)}, bf16[96,512]{1,0:T(8,128)(2,1)S(1)}, u32[]{:S(2)}, u32[]{:S(2)}) %collective-permute-start.50) | collective-permute-done | bytes 98336 | tf_op jit(solution)/shard_map/ppermute | solution.py:46
  243.1 5.3 %bulk_finish.1 = (f32[96,3456]{1,0:T(8,128)}, f32[96,3456]{1,0:T(8,128)}, f32[96,3456]{1,0:T(8,128)}) custom-call(f32[96,2560]{1,0:T(8,128)} %get-tuple-element.139.refs_0_, f32[96,2560]{1,0:T(8,128)} %get-tuple-element.140.refs_1_, f32[96,2560]{1,0:T(8,128)} %get-tuple-element.141.refs_2_, f32[96,896]{1,0:T(8,128)} %get-tuple-element.120.refs_1_.refs_0_.refs_3_, ...), custom_call_target="tpu_custom_call" | custom-call | flops 3317 | bytes 99532 | tf_op jit(solution)/shard_map/bulk_finish/pallas_call | solution.py:738
  (307 shorter events, 72.1 us)
Async XLA Ops:
  1.7 10.0 %collective-permute-start.2 = (bf16[64,1536]{1,0:T(8,128)(2,1)S(1)}, bf16[64,1536]{1,0:T(8,128)(2,1)S(1)}, u32[]{:S(2)}, u32[]{:S(2)}) collective-permute-start(bf16[64,1536]{1,0:T(8,128)(2,1)S(1)} %dynamic-slice_bitcast_fusion), channel_id=1, source_target_pairs={{0,6},{2,4},{4,2},{6,0},{8,14},{10,12},{12,10},{14,8},{16,22},{18,... | collective-permute-start | bytes 589832 | tf_op jit(solution)/shard_map/ppermute | solution.py:46
  22.1 23.9 %collective-permute-start.14 = (bf16[128,1536]{1,0:T(8,128)(2,1)S(1)}, bf16[128,1536]{1,0:T(8,128)(2,1)S(1)}, u32[]{:S(2)}, u32[]{:S(2)}) collective-permute-start(bf16[128,1536]{1,0:T(8,128)(2,1)S(1)} %get-tuple-element.95), channel_id=1, source_target_pairs={{0,0},{1,5},{2,2},{3,7},{4,4},{5,1},{6,6},{7,3},{8,8},{9,13},{10,1... | collective-permute-start | bytes 1179656 | tf_op jit(solution)/shard_map/ppermute | solution.py:859
  22.8 11.7 %collective-permute-start.8 = (bf16[512,128]{1,0:T(8,128)(2,1)S(1)}, bf16[512,128]{1,0:T(8,128)(2,1)S(1)}, u32[]{:S(2)}, u32[]{:S(2)}) collective-permute-start(bf16[512,128]{1,0:T(8,128)(2,1)S(1)} %get-tuple-element.85.refs_0_.refs_3_.refs_8_), channel_id=1, source_target_pairs={{0,24},{2,26},{4,28},{6,30},{8,0},{10,2},{12,4},{14,6},{16,8},{18,... | collective-permute-start | bytes 393224 | tf_op jit(solution)/shard_map/ppermute | solution.py:46
  26.6 12.1 %collective-permute-start.7 = (bf16[512,128]{1,0:T(8,128)(2,1)S(1)}, bf16[512,128]{1,0:T(8,128)(2,1)S(1)}, u32[]{:S(2)}, u32[]{:S(2)}) collective-permute-start(bf16[512,128]{1,0:T(8,128)(2,1)S(1)} %get-tuple-element.85.refs_0_.refs_3_.refs_8_), channel_id=1, source_target_pairs={{0,16},{2,18},{4,20},{6,22},{8,24},{10,26},{12,28},{14,30},{16,0},... | collective-permute-start | bytes 393224 | tf_op jit(solution)/shard_map/ppermute | solution.py:46
  26.6 12.1 %collective-permute-start.6 = (bf16[512,128]{1,0:T(8,128)(2,1)S(1)}, bf16[512,128]{1,0:T(8,128)(2,1)S(1)}, u32[]{:S(2)}, u32[]{:S(2)}) collective-permute-start(bf16[512,128]{1,0:T(8,128)(2,1)S(1)} %get-tuple-element.85.refs_0_.refs_3_.refs_8_), channel_id=1, source_target_pairs={{0,8},{2,10},{4,12},{6,14},{8,16},{10,18},{12,20},{14,22},{16,24},... | collective-permute-start | bytes 393224 | tf_op jit(solution)/shard_map/ppermute | solution.py:46
  46.7 15.9 %collective-permute-start.15 = (bf16[128,1536]{1,0:T(8,128)(2,1)}, bf16[128,1536]{1,0:T(8,128)(2,1)S(1)}, u32[]{:S(2)}, u32[]{:S(2)}) collective-permute-start(bf16[128,1536]{1,0:T(8,128)(2,1)} %touch.14.refs_7_.refs_6_), channel_id=1, source_target_pairs={{0,8},{2,10},{4,12},{6,14},{8,16},{10,18},{12,20},{14,22},{16,24},... | collective-permute-start | bytes 1179656 | tf_op jit(solution)/shard_map/ppermute | solution.py:46
  63.4 20.3 %collective-permute-start.21 = (bf16[128,1536]{1,0:T(8,128)(2,1)}, bf16[128,1536]{1,0:T(8,128)(2,1)S(1)}, u32[]{:S(2)}, u32[]{:S(2)}) collective-permute-start(bf16[128,1536]{1,0:T(8,128)(2,1)} %touch.15.refs_0_), channel_id=1, source_target_pairs={{0,1},{1,0},{2,3},{3,2},{4,5},{5,4},{6,7},{7,6},{8,9},{9,8},{10,11... | collective-permute-start | bytes 1179656 | tf_op jit(solution)/shard_map/ppermute | solution.py:50
  63.5 20.7 %collective-permute-start.20 = (bf16[64,1536]{1,0:T(8,128)(2,1)}, bf16[64,1536]{1,0:T(8,128)(2,1)S(1)}, u32[]{:S(2)}, u32[]{:S(2)}) collective-permute-start(bf16[64,1536]{1,0:T(8,128)(2,1)} %get-tuple-element.99.refs_1_), channel_id=1, source_target_pairs={{0,24},{2,26},{4,28},{6,30},{8,0},{10,2},{12,4},{14,6},{16,8},{18,... | collective-permute-start | bytes 589832 | tf_op jit(solution)/shard_map/ppermute | solution.py:46
  66.8 20.2 %collective-permute-start.19 = (bf16[64,1536]{1,0:T(8,128)(2,1)}, bf16[64,1536]{1,0:T(8,128)(2,1)S(1)}, u32[]{:S(2)}, u32[]{:S(2)}) collective-permute-start(bf16[64,1536]{1,0:T(8,128)(2,1)} %get-tuple-element.99.refs_1_), channel_id=1, source_target_pairs={{0,16},{2,18},{4,20},{6,22},{8,24},{10,26},{12,28},{14,30},{16,0},... | collective-permute-start | bytes 589832 | tf_op jit(solution)/shard_map/ppermute | solution.py:46
  67.5 19.6 %collective-permute-start.18 = (bf16[64,1536]{1,0:T(8,128)(2,1)}, bf16[64,1536]{1,0:T(8,128)(2,1)S(1)}, u32[]{:S(2)}, u32[]{:S(2)}) collective-permute-start(bf16[64,1536]{1,0:T(8,128)(2,1)} %get-tuple-element.99.refs_1_), channel_id=1, source_target_pairs={{0,8},{2,10},{4,12},{6,14},{8,16},{10,18},{12,20},{14,22},{16,24},... | collective-permute-start | bytes 589832 | tf_op jit(solution)/shard_map/ppermute | solution.py:46
  84.2 23.1 %collective-permute-start.17 = (bf16[128,1536]{1,0:T(8,128)(2,1)}, bf16[128,1536]{1,0:T(8,128)(2,1)S(1)}, u32[]{:S(2)}, u32[]{:S(2)}) collective-permute-start(bf16[128,1536]{1,0:T(8,128)(2,1)} %touch.16.refs_8_.refs_7_), channel_id=1, source_target_pairs={{0,8},{2,10},{4,12},{6,14},{8,16},{10,18},{12,20},{14,22},{16,24},... | collective-permute-start | bytes 1179656 | tf_op jit(solution)/shard_map/ppermute | solution.py:46
  103.8 13.3 %collective-permute-start.29 = (bf16[64,1536]{1,0:T(8,128)(2,1)}, bf16[64,1536]{1,0:T(8,128)(2,1)S(1)}, u32[]{:S(2)}, u32[]{:S(2)}) collective-permute-start(bf16[64,1536]{1,0:T(8,128)(2,1)} %touch.17), channel_id=1, source_target_pairs={{0,6},{2,4},{4,2},{6,0},{8,14},{10,12},{12,10},{14,8},{16,22},{18,... | collective-permute-start | bytes 589832 | tf_op jit(solution)/shard_map/ppermute | solution.py:46
  104.9 12.2 %collective-permute-start.28 = (bf16[64,1536]{1,0:T(8,128)(2,1)}, bf16[64,1536]{1,0:T(8,128)(2,1)S(1)}, u32[]{:S(2)}, u32[]{:S(2)}) collective-permute-start(bf16[64,1536]{1,0:T(8,128)(2,1)} %touch.17), channel_id=1, source_target_pairs={{0,4},{2,6},{4,0},{6,2},{8,12},{10,14},{12,8},{14,10},{16,20},{18,... | collective-permute-start | bytes 589832 | tf_op jit(solution)/shard_map/ppermute | solution.py:46
  105.7 11.5 %collective-permute-start.27 = (bf16[64,1536]{1,0:T(8,128)(2,1)}, bf16[64,1536]{1,0:T(8,128)(2,1)S(1)}, u32[]{:S(2)}, u32[]{:S(2)}) collective-permute-start(bf16[64,1536]{1,0:T(8,128)(2,1)} %touch.17), channel_id=1, source_target_pairs={{0,2},{2,0},{4,6},{6,4},{8,10},{10,8},{12,14},{14,12},{16,18},{18,... | collective-permute-start | bytes 589832 | tf_op jit(solution)/shard_map/ppermute | solution.py:46
  117.9 21.8 %collective-permute-start.30 = (bf16[256,1536]{1,0:T(8,128)(2,1)}, bf16[256,1536]{1,0:T(8,128)(2,1)S(1)}, u32[]{:S(2)}, u32[]{:S(2)}) collective-permute-start(bf16[256,1536]{1,0:T(8,128)(2,1)} %touch.18.refs_0_), channel_id=1, source_target_pairs={{0,4},{2,6},{4,0},{6,2},{8,12},{10,14},{12,8},{14,10},{16,20},{18,... | collective-permute-start | bytes 2359304 | tf_op jit(solution)/shard_map/ppermute | solution.py:46
  118.6 11.3 %collective-permute-start.31 = (bf16[64,1536]{1,0:T(8,128)(2,1)}, bf16[64,1536]{1,0:T(8,128)(2,1)S(1)}, u32[]{:S(2)}, u32[]{:S(2)}) collective-permute-start(bf16[64,1536]{1,0:T(8,128)(2,1)} %copy-done.52), channel_id=1, source_target_pairs={{0,1},{1,0},{2,3},{3,2},{4,5},{5,4},{6,7},{7,6},{8,9},{9,8},{10,11... | collective-permute-start | bytes 589832 | tf_op jit(solution)/shard_map/ppermute | solution.py:50
  118.6 12.8 %collective-permute-start.34 = (bf16[512,128]{1,0:T(8,128)(2,1)S(1)}, bf16[512,128]{1,0:T(8,128)(2,1)S(1)}, u32[]{:S(2)}, u32[]{:S(2)}) collective-permute-start(bf16[512,128]{1,0:T(8,128)(2,1)S(1)} %copy-done.83), channel_id=1, source_target_pairs={{0,24},{2,26},{4,28},{6,30},{8,0},{10,2},{12,4},{14,6},{16,8},{18,... | collective-permute-start | bytes 393224 | tf_op jit(solution)/shard_map/ppermute | solution.py:46
  120.0 12.9 %collective-permute-start.35 = (bf16[512,128]{1,0:T(8,128)(2,1)S(1)}, bf16[512,128]{1,0:T(8,128)(2,1)S(1)}, u32[]{:S(2)}, u32[]{:S(2)}) collective-permute-start(bf16[512,128]{1,0:T(8,128)(2,1)S(1)} %copy-done.82), channel_id=1, source_target_pairs={{0,16},{2,18},{4,20},{6,22},{8,24},{10,26},{12,28},{14,30},{16,0},... | collective-permute-start | bytes 393224 | tf_op jit(solution)/shard_map/ppermute | solution.py:46
  121.4 11.4 %collective-permute-start.36 = (bf16[512,128]{1,0:T(8,128)(2,1)S(1)}, bf16[512,128]{1,0:T(8,128)(2,1)S(1)}, u32[]{:S(2)}, u32[]{:S(2)}) collective-permute-start(bf16[512,128]{1,0:T(8,128)(2,1)S(1)} %copy-done.81), channel_id=1, source_target_pairs={{0,8},{2,10},{4,12},{6,14},{8,16},{10,18},{12,20},{14,22},{16,24},... | collective-permute-start | bytes 393224 | tf_op jit(solution)/shard_map/ppermute | solution.py:46
  130.0 12.8 %collective-permute-start.39 = (bf16[128,1536]{1,0:T(8,128)(2,1)S(1)}, bf16[128,1536]{1,0:T(8,128)(2,1)S(1)}, u32[]{:S(2)}, u32[]{:S(2)}) collective-permute-start(bf16[128,1536]{1,0:T(8,128)(2,1)S(1)} %copy-done.44), channel_id=1, source_target_pairs={{0,8},{2,10},{4,12},{6,14},{8,16},{10,18},{12,20},{14,22},{16,24},... | collective-permute-start | bytes 1179656 | tf_op jit(solution)/shard_map/ppermute | solution.py:46
  143.5 43.7 %collective-permute-start.43 = (bf16[128,384]{1,0:T(8,128)(2,1)}, bf16[128,384]{1,0:T(8,128)(2,1)S(1)}, u32[]{:S(2)}, u32[]{:S(2)}) collective-permute-start(bf16[128,384]{1,0:T(8,128)(2,1)} %get-tuple-element.123), channel_id=1, source_target_pairs={{0,2},{2,0},{4,6},{6,4},{8,10},{10,8},{12,14},{14,12},{16,18},{18,... | collective-permute-start | bytes 294920 | tf_op jit(solution)/shard_map/ppermute | solution.py:46
  144.9 44.6 %collective-permute-start.44 = (bf16[128,384]{1,0:T(8,128)(2,1)}, bf16[128,384]{1,0:T(8,128)(2,1)S(1)}, u32[]{:S(2)}, u32[]{:S(2)}) collective-permute-start(bf16[128,384]{1,0:T(8,128)(2,1)} %get-tuple-element.124), channel_id=1, source_target_pairs={{0,4},{2,6},{4,0},{6,2},{8,12},{10,14},{12,8},{14,10},{16,20},{18,... | collective-permute-start | bytes 294920 | tf_op jit(solution)/shard_map/ppermute | solution.py:46
  145.9 43.6 %collective-permute-start.45 = (bf16[128,384]{1,0:T(8,128)(2,1)S(1)}, bf16[128,384]{1,0:T(8,128)(2,1)S(1)}, u32[]{:S(2)}, u32[]{:S(2)}) collective-permute-start(bf16[128,384]{1,0:T(8,128)(2,1)S(1)} %copy-done.84), channel_id=1, source_target_pairs={{0,6},{2,4},{4,2},{6,0},{8,14},{10,12},{12,10},{14,8},{16,22},{18,... | collective-permute-start | bytes 294920 | tf_op jit(solution)/shard_map/ppermute | solution.py:46
  147.2 67.4 %collective-permute-start.47 = (bf16[384,512]{1,0:T(8,128)(2,1)}, bf16[384,512]{1,0:T(8,128)(2,1)S(1)}, u32[]{:S(2)}, u32[]{:S(2)}) collective-permute-start(bf16[384,512]{1,0:T(8,128)(2,1)} %get-tuple-element.128), channel_id=1, source_target_pairs={{0,24},{2,26},{4,28},{6,30},{8,0},{10,2},{12,4},{14,6},{16,8},{18,... | collective-permute-start | bytes 1179656 | tf_op jit(solution)/shard_map/ppermute | solution.py:46
  148.4 66.9 %collective-permute-start.48 = (bf16[384,512]{1,0:T(8,128)(2,1)}, bf16[384,512]{1,0:T(8,128)(2,1)}, u32[]{:S(2)}, u32[]{:S(2)}) collective-permute-start(bf16[384,512]{1,0:T(8,128)(2,1)} %get-tuple-element.129), channel_id=1, source_target_pairs={{0,16},{2,18},{4,20},{6,22},{8,24},{10,26},{12,28},{14,30},{16,0},... | collective-permute-start | bytes 1179656 | tf_op jit(solution)/shard_map/ppermute | solution.py:46
  187.2 28.8 %collective-permute-start.49 = (bf16[384,512]{1,0:T(8,128)(2,1)}, bf16[384,512]{1,0:T(8,128)(2,1)S(1)}, u32[]{:S(2)}, u32[]{:S(2)}) collective-permute-start(bf16[384,512]{1,0:T(8,128)(2,1)} %get-tuple-element.130), channel_id=1, source_target_pairs={{0,8},{2,10},{4,12},{6,14},{8,16},{10,18},{12,20},{14,22},{16,24},... | collective-permute-start | bytes 1179656 | tf_op jit(solution)/shard_map/ppermute | solution.py:46
  190.2 52.9 %collective-permute-start.53 = (bf16[3,96,2560]{2,1,0:T(8,128)(2,1)}, bf16[3,96,2560]{2,1,0:T(8,128)(2,1)}, u32[]{:S(2)}, u32[]{:S(2)}) collective-permute-start(bf16[3,96,2560]{2,1,0:T(8,128)(2,1)} %touch.24), channel_id=1, source_target_pairs={{0,2},{2,0},{4,6},{6,4},{8,10},{10,8},{12,14},{14,12},{16,18},{18,... | collective-permute-start | bytes 4423688 | tf_op jit(solution)/shard_map/ppermute | solution.py:46
  210.7 32.4 %collective-permute-start.54 = (bf16[3,96,896]{2,1,0:T(8,128)(2,1)}, bf16[3,96,896]{2,1,0:T(8,128)(2,1)}, u32[]{:S(2)}, u32[]{:S(2)}) collective-permute-start(bf16[3,96,896]{2,1,0:T(8,128)(2,1)} %get-tuple-element.145), channel_id=1, source_target_pairs={{0,2},{2,0},{4,6},{6,4},{8,10},{10,8},{12,14},{14,12},{16,18},{18,... | collective-permute-start | bytes 1548296 | tf_op jit(solution)/shard_map/ppermute | solution.py:46
  215.4 10.4 %collective-permute-start.42 = (bf16[128,1536]{1,0:T(8,128)(2,1)}, bf16[128,1536]{1,0:T(8,128)(2,1)S(1)}, u32[]{:S(2)}, u32[]{:S(2)}) collective-permute-start(bf16[128,1536]{1,0:T(8,128)(2,1)} %touch.23.refs_1_), channel_id=1, source_target_pairs={{0,1},{1,0},{2,3},{3,2},{4,5},{5,4},{6,7},{7,6},{8,9},{9,8},{10,11... | collective-permute-start | bytes 1179656 | tf_op jit(solution)/shard_map/ppermute | solution.py:50
  215.9 12.8 %collective-permute-start.46 = (bf16[128,1536]{1,0:T(8,128)(2,1)S(1)}, bf16[128,1536]{1,0:T(8,128)(2,1)S(1)}, u32[]{:S(2)}, u32[]{:S(2)}) collective-permute-start(bf16[128,1536]{1,0:T(8,128)(2,1)S(1)} %get-tuple-element.126.refs_2_), channel_id=1, source_target_pairs={{0,1},{1,0},{2,3},{3,2},{4,5},{5,4},{6,7},{7,6},{8,9},{9,8},{10,11... | collective-permute-start | bytes 1179656 | tf_op jit(solution)/shard_map/ppermute | solution.py:50
  227.6 10.2 %collective-permute-start.50 = (bf16[96,512]{1,0:T(8,128)(2,1)}, bf16[96,512]{1,0:T(8,128)(2,1)S(1)}, u32[]{:S(2)}, u32[]{:S(2)}) collective-permute-start(bf16[96,512]{1,0:T(8,128)(2,1)} %get-tuple-element.132), channel_id=1, source_target_pairs={{0,2},{2,0},{4,6},{6,4},{8,10},{10,8},{12,14},{14,12},{16,18},{18,... | collective-permute-start | bytes 294920 | tf_op jit(solution)/shard_map/ppermute | solution.py:46
  228.7 10.4 %collective-permute-start.51 = (bf16[96,512]{1,0:T(8,128)(2,1)}, bf16[96,512]{1,0:T(8,128)(2,1)S(1)}, u32[]{:S(2)}, u32[]{:S(2)}) collective-permute-start(bf16[96,512]{1,0:T(8,128)(2,1)} %get-tuple-element.133), channel_id=1, source_target_pairs={{0,4},{2,6},{4,0},{6,2},{8,12},{10,14},{12,8},{14,10},{16,20},{18,... | collective-permute-start | bytes 294920 | tf_op jit(solution)/shard_map/ppermute | solution.py:46
  (113 other events, 666.9 us)

commit v6 on v5

--- a/solution.py
+++ b/solution.py
@@ -959,13 +959,12 @@
     w_parts = [w_parts[0]] + [send(w_parts[s], shift_pairs(count, nz - s)) for s in range(1, nz)]
     h2_column = touch(h2_column, (h2_other, head_part))
     h2_other = touch(h2_other, (h2_column,))
-    g_blocks[-1] = touch(g_blocks[-1], (h2_column,))
     h2_rows = (h2_column, h2_other, swap_cores(h2_column), swap_cores(h2_other), h2)
     g_rows = (*g_blocks, *g_swapped, swap_cores(g_blocks[-1]), cotangent)
 
     tile = 512
     tiles = pl.cdiv(hidden, tile)
-    cut = (2 * tiles + 2) // 3
+    cut = (tiles + 1) // 2
 
     def bulk_part(chosen, begin, end, after):
         result = bulk_mlp(

time: 249 us -> 248 us (level)
    unnamed x170 -> x174, local copies, waits for them, and re-layouts: 19.9 us -> 19.1 us
  transfers between devices with their start and end apart: 60 -> 60, of which waited for: 20 -> 21; matrix products, arithmetic and copies ran while one was open for 2% -> 3% of each run, Pallas kernels for 52% -> 52%
where the time goes in v6:
time: 248 us; the launch traced here: 247 us
  Pallas kernels  137 us (55%)
  starting transfers between devices  54.5 us (22%)
  waiting for transfers between devices  27.7 us (11%)
  local copies, waits for them, and re-layouts  22.1 us (9%)
  other arithmetic  4.89 us (2%)
    pallas_call x2, Pallas kernels, bulk_mlp(): pl.pallas_call(ordered(body, len(after)), grid=(end - begin,), in_specs=[...  56.7 us
    ppermute x40, starting transfers between devices, send(): return lax.ppermute(value, 'ctx', pairs)  50.5 us
    pallas_call x3, Pallas kernels, hidden_call(): pl.pallas_call(ordered(body, len(after)), grid=(hidden // tile,), in_spec...  29.8 us
    pallas_call x13, Pallas kernels, kernel_call(): pl.pallas_call(ordered(body, len(after)), in_specs=[ANYWHERE] * len(after...  29.1 us
    ppermute x40, waiting for transfers between devices, send(): return lax.ppermute(value, 'ctx', pairs)  25.3 us
    unnamed x174, local copies, waits for them, and re-layouts  19.1 us
    pallas_call x1, Pallas kernels, attention_backward(): pl.pallas_call(ordered(attention_backward_kernel, len(after)), grid=(seqs...  9 us
    pallas_call x1, Pallas kernels, attention_forward(): pl.pallas_call(ordered(attention_forward_kernel, len(after)), grid=(seqs,...  6.5 us
  transfers between devices with their start and end apart: 60, of which 21 were waited for; matrix products, arithmetic and copies ran while one was open for 3% of the time, Pallas kernels for 52%

profile of v6, /device:TPU:0, one launch (start us, length us, event | category | flops | bytes accessed | tf_op | source)
XLA Modules:
  0.0 247.3 jit_solution(2975526969813437409)
XLA Ops:
  1.7 4.0 %collective-permute-start.2 = (bf16[64,1536]{1,0:T(8,128)(2,1)S(1)}, bf16[64,1536]{1,0:T(8,128)(2,1)S(1)}, u32[]{:S(2)}, u32[]{:S(2)}) collective-permute-start(bf16[64,1536]{1,0:T(8,128)(2,1)S(1)} %dynamic-slice_bitcast_fusion), channel_id=1, source_target_pairs={{0,6},{2,4},{4,2},{6,0},{8,14},{10,12},{12,10},{14,8},{16,22},{18,... | collective-permute-start | bytes 589832 | tf_op jit(solution)/shard_map/ppermute | solution.py:46
  11.7 3.1 %collective-permute-done.1.refs_3_ = bf16[64,1536]{1,0:T(8,128)(2,1)S(1)} collective-permute-done((bf16[64,1536]{1,0:T(8,128)(2,1)S(1)}, bf16[64,1536]{1,0:T(8,128)(2,1)S(1)}, u32[]{:S(2)}, u32[]{:S(2)}) %collective-permute-start.1) | collective-permute-done | bytes 196640 | tf_op jit(solution)/shard_map/ppermute | solution.py:46
  16.6 2.8 %query_key_value.1 = (bf16[2,4,64,1536]{3,2,1,0:T(8,128)(2,1)S(1)}, f32[512,384]{1,0:T(8,128)S(1)}, bf16[512,256]{1,0:T(8,128)(2,1)S(1)}, bf16[512,128]{1,0:T(8,128)(2,1)S(1)}, bf16[128,1536]{1,0:T(8,128)(2,1)S(1)}) custom-call(s32[2]{0:T(128)S(1)} %pad_add_fusion.refs_0_.refs_2_.refs_1_, bf16[2,64,1536]{2,1,0:T(8,128)(2,1)S(1)} %bitcast.16, ...), custom_call_target="tpu_custom_call" | custom-call | flops 6039797 | bytes 68224 | tf_op jit(solution)/shard_map/query_key_value/pallas_call | solution.py:88
  22.8 3.8 %collective-permute-start.8 = (bf16[512,128]{1,0:T(8,128)(2,1)S(1)}, bf16[512,128]{1,0:T(8,128)(2,1)S(1)}, u32[]{:S(2)}, u32[]{:S(2)}) collective-permute-start(bf16[512,128]{1,0:T(8,128)(2,1)S(1)} %get-tuple-element.85.refs_0_.refs_3_.refs_8_), channel_id=1, source_target_pairs={{0,24},{2,26},{4,28},{6,30},{8,0},{10,2},{12,4},{14,6},{16,8},{18,... | collective-permute-start | bytes 393224 | tf_op jit(solution)/shard_map/ppermute | solution.py:46
  27.6 6.8 %hidden_grad.1.refs_0_.refs_2_ = f32[128,3456]{1,0:T(8,128)} custom-call(bf16[512,128]{1,0:T(8,128)(2,1)} %copy-done.16, bf16[128,1536]{1,0:T(8,128)(2,1)} %refs_14_.3, bf16[1536,3456]{1,0:T(8,128)(2,1)} %refs_20_.3), custom_call_target="tpu_custom_call" | custom-call | flops 27179088 | bytes 127795 | tf_op jit(solution)/shard_map/hidden_grad/pallas_call | solution.py:397
  34.5 4.3 %collective-permute-done.7.refs_5_.refs_10_ = bf16[512,128]{1,0:T(8,128)(2,1)S(1)} collective-permute-done((bf16[512,128]{1,0:T(8,128)(2,1)S(1)}, bf16[512,128]{1,0:T(8,128)(2,1)S(1)}, u32[]{:S(2)}, u32[]{:S(2)}) %collective-permute-start.7) | collective-permute-done | bytes 131104 | tf_op jit(solution)/shard_map/ppermute | solution.py:46
  39.4 6.5 %attention_forward.1 = (bf16[2,64,192]{2,1,0:T(8,128)(2,1)}, bf16[2,64,192]{2,1,0:T(8,128)(2,1)}, bf16[2,64,192]{2,1,0:T(8,128)(2,1)}, bf16[2,64,192]{2,1,0:T(8,128)(2,1)}, f32[2,3,1,256]{3,2,1,0:T(1,128)}) custom-call(f32[128,3456]{1,0:T(8,128)} %hidden_grad.1.refs_0_.refs_2_, bf16[512,256]{1,0:T(8,128)(2,1)} %copy-done.17, f32[2,1024,256]{2,1,0:T(8,128)} %copy-done.2, ...), custom_call_target="tpu_custom_call" | custom-call | flops 12079595 | bytes 20971 | tf_op jit(solution)/shard_map/attention_forward/pallas_call | solution.py:302
  47.3 1.8 collective-permute-start.11
  50.8 2.1 collective-permute-done.11.refs_4_
  60.0 2.6 %middle.1 = (f32[128,1536]{1,0:T(8,128)}, bf16[128,1536]{1,0:T(8,128)(2,1)}, bf16[64,1536]{1,0:T(8,128)(2,1)}) custom-call(s32[2]{0:T(128)} %copy-done.32, bf16[128,1536]{1,0:T(8,128)(2,1)} %refs_0_.1, bf16[64,1536]{1,0:T(8,128)(2,1)} %copy-done.28, bf16[64,1536]{1,0:T(8,128)(2,1)} %copy-done.29, bf16[64,1536]{1,0:T(8,128)(2,1)} %copy-done.68, ...), custom_call_target="tpu_custom_call" | custom-call | bytes 25620 | tf_op jit(solution)/shard_map/middle/pallas_call | solution.py:88
  63.5 3.3 %collective-permute-start.20 = (bf16[64,1536]{1,0:T(8,128)(2,1)}, bf16[64,1536]{1,0:T(8,128)(2,1)S(1)}, u32[]{:S(2)}, u32[]{:S(2)}) collective-permute-start(bf16[64,1536]{1,0:T(8,128)(2,1)} %get-tuple-element.99.refs_1_), channel_id=1, source_target_pairs={{0,24},{2,26},{4,28},{6,30},{8,0},{10,2},{12,4},{14,6},{16,8},{18,... | collective-permute-start | bytes 589832 | tf_op jit(solution)/shard_map/ppermute | solution.py:46
  68.2 15.5 %own_mlp.1 = (bf16[64,1536]{1,0:T(8,128)(2,1)}, bf16[64,1536]{1,0:T(8,128)(2,1)}, bf16[128,3456]{1,0:T(8,128)(2,1)}, bf16[128,3456]{1,0:T(8,128)(2,1)}, bf16[128,3456]{1,0:T(8,128)(2,1)}) custom-call(bf16[128,1536]{1,0:T(8,128)(2,1)} %copy-done.56, bf16[128,1536]{1,0:T(8,128)(2,1)} %get-tuple-element.97.refs_1_.refs_6_.refs_5_, ...), custom_call_target="tpu_custom_call" | custom-call | flops 108716360 | bytes 264437 | tf_op jit(solution)/shard_map/own_mlp/pallas_call | solution.py:397
  84.2 2.8 %collective-permute-start.17 = (bf16[128,1536]{1,0:T(8,128)(2,1)}, bf16[128,1536]{1,0:T(8,128)(2,1)S(1)}, u32[]{:S(2)}, u32[]{:S(2)}) collective-permute-start(bf16[128,1536]{1,0:T(8,128)(2,1)} %touch.15.refs_8_.refs_7_), channel_id=1, source_target_pairs={{0,8},{2,10},{4,12},{6,14},{8,16},{10,18},{12,20},{14,22},{16,24},... | collective-permute-start | bytes 1179656 | tf_op jit(solution)/shard_map/ppermute | solution.py:46
  88.4 2.1 pack.1.refs_0_
  91.3 4.0 %back.1 = (f32[128,1536]{1,0:T(8,128)}, bf16[128,1536]{1,0:T(8,128)(2,1)}, bf16[64,1536]{1,0:T(8,128)(2,1)}, f32[1,1536]{1,0:T(1,128)}, bf16[128,192]{1,0:T(8,12...) custom-call(bf16[256,1536]{1,0:T(8,128)(2,1)} %pack.1.refs_0_, ...), custom_call_target="tpu_custom_call" | custom-call | flops 3019898 | bytes 59105 | tf_op jit(solution)/shard_map/back/pallas_call | solution.py:88
  95.8 1.9 collective-permute-start.25
  100.3 2.8 %collective-permute-done.26 = bf16[128,192]{1,0:T(8,128)(2,1)S(1)} collective-permute-done((bf16[128,192]{1,0:T(8,128)(2,1)}, bf16[128,192]{1,0:T(8,128)(2,1)S(1)}, u32[]{:S(2)}, u32[]{:S(2)}) %collective-permute-start.26) | collective-permute-done | bytes 49184 | tf_op jit(solution)/shard_map/ppermute | solution.py:46
  105.6 1.6 collective-permute-start.27
  108.0 9.0 %attention_backward.1 = (f32[512,256]{1,0:T(8,128)}, bf16[512,128]{1,0:T(8,128)(2,1)}, bf16[512,128]{1,0:T(8,128)(2,1)}, bf16[512,128]{1,0:T(8,128)(2,1)}, bf16[512,128]{1,0:T(8,128)(2,1)}) custom-call(bf16[128,1536]{1,0:T(8,128)(2,1)} %copy-done.43, bf16[512,256]{1,0:T(8,128)(2,1)} %copy-done.17, f32[2,1024,256]{2,1,0:T(8,128)} %copy-done.2, ...), custom_call_target="tpu_custom_call" | custom-call | flops 20132660 | bytes 20971 | tf_op jit(solution)/shard_map/attention_backward/pallas_call | solution.py:325
  122.4 7.5 %down.1.refs_0_ = bf16[128,1536]{1,0:T(8,128)(2,1)} custom-call(f32[512,256]{1,0:T(8,128)} %get-tuple-element.106.refs_0_.refs_1_.refs_2_, bf16[128,3456]{1,0:T(8,128)(2,1)} %get-tuple-element.98.refs_1_.refs_0_.refs_16_.refs_15_, bf16[1536,3456]{1,0:T(8,128)(2,1)} %refs_20_.3), custom_call_target="tpu_custom_call" | custom-call | flops 27179088 | bytes 118947 | tf_op jit(solution)/shard_map/down/pallas_call | solution.py:397
  133.5 6.1 %head_grad.1 = (f32[1,384]{1,0:T(1,128)}, bf16[128,384]{1,0:T(8,128)(2,1)}, bf16[128,384]{1,0:T(8,128)(2,1)}, bf16[128,384]{1,0:T(8,128)(2,1)}, bf16[128,384]{1,...) custom-call(bf16[128,1536]{1,0:T(8,128)(2,1)} %down.1.refs_0_, ...), custom_call_target="tpu_custom_call" | custom-call | flops 9059696 | bytes 76697 | tf_op jit(solution)/shard_map/head_grad/pallas_call | solution.py:88
  144.5 1.6 collective-permute-start.44
  149.7 31.9 %bulk_mlp.2 = (f32[96,2048]{1,0:T(8,128)}, f32[96,2048]{1,0:T(8,128)}, f32[96,2048]{1,0:T(8,128)}, bf16[3,96,2048]{2,1,0:T(8,128)(2,1)}, bf16[192,1024]{1,0:T(8,128)(2,1)}, /*index=5*/bf16[192,1024]{1,0:T(8,128)(2,1)}) custom-call(f32[1,384]{1,0:T(1,128)} %get-tuple-element.115.refs_2_.refs_0_, s32[2]{0:T(128)} %copy-done.32, ...), custom_call_target="tpu_custom_call" | custom-call | flops 21743271936 | bytes 25165824 | tf_op jit(solution)/shard_map/bulk_mlp/pallas_call | solution.py:691
  181.6 2.2 collective-permute-start.49
  185.5 24.9 %bulk_mlp.3 = (f32[96,1408]{1,0:T(8,128)}, f32[96,1408]{1,0:T(8,128)}, f32[96,1408]{1,0:T(8,128)}, bf16[3,96,1408]{2,1,0:T(8,128)(2,1)}) custom-call(s32[2]{0:T(128)} %copy-done.32, bf16[256,1536]{1,0:T(8,128)(2,1)} %touch.18.refs_1_.refs_2_, bf16[256,1536]{1,0:T(8,128)(2,1)} %touch.19.refs_3_.refs_2_, bf16[256,1536]{1,0:T(8,128)(2,1)} %copy-done.80, ...), custom_call_target="tpu_custom_call" | custom-call | flops 14948499456 | bytes 19267584 | tf_op jit(solution)/shard_map/bulk_mlp/pallas_call | solution.py:691
  212.8 2.0 input_grad.1
  218.6 2.5 %spread.1 = (f32[96,512]{1,0:T(8,128)}, bf16[96,512]{1,0:T(8,128)(2,1)}, bf16[96,512]{1,0:T(8,128)(2,1)}, bf16[96,512]{1,0:T(8,128)(2,1)}) custom-call(f32[96,1408]{1,0:T(8,128)} %get-tuple-element.120.refs_1_.refs_0_.refs_3_, s32[2]{0:T(128)} %copy-done.32, bf16[384,512]{1,0:T(8,128)(2,1)} %get-tuple-element.127.refs_2_, bf16[384,512]{1,0:T(8,128)(2,1)} %copy-done.52, ...), custom_call_target="tpu_custom_call" | custom-call | bytes 20643 | tf_op jit(solution)/shard_map/spread/pallas_call | solution.py:88
  222.5 3.4 %collective-permute-done.57 = f32[3456]{0:T(1024)S(1)} collective-permute-done((f32[3456]{0:T(1024)}, f32[3456]{0:T(1024)S(1)}, u32[]{:S(2)}, u32[]{:S(2)}) %collective-permute-start.57) | collective-permute-done | bytes 13856 | tf_op jit(solution)/shard_map/ppermute | solution.py:46
  231.3 1.9 collective-permute-done.58
  233.2 1.7 collective-permute-start.52
  237.2 1.7 collective-permute-done.52.refs_4_
  241.9 5.4 %bulk_finish.1 = (f32[96,3456]{1,0:T(8,128)}, f32[96,3456]{1,0:T(8,128)}, f32[96,3456]{1,0:T(8,128)}) custom-call(f32[96,2048]{1,0:T(8,128)} %get-tuple-element.139.refs_0_, f32[96,2048]{1,0:T(8,128)} %get-tuple-element.140.refs_1_, f32[96,2048]{1,0:T(8,128)} %get-tuple-element.141.refs_2_, f32[96,1408]{1,0:T(8,128)} %get-tuple-element.120.refs_1_.refs_0_.refs_3_, ...), custom_call_target="tpu_custom_call" | custom-call | flops 3317 | bytes 99532 | tf_op jit(solution)/shard_map/bulk_finish/pallas_call | solution.py:738
  (310 shorter events, 72.2 us)
Async XLA Ops:
  1.7 10.0 %collective-permute-start.2 = (bf16[64,1536]{1,0:T(8,128)(2,1)S(1)}, bf16[64,1536]{1,0:T(8,128)(2,1)S(1)}, u32[]{:S(2)}, u32[]{:S(2)}) collective-permute-start(bf16[64,1536]{1,0:T(8,128)(2,1)S(1)} %dynamic-slice_bitcast_fusion), channel_id=1, source_target_pairs={{0,6},{2,4},{4,2},{6,0},{8,14},{10,12},{12,10},{14,8},{16,22},{18,... | collective-permute-start | bytes 589832 | tf_op jit(solution)/shard_map/ppermute | solution.py:46
  5.7 9.1 %collective-permute-start.1 = (bf16[64,1536]{1,0:T(8,128)(2,1)S(1)}, bf16[64,1536]{1,0:T(8,128)(2,1)S(1)}, u32[]{:S(2)}, u32[]{:S(2)}) collective-permute-start(bf16[64,1536]{1,0:T(8,128)(2,1)S(1)} %dynamic-slice_bitcast_fusion), channel_id=1, source_target_pairs={{0,4},{2,6},{4,0},{6,2},{8,12},{10,14},{12,8},{14,10},{16,20},{18,... | collective-permute-start | bytes 589832 | tf_op jit(solution)/shard_map/ppermute | solution.py:46
  22.1 23.8 %collective-permute-start.14 = (bf16[128,1536]{1,0:T(8,128)(2,1)S(1)}, bf16[128,1536]{1,0:T(8,128)(2,1)S(1)}, u32[]{:S(2)}, u32[]{:S(2)}) collective-permute-start(bf16[128,1536]{1,0:T(8,128)(2,1)S(1)} %get-tuple-element.95), channel_id=1, source_target_pairs={{0,0},{1,5},{2,2},{3,7},{4,4},{5,1},{6,6},{7,3},{8,8},{9,13},{10,1... | collective-permute-start | bytes 1179656 | tf_op jit(solution)/shard_map/ppermute | solution.py:859
  22.8 11.7 %collective-permute-start.8 = (bf16[512,128]{1,0:T(8,128)(2,1)S(1)}, bf16[512,128]{1,0:T(8,128)(2,1)S(1)}, u32[]{:S(2)}, u32[]{:S(2)}) collective-permute-start(bf16[512,128]{1,0:T(8,128)(2,1)S(1)} %get-tuple-element.85.refs_0_.refs_3_.refs_8_), channel_id=1, source_target_pairs={{0,24},{2,26},{4,28},{6,30},{8,0},{10,2},{12,4},{14,6},{16,8},{18,... | collective-permute-start | bytes 393224 | tf_op jit(solution)/shard_map/ppermute | solution.py:46
  26.6 12.1 %collective-permute-start.7 = (bf16[512,128]{1,0:T(8,128)(2,1)S(1)}, bf16[512,128]{1,0:T(8,128)(2,1)S(1)}, u32[]{:S(2)}, u32[]{:S(2)}) collective-permute-start(bf16[512,128]{1,0:T(8,128)(2,1)S(1)} %get-tuple-element.85.refs_0_.refs_3_.refs_8_), channel_id=1, source_target_pairs={{0,16},{2,18},{4,20},{6,22},{8,24},{10,26},{12,28},{14,30},{16,0},... | collective-permute-start | bytes 393224 | tf_op jit(solution)/shard_map/ppermute | solution.py:46
  26.6 12.1 %collective-permute-start.6 = (bf16[512,128]{1,0:T(8,128)(2,1)S(1)}, bf16[512,128]{1,0:T(8,128)(2,1)S(1)}, u32[]{:S(2)}, u32[]{:S(2)}) collective-permute-start(bf16[512,128]{1,0:T(8,128)(2,1)S(1)} %get-tuple-element.85.refs_0_.refs_3_.refs_8_), channel_id=1, source_target_pairs={{0,8},{2,10},{4,12},{6,14},{8,16},{10,18},{12,20},{14,22},{16,24},... | collective-permute-start | bytes 393224 | tf_op jit(solution)/shard_map/ppermute | solution.py:46
  46.7 15.9 %collective-permute-start.15 = (bf16[128,1536]{1,0:T(8,128)(2,1)}, bf16[128,1536]{1,0:T(8,128)(2,1)S(1)}, u32[]{:S(2)}, u32[]{:S(2)}) collective-permute-start(bf16[128,1536]{1,0:T(8,128)(2,1)} %touch.13.refs_7_.refs_6_), channel_id=1, source_target_pairs={{0,8},{2,10},{4,12},{6,14},{8,16},{10,18},{12,20},{14,22},{16,24},... | collective-permute-start | bytes 1179656 | tf_op jit(solution)/shard_map/ppermute | solution.py:46
  57.7 9.7 %collective-permute-start.16 = (bf16[128,1536]{1,0:T(8,128)(2,1)S(1)}, bf16[128,1536]{1,0:T(8,128)(2,1)S(1)}, u32[]{:S(2)}, u32[]{:S(2)}) collective-permute-start(bf16[128,1536]{1,0:T(8,128)(2,1)S(1)} %copy-done.55), channel_id=1, source_target_pairs={{0,1},{1,0},{2,3},{3,2},{4,5},{5,4},{6,7},{7,6},{8,9},{9,8},{10,11... | collective-permute-start | bytes 1179656 | tf_op jit(solution)/shard_map/ppermute | solution.py:50
  63.3 20.4 %collective-permute-start.21 = (bf16[128,1536]{1,0:T(8,128)(2,1)}, bf16[128,1536]{1,0:T(8,128)(2,1)S(1)}, u32[]{:S(2)}, u32[]{:S(2)}) collective-permute-start(bf16[128,1536]{1,0:T(8,128)(2,1)} %touch.14.refs_0_), channel_id=1, source_target_pairs={{0,1},{1,0},{2,3},{3,2},{4,5},{5,4},{6,7},{7,6},{8,9},{9,8},{10,11... | collective-permute-start | bytes 1179656 | tf_op jit(solution)/shard_map/ppermute | solution.py:50
  63.5 20.8 %collective-permute-start.20 = (bf16[64,1536]{1,0:T(8,128)(2,1)}, bf16[64,1536]{1,0:T(8,128)(2,1)S(1)}, u32[]{:S(2)}, u32[]{:S(2)}) collective-permute-start(bf16[64,1536]{1,0:T(8,128)(2,1)} %get-tuple-element.99.refs_1_), channel_id=1, source_target_pairs={{0,24},{2,26},{4,28},{6,30},{8,0},{10,2},{12,4},{14,6},{16,8},{18,... | collective-permute-start | bytes 589832 | tf_op jit(solution)/shard_map/ppermute | solution.py:46
  66.7 20.3 %collective-permute-start.19 = (bf16[64,1536]{1,0:T(8,128)(2,1)}, bf16[64,1536]{1,0:T(8,128)(2,1)S(1)}, u32[]{:S(2)}, u32[]{:S(2)}) collective-permute-start(bf16[64,1536]{1,0:T(8,128)(2,1)} %get-tuple-element.99.refs_1_), channel_id=1, source_target_pairs={{0,16},{2,18},{4,20},{6,22},{8,24},{10,26},{12,28},{14,30},{16,0},... | collective-permute-start | bytes 589832 | tf_op jit(solution)/shard_map/ppermute | solution.py:46
  67.4 19.6 %collective-permute-start.18 = (bf16[64,1536]{1,0:T(8,128)(2,1)}, bf16[64,1536]{1,0:T(8,128)(2,1)S(1)}, u32[]{:S(2)}, u32[]{:S(2)}) collective-permute-start(bf16[64,1536]{1,0:T(8,128)(2,1)} %get-tuple-element.99.refs_1_), channel_id=1, source_target_pairs={{0,8},{2,10},{4,12},{6,14},{8,16},{10,18},{12,20},{14,22},{16,24},... | collective-permute-start | bytes 589832 | tf_op jit(solution)/shard_map/ppermute | solution.py:46
  84.2 23.0 %collective-permute-start.17 = (bf16[128,1536]{1,0:T(8,128)(2,1)}, bf16[128,1536]{1,0:T(8,128)(2,1)S(1)}, u32[]{:S(2)}, u32[]{:S(2)}) collective-permute-start(bf16[128,1536]{1,0:T(8,128)(2,1)} %touch.15.refs_8_.refs_7_), channel_id=1, source_target_pairs={{0,8},{2,10},{4,12},{6,14},{8,16},{10,18},{12,20},{14,22},{16,24},... | collective-permute-start | bytes 1179656 | tf_op jit(solution)/shard_map/ppermute | solution.py:46
  103.7 13.3 %collective-permute-start.29 = (bf16[64,1536]{1,0:T(8,128)(2,1)}, bf16[64,1536]{1,0:T(8,128)(2,1)S(1)}, u32[]{:S(2)}, u32[]{:S(2)}) collective-permute-start(bf16[64,1536]{1,0:T(8,128)(2,1)} %touch.16), channel_id=1, source_target_pairs={{0,6},{2,4},{4,2},{6,0},{8,14},{10,12},{12,10},{14,8},{16,22},{18,... | collective-permute-start | bytes 589832 | tf_op jit(solution)/shard_map/ppermute | solution.py:46
  104.9 12.2 %collective-permute-start.28 = (bf16[64,1536]{1,0:T(8,128)(2,1)}, bf16[64,1536]{1,0:T(8,128)(2,1)S(1)}, u32[]{:S(2)}, u32[]{:S(2)}) collective-permute-start(bf16[64,1536]{1,0:T(8,128)(2,1)} %touch.16), channel_id=1, source_target_pairs={{0,4},{2,6},{4,0},{6,2},{8,12},{10,14},{12,8},{14,10},{16,20},{18,... | collective-permute-start | bytes 589832 | tf_op jit(solution)/shard_map/ppermute | solution.py:46
  105.6 11.4 %collective-permute-start.27 = (bf16[64,1536]{1,0:T(8,128)(2,1)}, bf16[64,1536]{1,0:T(8,128)(2,1)S(1)}, u32[]{:S(2)}, u32[]{:S(2)}) collective-permute-start(bf16[64,1536]{1,0:T(8,128)(2,1)} %touch.16), channel_id=1, source_target_pairs={{0,2},{2,0},{4,6},{6,4},{8,10},{10,8},{12,14},{14,12},{16,18},{18,... | collective-permute-start | bytes 589832 | tf_op jit(solution)/shard_map/ppermute | solution.py:46
  117.8 21.8 %collective-permute-start.30 = (bf16[256,1536]{1,0:T(8,128)(2,1)}, bf16[256,1536]{1,0:T(8,128)(2,1)S(1)}, u32[]{:S(2)}, u32[]{:S(2)}) collective-permute-start(bf16[256,1536]{1,0:T(8,128)(2,1)} %touch.17.refs_0_), channel_id=1, source_target_pairs={{0,4},{2,6},{4,0},{6,2},{8,12},{10,14},{12,8},{14,10},{16,20},{18,... | collective-permute-start | bytes 2359304 | tf_op jit(solution)/shard_map/ppermute | solution.py:46
  118.6 11.3 %collective-permute-start.31 = (bf16[64,1536]{1,0:T(8,128)(2,1)}, bf16[64,1536]{1,0:T(8,128)(2,1)S(1)}, u32[]{:S(2)}, u32[]{:S(2)}) collective-permute-start(bf16[64,1536]{1,0:T(8,128)(2,1)} %copy-done.47), channel_id=1, source_target_pairs={{0,1},{1,0},{2,3},{3,2},{4,5},{5,4},{6,7},{7,6},{8,9},{9,8},{10,11... | collective-permute-start | bytes 589832 | tf_op jit(solution)/shard_map/ppermute | solution.py:50
  118.6 12.8 %collective-permute-start.34 = (bf16[512,128]{1,0:T(8,128)(2,1)S(1)}, bf16[512,128]{1,0:T(8,128)(2,1)S(1)}, u32[]{:S(2)}, u32[]{:S(2)}) collective-permute-start(bf16[512,128]{1,0:T(8,128)(2,1)S(1)} %copy-done.86), channel_id=1, source_target_pairs={{0,24},{2,26},{4,28},{6,30},{8,0},{10,2},{12,4},{14,6},{16,8},{18,... | collective-permute-start | bytes 393224 | tf_op jit(solution)/shard_map/ppermute | solution.py:46
  120.0 12.9 %collective-permute-start.35 = (bf16[512,128]{1,0:T(8,128)(2,1)S(1)}, bf16[512,128]{1,0:T(8,128)(2,1)S(1)}, u32[]{:S(2)}, u32[]{:S(2)}) collective-permute-start(bf16[512,128]{1,0:T(8,128)(2,1)S(1)} %copy-done.85), channel_id=1, source_target_pairs={{0,16},{2,18},{4,20},{6,22},{8,24},{10,26},{12,28},{14,30},{16,0},... | collective-permute-start | bytes 393224 | tf_op jit(solution)/shard_map/ppermute | solution.py:46
  121.4 11.4 %collective-permute-start.36 = (bf16[512,128]{1,0:T(8,128)(2,1)S(1)}, bf16[512,128]{1,0:T(8,128)(2,1)S(1)}, u32[]{:S(2)}, u32[]{:S(2)}) collective-permute-start(bf16[512,128]{1,0:T(8,128)(2,1)S(1)} %copy-done.84), channel_id=1, source_target_pairs={{0,8},{2,10},{4,12},{6,14},{8,16},{10,18},{12,20},{14,22},{16,24},... | collective-permute-start | bytes 393224 | tf_op jit(solution)/shard_map/ppermute | solution.py:46
  129.9 12.8 %collective-permute-start.39 = (bf16[128,1536]{1,0:T(8,128)(2,1)S(1)}, bf16[128,1536]{1,0:T(8,128)(2,1)S(1)}, u32[]{:S(2)}, u32[]{:S(2)}) collective-permute-start(bf16[128,1536]{1,0:T(8,128)(2,1)S(1)} %copy-done.44), channel_id=1, source_target_pairs={{0,8},{2,10},{4,12},{6,14},{8,16},{10,18},{12,20},{14,22},{16,24},... | collective-permute-start | bytes 1179656 | tf_op jit(solution)/shard_map/ppermute | solution.py:46
  142.7 39.0 %collective-permute-start.43 = (bf16[128,384]{1,0:T(8,128)(2,1)}, bf16[128,384]{1,0:T(8,128)(2,1)S(1)}, u32[]{:S(2)}, u32[]{:S(2)}) collective-permute-start(bf16[128,384]{1,0:T(8,128)(2,1)} %get-tuple-element.123), channel_id=1, source_target_pairs={{0,2},{2,0},{4,6},{6,4},{8,10},{10,8},{12,14},{14,12},{16,18},{18,... | collective-permute-start | bytes 294920 | tf_op jit(solution)/shard_map/ppermute | solution.py:46
  144.5 39.4 %collective-permute-start.44 = (bf16[128,384]{1,0:T(8,128)(2,1)}, bf16[128,384]{1,0:T(8,128)(2,1)S(1)}, u32[]{:S(2)}, u32[]{:S(2)}) collective-permute-start(bf16[128,384]{1,0:T(8,128)(2,1)} %get-tuple-element.124), channel_id=1, source_target_pairs={{0,4},{2,6},{4,0},{6,2},{8,12},{10,14},{12,8},{14,10},{16,20},{18,... | collective-permute-start | bytes 294920 | tf_op jit(solution)/shard_map/ppermute | solution.py:46
  146.1 37.8 %collective-permute-start.45 = (bf16[128,384]{1,0:T(8,128)(2,1)}, bf16[128,384]{1,0:T(8,128)(2,1)S(1)}, u32[]{:S(2)}, u32[]{:S(2)}) collective-permute-start(bf16[128,384]{1,0:T(8,128)(2,1)} %get-tuple-element.125), channel_id=1, source_target_pairs={{0,6},{2,4},{4,2},{6,0},{8,14},{10,12},{12,10},{14,8},{16,22},{18,... | collective-permute-start | bytes 294920 | tf_op jit(solution)/shard_map/ppermute | solution.py:46
  147.4 67.4 %collective-permute-start.47 = (bf16[384,512]{1,0:T(8,128)(2,1)}, bf16[384,512]{1,0:T(8,128)(2,1)S(1)}, u32[]{:S(2)}, u32[]{:S(2)}) collective-permute-start(bf16[384,512]{1,0:T(8,128)(2,1)} %get-tuple-element.128), channel_id=1, source_target_pairs={{0,24},{2,26},{4,28},{6,30},{8,0},{10,2},{12,4},{14,6},{16,8},{18,... | collective-permute-start | bytes 1179656 | tf_op jit(solution)/shard_map/ppermute | solution.py:46
  148.7 66.3 %collective-permute-start.48 = (bf16[384,512]{1,0:T(8,128)(2,1)}, bf16[384,512]{1,0:T(8,128)(2,1)S(1)}, u32[]{:S(2)}, u32[]{:S(2)}) collective-permute-start(bf16[384,512]{1,0:T(8,128)(2,1)} %get-tuple-element.129), channel_id=1, source_target_pairs={{0,16},{2,18},{4,20},{6,22},{8,24},{10,26},{12,28},{14,30},{16,0},... | collective-permute-start | bytes 1179656 | tf_op jit(solution)/shard_map/ppermute | solution.py:46
  181.6 36.0 %collective-permute-start.49 = (bf16[384,512]{1,0:T(8,128)(2,1)}, bf16[384,512]{1,0:T(8,128)(2,1)}, u32[]{:S(2)}, u32[]{:S(2)}) collective-permute-start(bf16[384,512]{1,0:T(8,128)(2,1)} %get-tuple-element.130), channel_id=1, source_target_pairs={{0,8},{2,10},{4,12},{6,14},{8,16},{10,18},{12,20},{14,22},{16,24},... | collective-permute-start | bytes 1179656 | tf_op jit(solution)/shard_map/ppermute | solution.py:46
  184.6 57.3 %collective-permute-start.53 = (bf16[3,96,2048]{2,1,0:T(8,128)(2,1)}, bf16[3,96,2048]{2,1,0:T(8,128)(2,1)}, u32[]{:S(2)}, u32[]{:S(2)}) collective-permute-start(bf16[3,96,2048]{2,1,0:T(8,128)(2,1)} %touch.22), channel_id=1, source_target_pairs={{0,2},{2,0},{4,6},{6,4},{8,10},{10,8},{12,14},{14,12},{16,18},{18,... | collective-permute-start | bytes 3538952 | tf_op jit(solution)/shard_map/ppermute | solution.py:46
  210.4 31.5 %collective-permute-start.54 = (bf16[3,96,1408]{2,1,0:T(8,128)(2,1)}, bf16[3,96,1408]{2,1,0:T(8,128)(2,1)}, u32[]{:S(2)}, u32[]{:S(2)}) collective-permute-start(bf16[3,96,1408]{2,1,0:T(8,128)(2,1)} %get-tuple-element.145), channel_id=1, source_target_pairs={{0,2},{2,0},{4,6},{6,4},{8,10},{10,8},{12,14},{14,12},{16,18},{18,... | collective-permute-start | bytes 2433032 | tf_op jit(solution)/shard_map/ppermute | solution.py:46
  215.0 12.3 %collective-permute-start.42 = (bf16[128,1536]{1,0:T(8,128)(2,1)}, bf16[128,1536]{1,0:T(8,128)(2,1)S(1)}, u32[]{:S(2)}, u32[]{:S(2)}) collective-permute-start(bf16[128,1536]{1,0:T(8,128)(2,1)} %touch.21.refs_1_), channel_id=1, source_target_pairs={{0,1},{1,0},{2,3},{3,2},{4,5},{5,4},{6,7},{7,6},{8,9},{9,8},{10,11... | collective-permute-start | bytes 1179656 | tf_op jit(solution)/shard_map/ppermute | solution.py:50
  216.7 13.4 %collective-permute-start.46 = (bf16[128,1536]{1,0:T(8,128)(2,1)S(1)}, bf16[128,1536]{1,0:T(8,128)(2,1)S(1)}, u32[]{:S(2)}, u32[]{:S(2)}) collective-permute-start(bf16[128,1536]{1,0:T(8,128)(2,1)S(1)} %get-tuple-element.126.refs_2_), channel_id=1, source_target_pairs={{0,1},{1,0},{2,3},{3,2},{4,5},{5,4},{6,7},{7,6},{8,9},{9,8},{10,11... | collective-permute-start | bytes 1179656 | tf_op jit(solution)/shard_map/ppermute | solution.py:50
  (115 other events, 730.0 us)

commit v7 on v6

--- a/solution.py
+++ b/solution.py
@@ -727,7 +727,7 @@
     rows, first_hidden = first[0].shape
     second_hidden = second[0].shape[1]
     hidden = first_hidden + second_hidden
-    block = rows // 3 if rows % 48 == 0 else rows
+    block = rows // 6 if rows % 96 == 0 else rows
 
     def spec(columns):
         return pl.BlockSpec((block, columns), lambda i: (i, 0))

time: 248 us -> 249 us (level)
  no operation moved by 1% of the time
where the time goes in v7:
time: 249 us; the launch traced here: 248 us
  Pallas kernels  137 us (55%)
  starting transfers between devices  54.5 us (22%)
  waiting for transfers between devices  27.7 us (11%)
  local copies, waits for them, and re-layouts  22.1 us (9%)
  other arithmetic  4.89 us (2%)
    pallas_call x2, Pallas kernels, bulk_mlp(): pl.pallas_call(ordered(body, len(after)), grid=(end - begin,), in_specs=[...  56.7 us
    ppermute x40, starting transfers between devices, send(): return lax.ppermute(value, 'ctx', pairs)  50.5 us
    pallas_call x3, Pallas kernels, hidden_call(): pl.pallas_call(ordered(body, len(after)), grid=(hidden // tile,), in_spec...  29.8 us
    pallas_call x13, Pallas kernels, kernel_call(): pl.pallas_call(ordered(body, len(after)), in_specs=[ANYWHERE] * len(after...  29.1 us
    ppermute x40, waiting for transfers between devices, send(): return lax.ppermute(value, 'ctx', pairs)  25.3 us
    unnamed x174, local copies, waits for them, and re-layouts  19.1 us
    pallas_call x1, Pallas kernels, attention_backward(): pl.pallas_call(ordered(attention_backward_kernel, len(after)), grid=(seqs...  9 us
    pallas_call x1, Pallas kernels, attention_forward(): pl.pallas_call(ordered(attention_forward_kernel, len(after)), grid=(seqs,...  6.5 us
  transfers between devices with their start and end apart: 60, of which 21 were waited for; matrix products, arithmetic and copies ran while one was open for 3% of the time, Pallas kernels for 52%

profile of v7, /device:TPU:0, one launch (start us, length us, event | category | flops | bytes accessed | tf_op | source)
XLA Modules:
  0.0 248.1 jit_solution(423754860134962258)
XLA Ops:
  1.7 4.0 %collective-permute-start.2 = (bf16[64,1536]{1,0:T(8,128)(2,1)S(1)}, bf16[64,1536]{1,0:T(8,128)(2,1)S(1)}, u32[]{:S(2)}, u32[]{:S(2)}) collective-permute-start(bf16[64,1536]{1,0:T(8,128)(2,1)S(1)} %dynamic-slice_bitcast_fusion), channel_id=1, source_target_pairs={{0,6},{2,4},{4,2},{6,0},{8,14},{10,12},{12,10},{14,8},{16,22},{18,... | collective-permute-start | bytes 589832 | tf_op jit(solution)/shard_map/ppermute | solution.py:46
  11.7 3.1 %collective-permute-done.1.refs_3_ = bf16[64,1536]{1,0:T(8,128)(2,1)S(1)} collective-permute-done((bf16[64,1536]{1,0:T(8,128)(2,1)S(1)}, bf16[64,1536]{1,0:T(8,128)(2,1)S(1)}, u32[]{:S(2)}, u32[]{:S(2)}) %collective-permute-start.1) | collective-permute-done | bytes 196640 | tf_op jit(solution)/shard_map/ppermute | solution.py:46
  16.6 2.8 %query_key_value.1 = (bf16[2,4,64,1536]{3,2,1,0:T(8,128)(2,1)S(1)}, f32[512,384]{1,0:T(8,128)S(1)}, bf16[512,256]{1,0:T(8,128)(2,1)S(1)}, bf16[512,128]{1,0:T(8,128)(2,1)S(1)}, bf16[128,1536]{1,0:T(8,128)(2,1)S(1)}) custom-call(s32[2]{0:T(128)S(1)} %pad_add_fusion.refs_0_.refs_2_.refs_1_, bf16[2,64,1536]{2,1,0:T(8,128)(2,1)S(1)} %bitcast.16, ...), custom_call_target="tpu_custom_call" | custom-call | flops 6039797 | bytes 68224 | tf_op jit(solution)/shard_map/query_key_value/pallas_call | solution.py:88
  22.8 3.8 %collective-permute-start.8 = (bf16[512,128]{1,0:T(8,128)(2,1)S(1)}, bf16[512,128]{1,0:T(8,128)(2,1)S(1)}, u32[]{:S(2)}, u32[]{:S(2)}) collective-permute-start(bf16[512,128]{1,0:T(8,128)(2,1)S(1)} %get-tuple-element.85.refs_0_.refs_3_.refs_8_), channel_id=1, source_target_pairs={{0,24},{2,26},{4,28},{6,30},{8,0},{10,2},{12,4},{14,6},{16,8},{18,... | collective-permute-start | bytes 393224 | tf_op jit(solution)/shard_map/ppermute | solution.py:46
  27.6 6.8 %hidden_grad.1.refs_0_.refs_2_ = f32[128,3456]{1,0:T(8,128)} custom-call(bf16[512,128]{1,0:T(8,128)(2,1)} %copy-done.16, bf16[128,1536]{1,0:T(8,128)(2,1)} %refs_14_.3, bf16[1536,3456]{1,0:T(8,128)(2,1)} %refs_20_.3), custom_call_target="tpu_custom_call" | custom-call | flops 27179088 | bytes 127795 | tf_op jit(solution)/shard_map/hidden_grad/pallas_call | solution.py:397
  34.5 4.3 %collective-permute-done.7.refs_5_.refs_10_ = bf16[512,128]{1,0:T(8,128)(2,1)S(1)} collective-permute-done((bf16[512,128]{1,0:T(8,128)(2,1)S(1)}, bf16[512,128]{1,0:T(8,128)(2,1)S(1)}, u32[]{:S(2)}, u32[]{:S(2)}) %collective-permute-start.7) | collective-permute-done | bytes 131104 | tf_op jit(solution)/shard_map/ppermute | solution.py:46
  39.4 6.5 %attention_forward.1 = (bf16[2,64,192]{2,1,0:T(8,128)(2,1)}, bf16[2,64,192]{2,1,0:T(8,128)(2,1)}, bf16[2,64,192]{2,1,0:T(8,128)(2,1)}, bf16[2,64,192]{2,1,0:T(8,128)(2,1)}, f32[2,3,1,256]{3,2,1,0:T(1,128)}) custom-call(f32[128,3456]{1,0:T(8,128)} %hidden_grad.1.refs_0_.refs_2_, bf16[512,256]{1,0:T(8,128)(2,1)} %copy-done.17, f32[2,1024,256]{2,1,0:T(8,128)} %copy-done.2, ...), custom_call_target="tpu_custom_call" | custom-call | flops 12079595 | bytes 20971 | tf_op jit(solution)/shard_map/attention_forward/pallas_call | solution.py:302
  47.3 1.8 collective-permute-start.11
  50.8 2.1 collective-permute-done.11.refs_4_
  60.0 2.6 %middle.1 = (f32[128,1536]{1,0:T(8,128)}, bf16[128,1536]{1,0:T(8,128)(2,1)}, bf16[64,1536]{1,0:T(8,128)(2,1)}) custom-call(s32[2]{0:T(128)} %copy-done.32, bf16[128,1536]{1,0:T(8,128)(2,1)} %refs_0_.1, bf16[64,1536]{1,0:T(8,128)(2,1)} %copy-done.28, bf16[64,1536]{1,0:T(8,128)(2,1)} %copy-done.29, bf16[64,1536]{1,0:T(8,128)(2,1)} %copy-done.68, ...), custom_call_target="tpu_custom_call" | custom-call | bytes 25620 | tf_op jit(solution)/shard_map/middle/pallas_call | solution.py:88
  63.5 3.3 %collective-permute-start.20 = (bf16[64,1536]{1,0:T(8,128)(2,1)}, bf16[64,1536]{1,0:T(8,128)(2,1)S(1)}, u32[]{:S(2)}, u32[]{:S(2)}) collective-permute-start(bf16[64,1536]{1,0:T(8,128)(2,1)} %get-tuple-element.99.refs_1_), channel_id=1, source_target_pairs={{0,24},{2,26},{4,28},{6,30},{8,0},{10,2},{12,4},{14,6},{16,8},{18,... | collective-permute-start | bytes 589832 | tf_op jit(solution)/shard_map/ppermute | solution.py:46
  68.2 15.5 %own_mlp.1 = (bf16[64,1536]{1,0:T(8,128)(2,1)}, bf16[64,1536]{1,0:T(8,128)(2,1)}, bf16[128,3456]{1,0:T(8,128)(2,1)}, bf16[128,3456]{1,0:T(8,128)(2,1)}, bf16[128,3456]{1,0:T(8,128)(2,1)}) custom-call(bf16[128,1536]{1,0:T(8,128)(2,1)} %copy-done.56, bf16[128,1536]{1,0:T(8,128)(2,1)} %get-tuple-element.97.refs_1_.refs_6_.refs_5_, ...), custom_call_target="tpu_custom_call" | custom-call | flops 108716360 | bytes 264437 | tf_op jit(solution)/shard_map/own_mlp/pallas_call | solution.py:397
  84.2 2.8 %collective-permute-start.17 = (bf16[128,1536]{1,0:T(8,128)(2,1)}, bf16[128,1536]{1,0:T(8,128)(2,1)S(1)}, u32[]{:S(2)}, u32[]{:S(2)}) collective-permute-start(bf16[128,1536]{1,0:T(8,128)(2,1)} %touch.15.refs_8_.refs_7_), channel_id=1, source_target_pairs={{0,8},{2,10},{4,12},{6,14},{8,16},{10,18},{12,20},{14,22},{16,24},... | collective-permute-start | bytes 1179656 | tf_op jit(solution)/shard_map/ppermute | solution.py:46
  88.4 2.1 pack.1.refs_0_
  91.3 4.0 %back.1 = (f32[128,1536]{1,0:T(8,128)}, bf16[128,1536]{1,0:T(8,128)(2,1)}, bf16[64,1536]{1,0:T(8,128)(2,1)}, f32[1,1536]{1,0:T(1,128)}, bf16[128,192]{1,0:T(8,12...) custom-call(bf16[256,1536]{1,0:T(8,128)(2,1)} %pack.1.refs_0_, ...), custom_call_target="tpu_custom_call" | custom-call | flops 3019898 | bytes 59105 | tf_op jit(solution)/shard_map/back/pallas_call | solution.py:88
  95.8 1.9 collective-permute-start.25
  100.3 2.8 %collective-permute-done.26 = bf16[128,192]{1,0:T(8,128)(2,1)S(1)} collective-permute-done((bf16[128,192]{1,0:T(8,128)(2,1)}, bf16[128,192]{1,0:T(8,128)(2,1)S(1)}, u32[]{:S(2)}, u32[]{:S(2)}) %collective-permute-start.26) | collective-permute-done | bytes 49184 | tf_op jit(solution)/shard_map/ppermute | solution.py:46
  105.6 1.6 collective-permute-start.27
  108.0 9.0 %attention_backward.1 = (f32[512,256]{1,0:T(8,128)}, bf16[512,128]{1,0:T(8,128)(2,1)}, bf16[512,128]{1,0:T(8,128)(2,1)}, bf16[512,128]{1,0:T(8,128)(2,1)}, bf16[512,128]{1,0:T(8,128)(2,1)}) custom-call(bf16[128,1536]{1,0:T(8,128)(2,1)} %copy-done.43, bf16[512,256]{1,0:T(8,128)(2,1)} %copy-done.17, f32[2,1024,256]{2,1,0:T(8,128)} %copy-done.2, ...), custom_call_target="tpu_custom_call" | custom-call | flops 20132660 | bytes 20971 | tf_op jit(solution)/shard_map/attention_backward/pallas_call | solution.py:325
  122.4 7.5 %down.1.refs_0_ = bf16[128,1536]{1,0:T(8,128)(2,1)} custom-call(f32[512,256]{1,0:T(8,128)} %get-tuple-element.106.refs_0_.refs_1_.refs_2_, bf16[128,3456]{1,0:T(8,128)(2,1)} %get-tuple-element.98.refs_1_.refs_0_.refs_16_.refs_15_, bf16[1536,3456]{1,0:T(8,128)(2,1)} %refs_20_.3), custom_call_target="tpu_custom_call" | custom-call | flops 27179088 | bytes 118947 | tf_op jit(solution)/shard_map/down/pallas_call | solution.py:397
  133.5 6.1 %head_grad.1 = (f32[1,384]{1,0:T(1,128)}, bf16[128,384]{1,0:T(8,128)(2,1)}, bf16[128,384]{1,0:T(8,128)(2,1)}, bf16[128,384]{1,0:T(8,128)(2,1)}, bf16[128,384]{1,...) custom-call(bf16[128,1536]{1,0:T(8,128)(2,1)} %down.1.refs_0_, ...), custom_call_target="tpu_custom_call" | custom-call | flops 9059696 | bytes 76697 | tf_op jit(solution)/shard_map/head_grad/pallas_call | solution.py:88
  144.5 1.6 collective-permute-start.44
  149.7 31.9 %bulk_mlp.2 = (f32[96,2048]{1,0:T(8,128)}, f32[96,2048]{1,0:T(8,128)}, f32[96,2048]{1,0:T(8,128)}, bf16[3,96,2048]{2,1,0:T(8,128)(2,1)}, bf16[192,1024]{1,0:T(8,128)(2,1)}, /*index=5*/bf16[192,1024]{1,0:T(8,128)(2,1)}) custom-call(f32[1,384]{1,0:T(1,128)} %get-tuple-element.115.refs_2_.refs_0_, s32[2]{0:T(128)} %copy-done.32, ...), custom_call_target="tpu_custom_call" | custom-call | flops 21743271936 | bytes 25165824 | tf_op jit(solution)/shard_map/bulk_mlp/pallas_call | solution.py:691
  181.6 2.2 collective-permute-start.49
  185.5 24.9 %bulk_mlp.3 = (f32[96,1408]{1,0:T(8,128)}, f32[96,1408]{1,0:T(8,128)}, f32[96,1408]{1,0:T(8,128)}, bf16[3,96,1408]{2,1,0:T(8,128)(2,1)}) custom-call(s32[2]{0:T(128)} %copy-done.32, bf16[256,1536]{1,0:T(8,128)(2,1)} %touch.18.refs_1_.refs_2_, bf16[256,1536]{1,0:T(8,128)(2,1)} %touch.19.refs_3_.refs_2_, bf16[256,1536]{1,0:T(8,128)(2,1)} %copy-done.80, ...), custom_call_target="tpu_custom_call" | custom-call | flops 14948499456 | bytes 19267584 | tf_op jit(solution)/shard_map/bulk_mlp/pallas_call | solution.py:691
  212.8 2.0 input_grad.1
  218.6 2.5 %spread.1 = (f32[96,512]{1,0:T(8,128)}, bf16[96,512]{1,0:T(8,128)(2,1)}, bf16[96,512]{1,0:T(8,128)(2,1)}, bf16[96,512]{1,0:T(8,128)(2,1)}) custom-call(f32[96,1408]{1,0:T(8,128)} %get-tuple-element.120.refs_1_.refs_0_.refs_3_, s32[2]{0:T(128)} %copy-done.32, bf16[384,512]{1,0:T(8,128)(2,1)} %get-tuple-element.127.refs_2_, bf16[384,512]{1,0:T(8,128)(2,1)} %copy-done.52, ...), custom_call_target="tpu_custom_call" | custom-call | bytes 20643 | tf_op jit(solution)/shard_map/spread/pallas_call | solution.py:88
  222.5 3.4 %collective-permute-done.57 = f32[3456]{0:T(1024)S(1)} collective-permute-done((f32[3456]{0:T(1024)}, f32[3456]{0:T(1024)S(1)}, u32[]{:S(2)}, u32[]{:S(2)}) %collective-permute-start.57) | collective-permute-done | bytes 13856 | tf_op jit(solution)/shard_map/ppermute | solution.py:46
  231.3 1.9 collective-permute-done.58
  233.2 1.7 collective-permute-start.52
  237.2 1.7 collective-permute-done.52.refs_4_
  241.9 6.1 %bulk_finish.1 = (f32[96,3456]{1,0:T(8,128)}, f32[96,3456]{1,0:T(8,128)}, f32[96,3456]{1,0:T(8,128)}) custom-call(f32[96,2048]{1,0:T(8,128)} %get-tuple-element.139.refs_0_, f32[96,2048]{1,0:T(8,128)} %get-tuple-element.140.refs_1_, f32[96,2048]{1,0:T(8,128)} %get-tuple-element.141.refs_2_, f32[96,1408]{1,0:T(8,128)} %get-tuple-element.120.refs_1_.refs_0_.refs_3_, ...), custom_call_target="tpu_custom_call" | custom-call | flops 3317 | bytes 99532 | tf_op jit(solution)/shard_map/bulk_finish/pallas_call | solution.py:738
  (310 shorter events, 72.2 us)
Async XLA Ops:
  1.7 10.0 %collective-permute-start.2 = (bf16[64,1536]{1,0:T(8,128)(2,1)S(1)}, bf16[64,1536]{1,0:T(8,128)(2,1)S(1)}, u32[]{:S(2)}, u32[]{:S(2)}) collective-permute-start(bf16[64,1536]{1,0:T(8,128)(2,1)S(1)} %dynamic-slice_bitcast_fusion), channel_id=1, source_target_pairs={{0,6},{2,4},{4,2},{6,0},{8,14},{10,12},{12,10},{14,8},{16,22},{18,... | collective-permute-start | bytes 589832 | tf_op jit(solution)/shard_map/ppermute | solution.py:46
  5.7 9.1 %collective-permute-start.1 = (bf16[64,1536]{1,0:T(8,128)(2,1)S(1)}, bf16[64,1536]{1,0:T(8,128)(2,1)S(1)}, u32[]{:S(2)}, u32[]{:S(2)}) collective-permute-start(bf16[64,1536]{1,0:T(8,128)(2,1)S(1)} %dynamic-slice_bitcast_fusion), channel_id=1, source_target_pairs={{0,4},{2,6},{4,0},{6,2},{8,12},{10,14},{12,8},{14,10},{16,20},{18,... | collective-permute-start | bytes 589832 | tf_op jit(solution)/shard_map/ppermute | solution.py:46
  22.1 23.8 %collective-permute-start.14 = (bf16[128,1536]{1,0:T(8,128)(2,1)S(1)}, bf16[128,1536]{1,0:T(8,128)(2,1)S(1)}, u32[]{:S(2)}, u32[]{:S(2)}) collective-permute-start(bf16[128,1536]{1,0:T(8,128)(2,1)S(1)} %get-tuple-element.95), channel_id=1, source_target_pairs={{0,0},{1,5},{2,2},{3,7},{4,4},{5,1},{6,6},{7,3},{8,8},{9,13},{10,1... | collective-permute-start | bytes 1179656 | tf_op jit(solution)/shard_map/ppermute | solution.py:859
  22.8 11.7 %collective-permute-start.8 = (bf16[512,128]{1,0:T(8,128)(2,1)S(1)}, bf16[512,128]{1,0:T(8,128)(2,1)S(1)}, u32[]{:S(2)}, u32[]{:S(2)}) collective-permute-start(bf16[512,128]{1,0:T(8,128)(2,1)S(1)} %get-tuple-element.85.refs_0_.refs_3_.refs_8_), channel_id=1, source_target_pairs={{0,24},{2,26},{4,28},{6,30},{8,0},{10,2},{12,4},{14,6},{16,8},{18,... | collective-permute-start | bytes 393224 | tf_op jit(solution)/shard_map/ppermute | solution.py:46
  26.6 12.1 %collective-permute-start.7 = (bf16[512,128]{1,0:T(8,128)(2,1)S(1)}, bf16[512,128]{1,0:T(8,128)(2,1)S(1)}, u32[]{:S(2)}, u32[]{:S(2)}) collective-permute-start(bf16[512,128]{1,0:T(8,128)(2,1)S(1)} %get-tuple-element.85.refs_0_.refs_3_.refs_8_), channel_id=1, source_target_pairs={{0,16},{2,18},{4,20},{6,22},{8,24},{10,26},{12,28},{14,30},{16,0},... | collective-permute-start | bytes 393224 | tf_op jit(solution)/shard_map/ppermute | solution.py:46
  26.6 12.1 %collective-permute-start.6 = (bf16[512,128]{1,0:T(8,128)(2,1)S(1)}, bf16[512,128]{1,0:T(8,128)(2,1)S(1)}, u32[]{:S(2)}, u32[]{:S(2)}) collective-permute-start(bf16[512,128]{1,0:T(8,128)(2,1)S(1)} %get-tuple-element.85.refs_0_.refs_3_.refs_8_), channel_id=1, source_target_pairs={{0,8},{2,10},{4,12},{6,14},{8,16},{10,18},{12,20},{14,22},{16,24},... | collective-permute-start | bytes 393224 | tf_op jit(solution)/shard_map/ppermute | solution.py:46
  46.7 15.9 %collective-permute-start.15 = (bf16[128,1536]{1,0:T(8,128)(2,1)}, bf16[128,1536]{1,0:T(8,128)(2,1)S(1)}, u32[]{:S(2)}, u32[]{:S(2)}) collective-permute-start(bf16[128,1536]{1,0:T(8,128)(2,1)} %touch.13.refs_7_.refs_6_), channel_id=1, source_target_pairs={{0,8},{2,10},{4,12},{6,14},{8,16},{10,18},{12,20},{14,22},{16,24},... | collective-permute-start | bytes 1179656 | tf_op jit(solution)/shard_map/ppermute | solution.py:46
  57.7 9.7 %collective-permute-start.16 = (bf16[128,1536]{1,0:T(8,128)(2,1)S(1)}, bf16[128,1536]{1,0:T(8,128)(2,1)S(1)}, u32[]{:S(2)}, u32[]{:S(2)}) collective-permute-start(bf16[128,1536]{1,0:T(8,128)(2,1)S(1)} %copy-done.55), channel_id=1, source_target_pairs={{0,1},{1,0},{2,3},{3,2},{4,5},{5,4},{6,7},{7,6},{8,9},{9,8},{10,11... | collective-permute-start | bytes 1179656 | tf_op jit(solution)/shard_map/ppermute | solution.py:50
  63.3 20.4 %collective-permute-start.21 = (bf16[128,1536]{1,0:T(8,128)(2,1)}, bf16[128,1536]{1,0:T(8,128)(2,1)S(1)}, u32[]{:S(2)}, u32[]{:S(2)}) collective-permute-start(bf16[128,1536]{1,0:T(8,128)(2,1)} %touch.14.refs_0_), channel_id=1, source_target_pairs={{0,1},{1,0},{2,3},{3,2},{4,5},{5,4},{6,7},{7,6},{8,9},{9,8},{10,11... | collective-permute-start | bytes 1179656 | tf_op jit(solution)/shard_map/ppermute | solution.py:50
  63.5 20.8 %collective-permute-start.20 = (bf16[64,1536]{1,0:T(8,128)(2,1)}, bf16[64,1536]{1,0:T(8,128)(2,1)S(1)}, u32[]{:S(2)}, u32[]{:S(2)}) collective-permute-start(bf16[64,1536]{1,0:T(8,128)(2,1)} %get-tuple-element.99.refs_1_), channel_id=1, source_target_pairs={{0,24},{2,26},{4,28},{6,30},{8,0},{10,2},{12,4},{14,6},{16,8},{18,... | collective-permute-start | bytes 589832 | tf_op jit(solution)/shard_map/ppermute | solution.py:46
  66.7 20.3 %collective-permute-start.19 = (bf16[64,1536]{1,0:T(8,128)(2,1)}, bf16[64,1536]{1,0:T(8,128)(2,1)S(1)}, u32[]{:S(2)}, u32[]{:S(2)}) collective-permute-start(bf16[64,1536]{1,0:T(8,128)(2,1)} %get-tuple-element.99.refs_1_), channel_id=1, source_target_pairs={{0,16},{2,18},{4,20},{6,22},{8,24},{10,26},{12,28},{14,30},{16,0},... | collective-permute-start | bytes 589832 | tf_op jit(solution)/shard_map/ppermute | solution.py:46
  67.4 19.6 %collective-permute-start.18 = (bf16[64,1536]{1,0:T(8,128)(2,1)}, bf16[64,1536]{1,0:T(8,128)(2,1)S(1)}, u32[]{:S(2)}, u32[]{:S(2)}) collective-permute-start(bf16[64,1536]{1,0:T(8,128)(2,1)} %get-tuple-element.99.refs_1_), channel_id=1, source_target_pairs={{0,8},{2,10},{4,12},{6,14},{8,16},{10,18},{12,20},{14,22},{16,24},... | collective-permute-start | bytes 589832 | tf_op jit(solution)/shard_map/ppermute | solution.py:46
  84.2 23.0 %collective-permute-start.17 = (bf16[128,1536]{1,0:T(8,128)(2,1)}, bf16[128,1536]{1,0:T(8,128)(2,1)S(1)}, u32[]{:S(2)}, u32[]{:S(2)}) collective-permute-start(bf16[128,1536]{1,0:T(8,128)(2,1)} %touch.15.refs_8_.refs_7_), channel_id=1, source_target_pairs={{0,8},{2,10},{4,12},{6,14},{8,16},{10,18},{12,20},{14,22},{16,24},... | collective-permute-start | bytes 1179656 | tf_op jit(solution)/shard_map/ppermute | solution.py:46
  103.7 13.3 %collective-permute-start.29 = (bf16[64,1536]{1,0:T(8,128)(2,1)}, bf16[64,1536]{1,0:T(8,128)(2,1)S(1)}, u32[]{:S(2)}, u32[]{:S(2)}) collective-permute-start(bf16[64,1536]{1,0:T(8,128)(2,1)} %touch.16), channel_id=1, source_target_pairs={{0,6},{2,4},{4,2},{6,0},{8,14},{10,12},{12,10},{14,8},{16,22},{18,... | collective-permute-start | bytes 589832 | tf_op jit(solution)/shard_map/ppermute | solution.py:46
  104.9 12.2 %collective-permute-start.28 = (bf16[64,1536]{1,0:T(8,128)(2,1)}, bf16[64,1536]{1,0:T(8,128)(2,1)S(1)}, u32[]{:S(2)}, u32[]{:S(2)}) collective-permute-start(bf16[64,1536]{1,0:T(8,128)(2,1)} %touch.16), channel_id=1, source_target_pairs={{0,4},{2,6},{4,0},{6,2},{8,12},{10,14},{12,8},{14,10},{16,20},{18,... | collective-permute-start | bytes 589832 | tf_op jit(solution)/shard_map/ppermute | solution.py:46
  105.6 11.4 %collective-permute-start.27 = (bf16[64,1536]{1,0:T(8,128)(2,1)}, bf16[64,1536]{1,0:T(8,128)(2,1)S(1)}, u32[]{:S(2)}, u32[]{:S(2)}) collective-permute-start(bf16[64,1536]{1,0:T(8,128)(2,1)} %touch.16), channel_id=1, source_target_pairs={{0,2},{2,0},{4,6},{6,4},{8,10},{10,8},{12,14},{14,12},{16,18},{18,... | collective-permute-start | bytes 589832 | tf_op jit(solution)/shard_map/ppermute | solution.py:46
  117.8 21.8 %collective-permute-start.30 = (bf16[256,1536]{1,0:T(8,128)(2,1)}, bf16[256,1536]{1,0:T(8,128)(2,1)S(1)}, u32[]{:S(2)}, u32[]{:S(2)}) collective-permute-start(bf16[256,1536]{1,0:T(8,128)(2,1)} %touch.17.refs_0_), channel_id=1, source_target_pairs={{0,4},{2,6},{4,0},{6,2},{8,12},{10,14},{12,8},{14,10},{16,20},{18,... | collective-permute-start | bytes 2359304 | tf_op jit(solution)/shard_map/ppermute | solution.py:46
  118.6 11.3 %collective-permute-start.31 = (bf16[64,1536]{1,0:T(8,128)(2,1)}, bf16[64,1536]{1,0:T(8,128)(2,1)S(1)}, u32[]{:S(2)}, u32[]{:S(2)}) collective-permute-start(bf16[64,1536]{1,0:T(8,128)(2,1)} %copy-done.47), channel_id=1, source_target_pairs={{0,1},{1,0},{2,3},{3,2},{4,5},{5,4},{6,7},{7,6},{8,9},{9,8},{10,11... | collective-permute-start | bytes 589832 | tf_op jit(solution)/shard_map/ppermute | solution.py:50
  118.6 12.8 %collective-permute-start.34 = (bf16[512,128]{1,0:T(8,128)(2,1)S(1)}, bf16[512,128]{1,0:T(8,128)(2,1)S(1)}, u32[]{:S(2)}, u32[]{:S(2)}) collective-permute-start(bf16[512,128]{1,0:T(8,128)(2,1)S(1)} %copy-done.86), channel_id=1, source_target_pairs={{0,24},{2,26},{4,28},{6,30},{8,0},{10,2},{12,4},{14,6},{16,8},{18,... | collective-permute-start | bytes 393224 | tf_op jit(solution)/shard_map/ppermute | solution.py:46
  120.0 12.9 %collective-permute-start.35 = (bf16[512,128]{1,0:T(8,128)(2,1)S(1)}, bf16[512,128]{1,0:T(8,128)(2,1)S(1)}, u32[]{:S(2)}, u32[]{:S(2)}) collective-permute-start(bf16[512,128]{1,0:T(8,128)(2,1)S(1)} %copy-done.85), channel_id=1, source_target_pairs={{0,16},{2,18},{4,20},{6,22},{8,24},{10,26},{12,28},{14,30},{16,0},... | collective-permute-start | bytes 393224 | tf_op jit(solution)/shard_map/ppermute | solution.py:46
  121.4 11.4 %collective-permute-start.36 = (bf16[512,128]{1,0:T(8,128)(2,1)S(1)}, bf16[512,128]{1,0:T(8,128)(2,1)S(1)}, u32[]{:S(2)}, u32[]{:S(2)}) collective-permute-start(bf16[512,128]{1,0:T(8,128)(2,1)S(1)} %copy-done.84), channel_id=1, source_target_pairs={{0,8},{2,10},{4,12},{6,14},{8,16},{10,18},{12,20},{14,22},{16,24},... | collective-permute-start | bytes 393224 | tf_op jit(solution)/shard_map/ppermute | solution.py:46
  129.9 12.8 %collective-permute-start.39 = (bf16[128,1536]{1,0:T(8,128)(2,1)S(1)}, bf16[128,1536]{1,0:T(8,128)(2,1)S(1)}, u32[]{:S(2)}, u32[]{:S(2)}) collective-permute-start(bf16[128,1536]{1,0:T(8,128)(2,1)S(1)} %copy-done.44), channel_id=1, source_target_pairs={{0,8},{2,10},{4,12},{6,14},{8,16},{10,18},{12,20},{14,22},{16,24},... | collective-permute-start | bytes 1179656 | tf_op jit(solution)/shard_map/ppermute | solution.py:46
  142.7 39.0 %collective-permute-start.43 = (bf16[128,384]{1,0:T(8,128)(2,1)}, bf16[128,384]{1,0:T(8,128)(2,1)S(1)}, u32[]{:S(2)}, u32[]{:S(2)}) collective-permute-start(bf16[128,384]{1,0:T(8,128)(2,1)} %get-tuple-element.123), channel_id=1, source_target_pairs={{0,2},{2,0},{4,6},{6,4},{8,10},{10,8},{12,14},{14,12},{16,18},{18,... | collective-permute-start | bytes 294920 | tf_op jit(solution)/shard_map/ppermute | solution.py:46
  144.5 39.4 %collective-permute-start.44 = (bf16[128,384]{1,0:T(8,128)(2,1)}, bf16[128,384]{1,0:T(8,128)(2,1)S(1)}, u32[]{:S(2)}, u32[]{:S(2)}) collective-permute-start(bf16[128,384]{1,0:T(8,128)(2,1)} %get-tuple-element.124), channel_id=1, source_target_pairs={{0,4},{2,6},{4,0},{6,2},{8,12},{10,14},{12,8},{14,10},{16,20},{18,... | collective-permute-start | bytes 294920 | tf_op jit(solution)/shard_map/ppermute | solution.py:46
  146.1 37.8 %collective-permute-start.45 = (bf16[128,384]{1,0:T(8,128)(2,1)}, bf16[128,384]{1,0:T(8,128)(2,1)S(1)}, u32[]{:S(2)}, u32[]{:S(2)}) collective-permute-start(bf16[128,384]{1,0:T(8,128)(2,1)} %get-tuple-element.125), channel_id=1, source_target_pairs={{0,6},{2,4},{4,2},{6,0},{8,14},{10,12},{12,10},{14,8},{16,22},{18,... | collective-permute-start | bytes 294920 | tf_op jit(solution)/shard_map/ppermute | solution.py:46
  147.4 67.4 %collective-permute-start.47 = (bf16[384,512]{1,0:T(8,128)(2,1)}, bf16[384,512]{1,0:T(8,128)(2,1)S(1)}, u32[]{:S(2)}, u32[]{:S(2)}) collective-permute-start(bf16[384,512]{1,0:T(8,128)(2,1)} %get-tuple-element.128), channel_id=1, source_target_pairs={{0,24},{2,26},{4,28},{6,30},{8,0},{10,2},{12,4},{14,6},{16,8},{18,... | collective-permute-start | bytes 1179656 | tf_op jit(solution)/shard_map/ppermute | solution.py:46
  148.7 66.3 %collective-permute-start.48 = (bf16[384,512]{1,0:T(8,128)(2,1)}, bf16[384,512]{1,0:T(8,128)(2,1)S(1)}, u32[]{:S(2)}, u32[]{:S(2)}) collective-permute-start(bf16[384,512]{1,0:T(8,128)(2,1)} %get-tuple-element.129), channel_id=1, source_target_pairs={{0,16},{2,18},{4,20},{6,22},{8,24},{10,26},{12,28},{14,30},{16,0},... | collective-permute-start | bytes 1179656 | tf_op jit(solution)/shard_map/ppermute | solution.py:46
  181.6 36.0 %collective-permute-start.49 = (bf16[384,512]{1,0:T(8,128)(2,1)}, bf16[384,512]{1,0:T(8,128)(2,1)}, u32[]{:S(2)}, u32[]{:S(2)}) collective-permute-start(bf16[384,512]{1,0:T(8,128)(2,1)} %get-tuple-element.130), channel_id=1, source_target_pairs={{0,8},{2,10},{4,12},{6,14},{8,16},{10,18},{12,20},{14,22},{16,24},... | collective-permute-start | bytes 1179656 | tf_op jit(solution)/shard_map/ppermute | solution.py:46
  184.6 57.3 %collective-permute-start.53 = (bf16[3,96,2048]{2,1,0:T(8,128)(2,1)}, bf16[3,96,2048]{2,1,0:T(8,128)(2,1)}, u32[]{:S(2)}, u32[]{:S(2)}) collective-permute-start(bf16[3,96,2048]{2,1,0:T(8,128)(2,1)} %touch.22), channel_id=1, source_target_pairs={{0,2},{2,0},{4,6},{6,4},{8,10},{10,8},{12,14},{14,12},{16,18},{18,... | collective-permute-start | bytes 3538952 | tf_op jit(solution)/shard_map/ppermute | solution.py:46
  210.4 31.5 %collective-permute-start.54 = (bf16[3,96,1408]{2,1,0:T(8,128)(2,1)}, bf16[3,96,1408]{2,1,0:T(8,128)(2,1)}, u32[]{:S(2)}, u32[]{:S(2)}) collective-permute-start(bf16[3,96,1408]{2,1,0:T(8,128)(2,1)} %get-tuple-element.145), channel_id=1, source_target_pairs={{0,2},{2,0},{4,6},{6,4},{8,10},{10,8},{12,14},{14,12},{16,18},{18,... | collective-permute-start | bytes 2433032 | tf_op jit(solution)/shard_map/ppermute | solution.py:46
  215.0 12.3 %collective-permute-start.42 = (bf16[128,1536]{1,0:T(8,128)(2,1)}, bf16[128,1536]{1,0:T(8,128)(2,1)S(1)}, u32[]{:S(2)}, u32[]{:S(2)}) collective-permute-start(bf16[128,1536]{1,0:T(8,128)(2,1)} %touch.21.refs_1_), channel_id=1, source_target_pairs={{0,1},{1,0},{2,3},{3,2},{4,5},{5,4},{6,7},{7,6},{8,9},{9,8},{10,11... | collective-permute-start | bytes 1179656 | tf_op jit(solution)/shard_map/ppermute | solution.py:50
  216.7 13.4 %collective-permute-start.46 = (bf16[128,1536]{1,0:T(8,128)(2,1)S(1)}, bf16[128,1536]{1,0:T(8,128)(2,1)S(1)}, u32[]{:S(2)}, u32[]{:S(2)}) collective-permute-start(bf16[128,1536]{1,0:T(8,128)(2,1)S(1)} %get-tuple-element.126.refs_2_), channel_id=1, source_target_pairs={{0,1},{1,0},{2,3},{3,2},{4,5},{5,4},{6,7},{7,6},{8,9},{9,8},{10,11... | collective-permute-start | bytes 1179656 | tf_op jit(solution)/shard_map/ppermute | solution.py:50
  (115 other events, 730.0 us)
